TPU v7x, 32 devices: a whole 2x2x4 slice. The times are simulated.
32 devices in a mesh: parts: 2 (over y), lat: 4 (over z), chan: 2 (over x), rep: 2 (over core).
Axes of the slice: x: 2, y: 2, z: 4, core: 2. Of those that a mesh axis runs over, the one named last changes fastest.
Arguments:
- field: bfloat16 [4, 32, 1440, 256], P(('parts', 'rep'), ('lat', 'chan')), parts along dimension 0, may hold values from -6 to 6
- cotangent: bfloat16 [4, 32, 1440, 256], P(('parts', 'rep'), ('lat', 'chan')), parts along dimension 0, may hold values from -6 to 6
- weights: bfloat16 [2, 128, 256, 256], P(None, 'lat', 'chan'), may hold values from -0.25 to 0.25
Outputs:
- grad_field: bfloat16 [4, 32, 1440, 256], P(('parts', 'rep'), ('lat', 'chan')), parts along dimension 0
- weight_grad: float32 [4, 128, 256, 256], P('parts', 'lat', 'chan'), parts along dimension 0
There are 2 independent parts, one for each index of `parts`. A program takes and returns all parts, laid end to end along the dimension named above; an argument that names none is the same for every part. Nothing has to cross between parts.
All inputs are finite; a program needn't handle non-finite values.
Results may differ from a plain program's by a relative error of at most 0.0077.
Values may be sent and summed in bfloat16 or wider, within the bound.
No kernel may reach another device: no remote copies, remote signals or barrier semaphores. Data moves between devices by JAX's collectives and lax.ppermute only.
A program may use at most 128 MiB of HBM per device.

v0:
```python
import math

import jax
import jax.numpy as jnp
from jax import lax
from jax.sharding import PartitionSpec as P

M = 128
LON = 1440


inv_sqrt_two = 0.7071067811865476
inv_sqrt_two_pi = 0.3989422804014327


def tables():
    lon_index = jnp.arange(LON, dtype=jnp.int32)
    mode_index = jnp.arange(M, dtype=jnp.int32)
    phase_angle = (mode_index[:, None] * lon_index[None, :] % LON).astype(jnp.float32) * (
        2.0 * math.pi / LON
    )
    norm_scale = 1.0 / math.sqrt(LON)
    mode_weight = jnp.where(mode_index == 0, 1.0, 2.0).astype(jnp.float32)[:, None]
    cosine = jnp.cos(phase_angle)
    sine_part = jnp.sin(phase_angle)
    forward_table = (jnp.stack([cosine.T, -sine_part.T], axis=1) * norm_scale).astype(jnp.bfloat16)
    inverse_table = (
        jnp.stack([mode_weight * cosine, -mode_weight * sine_part], axis=0) * norm_scale
    ).astype(jnp.bfloat16)
    return (forward_table, inverse_table)


def gelu_slope(values):
    cumulative = 0.5 * (1.0 + lax.erf(values * inv_sqrt_two))
    return cumulative + values * jnp.exp(-0.5 * values * values) * inv_sqrt_two_pi


def full_channels(blocks):
    return lax.all_gather(blocks, "chan", axis=1, tiled=True)


def spectral_terms(grad_split, weights):
    terms = jnp.einsum(
        "sqirjmo,kmoc->jksqirmc", grad_split, weights, preferred_element_type=jnp.float32
    )
    part_real = terms[0, 0] + terms[1, 1]
    part_imag = terms[1, 0] - terms[0, 1]
    return jnp.stack([part_real, part_imag], axis=4)


def shards(field, cotangent, weights):
    forward_table, inverse_table = tables()
    n_lat = lax.axis_size("lat")
    n_chan = lax.axis_size("chan")
    spectrum = jnp.einsum(
        "salc,lkm->sakmc", field, forward_table, preferred_element_type=jnp.float32
    ).astype(jnp.bfloat16)
    samples = spectrum.shape[0]
    rows_dev = spectrum.shape[1]
    gathered = full_channels(spectrum)
    moved = lax.all_to_all(gathered, "lat", split_axis=3, concat_axis=1, tiled=True)
    shaped = moved.reshape(samples, n_lat, n_chan, rows_dev, 2, moved.shape[3], moved.shape[4])
    modal = jnp.swapaxes(shaped, 1, 2).reshape(
        samples, n_chan * n_lat * rows_dev, 2, moved.shape[3], moved.shape[4]
    )
    mode_count = modal.shape[3]
    width = modal.shape[4]
    modal_split = modal.reshape(samples, n_chan, n_lat, rows_dev, 2, mode_count, width)
    products = jnp.einsum(
        "sqirkmc,jmoc->kjsqirmo", modal_split, weights, preferred_element_type=jnp.float32
    )
    mixed_real = products[0, 0] - products[1, 1]
    mixed_imag = products[0, 1] + products[1, 0]
    mixed = jnp.stack([mixed_real, mixed_imag], axis=4).astype(jnp.bfloat16)
    returned = lax.all_to_all(
        lax.all_to_all(mixed, "lat", split_axis=2, concat_axis=5, tiled=True),
        "chan",
        split_axis=1,
        concat_axis=1,
        tiled=True,
    )
    spatial = jnp.einsum(
        "sgxrkmo,kml->srlgo", returned, inverse_table, preferred_element_type=jnp.float32
    ).reshape(field.shape)
    scaled = (cotangent.astype(jnp.float32) * gelu_slope(spatial)).astype(jnp.bfloat16)
    grad_mixed = jnp.einsum(
        "salc,kml->sakmc", scaled, inverse_table, preferred_element_type=jnp.float32
    ).astype(jnp.bfloat16)
    grad_modal = lax.all_to_all(
        lax.all_to_all(grad_mixed, "lat", split_axis=3, concat_axis=1, tiled=True),
        "chan",
        split_axis=4,
        concat_axis=1,
        tiled=True,
    )
    outer = jnp.einsum("sakmc,sajmo->kjmoc", modal, grad_modal, preferred_element_type=jnp.float32)
    rows_total = modal.shape[1]
    local_grad = (
        jnp.stack([outer[0, 0] + outer[1, 1], outer[0, 1] - outer[1, 0]], axis=0) / rows_total
    )
    weight_grad = lax.psum(local_grad, "rep")
    grad_split = grad_modal.reshape(
        samples, n_chan, n_lat, rows_dev, 2, mode_count, grad_modal.shape[4]
    )
    summed = lax.psum_scatter(
        jnp.moveaxis(spectral_terms(grad_split, weights), 1, 0),
        "chan",
        scatter_dimension=0,
        tiled=True,
    )
    own_rows = summed[0].astype(jnp.bfloat16)
    arrived = lax.all_to_all(own_rows, "lat", split_axis=1, concat_axis=4, tiled=True)
    grad_spectrum = arrived.reshape(samples, rows_dev, 2, arrived.shape[4], arrived.shape[5])
    spatial_grad = jnp.einsum(
        "sakmc,lkm->salc", grad_spectrum, forward_table, preferred_element_type=jnp.float32
    )
    grad_field = (cotangent.astype(jnp.float32) + spatial_grad).astype(jnp.bfloat16)
    return (grad_field, weight_grad)


def solution(mesh):
    placed = (
        P(("parts", "rep"), ("lat", "chan"), None, None),
        P(("parts", "rep"), ("lat", "chan"), None, None),
        P(None, "lat", "chan", None),
    )
    return jax.shard_map(
        shards,
        mesh=mesh,
        in_specs=placed,
        out_specs=(
            P(("parts", "rep"), ("lat", "chan"), None, None),
            P("parts", "lat", "chan", None),
        ),
        check_vma=False,
    )
```

profile of v0, /device:TPU:0, one launch (start us, length us, event | category | flops | bytes accessed | tf_op | source)
XLA Modules:
  0.0 239.0 jit_solution(8877032321056773839)
XLA Ops:
  7.2 3.1 %sine_negate_fusion = (f32[1440,1,128]{2,0,1:T(8,128)S(1)}, f32[1440,1,128]{2,0,1:T(8,128)S(1)}) fusion(), kind=kLoop, calls=%fused_computation.62 | loop fusion | flops 1843200 | bytes 1474560 | tf_op jit(solution)/shard_map/neg | solution.py:26
  10.3 0.8 copy-done.2
  11.2 0.2 copy-done.4
  11.4 1.8 fusion.35
  13.2 24.2 %all-gather.2.cloned.1.call-done = bf16[1,8,2,128,256]{4,3,1,2,0:T(8,128)(2,1)} async-done(((bf16[1,4,2,128,256]{4,3,1,2,0:T(8,128)(2,1)}), bf16[1,8,2,128,256]{4,3,1,2,0:T(8,128)(2,1)}) %all-gather.2.cloned.1.call-update) | async-done | bytes 1048592 | tf_op jit(solution)/shard_map/all_gather | solution.py:39
  37.4 2.0 copy.65
  39.4 30.1 %all_to_all.86 = bf16[1,8,2,128,256]{4,1,2,0,3:T(8,128)(2,1)S(1)} all-to-all(bf16[1,8,2,128,256]{4,1,2,0,3:T(8,128)(2,1)S(1)} %copy.65), channel_id=1, replica_groups=mesh['parts'=2,'lat'=4,'chan'=2,'rep'=2] {'lat'}, dimensions={3} | all-to-all | bytes 2097152 | tf_op jit(solution)/shard_map/all_to_all | solution.py:61
  69.5 0.3 copy.66
  69.8 1.3 fusion.21
  71.3 0.1 fusion.65
  71.5 0.4 pad_maximum_fusion
  71.8 1.0 copy.72
  72.8 3.5 %all-to-all-start.1 = ((bf16[1,2,4,4,2,32,128]{6,3,1,5,4,0,2:T(4,128)(2,1)}), bf16[1,2,4,4,2,32,128]{6,3,1,5,4,0,2:T(4,128)(2,1)S(1)}, u32[]{:S(2)}, u32[]{:S(2)}) async-start(bf16[1,2,4,4,2,32,128]{6,3,1,5,4,0,2:T(4,128)(2,1)} %copy.72), calls=%async_computation.1 | async-start | bytes 1048576 | tf_op jit(solution)/shard_map/all_to_all | solution.py:76
  76.3 13.6 %all-to-all-done.1 = bf16[1,2,4,4,2,32,128]{6,3,1,5,4,0,2:T(4,128)(2,1)S(1)} async-done(((bf16[1,2,4,4,2,32,128]{6,3,1,5,4,0,2:T(4,128)(2,1)}), bf16[1,2,4,4,2,32,128]{6,3,1,5,4,0,2:T(4,128)(2,1)S(1)}, u32[]{:S(2)}, u32[]{:S(2)}) %all-to-all-start.1) | async-done | bytes 524320 | tf_op jit(solution)/shard_map/all_to_all | solution.py:76
  89.9 0.9 copy.73
  90.8 3.5 %all-to-all-start.2 = ((bf16[1,2,1,4,2,128,128]{6,5,4,3,2,0,1:T(8,128)(2,1)}), bf16[1,2,1,4,2,128,128]{6,5,4,3,2,0,1:T(8,128)(2,1)S(1)}, u32[]{:S(2)}, u32[]{:S(2)}) async-start(bf16[1,2,1,4,2,128,128]{6,5,4,3,2,0,1:T(8,128)(2,1)} %bitcast.28), calls=%async_computation.2 | async-start | bytes 1048576 | tf_op jit(solution)/shard_map/all_to_all | solution.py:75
  94.3 0.2 reduce-scatter.2.cloned.1.call-start
  94.6 3.1 %sine_multiply_fusion = (f32[1,128,1440]{1,2,0:T(8,128)S(1)}, f32[1,128,1440]{1,2,0:T(8,128)S(1)}) fusion(f32[128]{0:T(128)S(1)} %fusion.70, f32[128]{0:T(128)S(1)} %compare_select_fusion), kind=kLoop, calls=%fused_computation.57 | loop fusion | flops 2027520 | bytes 1475584 | tf_op jit(solution)/shard_map/mul | solution.py:28
  97.7 4.1 %all-to-all-done.2 = bf16[1,2,1,4,2,128,128]{6,5,4,3,2,0,1:T(8,128)(2,1)S(1)} async-done(((bf16[1,2,1,4,2,128,128]{6,5,4,3,2,0,1:T(8,128)(2,1)}), bf16[1,2,1,4,2,128,128]{6,5,4,3,2,0,1:T(8,128)(2,1)S(1)}, u32[]{:S(2)}, u32[]{:S(2)}) %all-to-all-start.2) | async-done | bytes 524320 | tf_op jit(solution)/shard_map/all_to_all | solution.py:75
  101.8 0.9 convolution_bitcast_fusion.1
  102.7 6.9 %copy.75 = f32[1,4,1440,2,128]{4,3,0,2,1:T(2,128)S(1)} copy(f32[1,4,1440,2,128]{4,2,1,3,0:T(8,128)S(1)} %convolution_bitcast_fusion.1) | data formatting | bytes 11796480 | tf_op jit(solution)/shard_map/sgxrkmo,kml->srlgo/transpose | solution.py:82
  109.7 3.1 %fusion.32 = bf16[1,4,2,128,256]{4,3,1,2,0:T(8,128)(2,1)S(1)} fusion(f32[1,4,1440,256]{3,0,2,1:T(1,128)S(1)} %bitcast.181, bf16[1,4,1440,256]{3,2,1,0:T(8,128)(2,1)S(1)} %copy-done.8, f32[1,128,1440]{1,2,0:T(8,128)S(1)} %copy-done.11, f32[1,128,1440]{1,2,0:T(8,128)S(1)} %copy-done.13), kind=kOutput, calls=%fused_computation.35 | convolution fusion | flops 772562944 | bytes 10846208 | tf_op jit(solution)/shard_map/salc,kml->sakmc/dot_general | solution.py:86
  112.9 0.4 copy.80
  113.3 15.5 %all_to_all.87 = bf16[1,4,2,128,256]{4,1,2,0,3:T(4,128)(2,1)S(1)} all-to-all(bf16[1,4,2,128,256]{4,1,2,0,3:T(4,128)(2,1)S(1)} %copy.80), channel_id=1, replica_groups=mesh['parts'=2,'lat'=4,'chan'=2,'rep'=2] {'lat'}, dimensions={3} | all-to-all | bytes 1048576 | tf_op jit(solution)/shard_map/all_to_all | solution.py:90
  128.9 1.9 copy.83
  130.8 2.1 reshape.502
  132.9 9.3 %all_to_all.88 = bf16[2,2,65536]{2,1,0:T(2,128)(2,1)S(1)} all-to-all(bf16[2,2,65536]{2,1,0:T(2,128)(2,1)S(1)} %reshape.502), channel_id=1, replica_groups=mesh['parts'=2,'lat'=4,'chan'=2,'rep'=2] {'chan'}, dimensions={0} | all-to-all | bytes 1048576 | tf_op jit(solution)/shard_map/all_to_all | solution.py:89
  142.1 1.0 reshape.503
  143.1 1.9 copy.113
  145.1 3.2 %fusion.18 = f32[2,2,1,2,4,4,32,256]{7,5,1,0,4,3,6,2:T(4,128)S(1)} fusion(bf16[2,4,4,2,32,128,1]{5,0,4,3,2,1,6:T(2,128)(2,1)S(1)} %bitcast.182, bf16[2,32,128,256]{3,2,1,0:T(8,128)(2,1)} %param.5), kind=kOutput, calls=%fused_computation.26 | convolution fusion | flops 268435456 | bytes 8912896 | tf_op jit(solution)/shard_map/sqirjmo,kmoc->jksqirmc/dot_general | solution.py:43
  148.3 0.3 fusion.38
  148.6 0.4 fusion.40
  149.0 0.5 maximum_bitcast_fusion
  149.5 2.5 %copy.90 = f32[2,1,4,4,2,32,256]{6,5,4,3,2,1,0:T(8,128)} copy(f32[2,1,4,4,2,32,256]{6,3,2,0,5,4,1:T(4,128)S(1)} %maximum_bitcast_fusion) | data formatting | bytes 4194304 | tf_op jit(solution)/shard_map/transpose | solution.py:106
  152.1 2.0 copy.153
  154.2 0.6 copy.94
  154.8 0.6 copy.93
  155.4 2.4 convolution_bitcast_fusion
  157.8 0.7 fusion.6
  158.5 0.7 fusion.8
  159.2 4.5 %maximum_multiply_fusion = f32[2,32,128,256]{3,2,1,0:T(8,128)} fusion(f32[1,32,128,256]{3,2,1,0:T(8,128)S(1)} %fusion.6, f32[1,32,128,256]{3,2,1,0:T(8,128)S(1)} %fusion.8), kind=kLoop, calls=%fused_computation.2 | loop fusion | flops 4194304 | bytes 16777216 | tf_op jit(solution)/shard_map/div | solution.py:99
  163.8 18.7 %reduce-scatter.2.cloned.1.call-done = f32[1,1,4,4,2,32,256]{6,5,4,3,2,1,0:T(8,128)} async-done(((f32[2,1,4,4,2,32,256]{6,5,4,3,2,1,0:T(8,128)}), f32[1,1,4,4,2,32,256]{6,5,4,3,2,1,0:T(8,128)}) %reduce-scatter.2.cloned.1.call-update) | async-done | bytes 1048592 | tf_op jit(solution)/shard_map/reduce_scatter | solution.py:105
  182.5 1.4 convert_bitcast_fusion
  184.0 0.4 copy.91
  184.4 18.9 %all_to_all.89 = bf16[1,4,4,2,32,256]{5,2,4,3,0,1:T(4,128)(2,1)S(1)} all-to-all(bf16[1,4,4,2,32,256]{5,2,4,3,0,1:T(4,128)(2,1)S(1)} %copy.91), channel_id=1, replica_groups=mesh['parts'=2,'lat'=4,'chan'=2,'rep'=2] {'lat'}, dimensions={1} | all-to-all | bytes 1048576 | tf_op jit(solution)/shard_map/all_to_all | solution.py:112
  203.4 2.5 %fusion.1 = bf16[1,4,1440,256]{3,2,1,0:T(8,128)(2,1)} fusion(bf16[1,4,1440,256]{3,2,1,0:T(8,128)(2,1)S(1)} %copy-done.9, bf16[4,2,128,256]{3,2,1,0:T(8,128)(2,1)S(1)} %bitcast.191, f32[1440,1,128]{2,0,1:T(8,128)S(1)} %copy-done.3, f32[1440,1,128]{2,0,1:T(8,128)S(1)} %copy-done.5), kind=kOutput, calls=%fused_computation.6 | convolution fusion | flops 760504320 | bytes 7897088 | tf_op jit(solution)/shard_map/sakmc,lkm->salc/dot_general | solution.py:114
  205.9 18.7 %all-reduce.2.cloned.1.call-done = f32[2,32,128,256]{3,2,1,0:T(8,128)} async-done(((f32[2,32,128,256]{3,2,1,0:T(8,128)}), f32[2,32,128,256]{3,2,1,0:T(8,128)}) %all-reduce.2.cloned.1.call-update) | async-done | bytes 8388624 | tf_op jit(solution)/shard_map/psum | solution.py:101
  224.6 7.9 %copy.155 = f32[2,32,128,256]{3,2,1,0:T(8,128)} copy(f32[2,32,128,256]{3,2,1,0:T(8,128)} %all-reduce.2.cloned.1.call-done) | data formatting | bytes 16777216
  (37 shorter events, 0.6 us)
Async XLA Ops:
  7.2 4.2 %copy-start = (bf16[1,4,1440,256]{3,2,1,0:T(8,128)(2,1)S(1)}, bf16[1,4,1440,256]{3,2,1,0:T(8,128)(2,1)}, u32[]{:S(2)}) copy-start(bf16[1,4,1440,256]{3,2,1,0:T(8,128)(2,1)} %param.3) | copy-start | bytes 8847364
  7.2 30.2 %all-gather.2.cloned.1.call-start = ((), (), s32[]{:S(2)}) async-start(), calls=%async_computation.7 | async-start | bytes 1572864 | tf_op jit(solution)/shard_map/all_gather | solution.py:39
  10.3 0.9 copy-start.2
  10.3 1.1 copy-start.4
  37.4 32.4 %copy-start.6 = (bf16[2,32,128,256]{3,2,1,0:T(8,128)(2,1)S(1)}, bf16[2,32,128,256]{3,2,1,0:T(8,128)(2,1)}, u32[]{:S(2)}) copy-start(bf16[2,32,128,256]{3,2,1,0:T(8,128)(2,1)} %param.5) | copy-start | bytes 12582916
  69.8 1.5 copy-start.7
  72.8 17.1 %all-to-all-start.1 = ((bf16[1,2,4,4,2,32,128]{6,3,1,5,4,0,2:T(4,128)(2,1)}), bf16[1,2,4,4,2,32,128]{6,3,1,5,4,0,2:T(4,128)(2,1)S(1)}, u32[]{:S(2)}, u32[]{:S(2)}) async-start(bf16[1,2,4,4,2,32,128]{6,3,1,5,4,0,2:T(4,128)(2,1)} %copy.72), calls=%async_computation.1 | async-start | bytes 1048576 | tf_op jit(solution)/shard_map/all_to_all | solution.py:76
  90.8 10.9 %all-to-all-start.2 = ((bf16[1,2,1,4,2,128,128]{6,5,4,3,2,0,1:T(8,128)(2,1)}), bf16[1,2,1,4,2,128,128]{6,5,4,3,2,0,1:T(8,128)(2,1)S(1)}, u32[]{:S(2)}, u32[]{:S(2)}) async-start(bf16[1,2,1,4,2,128,128]{6,5,4,3,2,0,1:T(8,128)(2,1)} %bitcast.28), calls=%async_computation.2 | async-start | bytes 1048576 | tf_op jit(solution)/shard_map/all_to_all | solution.py:75
  94.3 88.2 %reduce-scatter.2.cloned.1.call-start = ((), (), s32[]{:S(2)}) async-start(), calls=%async_computation.8 | async-start | bytes 3145728 | tf_op jit(solution)/shard_map/reduce_scatter | solution.py:105
  97.7 4.1 %copy-start.10 = (f32[1,128,1440]{1,2,0:T(8,128)}, f32[1,128,1440]{1,2,0:T(8,128)S(1)}, u32[]{:S(2)}) copy-start(f32[1,128,1440]{1,2,0:T(8,128)S(1)} %get-tuple-element.4) | copy-start | bytes 2211844
  97.7 4.1 %copy-start.12 = (f32[1,128,1440]{1,2,0:T(8,128)}, f32[1,128,1440]{1,2,0:T(8,128)S(1)}, u32[]{:S(2)}) copy-start(f32[1,128,1440]{1,2,0:T(8,128)S(1)} %get-tuple-element.5) | copy-start | bytes 2211844
  102.7 7.0 %copy-start.8 = (bf16[1,4,1440,256]{3,2,1,0:T(8,128)(2,1)S(1)}, bf16[1,4,1440,256]{3,2,1,0:T(8,128)(2,1)}, u32[]{:S(2)}) copy-start(bf16[1,4,1440,256]{3,2,1,0:T(8,128)(2,1)} %param.4) | copy-start | bytes 8847364
  102.7 7.0 %copy-start.11 = (f32[1,128,1440]{1,2,0:T(8,128)S(1)}, f32[1,128,1440]{1,2,0:T(8,128)}, u32[]{:S(2)}) copy-start(f32[1,128,1440]{1,2,0:T(8,128)} %copy-done.10) | copy-start | bytes 2211844
  102.7 7.0 %copy-start.13 = (f32[1,128,1440]{1,2,0:T(8,128)S(1)}, f32[1,128,1440]{1,2,0:T(8,128)}, u32[]{:S(2)}) copy-start(f32[1,128,1440]{1,2,0:T(8,128)} %copy-done.12) | copy-start | bytes 2211844
  152.1 72.5 %all-reduce.2.cloned.1.call-start = ((), (), s32[]{:S(2)}) async-start(), calls=%async_computation.9 | async-start | bytes 16777216 | tf_op jit(solution)/shard_map/psum | solution.py:101
  163.7 39.6 %copy-start.3 = (f32[1440,1,128]{2,0,1:T(8,128)S(1)}, f32[1440,1,128]{2,0,1:T(8,128)}, u32[]{:S(2)}) copy-start(f32[1440,1,128]{2,0,1:T(8,128)} %copy-done.2) | copy-start | bytes 2211844
  163.8 39.6 %copy-start.5 = (f32[1440,1,128]{2,0,1:T(8,128)S(1)}, f32[1440,1,128]{2,0,1:T(8,128)}, u32[]{:S(2)}) copy-start(f32[1440,1,128]{2,0,1:T(8,128)} %copy-done.4) | copy-start | bytes 2211844
  182.5 20.9 %copy-start.9 = (bf16[1,4,1440,256]{3,2,1,0:T(8,128)(2,1)S(1)}, bf16[1,4,1440,256]{3,2,1,0:T(8,128)(2,1)}, u32[]{:S(2)}) copy-start(bf16[1,4,1440,256]{3,2,1,0:T(8,128)(2,1)} %param.4) | copy-start | bytes 8847364
  224.6 7.9 %copy-start.1 = (bf16[1,4,1440,256]{3,2,1,0:T(8,128)(2,1)S(1)}, bf16[1,4,1440,256]{3,2,1,0:T(8,128)(2,1)}, u32[]{:S(2)}) copy-start(bf16[1,4,1440,256]{3,2,1,0:T(8,128)(2,1)} %param.3) | copy-start | bytes 8847364
Sparse Core Ops, SparseCore 0:
  13.4 23.9 all-gather.1
  152.2 30.2 reduce-scatter.1
  185.7 38.8 all-reduce.1
where the time goes:
time: 239 us
  waiting for transfers between devices  79.3 us (33%)
  blocking collectives  73.7 us (31%)
  local copies, waits for them, and re-layouts  33.9 us (14%)
  other arithmetic  15.4 us (6%)
  matrix products  15.3 us (6%)
  between operations  14.1 us (6%)
  starting transfers between devices  7.26 us (3%)
    all_to_all x1, blocking collectives, shards(): lax.all_to_all(gathered, 'lat', split_axis=3, concat_axis=1, tiled=True)  30.1 us
    all_gather x1, waiting for transfers between devices, full_channels(): return lax.all_gather(blocks, 'chan', axis=1, tiled=True)  24.2 us
    all_to_all x1, blocking collectives, shards(): lax.all_to_all(own_rows, 'lat', split_axis=1, concat_axis=4, tiled=True)  18.9 us
    reduce_scatter x1, waiting for transfers between devices, shards(): lax.psum_scatter(jnp.moveaxis(spectral_terms(grad_split, weights), 1, 0),...  18.7 us
    psum x1, waiting for transfers between devices, shards(): weight_grad = lax.psum(local_grad, 'rep')  18.7 us
    all_to_all x1, blocking collectives, shards(): lax.all_to_all(grad_mixed, 'lat', split_axis=3, concat_axis=1, tiled=True)  15.5 us
    all_to_all x1, waiting for transfers between devices, shards(): lax.all_to_all(mixed, 'lat', split_axis=2, concat_axis=5, tiled=True)  13.6 us
    unnamed x31, local copies, waits for them, and re-layouts  12.2 us
  transfers between devices with their start and end apart: 5, of which 5 were waited for; matrix products, arithmetic and copies ran while one was open for 8% of the time, Pallas kernels for 0%

commit v1 on v0

v1 whole, which is shorter than its diff:
```python
import functools
import math

import jax
import jax.numpy as jnp
import numpy as np
from jax import lax
from jax.experimental import pallas as pl
from jax.experimental.pallas import tpu as pltpu
from jax.sharding import PartitionSpec as P

inv_sqrt_two = 0.7071067811865476
inv_sqrt_two_pi = 0.3989422804014327
LANES = 128
VMEM_BYTES = 40 * 1024 * 1024
BF16 = jnp.bfloat16
F32 = jnp.float32


def gelu_slope(values):
    cumulative = 0.5 * (1.0 + lax.erf(values * inv_sqrt_two))
    return cumulative + values * jnp.exp(-0.5 * values * values) * inv_sqrt_two_pi


def tables(plan):
    lon, modes = plan.lon, plan.n_lat * plan.m_loc
    lon_index = np.arange(lon, dtype=np.int64)
    mode_index = np.arange(modes, dtype=np.int64)
    phase = (mode_index[:, None] * lon_index[None, :] % lon).astype(np.float32) * np.float32(
        2.0 * math.pi / lon
    )
    scale = np.float32(1.0 / math.sqrt(lon))
    weight = np.where(mode_index == 0, 1.0, 2.0).astype(np.float32)[:, None]
    parts = np.stack([np.cos(phase), -np.sin(phase)], axis=0)
    own = np.array([plan.mode_at(u) for u in range(plan.m_loc)])
    order = (np.arange(plan.n_lat)[:, None] * plan.m_loc + own[None, :]).reshape(-1)

    def placed(array):
        array = array[:, order].reshape(2, plan.n_lat, plan.m_loc, lon).transpose(1, 0, 2, 3)
        return array.reshape(2 * modes, lon).astype(jnp.bfloat16)

    return placed(parts * scale), placed(weight * parts * scale)


class Plan:
    def __init__(self, mesh, field, weights):
        self.n_lat, self.n_chan = mesh.shape["lat"], mesh.shape["chan"]
        self.n_parts, self.n_rep = mesh.shape["parts"], mesh.shape["rep"]
        self.rows, self.lon, self.width = field[1], field[2], field[3]
        self.m_loc, self.o_w = weights[1], weights[2]
        self.nq = self.n_parts * self.n_rep
        self.halves = 2 if self.m_loc % 16 == 0 else 1
        self.per_q = self.m_loc // self.nq
        self.mh = self.per_q // self.halves
        self.pieces = 2 if self.mh % 2 == 0 else 1
        self.mp = self.mh // self.pieces
        self.mu = self.m_loc // self.halves
        self.rk = 2 * self.rows
        self.wide = self.n_lat * self.rk
        self.groups = self.width // LANES

    def mode_at(self, u):
        h, rest = divmod(u, self.mu)
        q, t = divmod(rest, self.mh)
        return q * self.per_q + h * self.mh + t


def params(**more):
    return pltpu.CompilerParams(vmem_limit_bytes=VMEM_BYTES, **more)


def full(shape):
    return pl.BlockSpec(shape, lambda *_: (0,) * len(shape))


def spread_rows(plan, me, row, source, held):
    for s in range(plan.n_lat):
        base = (me ^ s) * 2 * plan.m_loc
        for k in range(2):
            block = source[pl.ds(pl.multiple_of(base + k * plan.m_loc, 8), plan.m_loc), :]
            for g in range(plan.groups):
                at = pl.ds(k * plan.rows + row, plan.m_loc, stride=plan.rk)
                held[s * plan.groups + g, at, :] = block[:, g * LANES : (g + 1) * LANES]


def emit_blocks(plan, held, outs):
    at = plan.mu * plan.rk
    for s in range(plan.n_lat):
        for h in range(plan.halves):
            for g in range(plan.groups):
                block = held[s * plan.groups + g, h * at : (h + 1) * at, :].astype(BF16)
                outs[s * plan.halves + h][:, g * LANES : (g + 1) * LANES] = block


def collect_rows(plan, me, blocks, flat, held):
    for s in range(plan.n_lat):
        base = (me ^ s) * 2 * plan.m_loc
        for h in range(plan.halves):
            for g in range(plan.groups):
                lanes = slice(g * LANES, (g + 1) * LANES)
                flat[g] = blocks[s * plan.halves + h][:, lanes].astype(F32)
                for row in range(plan.rows):
                    for k in range(2):
                        at = base + k * plan.m_loc + h * plan.mu
                        at = pl.multiple_of(at, min(plan.mu, 8))
                        held[row, pl.ds(at, plan.mu), lanes] = flat[
                            g, pl.ds(k * plan.rows + row, plan.mu, stride=plan.rk), :
                        ]


def block_shape(plan):
    return (plan.mu * plan.rk, plan.width)


def forward_dft(plan, me, table, field):
    n_out = plan.n_lat * plan.halves
    modes2 = table.shape[0]

    def body(me_ref, field_ref, table_ref, *refs):
        outs, (line, held) = refs[:n_out], refs[n_out:]
        row = pl.program_id(0)
        line[...] = jnp.dot(table_ref[...], field_ref[0], preferred_element_type=F32)
        spread_rows(plan, me_ref[0], row, line, held)

        @pl.when(row == plan.rows - 1)
        def _():
            emit_blocks(plan, held, outs)

    shape = block_shape(plan)
    return pl.pallas_call(
        body,
        grid_spec=pltpu.PrefetchScalarGridSpec(
            num_scalar_prefetch=1,
            grid=(plan.rows,),
            in_specs=[
                pl.BlockSpec((1, plan.lon, plan.width), lambda a, _: (a, 0, 0)),
                full(table.shape),
            ],
            out_specs=[full(shape)] * n_out,
            scratch_shapes=[
                pltpu.VMEM((modes2, plan.width), F32),
                pltpu.VMEM((plan.n_lat * plan.groups, plan.m_loc * plan.rk, LANES), F32),
            ],
        ),
        out_shape=[jax.ShapeDtypeStruct(shape, BF16)] * n_out,
        compiler_params=params(),
        cost_estimate=pl.CostEstimate(
            flops=2 * plan.rows * plan.lon * modes2 * plan.width,
            bytes_accessed=2 * plan.rows * plan.lon * plan.width,
            transcendentals=0,
        ),
        name="forward_dft",
    )(me, field, table)


def middle(plan, me, inverse_t, inverse, cotangent, blocks):
    n = plan.n_lat * plan.halves
    modes2 = inverse.shape[0]
    cut = next(c for c in (288, 480, 360, 240, 160, plan.lon) if plan.lon % c == 0)

    def body(me_ref, cot_ref, back_ref, inv_ref, *refs):
        ins, outs = refs[:n], refs[n : 2 * n]
        flat, held, scaled, line, out_held = refs[2 * n :]
        row = pl.program_id(0)

        @pl.when(row == 0)
        def _():
            collect_rows(plan, me_ref[0], ins, flat, held)

        mixed = held[row].astype(BF16)
        for at in range(0, plan.lon, cut):
            spatial = jnp.dot(back_ref[at : at + cut, :], mixed, preferred_element_type=F32)
            cot = cot_ref[0, at : at + cut, :].astype(F32)
            scaled[at : at + cut, :] = (cot * gelu_slope(spatial)).astype(BF16)
        line[...] = jnp.dot(inv_ref[...], scaled[...], preferred_element_type=F32)
        spread_rows(plan, me_ref[0], row, line, out_held)

        @pl.when(row == plan.rows - 1)
        def _():
            emit_blocks(plan, out_held, outs)

    shape = block_shape(plan)
    return pl.pallas_call(
        body,
        grid_spec=pltpu.PrefetchScalarGridSpec(
            num_scalar_prefetch=1,
            grid=(plan.rows,),
            in_specs=[
                pl.BlockSpec((1, plan.lon, plan.width), lambda a, _: (a, 0, 0)),
                full(inverse_t.shape),
                full(inverse.shape),
            ]
            + [full(shape)] * n,
            out_specs=[full(shape)] * n,
            scratch_shapes=[
                pltpu.VMEM((plan.groups, shape[0], LANES), F32),
                pltpu.VMEM((plan.rows, modes2, plan.width), F32),
                pltpu.VMEM((plan.lon, plan.width), BF16),
                pltpu.VMEM((modes2, plan.width), F32),
                pltpu.VMEM((plan.n_lat * plan.groups, plan.m_loc * plan.rk, LANES), F32),
            ],
        ),
        out_shape=[jax.ShapeDtypeStruct(shape, BF16)] * n,
        compiler_params=params(),
        cost_estimate=pl.CostEstimate(
            flops=4 * plan.rows * plan.lon * modes2 * plan.width,
            bytes_accessed=2 * plan.rows * plan.lon * plan.width,
            transcendentals=2 * plan.rows * plan.lon * plan.width,
        ),
        name="middle",
    )(me, cotangent, inverse_t, inverse, *blocks)


def final_dft(plan, me, table_t, cotangent, blocks):
    n = plan.n_lat * plan.halves
    modes2 = table_t.shape[1]

    def body(me_ref, cot_ref, table_ref, *refs):
        ins, out, (flat, held) = refs[:n], refs[n], refs[n + 1 :]
        row = pl.program_id(0)

        @pl.when(row == 0)
        def _():
            collect_rows(plan, me_ref[0], ins, flat, held)

        grad = jnp.dot(table_ref[...], held[row].astype(BF16), preferred_element_type=F32)
        out[0] = (cot_ref[0].astype(F32) + grad).astype(BF16)

    shape = block_shape(plan)
    return pl.pallas_call(
        body,
        grid_spec=pltpu.PrefetchScalarGridSpec(
            num_scalar_prefetch=1,
            grid=(plan.rows,),
            in_specs=[
                pl.BlockSpec((1, plan.lon, plan.width), lambda a, _: (a, 0, 0)),
                full(table_t.shape),
            ]
            + [full(shape)] * n,
            out_specs=pl.BlockSpec((1, plan.lon, plan.width), lambda a, _: (a, 0, 0)),
            scratch_shapes=[
                pltpu.VMEM((plan.groups, shape[0], LANES), F32),
                pltpu.VMEM((plan.rows, modes2, plan.width), F32),
            ],
        ),
        out_shape=jax.ShapeDtypeStruct(cotangent.shape, BF16),
        compiler_params=params(),
        cost_estimate=pl.CostEstimate(
            flops=2 * plan.rows * plan.lon * modes2 * plan.width,
            bytes_accessed=4 * plan.rows * plan.lon * plan.width,
            transcendentals=0,
        ),
        name="final_dft",
    )(me, cotangent, table_t, *blocks)


def turned(plan, block, first_sign):
    swapped = jnp.concatenate([block[:, plan.rows :, :], block[:, : plan.rows, :]], axis=1)
    real = lax.broadcasted_iota(jnp.int32, swapped.shape, 1) < plan.rows
    return jnp.where(real, first_sign * swapped, -first_sign * swapped)


def mix_specs(plan, h):
    own = pl.BlockSpec(
        (2, plan.nq, plan.mh, plan.o_w, plan.width), lambda *_: (0, 0, h, 0, 0)
    )
    there = full((2, plan.mp, plan.o_w, plan.width))
    return own, there


def weight_of(plan, own_ref, others, x, q, slot, t, j):
    if x == 0:
        return own_ref[j, q, t]
    piece, at = divmod(t, plan.mp)
    return others[((x - 1) * plan.pieces + piece) * plan.nq + slot][j, at]


def mix_forward(plan, h, ids, blocks, own, others):
    n, n_other = plan.n_lat, len(others)
    shape = block_shape(plan)

    def body(ids_ref, *refs):
        ins, own_ref = refs[:n], refs[n]
        there = refs[n + 1 : n + 1 + n_other]
        outs = refs[n + 1 + n_other : 2 * n + 1 + n_other]
        packed, plain, turn, held = refs[2 * n + 1 + n_other :]
        for s in range(n):
            block = ins[s][...].astype(F32).reshape(plan.mu, plan.rk, plan.width)
            plain[:, s * plan.rk : (s + 1) * plan.rk, :] = block
            turn[:, s * plan.rk : (s + 1) * plan.rk, :] = turned(plan, block, -1.0)
        packed[...] = plain[...].astype(BF16)
        for slot in range(plan.nq):
            q = ids_ref[1] ^ slot
            for t in range(plan.mh):
                u = q * plan.mh + t
                one, two = plain[u].astype(BF16), turn[u].astype(BF16)
                for x in range(plan.n_chan):
                    real = weight_of(plan, own_ref, there, x, q, slot, t, 0)
                    imag = weight_of(plan, own_ref, there, x, q, slot, t, 1)
                    dims = (((1,), (1,)), ((), ()))
                    held[ids_ref[2] ^ x, u] = lax.dot_general(
                        one, real, dims, preferred_element_type=F32
                    ) + lax.dot_general(two, imag, dims, preferred_element_type=F32)
        for s in range(n):
            lanes = [held[c, :, s * plan.rk : (s + 1) * plan.rk, :] for c in range(plan.n_chan)]
            outs[s][...] = jnp.concatenate(lanes, axis=2).reshape(shape).astype(BF16)

    own_spec, there_spec = mix_specs(plan, h)
    wide = (plan.mu, plan.wide, plan.width)
    return pl.pallas_call(
        body,
        grid_spec=pltpu.PrefetchScalarGridSpec(
            num_scalar_prefetch=1,
            grid=(1,),
            in_specs=[full(shape)] * n + [own_spec] + [there_spec] * n_other,
            out_specs=[full(shape)] * n + [full(wide)],
            scratch_shapes=[
                pltpu.VMEM(wide, F32),
                pltpu.VMEM(wide, F32),
                pltpu.VMEM((plan.n_chan, plan.mu, plan.wide, plan.o_w), F32),
            ],
        ),
        out_shape=[jax.ShapeDtypeStruct(shape, BF16)] * n + [jax.ShapeDtypeStruct(wide, BF16)],
        compiler_params=params(),
        cost_estimate=pl.CostEstimate(
            flops=64 * plan.mu * plan.width * plan.width * plan.wide,
            bytes_accessed=4 * plan.mu * plan.width * plan.width,
            transcendentals=0,
        ),
        name=f"mix_forward_{h}",
    )(ids, *blocks, own, *others)


def mix_backward(plan, h, ids, blocks, own, others):
    n, n_other = plan.n_lat, len(others)
    shape = block_shape(plan)

    def body(ids_ref, *refs):
        ins, own_ref = refs[:n], refs[n]
        there = refs[n + 1 : n + 1 + n_other]
        outs = refs[n + 1 + n_other : 2 * n + 1 + n_other]
        packed = refs[2 * n + 1 + n_other : 2 * n + 1 + n_other + plan.n_chan]
        plain, turn, held = refs[2 * n + 1 + n_other + plan.n_chan :]
        for s in range(n):
            block = ins[s][...].astype(F32).reshape(plan.mu, plan.rk, plan.width)
            flip = turned(plan, block, 1.0)
            for c in range(plan.n_chan):
                lanes = slice(c * plan.o_w, (c + 1) * plan.o_w)
                plain[c, :, s * plan.rk : (s + 1) * plan.rk, :] = block[:, :, lanes]
                turn[c, :, s * plan.rk : (s + 1) * plan.rk, :] = flip[:, :, lanes]
        for x in range(plan.n_chan):
            packed[x][...] = plain[ids_ref[2] ^ x].astype(BF16)
        for slot in range(plan.nq):
            q = ids_ref[1] ^ slot
            for t in range(plan.mh):
                u = q * plan.mh + t
                total = None
                for x in range(plan.n_chan):
                    real = weight_of(plan, own_ref, there, x, q, slot, t, 0)
                    imag = weight_of(plan, own_ref, there, x, q, slot, t, 1)
                    one = plain[ids_ref[2] ^ x, u].astype(BF16)
                    two = turn[ids_ref[2] ^ x, u].astype(BF16)
                    term = jnp.dot(one, real, preferred_element_type=F32) + jnp.dot(
                        two, imag, preferred_element_type=F32
                    )
                    total = term if total is None else total + term
                held[u] = total
        for s in range(n):
            outs[s][...] = held[:, s * plan.rk : (s + 1) * plan.rk, :].reshape(shape).astype(BF16)

    own_spec, there_spec = mix_specs(plan, h)
    part = (plan.mu, plan.wide, plan.o_w)
    return pl.pallas_call(
        body,
        grid_spec=pltpu.PrefetchScalarGridSpec(
            num_scalar_prefetch=1,
            grid=(1,),
            in_specs=[full(shape)] * n + [own_spec] + [there_spec] * n_other,
            out_specs=[full(shape)] * n + [full(part)] * plan.n_chan,
            scratch_shapes=[
                pltpu.VMEM((plan.n_chan, *part), F32),
                pltpu.VMEM((plan.n_chan, *part), F32),
                pltpu.VMEM((plan.mu, plan.wide, plan.width), F32),
            ],
        ),
        out_shape=[jax.ShapeDtypeStruct(shape, BF16)] * n
        + [jax.ShapeDtypeStruct(part, BF16)] * plan.n_chan,
        compiler_params=params(),
        cost_estimate=pl.CostEstimate(
            flops=64 * plan.mu * plan.width * plan.width * plan.wide,
            bytes_accessed=4 * plan.mu * plan.width * plan.width,
            transcendentals=0,
        ),
        name=f"mix_backward_{h}",
    )(ids, *blocks, own, *others)


def weight_gradient(plan, h, spectra, grads, before):
    n = len(spectra)
    scale = 1.0 / (plan.rows * plan.n_lat * plan.n_chan)

    def body(*refs):
        s_refs, g_refs, out = refs[:n], refs[n : 2 * n], refs[-1]
        for t in range(plan.mh):
            total = [None, None]
            s_all = jnp.concatenate([s_refs[i][t].astype(F32) for i in range(n)], axis=0)
            g_all = jnp.concatenate([g_refs[i][t].astype(F32) for i in range(n)], axis=0)
            groups = g_all.reshape(-1, plan.rk, plan.o_w)
            g_turn = turned(plan, groups, 1.0).reshape(g_all.shape)
            s_all = s_all.astype(BF16)
            for j, g in enumerate((g_all, g_turn)):
                total = lax.dot_general(
                    g.astype(BF16), s_all, (((0,), (0,)), ((), ())), preferred_element_type=F32
                )
                out[j, 0, 0, t] = total * scale

    out_shape = (2, plan.nq, plan.halves, plan.mh, plan.o_w, plan.width)
    earlier = [] if before is None else [before]
    return pl.pallas_call(
        body,
        grid=(plan.nq,),
        in_specs=[pl.BlockSpec((plan.mh, plan.wide, plan.width), lambda q: (q, 0, 0))] * n
        + [pl.BlockSpec((plan.mh, plan.wide, plan.o_w), lambda q: (q, 0, 0))] * n
        + [pl.BlockSpec(memory_space=pl.ANY)] * len(earlier),
        out_specs=pl.BlockSpec(
            (2, 1, 1, plan.mh, plan.o_w, plan.width), lambda q: (0, q, h, 0, 0, 0)
        ),
        out_shape=jax.ShapeDtypeStruct(out_shape, F32),
        input_output_aliases={2 * n: 0} if earlier else {},
        compiler_params=params(),
        cost_estimate=pl.CostEstimate(
            flops=4 * plan.mu * plan.wide * n * plan.o_w * plan.width,
            bytes_accessed=8 * plan.mu * plan.o_w * plan.width,
            transcendentals=0,
        ),
        name=f"weight_gradient_{h}",
    )(*spectra, *grads, *earlier)


def hop(value, axis, size, s):
    return lax.ppermute(value, axis, [(i, i ^ s) for i in range(size)])


def spread(values, axis, size):
    return [value if s == 0 else hop(value, axis, size, s) for s in range(size) for value in values]


def shards(plan, field, cotangent, weights):
    forward_np, inverse_np = tables(plan)
    forward, inverse = jnp.asarray(forward_np), jnp.asarray(inverse_np)
    forward_t, inverse_t = jnp.asarray(forward_np.T.copy()), jnp.asarray(inverse_np.T.copy())
    lat, chan = lax.axis_index("lat"), lax.axis_index("chan")
    q = lax.axis_index("rep") * plan.n_parts + lax.axis_index("parts")
    ids = jnp.stack([lat, q, chan]).astype(jnp.int32)

    own = weights.reshape(2, plan.nq, plan.per_q, plan.o_w, plan.width)
    mine = lax.dynamic_index_in_dim(own, q, 1, keepdims=False)
    others = [[] for _ in range(plan.halves)]
    for x in range(1, plan.n_chan):
        for h in range(plan.halves):
            for p in range(plan.pieces):
                at = (h * plan.pieces + p) * plan.mp
                got = [hop(mine[:, at : at + plan.mp], "chan", plan.n_chan, x)]
                got = spread(got, "parts", plan.n_parts)
                others[h] += spread(got, "rep", plan.n_rep)

    def to_lat(blocks, halves=range(plan.halves)):
        return [
            hop(blocks[s * len(halves) + i], "lat", plan.n_lat, s) if s else blocks[i]
            for s in range(plan.n_lat)
            for i in range(len(halves))
        ]

    field, cotangent = field[0], cotangent[0]
    spectra = to_lat(forward_dft(plan, ids, forward, field))
    packed_s, mixed = [], [None] * (plan.n_lat * plan.halves)
    for h in range(plan.halves):
        *out, packed = mix_forward(plan, h, ids, spectra[h :: plan.halves], own, others[h])
        packed_s.append(packed)
        mixed[h :: plan.halves] = to_lat(out, [h])
    grads = to_lat(middle(plan, ids, inverse_t, inverse, cotangent, mixed))
    packed_g, spectral = [], [None] * (plan.n_lat * plan.halves)
    for h in range(plan.halves):
        out = mix_backward(plan, h, ids, grads[h :: plan.halves], own, others[h])
        packed_g.append(out[plan.n_lat :])
        spectral[h :: plan.halves] = to_lat(out[: plan.n_lat], [h])
    grad_field = final_dft(plan, ids, forward_t, cotangent, spectral)

    weight_grad = None
    for h in range(plan.halves):
        s_all = spread(spread([packed_s[h]], "chan", plan.n_chan), "rep", plan.n_rep)
        g_all = [packed_g[h][0]]
        g_all += [hop(packed_g[h][x], "chan", plan.n_chan, x) for x in range(1, plan.n_chan)]
        g_all = spread(g_all, "rep", plan.n_rep)
        weight_grad = weight_gradient(plan, h, s_all, g_all, weight_grad)
    return (grad_field[None], weight_grad.reshape(weights.shape))


def solution(mesh):
    placed = (
        P(("parts", "rep"), ("lat", "chan"), None, None),
        P(("parts", "rep"), ("lat", "chan"), None, None),
        P(None, "lat", "chan", None),
    )

    def local(field, cotangent, weights):
        return shards(Plan(mesh, field.shape, weights.shape), field, cotangent, weights)

    return jax.shard_map(
        local,
        mesh=mesh,
        in_specs=placed,
        out_specs=(
            P(("parts", "rep"), ("lat", "chan"), None, None),
            P("parts", "lat", "chan", None),
        ),
        check_vma=False,
    )
```

time: 239 us -> 122 us (0.51)
  blocking collectives: 73.7 us -> 0 us
  starting transfers between devices: 7.26 us -> 52.6 us
  waiting for transfers between devices: 79.3 us -> 35.7 us
  local copies, waits for them, and re-layouts: 33.9 us -> 5.79 us
  Pallas kernels: 0 us -> 27.1 us
  other arithmetic: 15.4 us -> 0.08 us
  matrix products: 15.3 us -> 0 us
  between operations: 14.1 us -> 0.87 us
    all_to_all x4 -> x0, blocking collectives: 73.7 us -> none  [the longest x1 30.1 us: shards(): lax.all_to_all(gathered, 'lat', split_axis=3, concat_axis=1, tiled=True)]
    ppermute x0 -> x52, starting transfers between devices: none -> 52.6 us  [hop(): return lax.ppermute(value, axis, [(i, i ^ s) for i in range(size)])]
    ppermute x0 -> x52, waiting for transfers between devices: none -> 35.7 us  [hop(): return lax.ppermute(value, axis, [(i, i ^ s) for i in range(size)])]
    pallas_call x0 -> x9, Pallas kernels: none -> 27.1 us  [the longest x2 5.94 us: weight_gradient(): pl.pallas_call(body, grid=(plan.nq,), in_specs=[pl.BlockSpec((plan.mh, pl...]
    all_gather x1 -> x0, waiting for transfers between devices: 24.2 us -> none  [full_channels(): return lax.all_gather(blocks, 'chan', axis=1, tiled=True)]
    reduce_scatter x1 -> x0, waiting for transfers between devices: 18.7 us -> none  [shards(): lax.psum_scatter(jnp.moveaxis(spectral_terms(grad_split, weights), 1, 0),...]
    psum x1 -> x0, waiting for transfers between devices: 18.7 us -> none  [shards(): weight_grad = lax.psum(local_grad, 'rep')]
    all_to_all x2 -> x0, waiting for transfers between devices: 17.7 us -> none  [the longest x1 13.6 us: shards(): lax.all_to_all(mixed, 'lat', split_axis=2, concat_axis=5, tiled=True)]
  transfers between devices with their start and end apart: 5 -> 52, of which waited for: 5 -> 15; matrix products, arithmetic and copies ran while one was open for 8% -> 0% of each run, Pallas kernels for 0% -> 15%
where the time goes in v1:
time: 122 us
  starting transfers between devices  52.6 us (43%)
  waiting for transfers between devices  35.7 us (29%)
  Pallas kernels  27.1 us (22%)
  local copies, waits for them, and re-layouts  5.79 us (5%)
    ppermute x52, starting transfers between devices, hop(): return lax.ppermute(value, axis, [(i, i ^ s) for i in range(size)])  52.6 us
    ppermute x52, waiting for transfers between devices, hop(): return lax.ppermute(value, axis, [(i, i ^ s) for i in range(size)])  35.7 us
    pallas_call x2, Pallas kernels, weight_gradient(): pl.pallas_call(body, grid=(plan.nq,), in_specs=[pl.BlockSpec((plan.mh, pl...  5.94 us
    pallas_call x2, Pallas kernels, mix_forward(): pl.pallas_call(body, grid_spec=pltpu.PrefetchScalarGridSpec(num_scalar_pr...  5.84 us
    pallas_call x1, Pallas kernels, middle(): pl.pallas_call(body, grid_spec=pltpu.PrefetchScalarGridSpec(num_scalar_pr...  5.32 us
    pallas_call x2, Pallas kernels, mix_backward(): pl.pallas_call(body, grid_spec=pltpu.PrefetchScalarGridSpec(num_scalar_pr...  4.02 us
    pallas_call x1, Pallas kernels, final_dft(): pl.pallas_call(body, grid_spec=pltpu.PrefetchScalarGridSpec(num_scalar_pr...  3.63 us
    unnamed x16, local copies, waits for them, and re-layouts  3.36 us
  transfers between devices with their start and end apart: 52, of which 15 were waited for; matrix products, arithmetic and copies ran while one was open for 0% of the time, Pallas kernels for 15%

profile of v1, /device:TPU:0, one launch (start us, length us, event | category | flops | bytes accessed | tf_op | source)
XLA Modules:
  0.0 122.2 jit_solution(12611298168760509655)
XLA Ops:
  0.6 1.5 %dynamic-slice_bitcast_fusion = bf16[2,8,128,256]{3,2,1,0:T(8,128)(2,1)S(1)} fusion(bf16[2,4,8,128,256]{4,3,2,1,0:T(8,128)(2,1)} %bitcast.13, s32[]{:T(128)S(6)} %select_n.4), kind=kLoop, calls=%fused_computation | loop fusion | bytes 2097156 | tf_op jit(solution)/shard_map/jit(dynamic_index_in_dim)/squeeze | solution.py:457
  2.1 1.0 fusion
  3.1 2.9 %collective-permute-start.14 = (bf16[2,2,128,256]{3,2,1,0:T(8,128)(2,1)}, bf16[2,2,128,256]{3,2,1,0:T(8,128)(2,1)S(1)}, u32[]{:S(2)}, u32[]{:S(2)}) collective-permute-start(bf16[2,2,128,256]{3,2,1,0:T(8,128)(2,1)} %get-tuple-element.79), channel_id=1, source_target_pairs={{0,2},{2,0},{1,3},{3,1},{4,6},{6,4},{5,7},{7,5},{8,10},{10,8},{9,1... | collective-permute-start | bytes 786440 | tf_op jit(solution)/shard_map/ppermute | solution.py:441
  6.1 1.1 copy-done.2
  7.3 2.4 %forward_dft.1 = (bf16[128,256]{1,0:T(8,128)(2,1)S(1)}, bf16[128,256]{1,0:T(8,128)(2,1)S(1)}, bf16[128,256]{1,0:T(8,128)(2,1)S(1)}, bf16[128,256]{1,0:T(8,128)(2...) custom-call(s32[3]{0:T(128)S(1)} %pad_add_fusion.me_ref.ids_ref, ...), custom_call_target="tpu_custom_call" | custom-call | flops 754974720 | bytes 2949120 | tf_op jit(solution)/shard_map/forward_dft/pallas_call | solution.py:130
  9.7 2.1 %collective-permute-start.11 = (bf16[128,256]{1,0:T(8,128)(2,1)S(1)}, bf16[128,256]{1,0:T(8,128)(2,1)S(1)}, u32[]{:S(2)}, u32[]{:S(2)}) collective-permute-start(bf16[128,256]{1,0:T(8,128)(2,1)S(1)} %get-tuple-element.46), channel_id=1, source_target_pairs={{0,4},{4,0},{8,12},{12,8},{1,5},{5,1},{9,13},{13,9},{2,6},{6,2},{1... | collective-permute-start | bytes 196616 | tf_op jit(solution)/shard_map/ppermute | solution.py:441
  11.8 2.6 %collective-permute-start.12 = (bf16[128,256]{1,0:T(8,128)(2,1)S(1)}, bf16[128,256]{1,0:T(8,128)(2,1)S(1)}, u32[]{:S(2)}, u32[]{:S(2)}) collective-permute-start(bf16[128,256]{1,0:T(8,128)(2,1)S(1)} %get-tuple-element.47), channel_id=1, source_target_pairs={{0,8},{4,12},{8,0},{12,4},{1,9},{5,13},{9,1},{13,5},{2,10},{6,14},... | collective-permute-start | bytes 196616 | tf_op jit(solution)/shard_map/ppermute | solution.py:441
  14.4 1.8 %collective-permute-start = (bf16[128,256]{1,0:T(8,128)(2,1)S(1)}, bf16[128,256]{1,0:T(8,128)(2,1)S(1)}, u32[]{:S(2)}, u32[]{:S(2)}) collective-permute-start(bf16[128,256]{1,0:T(8,128)(2,1)S(1)} %get-tuple-element.41), channel_id=1, source_target_pairs={{0,4},{4,0},{8,12},{12,8},{1,5},{5,1},{9,13},{13,9},{2,6},{6,2},{1... | collective-permute-start | bytes 196616 | tf_op jit(solution)/shard_map/ppermute | solution.py:441
  16.2 2.4 %collective-permute-done.12.refs_2_ = bf16[128,256]{1,0:T(8,128)(2,1)S(1)} collective-permute-done((bf16[128,256]{1,0:T(8,128)(2,1)S(1)}, bf16[128,256]{1,0:T(8,128)(2,1)S(1)}, u32[]{:S(2)}, u32[]{:S(2)}) %collective-permute-start.12) | collective-permute-done | bytes 65568 | tf_op jit(solution)/shard_map/ppermute | solution.py:441
  18.6 1.3 %collective-permute-start.1 = (bf16[128,256]{1,0:T(8,128)(2,1)S(1)}, bf16[128,256]{1,0:T(8,128)(2,1)S(1)}, u32[]{:S(2)}, u32[]{:S(2)}) collective-permute-start(bf16[128,256]{1,0:T(8,128)(2,1)S(1)} %get-tuple-element.42), channel_id=1, source_target_pairs={{0,8},{4,12},{8,0},{12,4},{1,9},{5,13},{9,1},{13,5},{2,10},{6,14},... | collective-permute-start | bytes 196616 | tf_op jit(solution)/shard_map/ppermute | solution.py:441
  20.5 1.5 %collective-permute-start.7 = (bf16[2,2,128,256]{3,2,1,0:T(8,128)(2,1)}, bf16[2,2,128,256]{3,2,1,0:T(8,128)(2,1)S(1)}, u32[]{:S(2)}, u32[]{:S(2)}) collective-permute-start(bf16[2,2,128,256]{3,2,1,0:T(8,128)(2,1)} %get-tuple-element.80), channel_id=1, source_target_pairs={{0,2},{2,0},{1,3},{3,1},{4,6},{6,4},{5,7},{7,5},{8,10},{10,8},{9,1... | collective-permute-start | bytes 786440 | tf_op jit(solution)/shard_map/ppermute | solution.py:441
  22.5 1.5 %collective-permute-start.15 = (bf16[2,2,128,256]{3,2,1,0:T(8,128)(2,1)S(1)}, bf16[2,2,128,256]{3,2,1,0:T(8,128)(2,1)S(1)}, u32[]{:S(2)}, u32[]{:S(2)}) collective-permute-start(bf16[2,2,128,256]{3,2,1,0:T(8,128)(2,1)S(1)} %collective-permute-done.14.refs_5_), channel_id=1, source_target_pairs={{0,16},{16,0},{1,17},{17,1},{2,18},{18,2},{3,19},{19,3},{4,20},{20... | collective-permute-start | bytes 786440 | tf_op jit(solution)/shard_map/ppermute | solution.py:441
  24.5 4.7 %collective-permute-done.7.refs_9_ = bf16[2,2,128,256]{3,2,1,0:T(8,128)(2,1)S(1)} collective-permute-done((bf16[2,2,128,256]{3,2,1,0:T(8,128)(2,1)}, bf16[2,2,128,256]{3,2,1,0:T(8,128)(2,1)S(1)}, u32[]{:S(2)}, u32[]{:S(2)}) %collective-permute-start.7) | collective-permute-done | bytes 262176 | tf_op jit(solution)/shard_map/ppermute | solution.py:441
  29.3 2.8 %collective-permute-done.3.refs_5_ = bf16[2,2,128,256]{3,2,1,0:T(8,128)(2,1)S(1)} collective-permute-done((bf16[2,2,128,256]{3,2,1,0:T(8,128)(2,1)}, bf16[2,2,128,256]{3,2,1,0:T(8,128)(2,1)S(1)}, u32[]{:S(2)}, u32[]{:S(2)}) %collective-permute-start.3) | collective-permute-done | bytes 262176 | tf_op jit(solution)/shard_map/ppermute | solution.py:441
  32.1 1.5 %collective-permute-start.8 = (bf16[2,2,128,256]{3,2,1,0:T(8,128)(2,1)S(1)}, bf16[2,2,128,256]{3,2,1,0:T(8,128)(2,1)S(1)}, u32[]{:S(2)}, u32[]{:S(2)}) collective-permute-start(bf16[2,2,128,256]{3,2,1,0:T(8,128)(2,1)S(1)} %collective-permute-done.7.refs_9_), channel_id=1, source_target_pairs={{0,16},{16,0},{1,17},{17,1},{2,18},{18,2},{3,19},{19,3},{4,20},{20... | collective-permute-start | bytes 786440 | tf_op jit(solution)/shard_map/ppermute | solution.py:441
  34.8 6.5 %collective-permute-done.8.refs_10_ = bf16[2,2,128,256]{3,2,1,0:T(8,128)(2,1)S(1)} collective-permute-done((bf16[2,2,128,256]{3,2,1,0:T(8,128)(2,1)S(1)}, bf16[2,2,128,256]{3,2,1,0:T(8,128)(2,1)S(1)}, u32[]{:S(2)}, u32[]{:S(2)}) %collective-permute-start.8) | collective-permute-done | bytes 262176 | tf_op jit(solution)/shard_map/ppermute | solution.py:441
  41.3 3.2 %collective-permute-done.4.refs_6_ = bf16[2,2,128,256]{3,2,1,0:T(8,128)(2,1)S(1)} collective-permute-done((bf16[2,2,128,256]{3,2,1,0:T(8,128)(2,1)S(1)}, bf16[2,2,128,256]{3,2,1,0:T(8,128)(2,1)S(1)}, u32[]{:S(2)}, u32[]{:S(2)}) %collective-permute-start.4) | collective-permute-done | bytes 262176 | tf_op jit(solution)/shard_map/ppermute | solution.py:441
  45.1 2.4 %collective-permute-start.2 = (bf16[128,256]{1,0:T(8,128)(2,1)S(1)}, bf16[128,256]{1,0:T(8,128)(2,1)S(1)}, u32[]{:S(2)}, u32[]{:S(2)}) collective-permute-start(bf16[128,256]{1,0:T(8,128)(2,1)S(1)} %get-tuple-element.43), channel_id=1, source_target_pairs={{0,12},{4,8},{8,4},{12,0},{1,13},{5,9},{9,5},{13,1},{2,14},{6,10},... | collective-permute-start | bytes 196616 | tf_op jit(solution)/shard_map/ppermute | solution.py:441
  47.6 2.2 %copy-done.4 = bf16[2,32,128,256]{3,2,1,0:T(8,128)(2,1)S(1)} copy-done((bf16[2,32,128,256]{3,2,1,0:T(8,128)(2,1)S(1)}, bf16[2,32,128,256]{3,2,1,0:T(8,128)(2,1)}, u32[]{:S(2)}) %copy-start.4) | copy-done | bytes 4194328
  49.7 3.6 %mix_forward_1.1 = (bf16[128,256]{1,0:T(8,128)(2,1)S(1)}, bf16[128,256]{1,0:T(8,128)(2,1)S(1)}, bf16[128,256]{1,0:T(8,128)(2,1)S(1)}, bf16[128,256]{1,0:T(8,128)(2,1)S(1)}, bf16[16,32,256]{2,1,0:T(8,128)(2,1)S(1)}) custom-call(s32[3]{0:T(128)S(1)} %pad_add_fusion.me_ref.ids_ref, bf16[128,256]{1,0:T(8,128)(2,1)S(1)} %get-tuple-element.45.refs_0_, ...), custom_call_target="tpu_custom_call" | custom-call | flops 2147483648 | bytes 4194304 | tf_op jit(solution)/shard_map/mix_forward_1/pallas_call | solution.py:310
  53.5 1.9 %collective-permute-start.25 = (bf16[128,256]{1,0:T(8,128)(2,1)S(1)}, bf16[128,256]{1,0:T(8,128)(2,1)S(1)}, u32[]{:S(2)}, u32[]{:S(2)}) collective-permute-start(bf16[128,256]{1,0:T(8,128)(2,1)S(1)} %get-tuple-element.53), channel_id=1, source_target_pairs={{0,8},{4,12},{8,0},{12,4},{1,9},{5,13},{9,1},{13,5},{2,10},{6,14},... | collective-permute-start | bytes 196616 | tf_op jit(solution)/shard_map/ppermute | solution.py:441
  55.4 2.4 %collective-permute-start.27 = (bf16[128,256]{1,0:T(8,128)(2,1)S(1)}, bf16[128,256]{1,0:T(8,128)(2,1)S(1)}, u32[]{:S(2)}, u32[]{:S(2)}) collective-permute-start(bf16[128,256]{1,0:T(8,128)(2,1)S(1)} %get-tuple-element.55), channel_id=1, source_target_pairs={{0,12},{4,8},{8,4},{12,0},{1,13},{5,9},{9,5},{13,1},{2,14},{6,10},... | collective-permute-start | bytes 196616 | tf_op jit(solution)/shard_map/ppermute | solution.py:441
  57.8 2.3 %mix_forward_0.1 = (bf16[128,256]{1,0:T(8,128)(2,1)S(1)}, bf16[128,256]{1,0:T(8,128)(2,1)S(1)}, bf16[128,256]{1,0:T(8,128)(2,1)S(1)}, bf16[128,256]{1,0:T(8,128)(2,1)S(1)}, bf16[16,32,256]{2,1,0:T(8,128)(2,1)S(1)}) custom-call(s32[3]{0:T(128)S(1)} %pad_add_fusion.me_ref.ids_ref, bf16[128,256]{1,0:T(8,128)(2,1)S(1)} %get-tuple-element.40.refs_0_, ...), custom_call_target="tpu_custom_call" | custom-call | flops 2147483648 | bytes 4194304 | tf_op jit(solution)/shard_map/mix_forward_0/pallas_call | solution.py:310
  60.2 1.9 %collective-permute-start.24 = (bf16[128,256]{1,0:T(8,128)(2,1)S(1)}, bf16[128,256]{1,0:T(8,128)(2,1)S(1)}, u32[]{:S(2)}, u32[]{:S(2)}) collective-permute-start(bf16[128,256]{1,0:T(8,128)(2,1)S(1)} %get-tuple-element.52), channel_id=1, source_target_pairs={{0,8},{4,12},{8,0},{12,4},{1,9},{5,13},{9,1},{13,5},{2,10},{6,14},... | collective-permute-start | bytes 196616 | tf_op jit(solution)/shard_map/ppermute | solution.py:441
  62.1 2.4 %collective-permute-start.26 = (bf16[128,256]{1,0:T(8,128)(2,1)S(1)}, bf16[128,256]{1,0:T(8,128)(2,1)S(1)}, u32[]{:S(2)}, u32[]{:S(2)}) collective-permute-start(bf16[128,256]{1,0:T(8,128)(2,1)S(1)} %get-tuple-element.54), channel_id=1, source_target_pairs={{0,12},{4,8},{8,4},{12,0},{1,13},{5,9},{9,5},{13,1},{2,14},{6,10},... | collective-permute-start | bytes 196616 | tf_op jit(solution)/shard_map/ppermute | solution.py:441
  64.6 2.3 %collective-permute-done.24.refs_4_ = bf16[128,256]{1,0:T(8,128)(2,1)S(1)} collective-permute-done((bf16[128,256]{1,0:T(8,128)(2,1)S(1)}, bf16[128,256]{1,0:T(8,128)(2,1)S(1)}, u32[]{:S(2)}, u32[]{:S(2)}) %collective-permute-start.24) | collective-permute-done | bytes 65568 | tf_op jit(solution)/shard_map/ppermute | solution.py:441
  66.9 1.4 %collective-permute-done.26.refs_6_ = bf16[128,256]{1,0:T(8,128)(2,1)S(1)} collective-permute-done((bf16[128,256]{1,0:T(8,128)(2,1)S(1)}, bf16[128,256]{1,0:T(8,128)(2,1)S(1)}, u32[]{:S(2)}, u32[]{:S(2)}) %collective-permute-start.26) | collective-permute-done | bytes 65568 | tf_op jit(solution)/shard_map/ppermute | solution.py:441
  68.3 5.3 %middle.1 = (bf16[128,256]{1,0:T(8,128)(2,1)S(1)}, bf16[128,256]{1,0:T(8,128)(2,1)S(1)}, bf16[128,256]{1,0:T(8,128)(2,1)S(1)}, bf16[128,256]{1,0:T(8,128)(2,1)S(...) custom-call(s32[3]{0:T(128)S(1)} %pad_add_fusion.me_ref.ids_ref, ...), custom_call_target="tpu_custom_call" | custom-call | flops 1509949440 | bytes 2949120 | tf_op jit(solution)/shard_map/middle/pallas_call | solution.py:183
  74.3 2.3 %collective-permute-start.32 = (bf16[128,256]{1,0:T(8,128)(2,1)S(1)}, bf16[128,256]{1,0:T(8,128)(2,1)S(1)}, u32[]{:S(2)}, u32[]{:S(2)}) collective-permute-start(bf16[128,256]{1,0:T(8,128)(2,1)S(1)} %get-tuple-element.63), channel_id=1, source_target_pairs={{0,8},{4,12},{8,0},{12,4},{1,9},{5,13},{9,1},{13,5},{2,10},{6,14},... | collective-permute-start | bytes 196616 | tf_op jit(solution)/shard_map/ppermute | solution.py:441
  76.6 1.5 %collective-permute-start.33 = (bf16[128,256]{1,0:T(8,128)(2,1)S(1)}, bf16[128,256]{1,0:T(8,128)(2,1)S(1)}, u32[]{:S(2)}, u32[]{:S(2)}) collective-permute-start(bf16[128,256]{1,0:T(8,128)(2,1)S(1)} %get-tuple-element.64), channel_id=1, source_target_pairs={{0,12},{4,8},{8,4},{12,0},{1,13},{5,9},{9,5},{13,1},{2,14},{6,10},... | collective-permute-start | bytes 196616 | tf_op jit(solution)/shard_map/ppermute | solution.py:441
  78.1 1.4 %collective-permute-start.46 = (bf16[16,32,256]{2,1,0:T(8,128)(2,1)S(1)}, bf16[16,32,256]{2,1,0:T(8,128)(2,1)S(1)}, u32[]{:S(2)}, u32[]{:S(2)}) collective-permute-start(bf16[16,32,256]{2,1,0:T(8,128)(2,1)S(1)} %get-tuple-element.75.refs_0_), channel_id=1, source_target_pairs={{0,2},{2,0},{1,3},{3,1},{4,6},{6,4},{5,7},{7,5},{8,10},{10,8},{9,1... | collective-permute-start | bytes 786440 | tf_op jit(solution)/shard_map/ppermute | solution.py:441
  79.5 2.1 %collective-permute-start.29 = (bf16[128,256]{1,0:T(8,128)(2,1)S(1)}, bf16[128,256]{1,0:T(8,128)(2,1)S(1)}, u32[]{:S(2)}, u32[]{:S(2)}) collective-permute-start(bf16[128,256]{1,0:T(8,128)(2,1)S(1)} %get-tuple-element.58), channel_id=1, source_target_pairs={{0,8},{4,12},{8,0},{12,4},{1,9},{5,13},{9,1},{13,5},{2,10},{6,14},... | collective-permute-start | bytes 196616 | tf_op jit(solution)/shard_map/ppermute | solution.py:441
  81.6 2.3 %collective-permute-start.30 = (bf16[128,256]{1,0:T(8,128)(2,1)S(1)}, bf16[128,256]{1,0:T(8,128)(2,1)S(1)}, u32[]{:S(2)}, u32[]{:S(2)}) collective-permute-start(bf16[128,256]{1,0:T(8,128)(2,1)S(1)} %get-tuple-element.59), channel_id=1, source_target_pairs={{0,12},{4,8},{8,4},{12,0},{1,13},{5,9},{9,5},{13,1},{2,14},{6,10},... | collective-permute-start | bytes 196616 | tf_op jit(solution)/shard_map/ppermute | solution.py:441
  83.9 2.5 %mix_backward_1.1 = (bf16[128,256]{1,0:T(8,128)(2,1)S(1)}, bf16[128,256]{1,0:T(8,128)(2,1)S(1)}, bf16[128,256]{1,0:T(8,128)(2,1)S(1)}, bf16[128,256]{1,0:T(8,128...) custom-call(s32[3]{0:T(128)S(1)} %pad_add_fusion.me_ref.ids_ref, ...), custom_call_target="tpu_custom_call" | custom-call | flops 2147483648 | bytes 4194304 | tf_op jit(solution)/shard_map/mix_backward_1/pallas_call | solution.py:373
  87.2 1.3 %collective-permute-start.37 = (bf16[128,256]{1,0:T(8,128)(2,1)S(1)}, bf16[128,256]{1,0:T(8,128)(2,1)S(1)}, u32[]{:S(2)}, u32[]{:S(2)}) collective-permute-start(bf16[128,256]{1,0:T(8,128)(2,1)S(1)} %get-tuple-element.69), channel_id=1, source_target_pairs={{0,8},{4,12},{8,0},{12,4},{1,9},{5,13},{9,1},{13,5},{2,10},{6,14},... | collective-permute-start | bytes 196616 | tf_op jit(solution)/shard_map/ppermute | solution.py:441
  88.5 2.3 %collective-permute-start.39 = (bf16[128,256]{1,0:T(8,128)(2,1)S(1)}, bf16[128,256]{1,0:T(8,128)(2,1)S(1)}, u32[]{:S(2)}, u32[]{:S(2)}) collective-permute-start(bf16[128,256]{1,0:T(8,128)(2,1)S(1)} %get-tuple-element.71), channel_id=1, source_target_pairs={{0,12},{4,8},{8,4},{12,0},{1,13},{5,9},{9,5},{13,1},{2,14},{6,10},... | collective-permute-start | bytes 196616 | tf_op jit(solution)/shard_map/ppermute | solution.py:441
  90.9 1.5 %mix_backward_0.1 = (bf16[128,256]{1,0:T(8,128)(2,1)S(1)}, bf16[128,256]{1,0:T(8,128)(2,1)S(1)}, bf16[128,256]{1,0:T(8,128)(2,1)S(1)}, bf16[128,256]{1,0:T(8,128...) custom-call(s32[3]{0:T(128)S(1)} %pad_add_fusion.me_ref.ids_ref, ...), custom_call_target="tpu_custom_call" | custom-call | flops 2147483648 | bytes 4194304 | tf_op jit(solution)/shard_map/mix_backward_0/pallas_call | solution.py:373
  92.6 1.1 collective-permute-start.40
  94.6 1.5 %collective-permute-start.36 = (bf16[128,256]{1,0:T(8,128)(2,1)S(1)}, bf16[128,256]{1,0:T(8,128)(2,1)S(1)}, u32[]{:S(2)}, u32[]{:S(2)}) collective-permute-start(bf16[128,256]{1,0:T(8,128)(2,1)S(1)} %get-tuple-element.68), channel_id=1, source_target_pairs={{0,8},{4,12},{8,0},{12,4},{1,9},{5,13},{9,1},{13,5},{2,10},{6,14},... | collective-permute-start | bytes 196616 | tf_op jit(solution)/shard_map/ppermute | solution.py:441
  96.7 1.5 %collective-permute-start.38 = (bf16[128,256]{1,0:T(8,128)(2,1)S(1)}, bf16[128,256]{1,0:T(8,128)(2,1)S(1)}, u32[]{:S(2)}, u32[]{:S(2)}) collective-permute-start(bf16[128,256]{1,0:T(8,128)(2,1)S(1)} %get-tuple-element.70), channel_id=1, source_target_pairs={{0,12},{4,8},{8,4},{12,0},{1,13},{5,9},{9,5},{13,1},{2,14},{6,10},... | collective-permute-start | bytes 196616 | tf_op jit(solution)/shard_map/ppermute | solution.py:441
  98.2 3.4 %collective-permute-done.36.refs_4_ = bf16[128,256]{1,0:T(8,128)(2,1)S(1)} collective-permute-done((bf16[128,256]{1,0:T(8,128)(2,1)S(1)}, bf16[128,256]{1,0:T(8,128)(2,1)S(1)}, u32[]{:S(2)}, u32[]{:S(2)}) %collective-permute-start.36) | collective-permute-done | bytes 65568 | tf_op jit(solution)/shard_map/ppermute | solution.py:441
  101.6 1.2 collective-permute-start.49
  103.4 3.7 %collective-permute-done.49.refs_5_ = bf16[16,32,128]{2,1,0:T(8,128)(2,1)S(1)} collective-permute-done((bf16[16,32,128]{2,1,0:T(8,128)(2,1)S(1)}, bf16[16,32,128]{2,1,0:T(8,128)(2,1)S(1)}, u32[]{:S(2)}, u32[]{:S(2)}) %collective-permute-start.49) | collective-permute-done | bytes 131104 | tf_op jit(solution)/shard_map/ppermute | solution.py:441
  107.1 1.6 %collective-permute-start.43 = (bf16[16,32,128]{2,1,0:T(8,128)(2,1)S(1)}, bf16[16,32,128]{2,1,0:T(8,128)(2,1)S(1)}, u32[]{:S(2)}, u32[]{:S(2)}) collective-permute-start(bf16[16,32,128]{2,1,0:T(8,128)(2,1)S(1)} %get-tuple-element.74), channel_id=1, source_target_pairs={{0,2},{2,0},{1,3},{3,1},{4,6},{6,4},{5,7},{7,5},{8,10},{10,8},{9,1... | collective-permute-start | bytes 393224 | tf_op jit(solution)/shard_map/ppermute | solution.py:441
  109.3 2.7 %collective-permute-done.43.refs_5_ = bf16[16,32,128]{2,1,0:T(8,128)(2,1)S(1)} collective-permute-done((bf16[16,32,128]{2,1,0:T(8,128)(2,1)S(1)}, bf16[16,32,128]{2,1,0:T(8,128)(2,1)S(1)}, u32[]{:S(2)}, u32[]{:S(2)}) %collective-permute-start.43) | collective-permute-done | bytes 131104 | tf_op jit(solution)/shard_map/ppermute | solution.py:441
  112.6 3.6 %final_dft.1 = bf16[4,1440,256]{2,1,0:T(8,128)(2,1)} custom-call(s32[3]{0:T(128)S(1)} %pad_add_fusion.me_ref.ids_ref, bf16[4,1440,256]{2,1,0:T(8,128)(2,1)S(1)} %bitcast.11, bf16[1440,256]{1,0:T(8,128)(2,1)S(1)} %copy-done.3, bf16[128,256]{1,0:T(8,128)(2,1)S(1)} %get-tuple-element.60.refs_0_, bf16[128,256]{1,0:T(8,128)(2,1)S(1)} %get-tuple-element.65.refs_1_, ...), custom_call_target="tpu_custom_call" | custom-call | flops 754974720 | bytes 5898240 | tf_op jit(solution)/shard_map/final_dft/pallas_call | solution.py:230
  116.2 3.0 %weight_gradient_0.1.refs_8_ = f32[2,4,2,4,128,256]{5,4,3,2,1,0:T(8,128)} custom-call(bf16[16,32,256]{2,1,0:T(8,128)(2,1)S(1)} %get-tuple-element.75.refs_0_, bf16[16,32,256]{2,1,0:T(8,128)(2,1)S(1)} %collective-permute-done.46.refs_1_, bf16[16,32,256]{2,1,0:T(8,128)(2,1)S(1)} %collective-permute-done.47.refs_2_, ...), custom_call_target="tpu_custom_call" | custom-call | flops 268435456 | bytes 4194304 | tf_op jit(solution)/shard_map/weight_gradient_0/pallas_call | solution.py:419
  119.2 3.0 %weight_gradient_1.1 = f32[2,4,2,4,128,256]{5,4,3,2,1,0:T(8,128)} custom-call(bf16[16,32,256]{2,1,0:T(8,128)(2,1)S(1)} %get-tuple-element.72.refs_0_, bf16[16,32,256]{2,1,0:T(8,128)(2,1)S(1)} %collective-permute-done.40.refs_1_, bf16[16,32,256]{2,1,0:T(8,128)(2,1)S(1)} %collective-permute-done.41.refs_2_, ...), custom_call_target="tpu_custom_call", output_to_operand_aliasing={{}: (8, {})} | custom-call | flops 268435456 | bytes 4194304 | tf_op jit(solution)/shard_map/weight_gradient_1/pallas_call | solution.py:419
  (84 shorter events, 8.7 us)
Async XLA Ops:
  3.1 19.4 %collective-permute-start.14 = (bf16[2,2,128,256]{3,2,1,0:T(8,128)(2,1)}, bf16[2,2,128,256]{3,2,1,0:T(8,128)(2,1)S(1)}, u32[]{:S(2)}, u32[]{:S(2)}) collective-permute-start(bf16[2,2,128,256]{3,2,1,0:T(8,128)(2,1)} %get-tuple-element.79), channel_id=1, source_target_pairs={{0,2},{2,0},{1,3},{3,1},{4,6},{6,4},{5,7},{7,5},{8,10},{10,8},{9,1... | collective-permute-start | bytes 786440 | tf_op jit(solution)/shard_map/ppermute | solution.py:441
  6.0 18.0 %collective-permute-start.18 = (bf16[2,2,128,256]{3,2,1,0:T(8,128)(2,1)}, bf16[2,2,128,256]{3,2,1,0:T(8,128)(2,1)}, u32[]{:S(2)}, u32[]{:S(2)}) collective-permute-start(bf16[2,2,128,256]{3,2,1,0:T(8,128)(2,1)} %get-tuple-element.78), channel_id=1, source_target_pairs={{0,2},{2,0},{1,3},{3,1},{4,6},{6,4},{5,7},{7,5},{8,10},{10,8},{9,1... | collective-permute-start | bytes 786440 | tf_op jit(solution)/shard_map/ppermute | solution.py:441
  11.8 6.8 %collective-permute-start.12 = (bf16[128,256]{1,0:T(8,128)(2,1)S(1)}, bf16[128,256]{1,0:T(8,128)(2,1)S(1)}, u32[]{:S(2)}, u32[]{:S(2)}) collective-permute-start(bf16[128,256]{1,0:T(8,128)(2,1)S(1)} %get-tuple-element.47), channel_id=1, source_target_pairs={{0,8},{4,12},{8,0},{12,4},{1,9},{5,13},{9,1},{13,5},{2,10},{6,14},... | collective-permute-start | bytes 196616 | tf_op jit(solution)/shard_map/ppermute | solution.py:441
  14.4 6.1 %collective-permute-start.13 = (bf16[128,256]{1,0:T(8,128)(2,1)S(1)}, bf16[128,256]{1,0:T(8,128)(2,1)S(1)}, u32[]{:S(2)}, u32[]{:S(2)}) collective-permute-start(bf16[128,256]{1,0:T(8,128)(2,1)S(1)} %get-tuple-element.48), channel_id=1, source_target_pairs={{0,12},{4,8},{8,4},{12,0},{1,13},{5,9},{9,5},{13,1},{2,14},{6,10},... | collective-permute-start | bytes 196616 | tf_op jit(solution)/shard_map/ppermute | solution.py:441
  14.4 7.6 %collective-permute-start = (bf16[128,256]{1,0:T(8,128)(2,1)S(1)}, bf16[128,256]{1,0:T(8,128)(2,1)S(1)}, u32[]{:S(2)}, u32[]{:S(2)}) collective-permute-start(bf16[128,256]{1,0:T(8,128)(2,1)S(1)} %get-tuple-element.41), channel_id=1, source_target_pairs={{0,4},{4,0},{8,12},{12,8},{1,5},{5,1},{9,13},{13,9},{2,6},{6,2},{1... | collective-permute-start | bytes 196616 | tf_op jit(solution)/shard_map/ppermute | solution.py:441
  18.6 6.0 %collective-permute-start.1 = (bf16[128,256]{1,0:T(8,128)(2,1)S(1)}, bf16[128,256]{1,0:T(8,128)(2,1)S(1)}, u32[]{:S(2)}, u32[]{:S(2)}) collective-permute-start(bf16[128,256]{1,0:T(8,128)(2,1)S(1)} %get-tuple-element.42), channel_id=1, source_target_pairs={{0,8},{4,12},{8,0},{12,4},{1,9},{5,13},{9,1},{13,5},{2,10},{6,14},... | collective-permute-start | bytes 196616 | tf_op jit(solution)/shard_map/ppermute | solution.py:441
  20.5 8.8 %collective-permute-start.7 = (bf16[2,2,128,256]{3,2,1,0:T(8,128)(2,1)}, bf16[2,2,128,256]{3,2,1,0:T(8,128)(2,1)S(1)}, u32[]{:S(2)}, u32[]{:S(2)}) collective-permute-start(bf16[2,2,128,256]{3,2,1,0:T(8,128)(2,1)} %get-tuple-element.80), channel_id=1, source_target_pairs={{0,2},{2,0},{1,3},{3,1},{4,6},{6,4},{5,7},{7,5},{8,10},{10,8},{9,1... | collective-permute-start | bytes 786440 | tf_op jit(solution)/shard_map/ppermute | solution.py:441
  22.0 10.1 %collective-permute-start.3 = (bf16[2,2,128,256]{3,2,1,0:T(8,128)(2,1)}, bf16[2,2,128,256]{3,2,1,0:T(8,128)(2,1)S(1)}, u32[]{:S(2)}, u32[]{:S(2)}) collective-permute-start(bf16[2,2,128,256]{3,2,1,0:T(8,128)(2,1)} %get-tuple-element.81), channel_id=1, source_target_pairs={{0,2},{2,0},{1,3},{3,1},{4,6},{6,4},{5,7},{7,5},{8,10},{10,8},{9,1... | collective-permute-start | bytes 786440 | tf_op jit(solution)/shard_map/ppermute | solution.py:441
  22.5 11.1 %collective-permute-start.15 = (bf16[2,2,128,256]{3,2,1,0:T(8,128)(2,1)S(1)}, bf16[2,2,128,256]{3,2,1,0:T(8,128)(2,1)S(1)}, u32[]{:S(2)}, u32[]{:S(2)}) collective-permute-start(bf16[2,2,128,256]{3,2,1,0:T(8,128)(2,1)S(1)} %collective-permute-done.14.refs_5_), channel_id=1, source_target_pairs={{0,16},{16,0},{1,17},{17,1},{2,18},{18,2},{3,19},{19,3},{4,20},{20... | collective-permute-start | bytes 786440 | tf_op jit(solution)/shard_map/ppermute | solution.py:441
  24.0 10.2 %collective-permute-start.19 = (bf16[2,2,128,256]{3,2,1,0:T(8,128)(2,1)}, bf16[2,2,128,256]{3,2,1,0:T(8,128)(2,1)S(1)}, u32[]{:S(2)}, u32[]{:S(2)}) collective-permute-start(bf16[2,2,128,256]{3,2,1,0:T(8,128)(2,1)} %collective-permute-done.18.refs_9_), channel_id=1, source_target_pairs={{0,16},{16,0},{1,17},{17,1},{2,18},{18,2},{3,19},{19,3},{4,20},{20... | collective-permute-start | bytes 786440 | tf_op jit(solution)/shard_map/ppermute | solution.py:441
  24.5 9.7 %collective-permute-start.16 = (bf16[2,2,128,256]{3,2,1,0:T(8,128)(2,1)S(1)}, bf16[2,2,128,256]{3,2,1,0:T(8,128)(2,1)S(1)}, u32[]{:S(2)}, u32[]{:S(2)}) collective-permute-start(bf16[2,2,128,256]{3,2,1,0:T(8,128)(2,1)S(1)} %collective-permute-done.14.refs_5_), channel_id=1, source_target_pairs={{0,1},{1,0},{2,3},{3,2},{4,5},{5,4},{6,7},{7,6},{8,9},{9,8},{10,11... | collective-permute-start | bytes 786440 | tf_op jit(solution)/shard_map/ppermute | solution.py:441
  29.3 5.5 %collective-permute-start.20 = (bf16[2,2,128,256]{3,2,1,0:T(8,128)(2,1)}, bf16[2,2,128,256]{3,2,1,0:T(8,128)(2,1)S(1)}, u32[]{:S(2)}, u32[]{:S(2)}) collective-permute-start(bf16[2,2,128,256]{3,2,1,0:T(8,128)(2,1)} %collective-permute-done.18.refs_9_), channel_id=1, source_target_pairs={{0,1},{1,0},{2,3},{3,2},{4,5},{5,4},{6,7},{7,6},{8,9},{9,8},{10,11... | collective-permute-start | bytes 786440 | tf_op jit(solution)/shard_map/ppermute | solution.py:441
  32.1 9.2 %collective-permute-start.8 = (bf16[2,2,128,256]{3,2,1,0:T(8,128)(2,1)S(1)}, bf16[2,2,128,256]{3,2,1,0:T(8,128)(2,1)S(1)}, u32[]{:S(2)}, u32[]{:S(2)}) collective-permute-start(bf16[2,2,128,256]{3,2,1,0:T(8,128)(2,1)S(1)} %collective-permute-done.7.refs_9_), channel_id=1, source_target_pairs={{0,16},{16,0},{1,17},{17,1},{2,18},{18,2},{3,19},{19,3},{4,20},{20... | collective-permute-start | bytes 786440 | tf_op jit(solution)/shard_map/ppermute | solution.py:441
  33.6 11.0 %collective-permute-start.4 = (bf16[2,2,128,256]{3,2,1,0:T(8,128)(2,1)S(1)}, bf16[2,2,128,256]{3,2,1,0:T(8,128)(2,1)S(1)}, u32[]{:S(2)}, u32[]{:S(2)}) collective-permute-start(bf16[2,2,128,256]{3,2,1,0:T(8,128)(2,1)S(1)} %collective-permute-done.3.refs_5_), channel_id=1, source_target_pairs={{0,16},{16,0},{1,17},{17,1},{2,18},{18,2},{3,19},{19,3},{4,20},{20... | collective-permute-start | bytes 786440 | tf_op jit(solution)/shard_map/ppermute | solution.py:441
  34.3 10.3 %collective-permute-start.17 = (bf16[2,2,128,256]{3,2,1,0:T(8,128)(2,1)S(1)}, bf16[2,2,128,256]{3,2,1,0:T(8,128)(2,1)S(1)}, u32[]{:S(2)}, u32[]{:S(2)}) collective-permute-start(bf16[2,2,128,256]{3,2,1,0:T(8,128)(2,1)S(1)} %collective-permute-done.15.refs_6_), channel_id=1, source_target_pairs={{0,1},{1,0},{2,3},{3,2},{4,5},{5,4},{6,7},{7,6},{8,9},{9,8},{10,11... | collective-permute-start | bytes 786440 | tf_op jit(solution)/shard_map/ppermute | solution.py:441
  34.3 10.9 %collective-permute-start.21 = (bf16[2,2,128,256]{3,2,1,0:T(8,128)(2,1)S(1)}, bf16[2,2,128,256]{3,2,1,0:T(8,128)(2,1)S(1)}, u32[]{:S(2)}, u32[]{:S(2)}) collective-permute-start(bf16[2,2,128,256]{3,2,1,0:T(8,128)(2,1)S(1)} %collective-permute-done.19.refs_10_), channel_id=1, source_target_pairs={{0,1},{1,0},{2,3},{3,2},{4,5},{5,4},{6,7},{7,6},{8,9},{9,8},{10,11... | collective-permute-start | bytes 786440 | tf_op jit(solution)/shard_map/ppermute | solution.py:441
  34.8 18.7 %collective-permute-start.5 = (bf16[2,2,128,256]{3,2,1,0:T(8,128)(2,1)S(1)}, bf16[2,2,128,256]{3,2,1,0:T(8,128)(2,1)S(1)}, u32[]{:S(2)}, u32[]{:S(2)}) collective-permute-start(bf16[2,2,128,256]{3,2,1,0:T(8,128)(2,1)S(1)} %collective-permute-done.3.refs_5_), channel_id=1, source_target_pairs={{0,1},{1,0},{2,3},{3,2},{4,5},{5,4},{6,7},{7,6},{8,9},{9,8},{10,11... | collective-permute-start | bytes 786440 | tf_op jit(solution)/shard_map/ppermute | solution.py:441
  41.3 14.0 %collective-permute-start.9 = (bf16[2,2,128,256]{3,2,1,0:T(8,128)(2,1)S(1)}, bf16[2,2,128,256]{3,2,1,0:T(8,128)(2,1)S(1)}, u32[]{:S(2)}, u32[]{:S(2)}) collective-permute-start(bf16[2,2,128,256]{3,2,1,0:T(8,128)(2,1)S(1)} %collective-permute-done.7.refs_9_), channel_id=1, source_target_pairs={{0,1},{1,0},{2,3},{3,2},{4,5},{5,4},{6,7},{7,6},{8,9},{9,8},{10,11... | collective-permute-start | bytes 786440 | tf_op jit(solution)/shard_map/ppermute | solution.py:441
  44.6 13.2 %collective-permute-start.10 = (bf16[2,2,128,256]{3,2,1,0:T(8,128)(2,1)S(1)}, bf16[2,2,128,256]{3,2,1,0:T(8,128)(2,1)S(1)}, u32[]{:S(2)}, u32[]{:S(2)}) collective-permute-start(bf16[2,2,128,256]{3,2,1,0:T(8,128)(2,1)S(1)} %collective-permute-done.8.refs_10_), channel_id=1, source_target_pairs={{0,1},{1,0},{2,3},{3,2},{4,5},{5,4},{6,7},{7,6},{8,9},{9,8},{10,11... | collective-permute-start | bytes 786440 | tf_op jit(solution)/shard_map/ppermute | solution.py:441
  44.6 13.2 %collective-permute-start.6 = (bf16[2,2,128,256]{3,2,1,0:T(8,128)(2,1)S(1)}, bf16[2,2,128,256]{3,2,1,0:T(8,128)(2,1)S(1)}, u32[]{:S(2)}, u32[]{:S(2)}) collective-permute-start(bf16[2,2,128,256]{3,2,1,0:T(8,128)(2,1)S(1)} %collective-permute-done.4.refs_6_), channel_id=1, source_target_pairs={{0,1},{1,0},{2,3},{3,2},{4,5},{5,4},{6,7},{7,6},{8,9},{9,8},{10,11... | collective-permute-start | bytes 786440 | tf_op jit(solution)/shard_map/ppermute | solution.py:441
  45.1 8.2 %collective-permute-start.2 = (bf16[128,256]{1,0:T(8,128)(2,1)S(1)}, bf16[128,256]{1,0:T(8,128)(2,1)S(1)}, u32[]{:S(2)}, u32[]{:S(2)}) collective-permute-start(bf16[128,256]{1,0:T(8,128)(2,1)S(1)} %get-tuple-element.43), channel_id=1, source_target_pairs={{0,12},{4,8},{8,4},{12,0},{1,13},{5,9},{9,5},{13,1},{2,14},{6,10},... | collective-permute-start | bytes 196616 | tf_op jit(solution)/shard_map/ppermute | solution.py:441
  53.4 8.8 %collective-permute-start.23 = (bf16[128,256]{1,0:T(8,128)(2,1)S(1)}, bf16[128,256]{1,0:T(8,128)(2,1)S(1)}, u32[]{:S(2)}, u32[]{:S(2)}) collective-permute-start(bf16[128,256]{1,0:T(8,128)(2,1)S(1)} %get-tuple-element.51), channel_id=1, source_target_pairs={{0,4},{4,0},{8,12},{12,8},{1,5},{5,1},{9,13},{13,9},{2,6},{6,2},{1... | collective-permute-start | bytes 196616 | tf_op jit(solution)/shard_map/ppermute | solution.py:441
  53.5 11.1 %collective-permute-start.25 = (bf16[128,256]{1,0:T(8,128)(2,1)S(1)}, bf16[128,256]{1,0:T(8,128)(2,1)S(1)}, u32[]{:S(2)}, u32[]{:S(2)}) collective-permute-start(bf16[128,256]{1,0:T(8,128)(2,1)S(1)} %get-tuple-element.53), channel_id=1, source_target_pairs={{0,8},{4,12},{8,0},{12,4},{1,9},{5,13},{9,1},{13,5},{2,10},{6,14},... | collective-permute-start | bytes 196616 | tf_op jit(solution)/shard_map/ppermute | solution.py:441
  55.4 9.2 %collective-permute-start.27 = (bf16[128,256]{1,0:T(8,128)(2,1)S(1)}, bf16[128,256]{1,0:T(8,128)(2,1)S(1)}, u32[]{:S(2)}, u32[]{:S(2)}) collective-permute-start(bf16[128,256]{1,0:T(8,128)(2,1)S(1)} %get-tuple-element.55), channel_id=1, source_target_pairs={{0,12},{4,8},{8,4},{12,0},{1,13},{5,9},{9,5},{13,1},{2,14},{6,10},... | collective-permute-start | bytes 196616 | tf_op jit(solution)/shard_map/ppermute | solution.py:441
  60.2 6.7 %collective-permute-start.24 = (bf16[128,256]{1,0:T(8,128)(2,1)S(1)}, bf16[128,256]{1,0:T(8,128)(2,1)S(1)}, u32[]{:S(2)}, u32[]{:S(2)}) collective-permute-start(bf16[128,256]{1,0:T(8,128)(2,1)S(1)} %get-tuple-element.52), channel_id=1, source_target_pairs={{0,8},{4,12},{8,0},{12,4},{1,9},{5,13},{9,1},{13,5},{2,10},{6,14},... | collective-permute-start | bytes 196616 | tf_op jit(solution)/shard_map/ppermute | solution.py:441
  62.1 6.2 %collective-permute-start.26 = (bf16[128,256]{1,0:T(8,128)(2,1)S(1)}, bf16[128,256]{1,0:T(8,128)(2,1)S(1)}, u32[]{:S(2)}, u32[]{:S(2)}) collective-permute-start(bf16[128,256]{1,0:T(8,128)(2,1)S(1)} %get-tuple-element.54), channel_id=1, source_target_pairs={{0,12},{4,8},{8,4},{12,0},{1,13},{5,9},{9,5},{13,1},{2,14},{6,10},... | collective-permute-start | bytes 196616 | tf_op jit(solution)/shard_map/ppermute | solution.py:441
  73.7 5.8 %collective-permute-start.31 = (bf16[128,256]{1,0:T(8,128)(2,1)S(1)}, bf16[128,256]{1,0:T(8,128)(2,1)S(1)}, u32[]{:S(2)}, u32[]{:S(2)}) collective-permute-start(bf16[128,256]{1,0:T(8,128)(2,1)S(1)} %get-tuple-element.62), channel_id=1, source_target_pairs={{0,4},{4,0},{8,12},{12,8},{1,5},{5,1},{9,13},{13,9},{2,6},{6,2},{1... | collective-permute-start | bytes 196616 | tf_op jit(solution)/shard_map/ppermute | solution.py:441
  74.3 7.3 %collective-permute-start.32 = (bf16[128,256]{1,0:T(8,128)(2,1)S(1)}, bf16[128,256]{1,0:T(8,128)(2,1)S(1)}, u32[]{:S(2)}, u32[]{:S(2)}) collective-permute-start(bf16[128,256]{1,0:T(8,128)(2,1)S(1)} %get-tuple-element.63), channel_id=1, source_target_pairs={{0,8},{4,12},{8,0},{12,4},{1,9},{5,13},{9,1},{13,5},{2,10},{6,14},... | collective-permute-start | bytes 196616 | tf_op jit(solution)/shard_map/ppermute | solution.py:441
  76.6 7.3 %collective-permute-start.33 = (bf16[128,256]{1,0:T(8,128)(2,1)S(1)}, bf16[128,256]{1,0:T(8,128)(2,1)S(1)}, u32[]{:S(2)}, u32[]{:S(2)}) collective-permute-start(bf16[128,256]{1,0:T(8,128)(2,1)S(1)} %get-tuple-element.64), channel_id=1, source_target_pairs={{0,12},{4,8},{8,4},{12,0},{1,13},{5,9},{9,5},{13,1},{2,14},{6,10},... | collective-permute-start | bytes 196616 | tf_op jit(solution)/shard_map/ppermute | solution.py:441
  78.1 24.8 %collective-permute-start.46 = (bf16[16,32,256]{2,1,0:T(8,128)(2,1)S(1)}, bf16[16,32,256]{2,1,0:T(8,128)(2,1)S(1)}, u32[]{:S(2)}, u32[]{:S(2)}) collective-permute-start(bf16[16,32,256]{2,1,0:T(8,128)(2,1)S(1)} %get-tuple-element.75.refs_0_), channel_id=1, source_target_pairs={{0,2},{2,0},{1,3},{3,1},{4,6},{6,4},{5,7},{7,5},{8,10},{10,8},{9,1... | collective-permute-start | bytes 786440 | tf_op jit(solution)/shard_map/ppermute | solution.py:441
  79.5 7.8 %collective-permute-start.28 = (bf16[128,256]{1,0:T(8,128)(2,1)S(1)}, bf16[128,256]{1,0:T(8,128)(2,1)S(1)}, u32[]{:S(2)}, u32[]{:S(2)}) collective-permute-start(bf16[128,256]{1,0:T(8,128)(2,1)S(1)} %get-tuple-element.57), channel_id=1, source_target_pairs={{0,4},{4,0},{8,12},{12,8},{1,5},{5,1},{9,13},{13,9},{2,6},{6,2},{1... | collective-permute-start | bytes 196616 | tf_op jit(solution)/shard_map/ppermute | solution.py:441
  79.5 9.1 %collective-permute-start.29 = (bf16[128,256]{1,0:T(8,128)(2,1)S(1)}, bf16[128,256]{1,0:T(8,128)(2,1)S(1)}, u32[]{:S(2)}, u32[]{:S(2)}) collective-permute-start(bf16[128,256]{1,0:T(8,128)(2,1)S(1)} %get-tuple-element.58), channel_id=1, source_target_pairs={{0,8},{4,12},{8,0},{12,4},{1,9},{5,13},{9,1},{13,5},{2,10},{6,14},... | collective-permute-start | bytes 196616 | tf_op jit(solution)/shard_map/ppermute | solution.py:441
  81.6 9.3 %collective-permute-start.30 = (bf16[128,256]{1,0:T(8,128)(2,1)S(1)}, bf16[128,256]{1,0:T(8,128)(2,1)S(1)}, u32[]{:S(2)}, u32[]{:S(2)}) collective-permute-start(bf16[128,256]{1,0:T(8,128)(2,1)S(1)} %get-tuple-element.59), channel_id=1, source_target_pairs={{0,12},{4,8},{8,4},{12,0},{1,13},{5,9},{9,5},{13,1},{2,14},{6,10},... | collective-permute-start | bytes 196616 | tf_op jit(solution)/shard_map/ppermute | solution.py:441
  86.4 6.1 %collective-permute-start.35 = (bf16[128,256]{1,0:T(8,128)(2,1)S(1)}, bf16[128,256]{1,0:T(8,128)(2,1)S(1)}, u32[]{:S(2)}, u32[]{:S(2)}) collective-permute-start(bf16[128,256]{1,0:T(8,128)(2,1)S(1)} %get-tuple-element.67), channel_id=1, source_target_pairs={{0,4},{4,0},{8,12},{12,8},{1,5},{5,1},{9,13},{13,9},{2,6},{6,2},{1... | collective-permute-start | bytes 196616 | tf_op jit(solution)/shard_map/ppermute | solution.py:441
  87.2 5.3 %collective-permute-start.37 = (bf16[128,256]{1,0:T(8,128)(2,1)S(1)}, bf16[128,256]{1,0:T(8,128)(2,1)S(1)}, u32[]{:S(2)}, u32[]{:S(2)}) collective-permute-start(bf16[128,256]{1,0:T(8,128)(2,1)S(1)} %get-tuple-element.69), channel_id=1, source_target_pairs={{0,8},{4,12},{8,0},{12,4},{1,9},{5,13},{9,1},{13,5},{2,10},{6,14},... | collective-permute-start | bytes 196616 | tf_op jit(solution)/shard_map/ppermute | solution.py:441
  88.5 6.1 %collective-permute-start.39 = (bf16[128,256]{1,0:T(8,128)(2,1)S(1)}, bf16[128,256]{1,0:T(8,128)(2,1)S(1)}, u32[]{:S(2)}, u32[]{:S(2)}) collective-permute-start(bf16[128,256]{1,0:T(8,128)(2,1)S(1)} %get-tuple-element.71), channel_id=1, source_target_pairs={{0,12},{4,8},{8,4},{12,0},{1,13},{5,9},{9,5},{13,1},{2,14},{6,10},... | collective-permute-start | bytes 196616 | tf_op jit(solution)/shard_map/ppermute | solution.py:441
  92.5 16.3 %collective-permute-start.47 = (bf16[16,32,256]{2,1,0:T(8,128)(2,1)S(1)}, bf16[16,32,256]{2,1,0:T(8,128)(2,1)S(1)}, u32[]{:S(2)}, u32[]{:S(2)}) collective-permute-start(bf16[16,32,256]{2,1,0:T(8,128)(2,1)S(1)} %get-tuple-element.75.refs_0_), channel_id=1, source_target_pairs={{0,1},{1,0},{2,3},{3,2},{4,5},{5,4},{6,7},{7,6},{8,9},{9,8},{10,11... | collective-permute-start | bytes 786440 | tf_op jit(solution)/shard_map/ppermute | solution.py:441
  92.6 16.7 %collective-permute-start.40 = (bf16[16,32,256]{2,1,0:T(8,128)(2,1)S(1)}, bf16[16,32,256]{2,1,0:T(8,128)(2,1)S(1)}, u32[]{:S(2)}, u32[]{:S(2)}) collective-permute-start(bf16[16,32,256]{2,1,0:T(8,128)(2,1)S(1)} %get-tuple-element.72.refs_0_), channel_id=1, source_target_pairs={{0,2},{2,0},{1,3},{3,1},{4,6},{6,4},{5,7},{7,5},{8,10},{10,8},{9,1... | collective-permute-start | bytes 786440 | tf_op jit(solution)/shard_map/ppermute | solution.py:441
  94.6 7.0 %collective-permute-start.36 = (bf16[128,256]{1,0:T(8,128)(2,1)S(1)}, bf16[128,256]{1,0:T(8,128)(2,1)S(1)}, u32[]{:S(2)}, u32[]{:S(2)}) collective-permute-start(bf16[128,256]{1,0:T(8,128)(2,1)S(1)} %get-tuple-element.68), channel_id=1, source_target_pairs={{0,8},{4,12},{8,0},{12,4},{1,9},{5,13},{9,1},{13,5},{2,10},{6,14},... | collective-permute-start | bytes 196616 | tf_op jit(solution)/shard_map/ppermute | solution.py:441
  96.7 6.2 %collective-permute-start.38 = (bf16[128,256]{1,0:T(8,128)(2,1)S(1)}, bf16[128,256]{1,0:T(8,128)(2,1)S(1)}, u32[]{:S(2)}, u32[]{:S(2)}) collective-permute-start(bf16[128,256]{1,0:T(8,128)(2,1)S(1)} %get-tuple-element.70), channel_id=1, source_target_pairs={{0,12},{4,8},{8,4},{12,0},{1,13},{5,9},{9,5},{13,1},{2,14},{6,10},... | collective-permute-start | bytes 196616 | tf_op jit(solution)/shard_map/ppermute | solution.py:441
  101.6 5.5 %collective-permute-start.49 = (bf16[16,32,128]{2,1,0:T(8,128)(2,1)S(1)}, bf16[16,32,128]{2,1,0:T(8,128)(2,1)S(1)}, u32[]{:S(2)}, u32[]{:S(2)}) collective-permute-start(bf16[16,32,128]{2,1,0:T(8,128)(2,1)S(1)} %get-tuple-element.77), channel_id=1, source_target_pairs={{0,2},{2,0},{1,3},{3,1},{4,6},{6,4},{5,7},{7,5},{8,10},{10,8},{9,1... | collective-permute-start | bytes 393224 | tf_op jit(solution)/shard_map/ppermute | solution.py:441
  102.9 5.9 %collective-permute-start.50 = (bf16[16,32,128]{2,1,0:T(8,128)(2,1)S(1)}, bf16[16,32,128]{2,1,0:T(8,128)(2,1)S(1)}, u32[]{:S(2)}, u32[]{:S(2)}) collective-permute-start(bf16[16,32,128]{2,1,0:T(8,128)(2,1)S(1)} %get-tuple-element.76.refs_4_), channel_id=1, source_target_pairs={{0,1},{1,0},{2,3},{3,2},{4,5},{5,4},{6,7},{7,6},{8,9},{9,8},{10,11... | collective-permute-start | bytes 393224 | tf_op jit(solution)/shard_map/ppermute | solution.py:441
  102.9 13.3 %collective-permute-start.48 = (bf16[16,32,256]{2,1,0:T(8,128)(2,1)S(1)}, bf16[16,32,256]{2,1,0:T(8,128)(2,1)S(1)}, u32[]{:S(2)}, u32[]{:S(2)}) collective-permute-start(bf16[16,32,256]{2,1,0:T(8,128)(2,1)S(1)} %collective-permute-done.46.refs_1_), channel_id=1, source_target_pairs={{0,1},{1,0},{2,3},{3,2},{4,5},{5,4},{6,7},{7,6},{8,9},{9,8},{10,11... | collective-permute-start | bytes 786440 | tf_op jit(solution)/shard_map/ppermute | solution.py:441
  107.1 5.0 %collective-permute-start.43 = (bf16[16,32,128]{2,1,0:T(8,128)(2,1)S(1)}, bf16[16,32,128]{2,1,0:T(8,128)(2,1)S(1)}, u32[]{:S(2)}, u32[]{:S(2)}) collective-permute-start(bf16[16,32,128]{2,1,0:T(8,128)(2,1)S(1)} %get-tuple-element.74), channel_id=1, source_target_pairs={{0,2},{2,0},{1,3},{3,1},{4,6},{6,4},{5,7},{7,5},{8,10},{10,8},{9,1... | collective-permute-start | bytes 393224 | tf_op jit(solution)/shard_map/ppermute | solution.py:441
  108.8 10.4 %collective-permute-start.41 = (bf16[16,32,256]{2,1,0:T(8,128)(2,1)S(1)}, bf16[16,32,256]{2,1,0:T(8,128)(2,1)S(1)}, u32[]{:S(2)}, u32[]{:S(2)}) collective-permute-start(bf16[16,32,256]{2,1,0:T(8,128)(2,1)S(1)} %get-tuple-element.72.refs_0_), channel_id=1, source_target_pairs={{0,1},{1,0},{2,3},{3,2},{4,5},{5,4},{6,7},{7,6},{8,9},{9,8},{10,11... | collective-permute-start | bytes 786440 | tf_op jit(solution)/shard_map/ppermute | solution.py:441
  109.3 9.9 %collective-permute-start.42 = (bf16[16,32,256]{2,1,0:T(8,128)(2,1)S(1)}, bf16[16,32,256]{2,1,0:T(8,128)(2,1)S(1)}, u32[]{:S(2)}, u32[]{:S(2)}) collective-permute-start(bf16[16,32,256]{2,1,0:T(8,128)(2,1)S(1)} %collective-permute-done.40.refs_1_), channel_id=1, source_target_pairs={{0,1},{1,0},{2,3},{3,2},{4,5},{5,4},{6,7},{7,6},{8,9},{9,8},{10,11... | collective-permute-start | bytes 786440 | tf_op jit(solution)/shard_map/ppermute | solution.py:441
  112.1 7.1 %collective-permute-start.44 = (bf16[16,32,128]{2,1,0:T(8,128)(2,1)S(1)}, bf16[16,32,128]{2,1,0:T(8,128)(2,1)S(1)}, u32[]{:S(2)}, u32[]{:S(2)}) collective-permute-start(bf16[16,32,128]{2,1,0:T(8,128)(2,1)S(1)} %get-tuple-element.73.refs_4_), channel_id=1, source_target_pairs={{0,1},{1,0},{2,3},{3,2},{4,5},{5,4},{6,7},{7,6},{8,9},{9,8},{10,11... | collective-permute-start | bytes 393224 | tf_op jit(solution)/shard_map/ppermute | solution.py:441
  112.1 7.1 %collective-permute-start.45 = (bf16[16,32,128]{2,1,0:T(8,128)(2,1)S(1)}, bf16[16,32,128]{2,1,0:T(8,128)(2,1)S(1)}, u32[]{:S(2)}, u32[]{:S(2)}) collective-permute-start(bf16[16,32,128]{2,1,0:T(8,128)(2,1)S(1)} %collective-permute-done.43.refs_5_), channel_id=1, source_target_pairs={{0,1},{1,0},{2,3},{3,2},{4,5},{5,4},{6,7},{7,6},{8,9},{9,8},{10,11... | collective-permute-start | bytes 393224 | tf_op jit(solution)/shard_map/ppermute | solution.py:441
  (12 other events, 105.0 us)

commit v2 on v1

--- a/solution.py
+++ b/solution.py
@@ -12,6 +12,7 @@
 inv_sqrt_two = 0.7071067811865476
 inv_sqrt_two_pi = 0.3989422804014327
 LANES = 128
+MEBI = 1 << 20
 VMEM_BYTES = 40 * 1024 * 1024
 BF16 = jnp.bfloat16
 F32 = jnp.float32
@@ -52,8 +53,6 @@
         self.halves = 2 if self.m_loc % 16 == 0 else 1
         self.per_q = self.m_loc // self.nq
         self.mh = self.per_q // self.halves
-        self.pieces = 2 if self.mh % 2 == 0 else 1
-        self.mp = self.mh // self.pieces
         self.mu = self.m_loc // self.halves
         self.rk = 2 * self.rows
         self.wide = self.n_lat * self.rk
@@ -143,7 +142,7 @@
             ],
         ),
         out_shape=[jax.ShapeDtypeStruct(shape, BF16)] * n_out,
-        compiler_params=params(),
+        compiler_params=pltpu.CompilerParams(vmem_limit_bytes=60 * MEBI),
         cost_estimate=pl.CostEstimate(
             flops=2 * plan.rows * plan.lon * modes2 * plan.width,
             bytes_accessed=2 * plan.rows * plan.lon * plan.width,
@@ -260,154 +259,189 @@
     return jnp.where(real, first_sign * swapped, -first_sign * swapped)
 
 
-def mix_specs(plan, h):
-    own = pl.BlockSpec(
-        (2, plan.nq, plan.mh, plan.o_w, plan.width), lambda *_: (0, 0, h, 0, 0)
-    )
-    there = full((2, plan.mp, plan.o_w, plan.width))
-    return own, there
-
-
-def weight_of(plan, own_ref, others, x, q, slot, t, j):
-    if x == 0:
-        return own_ref[j, q, t]
-    piece, at = divmod(t, plan.mp)
-    return others[((x - 1) * plan.pieces + piece) * plan.nq + slot][j, at]
-
-
-def mix_forward(plan, h, ids, blocks, own, others):
-    n, n_other = plan.n_lat, len(others)
-    shape = block_shape(plan)
+def own_weights(plan, h):
+    shape = (2, plan.nq, plan.mh, plan.o_w, plan.width)
+    return pl.BlockSpec(shape, lambda *_: (0, 0, h, 0, 0))
+
+
+def pack(plan, h, blocks):
+    wide = (plan.mu, plan.wide, plan.width)
+
+    def body(*refs):
+        ins, out = refs[: plan.n_lat], refs[plan.n_lat]
+        parts = [ref[...].astype(F32).reshape(plan.mu, plan.rk, plan.width) for ref in ins]
+        out[...] = jnp.concatenate(parts, axis=1).astype(BF16)
+
+    return pl.pallas_call(
+        body,
+        out_shape=jax.ShapeDtypeStruct(wide, BF16),
+        compiler_params=params(),
+        cost_estimate=pl.CostEstimate(flops=0, bytes_accessed=2 * MEBI, transcendentals=0),
+        name=f"pack_{h}",
+    )(*blocks)
+
+
+def pack_gradients(plan, h, ids, blocks):
+    part = (plan.mu, plan.wide, plan.o_w)
 
     def body(ids_ref, *refs):
-        ins, own_ref = refs[:n], refs[n]
-        there = refs[n + 1 : n + 1 + n_other]
-        outs = refs[n + 1 + n_other : 2 * n + 1 + n_other]
-        packed, plain, turn, held = refs[2 * n + 1 + n_other :]
-        for s in range(n):
-            block = ins[s][...].astype(F32).reshape(plan.mu, plan.rk, plan.width)
-            plain[:, s * plan.rk : (s + 1) * plan.rk, :] = block
-            turn[:, s * plan.rk : (s + 1) * plan.rk, :] = turned(plan, block, -1.0)
-        packed[...] = plain[...].astype(BF16)
-        for slot in range(plan.nq):
-            q = ids_ref[1] ^ slot
-            for t in range(plan.mh):
-                u = q * plan.mh + t
-                one, two = plain[u].astype(BF16), turn[u].astype(BF16)
-                for x in range(plan.n_chan):
-                    real = weight_of(plan, own_ref, there, x, q, slot, t, 0)
-                    imag = weight_of(plan, own_ref, there, x, q, slot, t, 1)
-                    dims = (((1,), (1,)), ((), ()))
-                    held[ids_ref[2] ^ x, u] = lax.dot_general(
-                        one, real, dims, preferred_element_type=F32
-                    ) + lax.dot_general(two, imag, dims, preferred_element_type=F32)
-        for s in range(n):
-            lanes = [held[c, :, s * plan.rk : (s + 1) * plan.rk, :] for c in range(plan.n_chan)]
-            outs[s][...] = jnp.concatenate(lanes, axis=2).reshape(shape).astype(BF16)
-
-    own_spec, there_spec = mix_specs(plan, h)
-    wide = (plan.mu, plan.wide, plan.width)
+        ins, outs, held = refs[: plan.n_lat], refs[plan.n_lat : -1], refs[-1]
+        blocks = [ref[...].astype(F32).reshape(plan.mu, plan.rk, plan.width) for ref in ins]
+        every = jnp.concatenate(blocks, axis=1)
+        for c in range(plan.n_chan):
+            held[c] = every[:, :, c * plan.o_w : (c + 1) * plan.o_w]
+        for x in range(plan.n_chan):
+            outs[x][...] = held[ids_ref[2] ^ x].astype(BF16)
+
     return pl.pallas_call(
         body,
         grid_spec=pltpu.PrefetchScalarGridSpec(
             num_scalar_prefetch=1,
             grid=(1,),
-            in_specs=[full(shape)] * n + [own_spec] + [there_spec] * n_other,
-            out_specs=[full(shape)] * n + [full(wide)],
-            scratch_shapes=[
-                pltpu.VMEM(wide, F32),
-                pltpu.VMEM(wide, F32),
-                pltpu.VMEM((plan.n_chan, plan.mu, plan.wide, plan.o_w), F32),
-            ],
-        ),
-        out_shape=[jax.ShapeDtypeStruct(shape, BF16)] * n + [jax.ShapeDtypeStruct(wide, BF16)],
-        compiler_params=params(),
-        cost_estimate=pl.CostEstimate(
-            flops=64 * plan.mu * plan.width * plan.width * plan.wide,
-            bytes_accessed=4 * plan.mu * plan.width * plan.width,
-            transcendentals=0,
-        ),
-        name=f"mix_forward_{h}",
-    )(ids, *blocks, own, *others)
-
-
-def mix_backward(plan, h, ids, blocks, own, others):
-    n, n_other = plan.n_lat, len(others)
+            in_specs=[full(block_shape(plan))] * plan.n_lat,
+            out_specs=[full(part)] * plan.n_chan,
+            scratch_shapes=[pltpu.VMEM((plan.n_chan, *part), F32)],
+        ),
+        out_shape=[jax.ShapeDtypeStruct(part, BF16)] * plan.n_chan,
+        compiler_params=params(),
+        cost_estimate=pl.CostEstimate(flops=0, bytes_accessed=2 * MEBI, transcendentals=0),
+        name=f"pack_gradients_{h}",
+    )(ids, *blocks)
+
+
+def merge(plan, h, ids, pieces):
     shape = block_shape(plan)
 
     def body(ids_ref, *refs):
-        ins, own_ref = refs[:n], refs[n]
-        there = refs[n + 1 : n + 1 + n_other]
-        outs = refs[n + 1 + n_other : 2 * n + 1 + n_other]
-        packed = refs[2 * n + 1 + n_other : 2 * n + 1 + n_other + plan.n_chan]
-        plain, turn, held = refs[2 * n + 1 + n_other + plan.n_chan :]
-        for s in range(n):
-            block = ins[s][...].astype(F32).reshape(plan.mu, plan.rk, plan.width)
-            flip = turned(plan, block, 1.0)
-            for c in range(plan.n_chan):
-                lanes = slice(c * plan.o_w, (c + 1) * plan.o_w)
-                plain[c, :, s * plan.rk : (s + 1) * plan.rk, :] = block[:, :, lanes]
-                turn[c, :, s * plan.rk : (s + 1) * plan.rk, :] = flip[:, :, lanes]
+        ins, outs, held = refs[: plan.n_chan], refs[plan.n_chan : -1], refs[-1]
         for x in range(plan.n_chan):
-            packed[x][...] = plain[ids_ref[2] ^ x].astype(BF16)
-        for slot in range(plan.nq):
-            q = ids_ref[1] ^ slot
-            for t in range(plan.mh):
-                u = q * plan.mh + t
-                total = None
-                for x in range(plan.n_chan):
-                    real = weight_of(plan, own_ref, there, x, q, slot, t, 0)
-                    imag = weight_of(plan, own_ref, there, x, q, slot, t, 1)
-                    one = plain[ids_ref[2] ^ x, u].astype(BF16)
-                    two = turn[ids_ref[2] ^ x, u].astype(BF16)
-                    term = jnp.dot(one, real, preferred_element_type=F32) + jnp.dot(
-                        two, imag, preferred_element_type=F32
-                    )
-                    total = term if total is None else total + term
-                held[u] = total
-        for s in range(n):
-            outs[s][...] = held[:, s * plan.rk : (s + 1) * plan.rk, :].reshape(shape).astype(BF16)
-
-    own_spec, there_spec = mix_specs(plan, h)
+            held[ids_ref[2] ^ x] = ins[x][...].astype(F32)
+        every = jnp.concatenate([held[c] for c in range(plan.n_chan)], axis=2)
+        for s in range(plan.n_lat):
+            block = every[:, s * plan.rk : (s + 1) * plan.rk, :]
+            outs[s][...] = block.reshape(shape).astype(BF16)
+
     part = (plan.mu, plan.wide, plan.o_w)
     return pl.pallas_call(
         body,
         grid_spec=pltpu.PrefetchScalarGridSpec(
             num_scalar_prefetch=1,
             grid=(1,),
-            in_specs=[full(shape)] * n + [own_spec] + [there_spec] * n_other,
-            out_specs=[full(shape)] * n + [full(part)] * plan.n_chan,
-            scratch_shapes=[
-                pltpu.VMEM((plan.n_chan, *part), F32),
-                pltpu.VMEM((plan.n_chan, *part), F32),
-                pltpu.VMEM((plan.mu, plan.wide, plan.width), F32),
-            ],
-        ),
-        out_shape=[jax.ShapeDtypeStruct(shape, BF16)] * n
-        + [jax.ShapeDtypeStruct(part, BF16)] * plan.n_chan,
-        compiler_params=params(),
-        cost_estimate=pl.CostEstimate(
-            flops=64 * plan.mu * plan.width * plan.width * plan.wide,
-            bytes_accessed=4 * plan.mu * plan.width * plan.width,
-            transcendentals=0,
-        ),
+            in_specs=[full(part)] * plan.n_chan,
+            out_specs=[full(shape)] * plan.n_lat,
+            scratch_shapes=[pltpu.VMEM((plan.n_chan, *part), F32)],
+        ),
+        out_shape=[jax.ShapeDtypeStruct(shape, BF16)] * plan.n_lat,
+        compiler_params=params(),
+        cost_estimate=pl.CostEstimate(flops=0, bytes_accessed=2 * MEBI, transcendentals=0),
+        name=f"merge_{h}",
+    )(ids, *pieces)
+
+
+def mix_forward(plan, h, spectra, own):
+    wide = (plan.mu, plan.wide, plan.width)
+    tall = (plan.mu, plan.n_chan * plan.wide, plan.width)
+    part = (plan.mu, plan.wide, plan.o_w)
+
+    def body(*refs):
+        ins, own_ref = refs[: plan.n_chan], refs[plan.n_chan]
+        outs, every = refs[plan.n_chan + 1 : -1], refs[-1]
+        dims = (((1,), (1,)), ((), ()))
+        for q in range(plan.nq):
+            for t in range(plan.mh):
+                u = q * plan.mh + t
+                rows = jnp.concatenate([ref[u].astype(F32) for ref in ins], axis=0)
+                every[u] = rows.astype(BF16)
+                groups = rows.reshape(-1, plan.rk, plan.width)
+                turn = turned(plan, groups, -1.0).reshape(rows.shape)
+                mixed = lax.dot_general(
+                    rows.astype(BF16), own_ref[0, q, t], dims, preferred_element_type=F32
+                ) + lax.dot_general(
+                    turn.astype(BF16), own_ref[1, q, t], dims, preferred_element_type=F32
+                )
+                for x in range(plan.n_chan):
+                    outs[x][u] = mixed[x * plan.wide : (x + 1) * plan.wide].astype(BF16)
+
+    return pl.pallas_call(
+        body,
+        grid=(1,),
+        in_specs=[full(wide)] * plan.n_chan + [own_weights(plan, h)],
+        out_specs=[full(part)] * plan.n_chan + [full(tall)],
+        out_shape=[jax.ShapeDtypeStruct(part, BF16)] * plan.n_chan
+        + [jax.ShapeDtypeStruct(tall, BF16)],
+        compiler_params=params(),
+        cost_estimate=pl.CostEstimate(flops=0, bytes_accessed=7 * MEBI, transcendentals=0),
+        name=f"mix_forward_{h}",
+    )(*spectra, own)
+
+
+def mix_backward(plan, h, grads, own):
+    wide = (plan.mu, plan.wide, plan.width)
+    part = (plan.mu, plan.wide, plan.o_w)
+    tall = (plan.mu, plan.n_chan * plan.wide, plan.o_w)
+
+    def body(*refs):
+        ins, own_ref = refs[: plan.n_chan], refs[plan.n_chan]
+        outs, every = refs[plan.n_chan + 1 : -1], refs[-1]
+        for q in range(plan.nq):
+            for t in range(plan.mh):
+                u = q * plan.mh + t
+                rows = jnp.concatenate([ref[u].astype(F32) for ref in ins], axis=0)
+                every[u] = rows.astype(BF16)
+                groups = rows.reshape(-1, plan.rk, plan.o_w)
+                turn = turned(plan, groups, 1.0).reshape(rows.shape)
+                back = jnp.dot(
+                    rows.astype(BF16), own_ref[0, q, t], preferred_element_type=F32
+                ) + jnp.dot(turn.astype(BF16), own_ref[1, q, t], preferred_element_type=F32)
+                for x in range(plan.n_chan):
+                    outs[x][u] = back[x * plan.wide : (x + 1) * plan.wide].astype(outs[x].dtype)
+
+    return pl.pallas_call(
+        body,
+        grid=(1,),
+        in_specs=[full(part)] * plan.n_chan + [own_weights(plan, h)],
+        out_specs=[full(wide)] * plan.n_chan + [full(tall)],
+        out_shape=[jax.ShapeDtypeStruct(wide, F32)]
+        + [jax.ShapeDtypeStruct(wide, BF16)] * (plan.n_chan - 1)
+        + [jax.ShapeDtypeStruct(tall, BF16)],
+        compiler_params=params(),
+        cost_estimate=pl.CostEstimate(flops=0, bytes_accessed=7 * MEBI, transcendentals=0),
         name=f"mix_backward_{h}",
-    )(ids, *blocks, own, *others)
+    )(*grads, own)
+
+
+def merge_gradients(plan, h, parts):
+    wide = (plan.mu, plan.wide, plan.width)
+    shape = block_shape(plan)
+
+    def body(*refs):
+        ins, outs = refs[: plan.n_chan], refs[plan.n_chan :]
+        total = sum(ref[...].astype(F32) for ref in ins)
+        for s in range(plan.n_lat):
+            block = total[:, s * plan.rk : (s + 1) * plan.rk, :]
+            outs[s][...] = block.reshape(shape).astype(BF16)
+
+    return pl.pallas_call(
+        body,
+        out_shape=[jax.ShapeDtypeStruct(shape, BF16)] * plan.n_lat,
+        compiler_params=params(),
+        cost_estimate=pl.CostEstimate(flops=0, bytes_accessed=2 * MEBI, transcendentals=0),
+        name=f"merge_gradients_{h}",
+    )(*parts)
 
 
 def weight_gradient(plan, h, spectra, grads, before):
     n = len(spectra)
     scale = 1.0 / (plan.rows * plan.n_lat * plan.n_chan)
+    rows = plan.n_chan * plan.wide
 
     def body(*refs):
         s_refs, g_refs, out = refs[:n], refs[n : 2 * n], refs[-1]
         for t in range(plan.mh):
-            total = [None, None]
-            s_all = jnp.concatenate([s_refs[i][t].astype(F32) for i in range(n)], axis=0)
-            g_all = jnp.concatenate([g_refs[i][t].astype(F32) for i in range(n)], axis=0)
+            s_all = jnp.concatenate([ref[t].astype(F32) for ref in s_refs], axis=0).astype(BF16)
+            g_all = jnp.concatenate([ref[t].astype(F32) for ref in g_refs], axis=0)
             groups = g_all.reshape(-1, plan.rk, plan.o_w)
             g_turn = turned(plan, groups, 1.0).reshape(g_all.shape)
-            s_all = s_all.astype(BF16)
             for j, g in enumerate((g_all, g_turn)):
                 total = lax.dot_general(
                     g.astype(BF16), s_all, (((0,), (0,)), ((), ())), preferred_element_type=F32
@@ -419,8 +453,8 @@
     return pl.pallas_call(
         body,
         grid=(plan.nq,),
-        in_specs=[pl.BlockSpec((plan.mh, plan.wide, plan.width), lambda q: (q, 0, 0))] * n
-        + [pl.BlockSpec((plan.mh, plan.wide, plan.o_w), lambda q: (q, 0, 0))] * n
+        in_specs=[pl.BlockSpec((plan.mh, rows, plan.width), lambda q: (q, 0, 0))] * n
+        + [pl.BlockSpec((plan.mh, rows, plan.o_w), lambda q: (q, 0, 0))] * n
         + [pl.BlockSpec(memory_space=pl.ANY)] * len(earlier),
         out_specs=pl.BlockSpec(
             (2, 1, 1, plan.mh, plan.o_w, plan.width), lambda q: (0, q, h, 0, 0, 0)
@@ -428,11 +462,7 @@
         out_shape=jax.ShapeDtypeStruct(out_shape, F32),
         input_output_aliases={2 * n: 0} if earlier else {},
         compiler_params=params(),
-        cost_estimate=pl.CostEstimate(
-            flops=4 * plan.mu * plan.wide * n * plan.o_w * plan.width,
-            bytes_accessed=8 * plan.mu * plan.o_w * plan.width,
-            transcendentals=0,
-        ),
+        cost_estimate=pl.CostEstimate(flops=0, bytes_accessed=10 * MEBI, transcendentals=0),
         name=f"weight_gradient_{h}",
     )(*spectra, *grads, *earlier)
 
@@ -443,6 +473,10 @@
 
 def spread(values, axis, size):
     return [value if s == 0 else hop(value, axis, size, s) for s in range(size) for value in values]
+
+
+def after(value, *others):
+    return lax.optimization_barrier((value, *others))[0]
 
 
 def shards(plan, field, cotangent, weights):
@@ -452,47 +486,44 @@
     lat, chan = lax.axis_index("lat"), lax.axis_index("chan")
     q = lax.axis_index("rep") * plan.n_parts + lax.axis_index("parts")
     ids = jnp.stack([lat, q, chan]).astype(jnp.int32)
-
     own = weights.reshape(2, plan.nq, plan.per_q, plan.o_w, plan.width)
-    mine = lax.dynamic_index_in_dim(own, q, 1, keepdims=False)
-    others = [[] for _ in range(plan.halves)]
-    for x in range(1, plan.n_chan):
-        for h in range(plan.halves):
-            for p in range(plan.pieces):
-                at = (h * plan.pieces + p) * plan.mp
-                got = [hop(mine[:, at : at + plan.mp], "chan", plan.n_chan, x)]
-                got = spread(got, "parts", plan.n_parts)
-                others[h] += spread(got, "rep", plan.n_rep)
-
-    def to_lat(blocks, halves=range(plan.halves)):
-        return [
-            hop(blocks[s * len(halves) + i], "lat", plan.n_lat, s) if s else blocks[i]
-            for s in range(plan.n_lat)
-            for i in range(len(halves))
-        ]
+    halves, chans = range(plan.halves), range(plan.n_chan)
+
+    def to_lat(blocks):
+        return [hop(block, "lat", plan.n_lat, s) if s else block for s, block in enumerate(blocks)]
+
+    def over_chan(values):
+        return [hop(value, "chan", plan.n_chan, x) if x else value for x, value in enumerate(values)]
+
+    def rep_too(values):
+        return spread(values, "rep", plan.n_rep)
 
     field, cotangent = field[0], cotangent[0]
-    spectra = to_lat(forward_dft(plan, ids, forward, field))
-    packed_s, mixed = [], [None] * (plan.n_lat * plan.halves)
-    for h in range(plan.halves):
-        *out, packed = mix_forward(plan, h, ids, spectra[h :: plan.halves], own, others[h])
-        packed_s.append(packed)
-        mixed[h :: plan.halves] = to_lat(out, [h])
-    grads = to_lat(middle(plan, ids, inverse_t, inverse, cotangent, mixed))
-    packed_g, spectral = [], [None] * (plan.n_lat * plan.halves)
-    for h in range(plan.halves):
-        out = mix_backward(plan, h, ids, grads[h :: plan.halves], own, others[h])
-        packed_g.append(out[plan.n_lat :])
-        spectral[h :: plan.halves] = to_lat(out[: plan.n_lat], [h])
+    blocks = forward_dft(plan, ids, forward, field)
+    spectra = [None] * plan.halves
+    for h in halves:
+        packed = pack(plan, h, to_lat(blocks[h :: plan.halves]))
+        spectra[h] = over_chan([packed] * plan.n_chan)
+    mixed, every_s = [None] * len(blocks), []
+    for h in halves:
+        *pieces, tall = mix_forward(plan, h, spectra[h], own)
+        mixed[h :: plan.halves] = to_lat(merge(plan, h, ids, over_chan(pieces)))
+        every_s.append(tall)
+
+    grads = middle(plan, ids, inverse_t, inverse, cotangent, mixed)
+    spectral, every_g = [None] * len(blocks), []
+    for h in halves:
+        pieces = over_chan(pack_gradients(plan, h, ids, to_lat(grads[h :: plan.halves])))
+        *parts, tall = mix_backward(plan, h, pieces, own)
+        spectral[h :: plan.halves] = to_lat(merge_gradients(plan, h, over_chan(parts)))
+        every_g.append(tall)
     grad_field = final_dft(plan, ids, forward_t, cotangent, spectral)
 
     weight_grad = None
-    for h in range(plan.halves):
-        s_all = spread(spread([packed_s[h]], "chan", plan.n_chan), "rep", plan.n_rep)
-        g_all = [packed_g[h][0]]
-        g_all += [hop(packed_g[h][x], "chan", plan.n_chan, x) for x in range(1, plan.n_chan)]
-        g_all = spread(g_all, "rep", plan.n_rep)
-        weight_grad = weight_gradient(plan, h, s_all, g_all, weight_grad)
+    for h in halves:
+        weight_grad = weight_gradient(
+            plan, h, rep_too([every_s[h]]), rep_too([every_g[h]]), weight_grad
+        )
     return (grad_field[None], weight_grad.reshape(weights.shape))
 
 

time: 122 us -> 112 us (0.918)
  waiting for transfers between devices: 35.7 us -> 27.4 us
  local copies, waits for them, and re-layouts: 5.79 us -> 3.89 us
  Pallas kernels: 27.1 us -> 25.4 us
    ppermute x52 -> x36, waiting for transfers between devices: 35.7 us -> 27.4 us  [hop(): return lax.ppermute(value, axis, [(i, i ^ s) for i in range(size)])]
    pallas_call x6 -> x14, Pallas kernels: 15.8 us -> 11 us  [the longest x2 5.91 us: weight_gradient(): pl.pallas_call(body, grid=(plan.nq,), in_specs=[pl.BlockSpec((plan.mh, ro...]
    pallas_call x1, Pallas kernels: 2.39 us -> 5.41 us  [forward_dft(): pl.pallas_call(body, grid_spec=pltpu.PrefetchScalarGridSpec(num_scalar_pr...]
    squeeze x1 -> x0, local copies, waits for them, and re-layouts: 1.45 us -> none  [shards(): mine = lax.dynamic_index_in_dim(own, q, 1, keepdims=False)]
    ppermute x52 -> x36, starting transfers between devices: 52.6 us -> 53.7 us  [hop(): return lax.ppermute(value, axis, [(i, i ^ s) for i in range(size)])]
    unnamed x16 -> x18, local copies, waits for them, and re-layouts: 3.36 us -> 3.89 us
  transfers between devices with their start and end apart: 52 -> 36, of which waited for: 15 -> 14; matrix products, arithmetic and copies ran while one was open for 0% -> 0% of each run, Pallas kernels for 15% -> 9%
where the time goes in v2:
time: 112 us
  starting transfers between devices  53.7 us (48%)
  waiting for transfers between devices  27.4 us (24%)
  Pallas kernels  25.4 us (23%)
  local copies, waits for them, and re-layouts  3.89 us (3%)
    ppermute x36, starting transfers between devices, hop(): return lax.ppermute(value, axis, [(i, i ^ s) for i in range(size)])  53.7 us
    ppermute x36, waiting for transfers between devices, hop(): return lax.ppermute(value, axis, [(i, i ^ s) for i in range(size)])  27.4 us
    pallas_call x2, Pallas kernels, weight_gradient(): pl.pallas_call(body, grid=(plan.nq,), in_specs=[pl.BlockSpec((plan.mh, ro...  5.91 us
    pallas_call x1, Pallas kernels, forward_dft(): pl.pallas_call(body, grid_spec=pltpu.PrefetchScalarGridSpec(num_scalar_pr...  5.41 us
    pallas_call x1, Pallas kernels, middle(): pl.pallas_call(body, grid_spec=pltpu.PrefetchScalarGridSpec(num_scalar_pr...  5.34 us
    unnamed x18, local copies, waits for them, and re-layouts  3.89 us
    pallas_call x1, Pallas kernels, final_dft(): pl.pallas_call(body, grid_spec=pltpu.PrefetchScalarGridSpec(num_scalar_pr...  3.64 us
  transfers between devices with their start and end apart: 36, of which 14 were waited for; matrix products, arithmetic and copies ran while one was open for 0% of the time, Pallas kernels for 9%

profile of v2, /device:TPU:0, one launch (start us, length us, event | category | flops | bytes accessed | tf_op | source)
XLA Modules:
  0.0 111.8 jit_solution(14324981726347774344)
XLA Ops:
  1.2 5.4 %forward_dft.1 = (bf16[128,256]{1,0:T(8,128)(2,1)}, bf16[128,256]{1,0:T(8,128)(2,1)}, bf16[128,256]{1,0:T(8,128)(2,1)}, bf16[128,256]{1,0:T(8,128)(2,1)}, bf16[1...) custom-call(s32[3]{0:T(128)} %pad_add_fusion.me_ref.ids_ref, ...), custom_call_target="tpu_custom_call" | custom-call | flops 754974720 | bytes 2949120 | tf_op jit(solution)/shard_map/forward_dft/pallas_call | solution.py:129
  6.6 3.0 %collective-permute-start.5 = (bf16[128,256]{1,0:T(8,128)(2,1)}, bf16[128,256]{1,0:T(8,128)(2,1)S(1)}, u32[]{:S(2)}, u32[]{:S(2)}) collective-permute-start(bf16[128,256]{1,0:T(8,128)(2,1)} %get-tuple-element.58), channel_id=1, source_target_pairs={{0,4},{4,0},{8,12},{12,8},{1,5},{5,1},{9,13},{13,9},{2,6},{6,2},{1... | collective-permute-start | bytes 196616 | tf_op jit(solution)/shard_map/ppermute | solution.py:471
  9.7 2.6 %collective-permute-start.6 = (bf16[128,256]{1,0:T(8,128)(2,1)}, bf16[128,256]{1,0:T(8,128)(2,1)S(1)}, u32[]{:S(2)}, u32[]{:S(2)}) collective-permute-start(bf16[128,256]{1,0:T(8,128)(2,1)} %get-tuple-element.59), channel_id=1, source_target_pairs={{0,8},{4,12},{8,0},{12,4},{1,9},{5,13},{9,1},{13,5},{2,10},{6,14},... | collective-permute-start | bytes 196616 | tf_op jit(solution)/shard_map/ppermute | solution.py:471
  12.3 0.9 collective-permute-start
  13.2 3.5 %collective-permute-start.1 = (bf16[128,256]{1,0:T(8,128)(2,1)}, bf16[128,256]{1,0:T(8,128)(2,1)S(1)}, u32[]{:S(2)}, u32[]{:S(2)}) collective-permute-start(bf16[128,256]{1,0:T(8,128)(2,1)} %get-tuple-element.52), channel_id=1, source_target_pairs={{0,8},{4,12},{8,0},{12,4},{1,9},{5,13},{9,1},{13,5},{2,10},{6,14},... | collective-permute-start | bytes 196616 | tf_op jit(solution)/shard_map/ppermute | solution.py:471
  17.3 1.8 %collective-permute-done.7.refs_3_ = bf16[128,256]{1,0:T(8,128)(2,1)S(1)} collective-permute-done((bf16[128,256]{1,0:T(8,128)(2,1)}, bf16[128,256]{1,0:T(8,128)(2,1)S(1)}, u32[]{:S(2)}, u32[]{:S(2)}) %collective-permute-start.7) | collective-permute-done | bytes 65568 | tf_op jit(solution)/shard_map/ppermute | solution.py:471
  19.1 0.8 copy-done.5
  19.9 1.6 %collective-permute-start.8 = (bf16[16,32,256]{2,1,0:T(8,128)(2,1)S(1)}, bf16[16,32,256]{2,1,0:T(8,128)(2,1)S(1)}, u32[]{:S(2)}, u32[]{:S(2)}) collective-permute-start(bf16[16,32,256]{2,1,0:T(8,128)(2,1)S(1)} %pack_1.1.refs_0_), channel_id=1, source_target_pairs={{0,2},{2,0},{1,3},{3,1},{4,6},{6,4},{5,7},{7,5},{8,10},{10,8},{9,1... | collective-permute-start | bytes 786440 | tf_op jit(solution)/shard_map/ppermute | solution.py:471
  21.5 2.0 %collective-permute-done.1.refs_2_ = bf16[128,256]{1,0:T(8,128)(2,1)S(1)} collective-permute-done((bf16[128,256]{1,0:T(8,128)(2,1)}, bf16[128,256]{1,0:T(8,128)(2,1)S(1)}, u32[]{:S(2)}, u32[]{:S(2)}) %collective-permute-start.1) | collective-permute-done | bytes 65568 | tf_op jit(solution)/shard_map/ppermute | solution.py:471
  23.5 0.8 copy-done.4
  24.3 1.6 %collective-permute-start.3 = (bf16[16,32,256]{2,1,0:T(8,128)(2,1)S(1)}, bf16[16,32,256]{2,1,0:T(8,128)(2,1)S(1)}, u32[]{:S(2)}, u32[]{:S(2)}) collective-permute-start(bf16[16,32,256]{2,1,0:T(8,128)(2,1)S(1)} %pack_0.1.refs_0_), channel_id=1, source_target_pairs={{0,2},{2,0},{1,3},{3,1},{4,6},{6,4},{5,7},{7,5},{8,10},{10,8},{9,1... | collective-permute-start | bytes 786440 | tf_op jit(solution)/shard_map/ppermute | solution.py:471
  25.9 2.2 %collective-permute-done.8.refs_1_ = bf16[16,32,256]{2,1,0:T(8,128)(2,1)S(1)} collective-permute-done((bf16[16,32,256]{2,1,0:T(8,128)(2,1)S(1)}, bf16[16,32,256]{2,1,0:T(8,128)(2,1)S(1)}, u32[]{:S(2)}, u32[]{:S(2)}) %collective-permute-start.8) | collective-permute-done | bytes 262176 | tf_op jit(solution)/shard_map/ppermute | solution.py:471
  28.1 2.2 %copy-done = bf16[2,32,128,256]{3,2,1,0:T(8,128)(2,1)S(1)} copy-done((bf16[2,32,128,256]{3,2,1,0:T(8,128)(2,1)S(1)}, bf16[2,32,128,256]{3,2,1,0:T(8,128)(2,1)}, u32[]{:S(2)}) %copy-start) | copy-done | bytes 4194328
  30.3 0.8 mix_forward_1.1
  31.1 1.6 %collective-permute-start.9 = (bf16[16,32,128]{2,1,0:T(8,128)(2,1)S(1)}, bf16[16,32,128]{2,1,0:T(8,128)(2,1)S(1)}, u32[]{:S(2)}, u32[]{:S(2)}) collective-permute-start(bf16[16,32,128]{2,1,0:T(8,128)(2,1)S(1)} %get-tuple-element.62), channel_id=1, source_target_pairs={{0,2},{2,0},{1,3},{3,1},{4,6},{6,4},{5,7},{7,5},{8,10},{10,8},{9,1... | collective-permute-start | bytes 393224 | tf_op jit(solution)/shard_map/ppermute | solution.py:471
  32.7 0.7 collective-permute-done.3.refs_1_
  33.4 0.8 mix_forward_0.1
  34.2 1.6 %collective-permute-start.4 = (bf16[16,32,128]{2,1,0:T(8,128)(2,1)S(1)}, bf16[16,32,128]{2,1,0:T(8,128)(2,1)S(1)}, u32[]{:S(2)}, u32[]{:S(2)}) collective-permute-start(bf16[16,32,128]{2,1,0:T(8,128)(2,1)S(1)} %get-tuple-element.55), channel_id=1, source_target_pairs={{0,2},{2,0},{1,3},{3,1},{4,6},{6,4},{5,7},{7,5},{8,10},{10,8},{9,1... | collective-permute-start | bytes 393224 | tf_op jit(solution)/shard_map/ppermute | solution.py:471
  35.8 0.9 collective-permute-done.9.refs_1_
  37.3 3.5 %collective-permute-start.11 = (bf16[128,256]{1,0:T(8,128)(2,1)S(1)}, bf16[128,256]{1,0:T(8,128)(2,1)S(1)}, u32[]{:S(2)}, u32[]{:S(2)}) collective-permute-start(bf16[128,256]{1,0:T(8,128)(2,1)S(1)} %get-tuple-element.65), channel_id=1, source_target_pairs={{0,4},{4,0},{8,12},{12,8},{1,5},{5,1},{9,13},{13,9},{2,6},{6,2},{1... | collective-permute-start | bytes 196616 | tf_op jit(solution)/shard_map/ppermute | solution.py:471
  40.7 2.3 %collective-permute-start.13 = (bf16[128,256]{1,0:T(8,128)(2,1)S(1)}, bf16[128,256]{1,0:T(8,128)(2,1)S(1)}, u32[]{:S(2)}, u32[]{:S(2)}) collective-permute-start(bf16[128,256]{1,0:T(8,128)(2,1)S(1)} %get-tuple-element.67), channel_id=1, source_target_pairs={{0,8},{4,12},{8,0},{12,4},{1,9},{5,13},{9,1},{13,5},{2,10},{6,14},... | collective-permute-start | bytes 196616 | tf_op jit(solution)/shard_map/ppermute | solution.py:471
  43.0 1.4 %collective-permute-start.15 = (bf16[128,256]{1,0:T(8,128)(2,1)S(1)}, bf16[128,256]{1,0:T(8,128)(2,1)S(1)}, u32[]{:S(2)}, u32[]{:S(2)}) collective-permute-start(bf16[128,256]{1,0:T(8,128)(2,1)S(1)} %get-tuple-element.69), channel_id=1, source_target_pairs={{0,12},{4,8},{8,4},{12,0},{1,13},{5,9},{9,5},{13,1},{2,14},{6,10},... | collective-permute-start | bytes 196616 | tf_op jit(solution)/shard_map/ppermute | solution.py:471
  45.0 0.6 collective-permute-start.10
  45.6 2.4 %collective-permute-start.12 = (bf16[128,256]{1,0:T(8,128)(2,1)S(1)}, bf16[128,256]{1,0:T(8,128)(2,1)S(1)}, u32[]{:S(2)}, u32[]{:S(2)}) collective-permute-start(bf16[128,256]{1,0:T(8,128)(2,1)S(1)} %get-tuple-element.66), channel_id=1, source_target_pairs={{0,8},{4,12},{8,0},{12,4},{1,9},{5,13},{9,1},{13,5},{2,10},{6,14},... | collective-permute-start | bytes 196616 | tf_op jit(solution)/shard_map/ppermute | solution.py:471
  48.1 1.4 %collective-permute-start.14 = (bf16[128,256]{1,0:T(8,128)(2,1)S(1)}, bf16[128,256]{1,0:T(8,128)(2,1)S(1)}, u32[]{:S(2)}, u32[]{:S(2)}) collective-permute-start(bf16[128,256]{1,0:T(8,128)(2,1)S(1)} %get-tuple-element.68), channel_id=1, source_target_pairs={{0,12},{4,8},{8,4},{12,0},{1,13},{5,9},{9,5},{13,1},{2,14},{6,10},... | collective-permute-start | bytes 196616 | tf_op jit(solution)/shard_map/ppermute | solution.py:471
  49.9 0.9 collective-permute-done.12.refs_4_
  50.8 3.5 %collective-permute-done.14.refs_6_ = bf16[128,256]{1,0:T(8,128)(2,1)S(1)} collective-permute-done((bf16[128,256]{1,0:T(8,128)(2,1)S(1)}, bf16[128,256]{1,0:T(8,128)(2,1)S(1)}, u32[]{:S(2)}, u32[]{:S(2)}) %collective-permute-start.14) | collective-permute-done | bytes 65568 | tf_op jit(solution)/shard_map/ppermute | solution.py:471
  54.4 5.3 %middle.1 = (bf16[128,256]{1,0:T(8,128)(2,1)S(1)}, bf16[128,256]{1,0:T(8,128)(2,1)S(1)}, bf16[128,256]{1,0:T(8,128)(2,1)S(1)}, bf16[128,256]{1,0:T(8,128)(2,1)S(...) custom-call(s32[3]{0:T(128)S(1)} %copy-done.6, ...), custom_call_target="tpu_custom_call" | custom-call | flops 1509949440 | bytes 2949120 | tf_op jit(solution)/shard_map/middle/pallas_call | solution.py:182
  59.8 1.8 %collective-permute-start.22 = (bf16[128,256]{1,0:T(8,128)(2,1)S(1)}, bf16[128,256]{1,0:T(8,128)(2,1)S(1)}, u32[]{:S(2)}, u32[]{:S(2)}) collective-permute-start(bf16[128,256]{1,0:T(8,128)(2,1)S(1)} %get-tuple-element.81), channel_id=1, source_target_pairs={{0,8},{4,12},{8,0},{12,4},{1,9},{5,13},{9,1},{13,5},{2,10},{6,14},... | collective-permute-start | bytes 196616 | tf_op jit(solution)/shard_map/ppermute | solution.py:471
  61.6 2.5 %collective-permute-start.23 = (bf16[128,256]{1,0:T(8,128)(2,1)S(1)}, bf16[128,256]{1,0:T(8,128)(2,1)S(1)}, u32[]{:S(2)}, u32[]{:S(2)}) collective-permute-start(bf16[128,256]{1,0:T(8,128)(2,1)S(1)} %get-tuple-element.82), channel_id=1, source_target_pairs={{0,12},{4,8},{8,4},{12,0},{1,13},{5,9},{9,5},{13,1},{2,14},{6,10},... | collective-permute-start | bytes 196616 | tf_op jit(solution)/shard_map/ppermute | solution.py:471
  64.2 0.9 collective-permute-done.22.refs_2_
  65.0 2.7 %collective-permute-done.23.refs_3_ = bf16[128,256]{1,0:T(8,128)(2,1)S(1)} collective-permute-done((bf16[128,256]{1,0:T(8,128)(2,1)S(1)}, bf16[128,256]{1,0:T(8,128)(2,1)S(1)}, u32[]{:S(2)}, u32[]{:S(2)}) %collective-permute-start.23) | collective-permute-done | bytes 65568 | tf_op jit(solution)/shard_map/ppermute | solution.py:471
  68.3 1.6 %collective-permute-start.24 = (bf16[16,32,128]{2,1,0:T(8,128)(2,1)S(1)}, bf16[16,32,128]{2,1,0:T(8,128)(2,1)S(1)}, u32[]{:S(2)}, u32[]{:S(2)}) collective-permute-start(bf16[16,32,128]{2,1,0:T(8,128)(2,1)S(1)} %get-tuple-element.84), channel_id=1, source_target_pairs={{0,2},{2,0},{1,3},{3,1},{4,6},{6,4},{5,7},{7,5},{8,10},{10,8},{9,1... | collective-permute-start | bytes 393224 | tf_op jit(solution)/shard_map/ppermute | solution.py:471
  70.4 3.1 %collective-permute-start.17 = (bf16[128,256]{1,0:T(8,128)(2,1)S(1)}, bf16[128,256]{1,0:T(8,128)(2,1)S(1)}, u32[]{:S(2)}, u32[]{:S(2)}) collective-permute-start(bf16[128,256]{1,0:T(8,128)(2,1)S(1)} %get-tuple-element.72), channel_id=1, source_target_pairs={{0,8},{4,12},{8,0},{12,4},{1,9},{5,13},{9,1},{13,5},{2,10},{6,14},... | collective-permute-start | bytes 196616 | tf_op jit(solution)/shard_map/ppermute | solution.py:471
  73.5 2.4 %collective-permute-start.18 = (bf16[128,256]{1,0:T(8,128)(2,1)S(1)}, bf16[128,256]{1,0:T(8,128)(2,1)S(1)}, u32[]{:S(2)}, u32[]{:S(2)}) collective-permute-start(bf16[128,256]{1,0:T(8,128)(2,1)S(1)} %get-tuple-element.73), channel_id=1, source_target_pairs={{0,12},{4,8},{8,4},{12,0},{1,13},{5,9},{9,5},{13,1},{2,14},{6,10},... | collective-permute-start | bytes 196616 | tf_op jit(solution)/shard_map/ppermute | solution.py:471
  76.3 1.6 %collective-permute-start.25 = (bf16[16,32,256]{2,1,0:T(8,128)(2,1)S(1)}, bf16[16,32,256]{2,1,0:T(8,128)(2,1)S(1)}, u32[]{:S(2)}, u32[]{:S(2)}) collective-permute-start(bf16[16,32,256]{2,1,0:T(8,128)(2,1)S(1)} %get-tuple-element.86), channel_id=1, source_target_pairs={{0,2},{2,0},{1,3},{3,1},{4,6},{6,4},{5,7},{7,5},{8,10},{10,8},{9,1... | collective-permute-start | bytes 786440 | tf_op jit(solution)/shard_map/ppermute | solution.py:471
  77.9 1.7 %collective-permute-done.18.refs_3_ = bf16[128,256]{1,0:T(8,128)(2,1)S(1)} collective-permute-done((bf16[128,256]{1,0:T(8,128)(2,1)S(1)}, bf16[128,256]{1,0:T(8,128)(2,1)S(1)}, u32[]{:S(2)}, u32[]{:S(2)}) %collective-permute-start.18) | collective-permute-done | bytes 65568 | tf_op jit(solution)/shard_map/ppermute | solution.py:471
  80.3 1.4 %collective-permute-start.19 = (bf16[16,32,128]{2,1,0:T(8,128)(2,1)S(1)}, bf16[16,32,128]{2,1,0:T(8,128)(2,1)S(1)}, u32[]{:S(2)}, u32[]{:S(2)}) collective-permute-start(bf16[16,32,128]{2,1,0:T(8,128)(2,1)S(1)} %get-tuple-element.75), channel_id=1, source_target_pairs={{0,2},{2,0},{1,3},{3,1},{4,6},{6,4},{5,7},{7,5},{8,10},{10,8},{9,1... | collective-permute-start | bytes 393224 | tf_op jit(solution)/shard_map/ppermute | solution.py:471
  81.6 4.2 %collective-permute-done.19.refs_1_ = bf16[16,32,128]{2,1,0:T(8,128)(2,1)S(1)} collective-permute-done((bf16[16,32,128]{2,1,0:T(8,128)(2,1)S(1)}, bf16[16,32,128]{2,1,0:T(8,128)(2,1)S(1)}, u32[]{:S(2)}, u32[]{:S(2)}) %collective-permute-start.19) | collective-permute-done | bytes 131104 | tf_op jit(solution)/shard_map/ppermute | solution.py:471
  86.2 1.4 %collective-permute-start.20 = (bf16[16,32,256]{2,1,0:T(8,128)(2,1)S(1)}, bf16[16,32,256]{2,1,0:T(8,128)(2,1)S(1)}, u32[]{:S(2)}, u32[]{:S(2)}) collective-permute-start(bf16[16,32,256]{2,1,0:T(8,128)(2,1)S(1)} %get-tuple-element.77), channel_id=1, source_target_pairs={{0,2},{2,0},{1,3},{3,1},{4,6},{6,4},{5,7},{7,5},{8,10},{10,8},{9,1... | collective-permute-start | bytes 786440 | tf_op jit(solution)/shard_map/ppermute | solution.py:471
  88.2 5.1 %collective-permute-done.20.refs_1_ = bf16[16,32,256]{2,1,0:T(8,128)(2,1)S(1)} collective-permute-done((bf16[16,32,256]{2,1,0:T(8,128)(2,1)S(1)}, bf16[16,32,256]{2,1,0:T(8,128)(2,1)S(1)}, u32[]{:S(2)}, u32[]{:S(2)}) %collective-permute-start.20) | collective-permute-done | bytes 262176 | tf_op jit(solution)/shard_map/ppermute | solution.py:471
  93.3 2.9 %collective-permute-start.29 = (bf16[128,256]{1,0:T(8,128)(2,1)S(1)}, bf16[128,256]{1,0:T(8,128)(2,1)S(1)}, u32[]{:S(2)}, u32[]{:S(2)}) collective-permute-start(bf16[128,256]{1,0:T(8,128)(2,1)S(1)} %get-tuple-element.91), channel_id=1, source_target_pairs={{0,8},{4,12},{8,0},{12,4},{1,9},{5,13},{9,1},{13,5},{2,10},{6,14},... | collective-permute-start | bytes 196616 | tf_op jit(solution)/shard_map/ppermute | solution.py:471
  96.2 1.5 %collective-permute-start.31 = (bf16[128,256]{1,0:T(8,128)(2,1)S(1)}, bf16[128,256]{1,0:T(8,128)(2,1)S(1)}, u32[]{:S(2)}, u32[]{:S(2)}) collective-permute-start(bf16[128,256]{1,0:T(8,128)(2,1)S(1)} %get-tuple-element.93), channel_id=1, source_target_pairs={{0,12},{4,8},{8,4},{12,0},{1,13},{5,9},{9,5},{13,1},{2,14},{6,10},... | collective-permute-start | bytes 196616 | tf_op jit(solution)/shard_map/ppermute | solution.py:471
  97.8 2.9 %collective-permute-start.28 = (bf16[128,256]{1,0:T(8,128)(2,1)S(1)}, bf16[128,256]{1,0:T(8,128)(2,1)S(1)}, u32[]{:S(2)}, u32[]{:S(2)}) collective-permute-start(bf16[128,256]{1,0:T(8,128)(2,1)S(1)} %get-tuple-element.90), channel_id=1, source_target_pairs={{0,8},{4,12},{8,0},{12,4},{1,9},{5,13},{9,1},{13,5},{2,10},{6,14},... | collective-permute-start | bytes 196616 | tf_op jit(solution)/shard_map/ppermute | solution.py:471
  100.6 1.5 %collective-permute-start.30 = (bf16[128,256]{1,0:T(8,128)(2,1)S(1)}, bf16[128,256]{1,0:T(8,128)(2,1)S(1)}, u32[]{:S(2)}, u32[]{:S(2)}) collective-permute-start(bf16[128,256]{1,0:T(8,128)(2,1)S(1)} %get-tuple-element.92), channel_id=1, source_target_pairs={{0,12},{4,8},{8,4},{12,0},{1,13},{5,9},{9,5},{13,1},{2,14},{6,10},... | collective-permute-start | bytes 196616 | tf_op jit(solution)/shard_map/ppermute | solution.py:471
  102.2 3.0 %weight_gradient_0.1.refs_4_ = f32[2,4,2,4,128,256]{5,4,3,2,1,0:T(8,128)} custom-call(bf16[16,64,256]{2,1,0:T(8,128)(2,1)S(1)} %get-tuple-element.96.refs_0_, bf16[16,64,256]{2,1,0:T(8,128)(2,1)S(1)} %collective-permute-done.34.refs_1_, bf16[16,64,128]{2,1,0:T(8,128)(2,1)S(1)} %get-tuple-element.97.refs_2_, ...), custom_call_target="tpu_custom_call" | custom-call | bytes 10485760 | tf_op jit(solution)/shard_map/weight_gradient_0/pallas_call | solution.py:453
  105.1 3.0 %weight_gradient_1.1 = f32[2,4,2,4,128,256]{5,4,3,2,1,0:T(8,128)} custom-call(bf16[16,64,256]{2,1,0:T(8,128)(2,1)S(1)} %get-tuple-element.94.refs_0_, bf16[16,64,256]{2,1,0:T(8,128)(2,1)S(1)} %collective-permute-done.32.refs_1_, bf16[16,64,128]{2,1,0:T(8,128)(2,1)S(1)} %get-tuple-element.95.refs_2_, ...), custom_call_target="tpu_custom_call", output_to_operand_aliasing={{}: (4, {})} | custom-call | bytes 10485760 | tf_op jit(solution)/shard_map/weight_gradient_1/pallas_call | solution.py:453
  108.1 3.6 %final_dft.1 = bf16[4,1440,256]{2,1,0:T(8,128)(2,1)} custom-call(s32[3]{0:T(128)S(1)} %copy-done.6, bf16[4,1440,256]{2,1,0:T(8,128)(2,1)S(1)} %bitcast.13, bf16[1440,256]{1,0:T(8,128)(2,1)S(1)} %copy-done.3, bf16[128,256]{1,0:T(8,128)(2,1)S(1)} %get-tuple-element.78.refs_0_, bf16[128,256]{1,0:T(8,128)(2,1)S(1)} %get-tuple-element.87.refs_1_, ...), custom_call_target="tpu_custom_call" | custom-call | flops 754974720 | bytes 5898240 | tf_op jit(solution)/shard_map/final_dft/pallas_call | solution.py:229
  (60 shorter events, 6.3 us)
Async XLA Ops:
  6.6 10.0 %collective-permute-start.5 = (bf16[128,256]{1,0:T(8,128)(2,1)}, bf16[128,256]{1,0:T(8,128)(2,1)S(1)}, u32[]{:S(2)}, u32[]{:S(2)}) collective-permute-start(bf16[128,256]{1,0:T(8,128)(2,1)} %get-tuple-element.58), channel_id=1, source_target_pairs={{0,4},{4,0},{8,12},{12,8},{1,5},{5,1},{9,13},{13,9},{2,6},{6,2},{1... | collective-permute-start | bytes 196616 | tf_op jit(solution)/shard_map/ppermute | solution.py:471
  9.7 7.6 %collective-permute-start.6 = (bf16[128,256]{1,0:T(8,128)(2,1)}, bf16[128,256]{1,0:T(8,128)(2,1)S(1)}, u32[]{:S(2)}, u32[]{:S(2)}) collective-permute-start(bf16[128,256]{1,0:T(8,128)(2,1)} %get-tuple-element.59), channel_id=1, source_target_pairs={{0,8},{4,12},{8,0},{12,4},{1,9},{5,13},{9,1},{13,5},{2,10},{6,14},... | collective-permute-start | bytes 196616 | tf_op jit(solution)/shard_map/ppermute | solution.py:471
  12.3 6.8 %collective-permute-start.7 = (bf16[128,256]{1,0:T(8,128)(2,1)}, bf16[128,256]{1,0:T(8,128)(2,1)S(1)}, u32[]{:S(2)}, u32[]{:S(2)}) collective-permute-start(bf16[128,256]{1,0:T(8,128)(2,1)} %get-tuple-element.60), channel_id=1, source_target_pairs={{0,12},{4,8},{8,4},{12,0},{1,13},{5,9},{9,5},{13,1},{2,14},{6,10},... | collective-permute-start | bytes 196616 | tf_op jit(solution)/shard_map/ppermute | solution.py:471
  12.3 9.2 %collective-permute-start = (bf16[128,256]{1,0:T(8,128)(2,1)}, bf16[128,256]{1,0:T(8,128)(2,1)S(1)}, u32[]{:S(2)}, u32[]{:S(2)}) collective-permute-start(bf16[128,256]{1,0:T(8,128)(2,1)} %get-tuple-element.51), channel_id=1, source_target_pairs={{0,4},{4,0},{8,12},{12,8},{1,5},{5,1},{9,13},{13,9},{2,6},{6,2},{1... | collective-permute-start | bytes 196616 | tf_op jit(solution)/shard_map/ppermute | solution.py:471
  13.2 10.3 %collective-permute-start.1 = (bf16[128,256]{1,0:T(8,128)(2,1)}, bf16[128,256]{1,0:T(8,128)(2,1)S(1)}, u32[]{:S(2)}, u32[]{:S(2)}) collective-permute-start(bf16[128,256]{1,0:T(8,128)(2,1)} %get-tuple-element.52), channel_id=1, source_target_pairs={{0,8},{4,12},{8,0},{12,4},{1,9},{5,13},{9,1},{13,5},{2,10},{6,14},... | collective-permute-start | bytes 196616 | tf_op jit(solution)/shard_map/ppermute | solution.py:471
  16.7 6.8 %collective-permute-start.2 = (bf16[128,256]{1,0:T(8,128)(2,1)}, bf16[128,256]{1,0:T(8,128)(2,1)S(1)}, u32[]{:S(2)}, u32[]{:S(2)}) collective-permute-start(bf16[128,256]{1,0:T(8,128)(2,1)} %get-tuple-element.53), channel_id=1, source_target_pairs={{0,12},{4,8},{8,4},{12,0},{1,13},{5,9},{9,5},{13,1},{2,14},{6,10},... | collective-permute-start | bytes 196616 | tf_op jit(solution)/shard_map/ppermute | solution.py:471
  19.1 0.8 copy-start.5
  19.9 8.2 %collective-permute-start.8 = (bf16[16,32,256]{2,1,0:T(8,128)(2,1)S(1)}, bf16[16,32,256]{2,1,0:T(8,128)(2,1)S(1)}, u32[]{:S(2)}, u32[]{:S(2)}) collective-permute-start(bf16[16,32,256]{2,1,0:T(8,128)(2,1)S(1)} %pack_1.1.refs_0_), channel_id=1, source_target_pairs={{0,2},{2,0},{1,3},{3,1},{4,6},{6,4},{5,7},{7,5},{8,10},{10,8},{9,1... | collective-permute-start | bytes 786440 | tf_op jit(solution)/shard_map/ppermute | solution.py:471
  23.5 0.8 copy-start.4
  24.3 9.0 %collective-permute-start.3 = (bf16[16,32,256]{2,1,0:T(8,128)(2,1)S(1)}, bf16[16,32,256]{2,1,0:T(8,128)(2,1)S(1)}, u32[]{:S(2)}, u32[]{:S(2)}) collective-permute-start(bf16[16,32,256]{2,1,0:T(8,128)(2,1)S(1)} %pack_0.1.refs_0_), channel_id=1, source_target_pairs={{0,2},{2,0},{1,3},{3,1},{4,6},{6,4},{5,7},{7,5},{8,10},{10,8},{9,1... | collective-permute-start | bytes 786440 | tf_op jit(solution)/shard_map/ppermute | solution.py:471
  28.1 2.2 %copy-start = (bf16[2,32,128,256]{3,2,1,0:T(8,128)(2,1)S(1)}, bf16[2,32,128,256]{3,2,1,0:T(8,128)(2,1)}, u32[]{:S(2)}) copy-start(bf16[2,32,128,256]{3,2,1,0:T(8,128)(2,1)} %param.9) | copy-start | bytes 12582916
  30.3 3.1 %copy-start.1 = (bf16[2,32,128,256]{3,2,1,0:T(8,128)(2,1)S(1)}, bf16[2,32,128,256]{3,2,1,0:T(8,128)(2,1)}, u32[]{:S(2)}) copy-start(bf16[2,32,128,256]{3,2,1,0:T(8,128)(2,1)} %param.9) | copy-start | bytes 12582916
  30.3 6.4 %copy-start.6 = (s32[3]{0:T(128)S(1)}, s32[3]{0:T(128)}, u32[]{:S(2)}) copy-start(s32[3]{0:T(128)} %pad_add_fusion.me_ref.ids_ref) | copy-start | bytes 40
  30.3 24.1 %copy-start.2 = (bf16[1,4,1440,256]{3,2,1,0:T(8,128)(2,1)S(1)}, bf16[1,4,1440,256]{3,2,1,0:T(8,128)(2,1)}, u32[]{:S(2)}) copy-start(bf16[1,4,1440,256]{3,2,1,0:T(8,128)(2,1)} %param.8) | copy-start | bytes 8847364
  30.3 24.1 %copy-start.7 = (bf16[256,1440]{1,0:T(8,128)(2,1)S(1)}, bf16[256,1440]{1,0:T(8,128)(2,1)}, u32[]{:S(2)}) copy-start(bf16[256,1440]{1,0:T(8,128)(2,1)} %constant.26.clone.inv_ref) | copy-start | bytes 2211844
  30.3 24.1 %copy-start.8 = (bf16[1440,256]{1,0:T(8,128)(2,1)S(1)}, bf16[1440,256]{1,0:T(8,128)(2,1)}, u32[]{:S(2)}) copy-start(bf16[1440,256]{1,0:T(8,128)(2,1)} %constant.28.clone.back_ref) | copy-start | bytes 2211844
  31.1 5.5 %collective-permute-start.9 = (bf16[16,32,128]{2,1,0:T(8,128)(2,1)S(1)}, bf16[16,32,128]{2,1,0:T(8,128)(2,1)S(1)}, u32[]{:S(2)}, u32[]{:S(2)}) collective-permute-start(bf16[16,32,128]{2,1,0:T(8,128)(2,1)S(1)} %get-tuple-element.62), channel_id=1, source_target_pairs={{0,2},{2,0},{1,3},{3,1},{4,6},{6,4},{5,7},{7,5},{8,10},{10,8},{9,1... | collective-permute-start | bytes 393224 | tf_op jit(solution)/shard_map/ppermute | solution.py:471
  34.2 10.2 %collective-permute-start.4 = (bf16[16,32,128]{2,1,0:T(8,128)(2,1)S(1)}, bf16[16,32,128]{2,1,0:T(8,128)(2,1)S(1)}, u32[]{:S(2)}, u32[]{:S(2)}) collective-permute-start(bf16[16,32,128]{2,1,0:T(8,128)(2,1)S(1)} %get-tuple-element.55), channel_id=1, source_target_pairs={{0,2},{2,0},{1,3},{3,1},{4,6},{6,4},{5,7},{7,5},{8,10},{10,8},{9,1... | collective-permute-start | bytes 393224 | tf_op jit(solution)/shard_map/ppermute | solution.py:471
  37.3 10.8 %collective-permute-start.11 = (bf16[128,256]{1,0:T(8,128)(2,1)S(1)}, bf16[128,256]{1,0:T(8,128)(2,1)S(1)}, u32[]{:S(2)}, u32[]{:S(2)}) collective-permute-start(bf16[128,256]{1,0:T(8,128)(2,1)S(1)} %get-tuple-element.65), channel_id=1, source_target_pairs={{0,4},{4,0},{8,12},{12,8},{1,5},{5,1},{9,13},{13,9},{2,6},{6,2},{1... | collective-permute-start | bytes 196616 | tf_op jit(solution)/shard_map/ppermute | solution.py:471
  40.7 8.7 %collective-permute-start.13 = (bf16[128,256]{1,0:T(8,128)(2,1)S(1)}, bf16[128,256]{1,0:T(8,128)(2,1)S(1)}, u32[]{:S(2)}, u32[]{:S(2)}) collective-permute-start(bf16[128,256]{1,0:T(8,128)(2,1)S(1)} %get-tuple-element.67), channel_id=1, source_target_pairs={{0,8},{4,12},{8,0},{12,4},{1,9},{5,13},{9,1},{13,5},{2,10},{6,14},... | collective-permute-start | bytes 196616 | tf_op jit(solution)/shard_map/ppermute | solution.py:471
  43.0 6.5 %collective-permute-start.15 = (bf16[128,256]{1,0:T(8,128)(2,1)S(1)}, bf16[128,256]{1,0:T(8,128)(2,1)S(1)}, u32[]{:S(2)}, u32[]{:S(2)}) collective-permute-start(bf16[128,256]{1,0:T(8,128)(2,1)S(1)} %get-tuple-element.69), channel_id=1, source_target_pairs={{0,12},{4,8},{8,4},{12,0},{1,13},{5,9},{9,5},{13,1},{2,14},{6,10},... | collective-permute-start | bytes 196616 | tf_op jit(solution)/shard_map/ppermute | solution.py:471
  45.0 4.9 %collective-permute-start.10 = (bf16[128,256]{1,0:T(8,128)(2,1)S(1)}, bf16[128,256]{1,0:T(8,128)(2,1)S(1)}, u32[]{:S(2)}, u32[]{:S(2)}) collective-permute-start(bf16[128,256]{1,0:T(8,128)(2,1)S(1)} %get-tuple-element.64), channel_id=1, source_target_pairs={{0,4},{4,0},{8,12},{12,8},{1,5},{5,1},{9,13},{13,9},{2,6},{6,2},{1... | collective-permute-start | bytes 196616 | tf_op jit(solution)/shard_map/ppermute | solution.py:471
  45.6 5.2 %collective-permute-start.12 = (bf16[128,256]{1,0:T(8,128)(2,1)S(1)}, bf16[128,256]{1,0:T(8,128)(2,1)S(1)}, u32[]{:S(2)}, u32[]{:S(2)}) collective-permute-start(bf16[128,256]{1,0:T(8,128)(2,1)S(1)} %get-tuple-element.66), channel_id=1, source_target_pairs={{0,8},{4,12},{8,0},{12,4},{1,9},{5,13},{9,1},{13,5},{2,10},{6,14},... | collective-permute-start | bytes 196616 | tf_op jit(solution)/shard_map/ppermute | solution.py:471
  48.1 6.3 %collective-permute-start.14 = (bf16[128,256]{1,0:T(8,128)(2,1)S(1)}, bf16[128,256]{1,0:T(8,128)(2,1)S(1)}, u32[]{:S(2)}, u32[]{:S(2)}) collective-permute-start(bf16[128,256]{1,0:T(8,128)(2,1)S(1)} %get-tuple-element.68), channel_id=1, source_target_pairs={{0,12},{4,8},{8,4},{12,0},{1,13},{5,9},{9,5},{13,1},{2,14},{6,10},... | collective-permute-start | bytes 196616 | tf_op jit(solution)/shard_map/ppermute | solution.py:471
  59.7 4.5 %collective-permute-start.21 = (bf16[128,256]{1,0:T(8,128)(2,1)S(1)}, bf16[128,256]{1,0:T(8,128)(2,1)S(1)}, u32[]{:S(2)}, u32[]{:S(2)}) collective-permute-start(bf16[128,256]{1,0:T(8,128)(2,1)S(1)} %get-tuple-element.80), channel_id=1, source_target_pairs={{0,4},{4,0},{8,12},{12,8},{1,5},{5,1},{9,13},{13,9},{2,6},{6,2},{1... | collective-permute-start | bytes 196616 | tf_op jit(solution)/shard_map/ppermute | solution.py:471
  59.8 5.2 %collective-permute-start.22 = (bf16[128,256]{1,0:T(8,128)(2,1)S(1)}, bf16[128,256]{1,0:T(8,128)(2,1)S(1)}, u32[]{:S(2)}, u32[]{:S(2)}) collective-permute-start(bf16[128,256]{1,0:T(8,128)(2,1)S(1)} %get-tuple-element.81), channel_id=1, source_target_pairs={{0,8},{4,12},{8,0},{12,4},{1,9},{5,13},{9,1},{13,5},{2,10},{6,14},... | collective-permute-start | bytes 196616 | tf_op jit(solution)/shard_map/ppermute | solution.py:471
  61.6 6.1 %collective-permute-start.23 = (bf16[128,256]{1,0:T(8,128)(2,1)S(1)}, bf16[128,256]{1,0:T(8,128)(2,1)S(1)}, u32[]{:S(2)}, u32[]{:S(2)}) collective-permute-start(bf16[128,256]{1,0:T(8,128)(2,1)S(1)} %get-tuple-element.82), channel_id=1, source_target_pairs={{0,12},{4,8},{8,4},{12,0},{1,13},{5,9},{9,5},{13,1},{2,14},{6,10},... | collective-permute-start | bytes 196616 | tf_op jit(solution)/shard_map/ppermute | solution.py:471
  68.3 5.2 %collective-permute-start.24 = (bf16[16,32,128]{2,1,0:T(8,128)(2,1)S(1)}, bf16[16,32,128]{2,1,0:T(8,128)(2,1)S(1)}, u32[]{:S(2)}, u32[]{:S(2)}) collective-permute-start(bf16[16,32,128]{2,1,0:T(8,128)(2,1)S(1)} %get-tuple-element.84), channel_id=1, source_target_pairs={{0,2},{2,0},{1,3},{3,1},{4,6},{6,4},{5,7},{7,5},{8,10},{10,8},{9,1... | collective-permute-start | bytes 393224 | tf_op jit(solution)/shard_map/ppermute | solution.py:471
  69.9 6.4 %collective-permute-start.16 = (bf16[128,256]{1,0:T(8,128)(2,1)S(1)}, bf16[128,256]{1,0:T(8,128)(2,1)S(1)}, u32[]{:S(2)}, u32[]{:S(2)}) collective-permute-start(bf16[128,256]{1,0:T(8,128)(2,1)S(1)} %get-tuple-element.71), channel_id=1, source_target_pairs={{0,4},{4,0},{8,12},{12,8},{1,5},{5,1},{9,13},{13,9},{2,6},{6,2},{1... | collective-permute-start | bytes 196616 | tf_op jit(solution)/shard_map/ppermute | solution.py:471
  69.9 23.4 %collective-permute-start.34 = (bf16[16,64,256]{2,1,0:T(8,128)(2,1)S(1)}, bf16[16,64,256]{2,1,0:T(8,128)(2,1)S(1)}, u32[]{:S(2)}, u32[]{:S(2)}) collective-permute-start(bf16[16,64,256]{2,1,0:T(8,128)(2,1)S(1)} %get-tuple-element.96.refs_0_), channel_id=1, source_target_pairs={{0,1},{1,0},{2,3},{3,2},{4,5},{5,4},{6,7},{7,6},{8,9},{9,8},{10,11... | collective-permute-start | bytes 1572872 | tf_op jit(solution)/shard_map/ppermute | solution.py:471
  69.9 26.4 %collective-permute-start.32 = (bf16[16,64,256]{2,1,0:T(8,128)(2,1)S(1)}, bf16[16,64,256]{2,1,0:T(8,128)(2,1)S(1)}, u32[]{:S(2)}, u32[]{:S(2)}) collective-permute-start(bf16[16,64,256]{2,1,0:T(8,128)(2,1)S(1)} %get-tuple-element.94.refs_0_), channel_id=1, source_target_pairs={{0,1},{1,0},{2,3},{3,2},{4,5},{5,4},{6,7},{7,6},{8,9},{9,8},{10,11... | collective-permute-start | bytes 1572872 | tf_op jit(solution)/shard_map/ppermute | solution.py:471
  70.4 7.5 %collective-permute-start.17 = (bf16[128,256]{1,0:T(8,128)(2,1)S(1)}, bf16[128,256]{1,0:T(8,128)(2,1)S(1)}, u32[]{:S(2)}, u32[]{:S(2)}) collective-permute-start(bf16[128,256]{1,0:T(8,128)(2,1)S(1)} %get-tuple-element.72), channel_id=1, source_target_pairs={{0,8},{4,12},{8,0},{12,4},{1,9},{5,13},{9,1},{13,5},{2,10},{6,14},... | collective-permute-start | bytes 196616 | tf_op jit(solution)/shard_map/ppermute | solution.py:471
  73.5 6.1 %collective-permute-start.18 = (bf16[128,256]{1,0:T(8,128)(2,1)S(1)}, bf16[128,256]{1,0:T(8,128)(2,1)S(1)}, u32[]{:S(2)}, u32[]{:S(2)}) collective-permute-start(bf16[128,256]{1,0:T(8,128)(2,1)S(1)} %get-tuple-element.73), channel_id=1, source_target_pairs={{0,12},{4,8},{8,4},{12,0},{1,13},{5,9},{9,5},{13,1},{2,14},{6,10},... | collective-permute-start | bytes 196616 | tf_op jit(solution)/shard_map/ppermute | solution.py:471
  76.3 11.3 %collective-permute-start.25 = (bf16[16,32,256]{2,1,0:T(8,128)(2,1)S(1)}, bf16[16,32,256]{2,1,0:T(8,128)(2,1)S(1)}, u32[]{:S(2)}, u32[]{:S(2)}) collective-permute-start(bf16[16,32,256]{2,1,0:T(8,128)(2,1)S(1)} %get-tuple-element.86), channel_id=1, source_target_pairs={{0,2},{2,0},{1,3},{3,1},{4,6},{6,4},{5,7},{7,5},{8,10},{10,8},{9,1... | collective-permute-start | bytes 786440 | tf_op jit(solution)/shard_map/ppermute | solution.py:471
  80.3 5.5 %collective-permute-start.19 = (bf16[16,32,128]{2,1,0:T(8,128)(2,1)S(1)}, bf16[16,32,128]{2,1,0:T(8,128)(2,1)S(1)}, u32[]{:S(2)}, u32[]{:S(2)}) collective-permute-start(bf16[16,32,128]{2,1,0:T(8,128)(2,1)S(1)} %get-tuple-element.75), channel_id=1, source_target_pairs={{0,2},{2,0},{1,3},{3,1},{4,6},{6,4},{5,7},{7,5},{8,10},{10,8},{9,1... | collective-permute-start | bytes 393224 | tf_op jit(solution)/shard_map/ppermute | solution.py:471
  86.2 7.0 %collective-permute-start.20 = (bf16[16,32,256]{2,1,0:T(8,128)(2,1)S(1)}, bf16[16,32,256]{2,1,0:T(8,128)(2,1)S(1)}, u32[]{:S(2)}, u32[]{:S(2)}) collective-permute-start(bf16[16,32,256]{2,1,0:T(8,128)(2,1)S(1)} %get-tuple-element.77), channel_id=1, source_target_pairs={{0,2},{2,0},{1,3},{3,1},{4,6},{6,4},{5,7},{7,5},{8,10},{10,8},{9,1... | collective-permute-start | bytes 786440 | tf_op jit(solution)/shard_map/ppermute | solution.py:471
  87.6 10.2 %collective-permute-start.35 = (bf16[16,64,128]{2,1,0:T(8,128)(2,1)S(1)}, bf16[16,64,128]{2,1,0:T(8,128)(2,1)S(1)}, u32[]{:S(2)}, u32[]{:S(2)}) collective-permute-start(bf16[16,64,128]{2,1,0:T(8,128)(2,1)S(1)} %get-tuple-element.97.refs_2_), channel_id=1, source_target_pairs={{0,1},{1,0},{2,3},{3,2},{4,5},{5,4},{6,7},{7,6},{8,9},{9,8},{10,11... | collective-permute-start | bytes 786440 | tf_op jit(solution)/shard_map/ppermute | solution.py:471
  87.6 10.2 %collective-permute-start.33 = (bf16[16,64,128]{2,1,0:T(8,128)(2,1)S(1)}, bf16[16,64,128]{2,1,0:T(8,128)(2,1)S(1)}, u32[]{:S(2)}, u32[]{:S(2)}) collective-permute-start(bf16[16,64,128]{2,1,0:T(8,128)(2,1)S(1)} %get-tuple-element.95.refs_2_), channel_id=1, source_target_pairs={{0,1},{1,0},{2,3},{3,2},{4,5},{5,4},{6,7},{7,6},{8,9},{9,8},{10,11... | collective-permute-start | bytes 786440 | tf_op jit(solution)/shard_map/ppermute | solution.py:471
  93.3 7.4 %collective-permute-start.27 = (bf16[128,256]{1,0:T(8,128)(2,1)S(1)}, bf16[128,256]{1,0:T(8,128)(2,1)S(1)}, u32[]{:S(2)}, u32[]{:S(2)}) collective-permute-start(bf16[128,256]{1,0:T(8,128)(2,1)S(1)} %get-tuple-element.89), channel_id=1, source_target_pairs={{0,4},{4,0},{8,12},{12,8},{1,5},{5,1},{9,13},{13,9},{2,6},{6,2},{1... | collective-permute-start | bytes 196616 | tf_op jit(solution)/shard_map/ppermute | solution.py:471
  93.3 14.8 %collective-permute-start.29 = (bf16[128,256]{1,0:T(8,128)(2,1)S(1)}, bf16[128,256]{1,0:T(8,128)(2,1)S(1)}, u32[]{:S(2)}, u32[]{:S(2)}) collective-permute-start(bf16[128,256]{1,0:T(8,128)(2,1)S(1)} %get-tuple-element.91), channel_id=1, source_target_pairs={{0,8},{4,12},{8,0},{12,4},{1,9},{5,13},{9,1},{13,5},{2,10},{6,14},... | collective-permute-start | bytes 196616 | tf_op jit(solution)/shard_map/ppermute | solution.py:471
  96.2 11.9 %collective-permute-start.31 = (bf16[128,256]{1,0:T(8,128)(2,1)S(1)}, bf16[128,256]{1,0:T(8,128)(2,1)S(1)}, u32[]{:S(2)}, u32[]{:S(2)}) collective-permute-start(bf16[128,256]{1,0:T(8,128)(2,1)S(1)} %get-tuple-element.93), channel_id=1, source_target_pairs={{0,12},{4,8},{8,4},{12,0},{1,13},{5,9},{9,5},{13,1},{2,14},{6,10},... | collective-permute-start | bytes 196616 | tf_op jit(solution)/shard_map/ppermute | solution.py:471
  97.8 10.3 %collective-permute-start.26 = (bf16[128,256]{1,0:T(8,128)(2,1)S(1)}, bf16[128,256]{1,0:T(8,128)(2,1)S(1)}, u32[]{:S(2)}, u32[]{:S(2)}) collective-permute-start(bf16[128,256]{1,0:T(8,128)(2,1)S(1)} %get-tuple-element.88), channel_id=1, source_target_pairs={{0,4},{4,0},{8,12},{12,8},{1,5},{5,1},{9,13},{13,9},{2,6},{6,2},{1... | collective-permute-start | bytes 196616 | tf_op jit(solution)/shard_map/ppermute | solution.py:471
  97.8 10.3 %collective-permute-start.28 = (bf16[128,256]{1,0:T(8,128)(2,1)S(1)}, bf16[128,256]{1,0:T(8,128)(2,1)S(1)}, u32[]{:S(2)}, u32[]{:S(2)}) collective-permute-start(bf16[128,256]{1,0:T(8,128)(2,1)S(1)} %get-tuple-element.90), channel_id=1, source_target_pairs={{0,8},{4,12},{8,0},{12,4},{1,9},{5,13},{9,1},{13,5},{2,10},{6,14},... | collective-permute-start | bytes 196616 | tf_op jit(solution)/shard_map/ppermute | solution.py:471
  100.6 7.5 %collective-permute-start.30 = (bf16[128,256]{1,0:T(8,128)(2,1)S(1)}, bf16[128,256]{1,0:T(8,128)(2,1)S(1)}, u32[]{:S(2)}, u32[]{:S(2)}) collective-permute-start(bf16[128,256]{1,0:T(8,128)(2,1)S(1)} %get-tuple-element.92), channel_id=1, source_target_pairs={{0,12},{4,8},{8,4},{12,0},{1,13},{5,9},{9,5},{13,1},{2,14},{6,10},... | collective-permute-start | bytes 196616 | tf_op jit(solution)/shard_map/ppermute | solution.py:471
  105.1 3.0 %copy-start.3 = (bf16[1440,256]{1,0:T(8,128)(2,1)S(1)}, bf16[1440,256]{1,0:T(8,128)(2,1)}, u32[]{:S(2)}) copy-start(bf16[1440,256]{1,0:T(8,128)(2,1)} %constant.27.clone.table_ref) | copy-start | bytes 2211844

commit v3 on v0

v3 whole, which is shorter than its diff:
```python
import functools
import math

import jax
import jax.numpy as jnp
import numpy as np
from jax import lax
from jax.experimental import pallas as pl
from jax.experimental.pallas import tpu as pltpu
from jax.sharding import PartitionSpec as P

inv_sqrt_two = 0.7071067811865476
inv_sqrt_two_pi = 0.3989422804014327
LANES = 128
MEBI = 1 << 20
VMEM_BYTES = 24 * 1024 * 1024
BF16 = jnp.bfloat16
F32 = jnp.float32


def gelu_slope(values):
    cumulative = 0.5 * (1.0 + lax.erf(values * inv_sqrt_two))
    return cumulative + values * jnp.exp(-0.5 * values * values) * inv_sqrt_two_pi


def tables(plan):
    lon, modes = plan.lon, plan.n_lat * plan.m_loc
    lon_index = np.arange(lon, dtype=np.int64)
    mode_index = np.arange(modes, dtype=np.int64)
    phase = (mode_index[:, None] * lon_index[None, :] % lon).astype(np.float32) * np.float32(
        2.0 * math.pi / lon
    )
    scale = np.float32(1.0 / math.sqrt(lon))
    weight = np.where(mode_index == 0, 1.0, 2.0).astype(np.float32)[:, None]
    parts = np.stack([np.cos(phase), -np.sin(phase)], axis=0)

    def placed(array):
        array = array.reshape(2, plan.n_lat, plan.m_loc, lon).transpose(1, 0, 2, 3)
        return array.reshape(2 * modes, lon).astype(jnp.bfloat16)

    return placed(parts * scale), placed(weight * parts * scale)


class Plan:
    def __init__(self, mesh, field, weights):
        self.n_lat, self.n_chan = mesh.shape["lat"], mesh.shape["chan"]
        self.n_parts, self.n_rep = mesh.shape["parts"], mesh.shape["rep"]
        self.rows, self.lon, self.width = field[1], field[2], field[3]
        self.m_loc, self.o_w = weights[1], weights[2]
        self.halves = 2 if self.m_loc % 16 == 0 else 1
        self.mu = self.m_loc // self.halves
        self.rk = 2 * self.rows
        self.wide = self.n_lat * self.rk
        self.groups = self.width // LANES


def params(limit=VMEM_BYTES):
    return pltpu.CompilerParams(vmem_limit_bytes=limit)


VMEM = pl.BlockSpec(memory_space=pltpu.VMEM)
ANY = pl.BlockSpec(memory_space=pl.ANY)


def whole(body, name, outs, scratch=(), ins=None, out_specs=None, mebi=2, limit=VMEM_BYTES):
    def call(*operands):
        return pl.pallas_call(
            body,
            in_specs=ins or [VMEM] * len(operands),
            out_specs=out_specs or [VMEM] * len(outs),
            out_shape=outs,
            scratch_shapes=scratch,
            compiler_params=params(limit),
            cost_estimate=pl.CostEstimate(
                flops=0, bytes_accessed=mebi * MEBI, transcendentals=0
            ),
            name=name,
        )(*operands)

    return call


def like(shape, dtype=BF16):
    return jax.ShapeDtypeStruct(shape, dtype)


def spread_rows(plan, me, row, source, held):
    for s in range(plan.n_lat):
        base = (me ^ s) * 2 * plan.m_loc
        for k in range(2):
            block = source[pl.ds(pl.multiple_of(base + k * plan.m_loc, 8), plan.m_loc), :]
            for g in range(plan.groups):
                at = pl.ds(k * plan.rows + row, plan.m_loc, stride=plan.rk)
                held[s * plan.groups + g, at, :] = block[:, g * LANES : (g + 1) * LANES]


def emit_blocks(plan, held, outs):
    at = plan.mu * plan.rk
    for s in range(plan.n_lat):
        for h in range(plan.halves):
            for g in range(plan.groups):
                block = held[s * plan.groups + g, h * at : (h + 1) * at, :].astype(BF16)
                outs[s * plan.halves + h][:, g * LANES : (g + 1) * LANES] = block


def collect_rows(plan, me, blocks, flat, held):
    for s in range(plan.n_lat):
        base = (me ^ s) * 2 * plan.m_loc
        for g in range(plan.groups):
            lanes = slice(g * LANES, (g + 1) * LANES)
            flat[g] = blocks[s][:, lanes].astype(F32)
            for row in range(plan.rows):
                for k in range(2):
                    at = pl.multiple_of(base + k * plan.m_loc, 8)
                    held[row, pl.ds(at, plan.m_loc), lanes] = flat[
                        g, pl.ds(k * plan.rows + row, plan.m_loc, stride=plan.rk), :
                    ]


def block_shape(plan):
    return (plan.mu * plan.rk, plan.width)


def row_copies(source, target, sems):
    rows = target.shape[0]
    return [pltpu.make_async_copy(source.at[r], target.at[r], sems.at[r]) for r in range(rows)]


def forward_dft(plan, table, field):
    n = plan.n_lat * plan.halves
    shape = block_shape(plan)

    def body(field_ref, table_ref, *refs):
        outs, (rows, table_buf, line, held, sems, table_sem) = refs[:n], refs[n:]
        table_copy = pltpu.make_async_copy(table_ref, table_buf, table_sem)
        table_copy.start()
        copies = row_copies(field_ref, rows, sems)
        for copy in copies:
            copy.start()
        table_copy.wait()
        for row in range(plan.rows):
            copies[row].wait()
            line[...] = jnp.dot(table_buf[...], rows[row], preferred_element_type=F32)
            spread_rows(plan, lax.axis_index("lat"), row, line, held)
        emit_blocks(plan, held, outs)

    return whole(
        body,
        "forward_dft",
        [like(shape)] * n,
        [
            pltpu.VMEM(field.shape, BF16),
            pltpu.VMEM(table.shape, BF16),
            pltpu.VMEM((table.shape[0], plan.width), F32),
            pltpu.VMEM((plan.n_lat * plan.groups, plan.m_loc * plan.rk, LANES), F32),
            pltpu.SemaphoreType.DMA((plan.rows,)),
            pltpu.SemaphoreType.DMA,
        ],
        ins=[ANY, ANY],
        mebi=6,
        limit=60 * MEBI,
    )(field, table)


def middle(plan, inverse_t, inverse, cotangent, blocks):
    n_in, n = len(blocks), plan.n_lat * plan.halves
    modes2 = inverse.shape[0]
    shape = block_shape(plan)
    cut = next(c for c in (288, 480, 360, 240, 160, plan.lon) if plan.lon % c == 0)

    def body(cot_ref, back_ref, inv_ref, *refs):
        ins, outs = refs[:n_in][::-1], refs[n_in : n_in + n]
        flat, held, scaled, line, out_held = refs[n_in + n :]
        lat = lax.axis_index("lat")
        collect_rows(plan, lat, ins, flat, held)
        for row in range(plan.rows):
            mixed = held[row].astype(BF16)
            for at in range(0, plan.lon, cut):
                spatial = jnp.dot(back_ref[at : at + cut, :], mixed, preferred_element_type=F32)
                cot = cot_ref[row, at : at + cut, :].astype(F32)
                scaled[row % 2, at : at + cut, :] = (cot * gelu_slope(spatial)).astype(BF16)
            line[row % 2] = jnp.dot(inv_ref[...], scaled[row % 2], preferred_element_type=F32)
            spread_rows(plan, lat, row, line.at[row % 2], out_held)
        emit_blocks(plan, out_held, outs)

    return whole(
        body,
        "middle",
        [like(shape)] * n,
        [
            pltpu.VMEM((plan.groups, plan.m_loc * plan.rk, LANES), F32),
            pltpu.VMEM((plan.rows, modes2, plan.width), F32),
            pltpu.VMEM((2, plan.lon, plan.width), BF16),
            pltpu.VMEM((2, modes2, plan.width), F32),
            pltpu.VMEM((plan.n_lat * plan.groups, plan.m_loc * plan.rk, LANES), F32),
        ],
        mebi=12,
    )(cotangent, inverse_t, inverse, *blocks[::-1])


def final_dft(plan, table_t, cotangent, blocks):
    n = len(blocks)

    def body(cot_ref, table_ref, *refs):
        ins, out_ref, (flat, held, done, sems) = refs[:n][::-1], refs[n], refs[n + 1 :]
        collect_rows(plan, lax.axis_index("lat"), ins, flat, held)
        backs = row_copies(done, out_ref, sems)
        for row in range(plan.rows):
            grad = jnp.dot(table_ref[...], held[row].astype(BF16), preferred_element_type=F32)
            done[row] = (cot_ref[row].astype(F32) + grad).astype(BF16)
            backs[row].start()
        for back in backs:
            back.wait()

    return whole(
        body,
        "final_dft",
        [like(cotangent.shape)],
        [
            pltpu.VMEM((plan.groups, plan.m_loc * plan.rk, LANES), F32),
            pltpu.VMEM((plan.rows, table_t.shape[1], plan.width), F32),
            pltpu.VMEM(cotangent.shape, BF16),
            pltpu.SemaphoreType.DMA((plan.rows,)),
        ],
        out_specs=[ANY],
        mebi=8,
    )(cotangent, table_t, *blocks[::-1])[0]


def turned(plan, block, first_sign):
    swapped = jnp.concatenate([block[:, plan.rows :, :], block[:, : plan.rows, :]], axis=1)
    real = lax.broadcasted_iota(jnp.int32, swapped.shape, 1) < plan.rows
    return jnp.where(real, first_sign * swapped, -first_sign * swapped)


def pack(plan, h, blocks):
    def body(*refs):
        ins, out = refs[: plan.n_lat][::-1], refs[plan.n_lat]
        parts = [ref[...].astype(F32).reshape(plan.mu, plan.rk, plan.width) for ref in ins]
        out[...] = jnp.concatenate(parts, axis=1).astype(BF16)

    return whole(body, f"pack_{h}", [like((plan.mu, plan.wide, plan.width))])(*blocks[::-1])[0]


def pack_gradients(plan, h, blocks):
    part = (plan.mu, plan.wide, plan.o_w)

    def body(*refs):
        ins, outs, held = refs[: plan.n_lat][::-1], refs[plan.n_lat : -1], refs[-1]
        blocks = [ref[...].astype(F32).reshape(plan.mu, plan.rk, plan.width) for ref in ins]
        every = jnp.concatenate(blocks, axis=1)
        for c in range(plan.n_chan):
            held[c] = every[:, :, c * plan.o_w : (c + 1) * plan.o_w]
        for x in range(plan.n_chan):
            outs[x][...] = held[lax.axis_index("chan") ^ x].astype(BF16)

    scratch = [pltpu.VMEM((plan.n_chan, *part), F32)]
    return whole(body, f"pack_gradients_{h}", [like(part)] * plan.n_chan, scratch)(*blocks[::-1])


def merge(plan, pieces):
    shape = (plan.m_loc * plan.rk, plan.width)
    part = (plan.m_loc, plan.wide, plan.o_w)

    def body(*refs):
        ins, outs, held = refs[: -plan.n_lat - 1], refs[-plan.n_lat - 1 : -1], refs[-1]
        for i, ref in enumerate(ins):
            h, x = divmod(i, plan.n_chan)
            held[lax.axis_index("chan") ^ x, h * plan.mu : (h + 1) * plan.mu] = ref[...].astype(F32)
        every = jnp.concatenate([held[c] for c in range(plan.n_chan)], axis=2)
        for s in range(plan.n_lat):
            block = every[:, s * plan.rk : (s + 1) * plan.rk, :]
            outs[s][...] = block.reshape(shape).astype(BF16)

    scratch = [pltpu.VMEM((plan.n_chan, *part), F32)]
    flat = [piece for half in pieces for piece in half]
    return whole(body, "merge", [like(shape)] * plan.n_lat, scratch)(*flat)


def mix_forward(plan, h, spectra, own):
    part = (plan.mu, plan.wide, plan.o_w)
    tall = (plan.mu, plan.n_chan * plan.wide, plan.width)

    def body(*refs):
        ins, own_ref = refs[: plan.n_chan], refs[plan.n_chan]
        outs, every = refs[plan.n_chan + 1 : -1], refs[-1]
        dims = (((1,), (1,)), ((), ()))
        for u in range(plan.mu):
            at = h * plan.mu + u
            rows = jnp.concatenate([ref[u].astype(F32) for ref in ins], axis=0)
            every[u] = rows.astype(BF16)
            groups = rows.reshape(-1, plan.rk, plan.width)
            turn = turned(plan, groups, -1.0).reshape(rows.shape)
            mixed = lax.dot_general(
                rows.astype(BF16), own_ref[0, at], dims, preferred_element_type=F32
            ) + lax.dot_general(
                turn.astype(BF16), own_ref[1, at], dims, preferred_element_type=F32
            )
            for x in range(plan.n_chan):
                outs[x][u] = mixed[x * plan.wide : (x + 1) * plan.wide].astype(BF16)

    outs = [like(part)] * plan.n_chan + [like(tall)]
    return whole(body, f"mix_forward_{h}", outs, mebi=3)(*spectra, own)


def mix_backward(plan, h, grads, own):
    wide = (plan.mu, plan.wide, plan.width)
    tall = (plan.mu, plan.n_chan * plan.wide, plan.o_w)

    def body(*refs):
        ins, own_ref = refs[: plan.n_chan], refs[plan.n_chan]
        outs, every = refs[plan.n_chan + 1 : -1], refs[-1]
        for u in range(plan.mu):
            at = h * plan.mu + u
            rows = jnp.concatenate([ref[u].astype(F32) for ref in ins], axis=0)
            every[u] = rows.astype(BF16)
            groups = rows.reshape(-1, plan.rk, plan.o_w)
            turn = turned(plan, groups, 1.0).reshape(rows.shape)
            back = jnp.dot(
                rows.astype(BF16), own_ref[0, at], preferred_element_type=F32
            ) + jnp.dot(turn.astype(BF16), own_ref[1, at], preferred_element_type=F32)
            for x in range(plan.n_chan):
                outs[x][u] = back[x * plan.wide : (x + 1) * plan.wide].astype(outs[x].dtype)

    outs = [like(wide, F32)] + [like(wide)] * (plan.n_chan - 1) + [like(tall)]
    return whole(body, f"mix_backward_{h}", outs, mebi=3)(*grads, own)


def merge_gradients(plan, parts):
    shape = (plan.m_loc * plan.rk, plan.width)

    def body(*refs):
        ins, outs = refs[: -plan.n_lat], refs[-plan.n_lat :]
        for h in range(plan.halves):
            total = sum(ref[...].astype(F32) for ref in ins[h * plan.n_chan : (h + 1) * plan.n_chan])
            at = plan.mu * plan.rk
            for s in range(plan.n_lat):
                block = total[:, s * plan.rk : (s + 1) * plan.rk, :]
                outs[s][h * at : (h + 1) * at, :] = block.reshape(at, plan.width).astype(BF16)

    flat = [part for half in parts for part in half]
    return whole(body, "merge_gradients", [like(shape)] * plan.n_lat)(*flat)


def weight_gradient(plan, h, spectra, grads, before):
    step = 4
    n, n_g = len(spectra), len(grads)
    scale = 1.0 / (plan.rows * plan.n_lat * plan.n_chan)

    def body(*refs):
        s_refs, g_refs, out = refs[:n], refs[n : n + n_g], refs[-1]
        for t in range(step):
            s_all = jnp.concatenate([ref[t].astype(F32) for ref in s_refs], axis=0).astype(BF16)
            g_all = jnp.concatenate([ref[t].astype(F32) for ref in g_refs], axis=0)
            groups = g_all.reshape(-1, plan.rk, plan.o_w)
            g_turn = turned(plan, groups, 1.0).reshape(g_all.shape)
            for j, g in enumerate((g_all, g_turn)):
                total = lax.dot_general(
                    g.astype(BF16), s_all, (((0,), (0,)), ((), ())), preferred_element_type=F32
                )
                out[j, t] = total * scale

    out_shape = (2, plan.m_loc, plan.o_w, plan.width)
    steps = plan.mu // step
    earlier = [] if before is None else [before]
    return pl.pallas_call(
        body,
        grid=(steps,),
        in_specs=[
            pl.BlockSpec((step, *array.shape[1:]), lambda q: (q, 0, 0))
            for array in (*spectra, *grads)
        ]
        + [pl.BlockSpec(memory_space=pl.ANY)] * len(earlier),
        out_specs=pl.BlockSpec(
            (2, step, plan.o_w, plan.width), lambda q: (0, h * steps + q, 0, 0)
        ),
        out_shape=jax.ShapeDtypeStruct(out_shape, F32),
        input_output_aliases={n + n_g: 0} if earlier else {},
        compiler_params=params(),
        cost_estimate=pl.CostEstimate(flops=0, bytes_accessed=10 * MEBI, transcendentals=0),
        name=f"weight_gradient_{h}",
    )(*spectra, *grads, *earlier)


def hop(value, axis, size, s):
    return lax.ppermute(value, axis, [(i, i ^ s) for i in range(size)])


def spread(values, axis, size):
    return [value if s == 0 else hop(value, axis, size, s) for s in range(size) for value in values]


def after(value, *others):
    return lax.optimization_barrier((value, *others))[0]


def shards(plan, field, cotangent, weights):
    forward_np, inverse_np = tables(plan)
    forward, inverse = jnp.asarray(forward_np), jnp.asarray(inverse_np)
    forward_t, inverse_t = jnp.asarray(forward_np.T.copy()), jnp.asarray(inverse_np.T.copy())
    halves = range(plan.halves)

    def to_lat(blocks):
        moved = list(blocks)
        for s in range(plan.n_lat - 1, 0, -1):
            moved[s] = hop(blocks[s], "lat", plan.n_lat, s)
        return moved

    def over_chan(values):
        return [hop(value, "chan", plan.n_chan, x) if x else value for x, value in enumerate(values)]

    def rep_too(values):
        return spread(values, "rep", plan.n_rep)

    field, cotangent = field[0], cotangent[0]
    blocks = forward_dft(plan, forward, field)
    pieces, every_s = [], []
    for h in halves:
        packed = pack(plan, h, to_lat(blocks[h :: plan.halves]))
        *parts, tall = mix_forward(plan, h, over_chan([packed] * plan.n_chan), weights)
        pieces.append(over_chan(parts))
        every_s.append(rep_too([tall]))
    mixed = to_lat(merge(plan, pieces))

    mixed, every_s = lax.optimization_barrier((mixed[::-1], every_s))
    mixed = mixed[::-1]
    blocks = middle(plan, inverse_t, inverse, cotangent, mixed)
    pieces, every_g = [], []
    for h in halves:
        grads = pack_gradients(plan, h, to_lat(blocks[h :: plan.halves]))
        *parts, tall = mix_backward(plan, h, over_chan(grads), weights)
        pieces.append(over_chan(parts))
        every_g.append(rep_too([tall]))
    spectral = to_lat(merge_gradients(plan, pieces))
    grad_field = final_dft(plan, forward_t, cotangent, spectral)

    weight_grad = None
    for h in halves:
        weight_grad = weight_gradient(plan, h, every_s[h], every_g[h], weight_grad)
    return (grad_field[None], weight_grad)


def solution(mesh):
    placed = (
        P(("parts", "rep"), ("lat", "chan"), None, None),
        P(("parts", "rep"), ("lat", "chan"), None, None),
        P(None, "lat", "chan", None),
    )

    def local(field, cotangent, weights):
        return shards(Plan(mesh, field.shape, weights.shape), field, cotangent, weights)

    return jax.shard_map(
        local,
        mesh=mesh,
        in_specs=placed,
        out_specs=(
            P(("parts", "rep"), ("lat", "chan"), None, None),
            P("parts", "lat", "chan", None),
        ),
        check_vma=False,
    )
```

time: 239 us -> 105 us (0.44)
  blocking collectives: 73.7 us -> 0 us
  waiting for transfers between devices: 79.3 us -> 38.4 us
  starting transfers between devices: 7.26 us -> 41.6 us
  local copies, waits for them, and re-layouts: 33.9 us -> 4.08 us
  Pallas kernels: 0 us -> 20.2 us
  other arithmetic: 15.4 us -> 0 us
  matrix products: 15.3 us -> 0 us
  between operations: 14.1 us -> 0.79 us
    all_to_all x4 -> x0, blocking collectives: 73.7 us -> none  [the longest x1 30.1 us: shards(): lax.all_to_all(gathered, 'lat', split_axis=3, concat_axis=1, tiled=True)]
    ppermute x0 -> x30, starting transfers between devices: none -> 41.6 us  [hop(): return lax.ppermute(value, axis, [(i, i ^ s) for i in range(size)])]
    ppermute x0 -> x30, waiting for transfers between devices: none -> 38.4 us  [hop(): return lax.ppermute(value, axis, [(i, i ^ s) for i in range(size)])]
    all_gather x1 -> x0, waiting for transfers between devices: 24.2 us -> none  [full_channels(): return lax.all_gather(blocks, 'chan', axis=1, tiled=True)]
    pallas_call x0 -> x15, Pallas kernels: none -> 20.2 us  [the longest x13 14.3 us: call(): pl.pallas_call(body, in_specs=ins or [VMEM] * len(operands), out_specs=ou...]
    reduce_scatter x1 -> x0, waiting for transfers between devices: 18.7 us -> none  [shards(): lax.psum_scatter(jnp.moveaxis(spectral_terms(grad_split, weights), 1, 0),...]
    psum x1 -> x0, waiting for transfers between devices: 18.7 us -> none  [shards(): weight_grad = lax.psum(local_grad, 'rep')]
    all_to_all x2 -> x0, waiting for transfers between devices: 17.7 us -> none  [the longest x1 13.6 us: shards(): lax.all_to_all(mixed, 'lat', split_axis=2, concat_axis=5, tiled=True)]
  transfers between devices with their start and end apart: 5 -> 30, of which waited for: 5 -> 15; matrix products, arithmetic and copies ran while one was open for 8% -> 0% of each run, Pallas kernels for 0% -> 8%
where the time goes in v3:
time: 105 us
  starting transfers between devices  41.6 us (40%)
  waiting for transfers between devices  38.4 us (37%)
  Pallas kernels  20.2 us (19%)
  local copies, waits for them, and re-layouts  4.08 us (4%)
    ppermute x30, starting transfers between devices, hop(): return lax.ppermute(value, axis, [(i, i ^ s) for i in range(size)])  41.6 us
    ppermute x30, waiting for transfers between devices, hop(): return lax.ppermute(value, axis, [(i, i ^ s) for i in range(size)])  38.4 us
    pallas_call x13, Pallas kernels, call(): pl.pallas_call(body, in_specs=ins or [VMEM] * len(operands), out_specs=ou...  14.3 us
    pallas_call x2, Pallas kernels, weight_gradient(): pl.pallas_call(body, grid=(steps,), in_specs=[pl.BlockSpec((step, *array....  5.91 us
    unnamed x16, local copies, waits for them, and re-layouts  4.08 us
  transfers between devices with their start and end apart: 30, of which 15 were waited for; matrix products, arithmetic and copies ran while one was open for 0% of the time, Pallas kernels for 8%

profile of v3, /device:TPU:0, one launch (start us, length us, event | category | flops | bytes accessed | tf_op | source)
XLA Modules:
  0.0 105.2 jit_solution(18170334576805507133)
XLA Ops:
  0.6 5.1 %forward_dft.1 = (bf16[128,256]{1,0:T(8,128)(2,1)}, bf16[128,256]{1,0:T(8,128)(2,1)}, bf16[128,256]{1,0:T(8,128)(2,1)}, bf16[128,256]{1,0:T(8,128)(2,1)}, bf16[1...) custom-call(bf16[4,1440,256]{2,1,0:T(8,128)(2,1)} %bitcast.5, ...), custom_call_target="tpu_custom_call" | custom-call | bytes 6291456 | tf_op jit(solution)/shard_map/forward_dft/pallas_call | solution.py:67
  5.7 5.1 %collective-permute-start.5 = (bf16[128,256]{1,0:T(8,128)(2,1)}, bf16[128,256]{1,0:T(8,128)(2,1)S(1)}, u32[]{:S(2)}, u32[]{:S(2)}) collective-permute-start(bf16[128,256]{1,0:T(8,128)(2,1)} %get-tuple-element.56), channel_id=1, source_target_pairs={{0,12},{4,8},{8,4},{12,0},{1,13},{5,9},{9,5},{13,1},{2,14},{6,10},... | collective-permute-start | bytes 196616 | tf_op jit(solution)/shard_map/ppermute | solution.py:386
  10.8 0.6 collective-permute-start.7
  11.5 3.7 %collective-permute-start = (bf16[128,256]{1,0:T(8,128)(2,1)}, bf16[128,256]{1,0:T(8,128)(2,1)S(1)}, u32[]{:S(2)}, u32[]{:S(2)}) collective-permute-start(bf16[128,256]{1,0:T(8,128)(2,1)} %get-tuple-element.50), channel_id=1, source_target_pairs={{0,12},{4,8},{8,4},{12,0},{1,13},{5,9},{9,5},{13,1},{2,14},{6,10},... | collective-permute-start | bytes 196616 | tf_op jit(solution)/shard_map/ppermute | solution.py:386
  15.2 1.0 collective-permute-start.2
  16.2 3.4 %collective-permute-done.6.refs_1_ = bf16[128,256]{1,0:T(8,128)(2,1)S(1)} collective-permute-done((bf16[128,256]{1,0:T(8,128)(2,1)}, bf16[128,256]{1,0:T(8,128)(2,1)S(1)}, u32[]{:S(2)}, u32[]{:S(2)}) %collective-permute-start.6) | collective-permute-done | bytes 65568 | tf_op jit(solution)/shard_map/ppermute | solution.py:386
  19.6 0.8 copy-done.7
  20.5 1.2 %collective-permute-start.8 = (bf16[16,32,256]{2,1,0:T(8,128)(2,1)S(1)}, bf16[16,32,256]{2,1,0:T(8,128)(2,1)S(1)}, u32[]{:S(2)}, u32[]{:S(2)}) collective-permute-start(bf16[16,32,256]{2,1,0:T(8,128)(2,1)S(1)} %pack_1.1.refs_0_), channel_id=1, source_target_pairs={{0,2},{2,0},{1,3},{3,1},{4,6},{6,4},{5,7},{7,5},{8,10},{10,8},{9,1... | collective-permute-start | bytes 786440 | tf_op jit(solution)/shard_map/ppermute | solution.py:386
  21.7 0.6 collective-permute-done.1.refs_1_
  22.3 0.8 copy-done.6
  23.1 1.6 %collective-permute-start.3 = (bf16[16,32,256]{2,1,0:T(8,128)(2,1)S(1)}, bf16[16,32,256]{2,1,0:T(8,128)(2,1)S(1)}, u32[]{:S(2)}, u32[]{:S(2)}) collective-permute-start(bf16[16,32,256]{2,1,0:T(8,128)(2,1)S(1)} %pack_0.1.refs_0_), channel_id=1, source_target_pairs={{0,2},{2,0},{1,3},{3,1},{4,6},{6,4},{5,7},{7,5},{8,10},{10,8},{9,1... | collective-permute-start | bytes 786440 | tf_op jit(solution)/shard_map/ppermute | solution.py:386
  24.7 3.7 %collective-permute-done.8.refs_1_ = bf16[16,32,256]{2,1,0:T(8,128)(2,1)S(1)} collective-permute-done((bf16[16,32,256]{2,1,0:T(8,128)(2,1)S(1)}, bf16[16,32,256]{2,1,0:T(8,128)(2,1)S(1)}, u32[]{:S(2)}, u32[]{:S(2)}) %collective-permute-start.8) | collective-permute-done | bytes 262176 | tf_op jit(solution)/shard_map/ppermute | solution.py:386
  28.4 2.2 %copy-done = bf16[2,32,128,256]{3,2,1,0:T(8,128)(2,1)S(1)} copy-done((bf16[2,32,128,256]{3,2,1,0:T(8,128)(2,1)S(1)}, bf16[2,32,128,256]{3,2,1,0:T(8,128)(2,1)}, u32[]{:S(2)}) %copy-start) | copy-done | bytes 4194328
  30.6 0.8 mix_forward_1.1
  31.5 1.1 %collective-permute-done.3.refs_1_ = bf16[16,32,256]{2,1,0:T(8,128)(2,1)S(1)} collective-permute-done((bf16[16,32,256]{2,1,0:T(8,128)(2,1)S(1)}, bf16[16,32,256]{2,1,0:T(8,128)(2,1)S(1)}, u32[]{:S(2)}, u32[]{:S(2)}) %collective-permute-start.3) | collective-permute-done | bytes 262176 | tf_op jit(solution)/shard_map/ppermute | solution.py:386
  32.7 0.8 mix_forward_0.1
  33.7 1.5 %collective-permute-start.9 = (bf16[16,32,128]{2,1,0:T(8,128)(2,1)S(1)}, bf16[16,32,128]{2,1,0:T(8,128)(2,1)S(1)}, u32[]{:S(2)}, u32[]{:S(2)}) collective-permute-start(bf16[16,32,128]{2,1,0:T(8,128)(2,1)S(1)} %get-tuple-element.61), channel_id=1, source_target_pairs={{0,2},{2,0},{1,3},{3,1},{4,6},{6,4},{5,7},{7,5},{8,10},{10,8},{9,1... | collective-permute-start | bytes 393224 | tf_op jit(solution)/shard_map/ppermute | solution.py:386
  35.2 0.6 collective-permute-start.4
  35.7 4.3 %collective-permute-done.9.refs_3_ = bf16[16,32,128]{2,1,0:T(8,128)(2,1)S(1)} collective-permute-done((bf16[16,32,128]{2,1,0:T(8,128)(2,1)S(1)}, bf16[16,32,128]{2,1,0:T(8,128)(2,1)S(1)}, u32[]{:S(2)}, u32[]{:S(2)}) %collective-permute-start.9) | collective-permute-done | bytes 131104 | tf_op jit(solution)/shard_map/ppermute | solution.py:386
  40.0 2.4 %collective-permute-done.4.refs_1_ = bf16[16,32,128]{2,1,0:T(8,128)(2,1)S(1)} collective-permute-done((bf16[16,32,128]{2,1,0:T(8,128)(2,1)S(1)}, bf16[16,32,128]{2,1,0:T(8,128)(2,1)S(1)}, u32[]{:S(2)}, u32[]{:S(2)}) %collective-permute-start.4) | collective-permute-done | bytes 131104 | tf_op jit(solution)/shard_map/ppermute | solution.py:386
  42.5 2.9 %collective-permute-start.10 = (bf16[256,256]{1,0:T(8,128)(2,1)S(1)}, bf16[256,256]{1,0:T(8,128)(2,1)S(1)}, u32[]{:S(2)}, u32[]{:S(2)}) collective-permute-start(bf16[256,256]{1,0:T(8,128)(2,1)S(1)} %get-tuple-element.62), channel_id=1, source_target_pairs={{0,12},{4,8},{8,4},{12,0},{1,13},{5,9},{9,5},{13,1},{2,14},{6,10},... | collective-permute-start | bytes 393224 | tf_op jit(solution)/shard_map/ppermute | solution.py:386
  45.5 1.5 %collective-permute-start.12 = (bf16[256,256]{1,0:T(8,128)(2,1)S(1)}, bf16[256,256]{1,0:T(8,128)(2,1)S(1)}, u32[]{:S(2)}, u32[]{:S(2)}) collective-permute-start(bf16[256,256]{1,0:T(8,128)(2,1)S(1)} %get-tuple-element.64), channel_id=1, source_target_pairs={{0,4},{4,0},{8,12},{12,8},{1,5},{5,1},{9,13},{13,9},{2,6},{6,2},{1... | collective-permute-start | bytes 393224 | tf_op jit(solution)/shard_map/ppermute | solution.py:386
  47.0 3.9 %collective-permute-done.10.refs_0_ = bf16[256,256]{1,0:T(8,128)(2,1)S(1)} collective-permute-done((bf16[256,256]{1,0:T(8,128)(2,1)S(1)}, bf16[256,256]{1,0:T(8,128)(2,1)S(1)}, u32[]{:S(2)}, u32[]{:S(2)}) %collective-permute-start.10) | collective-permute-done | bytes 131104 | tf_op jit(solution)/shard_map/ppermute | solution.py:386
  50.9 4.2 %collective-permute-done.11.refs_1_ = bf16[256,256]{1,0:T(8,128)(2,1)S(1)} collective-permute-done((bf16[256,256]{1,0:T(8,128)(2,1)S(1)}, bf16[256,256]{1,0:T(8,128)(2,1)S(1)}, u32[]{:S(2)}, u32[]{:S(2)}) %collective-permute-start.11) | collective-permute-done | bytes 131104 | tf_op jit(solution)/shard_map/ppermute | solution.py:386
  55.1 3.9 %middle.1 = (bf16[128,256]{1,0:T(8,128)(2,1)S(1)}, bf16[128,256]{1,0:T(8,128)(2,1)S(1)}, bf16[128,256]{1,0:T(8,128)(2,1)S(1)}, bf16[128,256]{1,0:T(8,128)(2,1)S(...) custom-call(bf16[4,1440,256]{2,1,0:T(8,128)(2,1)S(1)} %bitcast.3, ...), custom_call_target="tpu_custom_call" | custom-call | bytes 12582912 | tf_op jit(solution)/shard_map/middle/pallas_call | solution.py:67
  59.0 2.7 %collective-permute-start.20 = (bf16[128,256]{1,0:T(8,128)(2,1)S(1)}, bf16[128,256]{1,0:T(8,128)(2,1)S(1)}, u32[]{:S(2)}, u32[]{:S(2)}) collective-permute-start(bf16[128,256]{1,0:T(8,128)(2,1)S(1)} %get-tuple-element.80), channel_id=1, source_target_pairs={{0,12},{4,8},{8,4},{12,0},{1,13},{5,9},{9,5},{13,1},{2,14},{6,10},... | collective-permute-start | bytes 196616 | tf_op jit(solution)/shard_map/ppermute | solution.py:386
  61.7 1.7 %collective-permute-start.22 = (bf16[128,256]{1,0:T(8,128)(2,1)S(1)}, bf16[128,256]{1,0:T(8,128)(2,1)S(1)}, u32[]{:S(2)}, u32[]{:S(2)}) collective-permute-start(bf16[128,256]{1,0:T(8,128)(2,1)S(1)} %get-tuple-element.82), channel_id=1, source_target_pairs={{0,4},{4,0},{8,12},{12,8},{1,5},{5,1},{9,13},{13,9},{2,6},{6,2},{1... | collective-permute-start | bytes 196616 | tf_op jit(solution)/shard_map/ppermute | solution.py:386
  63.4 2.7 %collective-permute-start.15 = (bf16[128,256]{1,0:T(8,128)(2,1)S(1)}, bf16[128,256]{1,0:T(8,128)(2,1)S(1)}, u32[]{:S(2)}, u32[]{:S(2)}) collective-permute-start(bf16[128,256]{1,0:T(8,128)(2,1)S(1)} %get-tuple-element.72), channel_id=1, source_target_pairs={{0,12},{4,8},{8,4},{12,0},{1,13},{5,9},{9,5},{13,1},{2,14},{6,10},... | collective-permute-start | bytes 196616 | tf_op jit(solution)/shard_map/ppermute | solution.py:386
  66.1 1.7 %collective-permute-start.17 = (bf16[128,256]{1,0:T(8,128)(2,1)S(1)}, bf16[128,256]{1,0:T(8,128)(2,1)S(1)}, u32[]{:S(2)}, u32[]{:S(2)}) collective-permute-start(bf16[128,256]{1,0:T(8,128)(2,1)S(1)} %get-tuple-element.74), channel_id=1, source_target_pairs={{0,4},{4,0},{8,12},{12,8},{1,5},{5,1},{9,13},{13,9},{2,6},{6,2},{1... | collective-permute-start | bytes 196616 | tf_op jit(solution)/shard_map/ppermute | solution.py:386
  67.8 2.9 %collective-permute-done.21.refs_1_ = bf16[128,256]{1,0:T(8,128)(2,1)S(1)} collective-permute-done((bf16[128,256]{1,0:T(8,128)(2,1)S(1)}, bf16[128,256]{1,0:T(8,128)(2,1)S(1)}, u32[]{:S(2)}, u32[]{:S(2)}) %collective-permute-start.21) | collective-permute-done | bytes 65568 | tf_op jit(solution)/shard_map/ppermute | solution.py:386
  70.8 2.2 %collective-permute-start.23 = (bf16[16,32,128]{2,1,0:T(8,128)(2,1)S(1)}, bf16[16,32,128]{2,1,0:T(8,128)(2,1)S(1)}, u32[]{:S(2)}, u32[]{:S(2)}) collective-permute-start(bf16[16,32,128]{2,1,0:T(8,128)(2,1)S(1)} %get-tuple-element.85), channel_id=1, source_target_pairs={{0,2},{2,0},{1,3},{3,1},{4,6},{6,4},{5,7},{7,5},{8,10},{10,8},{9,1... | collective-permute-start | bytes 393224 | tf_op jit(solution)/shard_map/ppermute | solution.py:386
  73.0 0.7 collective-permute-done.16.refs_1_
  73.8 1.6 %collective-permute-start.18 = (bf16[16,32,128]{2,1,0:T(8,128)(2,1)S(1)}, bf16[16,32,128]{2,1,0:T(8,128)(2,1)S(1)}, u32[]{:S(2)}, u32[]{:S(2)}) collective-permute-start(bf16[16,32,128]{2,1,0:T(8,128)(2,1)S(1)} %get-tuple-element.77), channel_id=1, source_target_pairs={{0,2},{2,0},{1,3},{3,1},{4,6},{6,4},{5,7},{7,5},{8,10},{10,8},{9,1... | collective-permute-start | bytes 393224 | tf_op jit(solution)/shard_map/ppermute | solution.py:386
  75.4 0.6 collective-permute-done.23.refs_1_
  76.0 0.4 mix_backward_1.1
  76.4 2.4 %collective-permute-start.24 = (bf16[16,32,256]{2,1,0:T(8,128)(2,1)S(1)}, bf16[16,32,256]{2,1,0:T(8,128)(2,1)S(1)}, u32[]{:S(2)}, u32[]{:S(2)}) collective-permute-start(bf16[16,32,256]{2,1,0:T(8,128)(2,1)S(1)} %get-tuple-element.87), channel_id=1, source_target_pairs={{0,2},{2,0},{1,3},{3,1},{4,6},{6,4},{5,7},{7,5},{8,10},{10,8},{9,1... | collective-permute-start | bytes 786440 | tf_op jit(solution)/shard_map/ppermute | solution.py:386
  78.8 1.5 %collective-permute-done.18.refs_1_ = bf16[16,32,128]{2,1,0:T(8,128)(2,1)S(1)} collective-permute-done((bf16[16,32,128]{2,1,0:T(8,128)(2,1)S(1)}, bf16[16,32,128]{2,1,0:T(8,128)(2,1)S(1)}, u32[]{:S(2)}, u32[]{:S(2)}) %collective-permute-start.18) | collective-permute-done | bytes 131104 | tf_op jit(solution)/shard_map/ppermute | solution.py:386
  80.2 0.4 mix_backward_0.1
  80.7 1.7 %collective-permute-start.19 = (bf16[16,32,256]{2,1,0:T(8,128)(2,1)S(1)}, bf16[16,32,256]{2,1,0:T(8,128)(2,1)S(1)}, u32[]{:S(2)}, u32[]{:S(2)}) collective-permute-start(bf16[16,32,256]{2,1,0:T(8,128)(2,1)S(1)} %get-tuple-element.79), channel_id=1, source_target_pairs={{0,2},{2,0},{1,3},{3,1},{4,6},{6,4},{5,7},{7,5},{8,10},{10,8},{9,1... | collective-permute-start | bytes 786440 | tf_op jit(solution)/shard_map/ppermute | solution.py:386
  82.3 0.5 collective-permute-start.28
  82.8 3.1 %collective-permute-done.24.refs_3_ = bf16[16,32,256]{2,1,0:T(8,128)(2,1)S(1)} collective-permute-done((bf16[16,32,256]{2,1,0:T(8,128)(2,1)S(1)}, bf16[16,32,256]{2,1,0:T(8,128)(2,1)S(1)}, u32[]{:S(2)}, u32[]{:S(2)}) %collective-permute-start.24) | collective-permute-done | bytes 262176 | tf_op jit(solution)/shard_map/ppermute | solution.py:386
  86.0 4.4 %collective-permute-done.19.refs_1_ = bf16[16,32,256]{2,1,0:T(8,128)(2,1)S(1)} collective-permute-done((bf16[16,32,256]{2,1,0:T(8,128)(2,1)S(1)}, bf16[16,32,256]{2,1,0:T(8,128)(2,1)S(1)}, u32[]{:S(2)}, u32[]{:S(2)}) %collective-permute-start.19) | collective-permute-done | bytes 262176 | tf_op jit(solution)/shard_map/ppermute | solution.py:386
  90.5 2.2 %collective-permute-start.25 = (bf16[256,256]{1,0:T(8,128)(2,1)S(1)}, bf16[256,256]{1,0:T(8,128)(2,1)S(1)}, u32[]{:S(2)}, u32[]{:S(2)}) collective-permute-start(bf16[256,256]{1,0:T(8,128)(2,1)S(1)} %get-tuple-element.88), channel_id=1, source_target_pairs={{0,12},{4,8},{8,4},{12,0},{1,13},{5,9},{9,5},{13,1},{2,14},{6,10},... | collective-permute-start | bytes 393224 | tf_op jit(solution)/shard_map/ppermute | solution.py:386
  92.7 2.2 %collective-permute-start.27 = (bf16[256,256]{1,0:T(8,128)(2,1)S(1)}, bf16[256,256]{1,0:T(8,128)(2,1)S(1)}, u32[]{:S(2)}, u32[]{:S(2)}) collective-permute-start(bf16[256,256]{1,0:T(8,128)(2,1)S(1)} %get-tuple-element.90), channel_id=1, source_target_pairs={{0,4},{4,0},{8,12},{12,8},{1,5},{5,1},{9,13},{13,9},{2,6},{6,2},{1... | collective-permute-start | bytes 393224 | tf_op jit(solution)/shard_map/ppermute | solution.py:386
  94.9 3.0 %weight_gradient_0.1.refs_4_ = f32[2,32,128,256]{3,2,1,0:T(8,128)} custom-call(bf16[16,64,256]{2,1,0:T(8,128)(2,1)S(1)} %get-tuple-element.95.refs_0_, bf16[16,64,256]{2,1,0:T(8,128)(2,1)S(1)} %collective-permute-done.13.refs_1_, bf16[16,64,128]{2,1,0:T(8,128)(2,1)S(1)} %get-tuple-element.97.refs_2_, bf16[16,64,128]{2,1,0:T(8,128)(2,1)S(1)} %collective-permute-done.29.refs_3_), custom_call_target="tpu_custom_call" | custom-call | bytes 10485760 | tf_op jit(solution)/shard_map/weight_gradient_0/pallas_call | solution.py:366
  97.9 3.0 %weight_gradient_1.1 = f32[2,32,128,256]{3,2,1,0:T(8,128)} custom-call(bf16[16,64,256]{2,1,0:T(8,128)(2,1)S(1)} %get-tuple-element.92.refs_0_, bf16[16,64,256]{2,1,0:T(8,128)(2,1)S(1)} %collective-permute-done.14.refs_1_, bf16[16,64,128]{2,1,0:T(8,128)(2,1)S(1)} %get-tuple-element.94.refs_2_, ...), custom_call_target="tpu_custom_call", output_to_operand_aliasing={{}: (4, {})} | custom-call | bytes 10485760 | tf_op jit(solution)/shard_map/weight_gradient_1/pallas_call | solution.py:366
  100.8 1.9 %collective-permute-done.26.refs_1_ = bf16[256,256]{1,0:T(8,128)(2,1)S(1)} collective-permute-done((bf16[256,256]{1,0:T(8,128)(2,1)S(1)}, bf16[256,256]{1,0:T(8,128)(2,1)S(1)}, u32[]{:S(2)}, u32[]{:S(2)}) %collective-permute-start.26) | collective-permute-done | bytes 131104 | tf_op jit(solution)/shard_map/ppermute | solution.py:386
  102.7 2.4 %final_dft.1 = bf16[4,1440,256]{2,1,0:T(8,128)(2,1)} custom-call(bf16[4,1440,256]{2,1,0:T(8,128)(2,1)S(1)} %bitcast.4, bf16[1440,256]{1,0:T(8,128)(2,1)S(1)} %copy-done.4, bf16[256,256]{1,0:T(8,128)(2,1)S(1)} %collective-permute-done.25.refs_0_, bf16[256,256]{1,0:T(8,128)(2,1)S(1)} %collective-permute-done.26.refs_1_, ...), custom_call_target="tpu_custom_call" | custom-call | bytes 8388608 | tf_op jit(solution)/shard_map/final_dft/pallas_call | solution.py:67
  (43 shorter events, 0.8 us)
Async XLA Ops:
  5.7 9.5 %collective-permute-start.5 = (bf16[128,256]{1,0:T(8,128)(2,1)}, bf16[128,256]{1,0:T(8,128)(2,1)S(1)}, u32[]{:S(2)}, u32[]{:S(2)}) collective-permute-start(bf16[128,256]{1,0:T(8,128)(2,1)} %get-tuple-element.56), channel_id=1, source_target_pairs={{0,12},{4,8},{8,4},{12,0},{1,13},{5,9},{9,5},{13,1},{2,14},{6,10},... | collective-permute-start | bytes 196616 | tf_op jit(solution)/shard_map/ppermute | solution.py:386
  10.8 8.8 %collective-permute-start.6 = (bf16[128,256]{1,0:T(8,128)(2,1)}, bf16[128,256]{1,0:T(8,128)(2,1)S(1)}, u32[]{:S(2)}, u32[]{:S(2)}) collective-permute-start(bf16[128,256]{1,0:T(8,128)(2,1)} %get-tuple-element.57), channel_id=1, source_target_pairs={{0,8},{4,12},{8,0},{12,4},{1,9},{5,13},{9,1},{13,5},{2,10},{6,14},... | collective-permute-start | bytes 196616 | tf_op jit(solution)/shard_map/ppermute | solution.py:386
  10.8 8.8 %collective-permute-start.7 = (bf16[128,256]{1,0:T(8,128)(2,1)}, bf16[128,256]{1,0:T(8,128)(2,1)S(1)}, u32[]{:S(2)}, u32[]{:S(2)}) collective-permute-start(bf16[128,256]{1,0:T(8,128)(2,1)} %get-tuple-element.58), channel_id=1, source_target_pairs={{0,4},{4,0},{8,12},{12,8},{1,5},{5,1},{9,13},{13,9},{2,6},{6,2},{1... | collective-permute-start | bytes 196616 | tf_op jit(solution)/shard_map/ppermute | solution.py:386
  11.5 10.2 %collective-permute-start = (bf16[128,256]{1,0:T(8,128)(2,1)}, bf16[128,256]{1,0:T(8,128)(2,1)S(1)}, u32[]{:S(2)}, u32[]{:S(2)}) collective-permute-start(bf16[128,256]{1,0:T(8,128)(2,1)} %get-tuple-element.50), channel_id=1, source_target_pairs={{0,12},{4,8},{8,4},{12,0},{1,13},{5,9},{9,5},{13,1},{2,14},{6,10},... | collective-permute-start | bytes 196616 | tf_op jit(solution)/shard_map/ppermute | solution.py:386
  15.2 7.0 %collective-permute-start.1 = (bf16[128,256]{1,0:T(8,128)(2,1)}, bf16[128,256]{1,0:T(8,128)(2,1)S(1)}, u32[]{:S(2)}, u32[]{:S(2)}) collective-permute-start(bf16[128,256]{1,0:T(8,128)(2,1)} %get-tuple-element.51), channel_id=1, source_target_pairs={{0,8},{4,12},{8,0},{12,4},{1,9},{5,13},{9,1},{13,5},{2,10},{6,14},... | collective-permute-start | bytes 196616 | tf_op jit(solution)/shard_map/ppermute | solution.py:386
  15.2 7.0 %collective-permute-start.2 = (bf16[128,256]{1,0:T(8,128)(2,1)}, bf16[128,256]{1,0:T(8,128)(2,1)S(1)}, u32[]{:S(2)}, u32[]{:S(2)}) collective-permute-start(bf16[128,256]{1,0:T(8,128)(2,1)} %get-tuple-element.52), channel_id=1, source_target_pairs={{0,4},{4,0},{8,12},{12,8},{1,5},{5,1},{9,13},{13,9},{2,6},{6,2},{1... | collective-permute-start | bytes 196616 | tf_op jit(solution)/shard_map/ppermute | solution.py:386
  19.6 0.8 copy-start.7
  20.5 7.9 %collective-permute-start.8 = (bf16[16,32,256]{2,1,0:T(8,128)(2,1)S(1)}, bf16[16,32,256]{2,1,0:T(8,128)(2,1)S(1)}, u32[]{:S(2)}, u32[]{:S(2)}) collective-permute-start(bf16[16,32,256]{2,1,0:T(8,128)(2,1)S(1)} %pack_1.1.refs_0_), channel_id=1, source_target_pairs={{0,2},{2,0},{1,3},{3,1},{4,6},{6,4},{5,7},{7,5},{8,10},{10,8},{9,1... | collective-permute-start | bytes 786440 | tf_op jit(solution)/shard_map/ppermute | solution.py:386
  22.3 0.8 copy-start.6
  23.1 9.4 %collective-permute-start.3 = (bf16[16,32,256]{2,1,0:T(8,128)(2,1)S(1)}, bf16[16,32,256]{2,1,0:T(8,128)(2,1)S(1)}, u32[]{:S(2)}, u32[]{:S(2)}) collective-permute-start(bf16[16,32,256]{2,1,0:T(8,128)(2,1)S(1)} %pack_0.1.refs_0_), channel_id=1, source_target_pairs={{0,2},{2,0},{1,3},{3,1},{4,6},{6,4},{5,7},{7,5},{8,10},{10,8},{9,1... | collective-permute-start | bytes 786440 | tf_op jit(solution)/shard_map/ppermute | solution.py:386
  28.4 2.2 %copy-start = (bf16[2,32,128,256]{3,2,1,0:T(8,128)(2,1)S(1)}, bf16[2,32,128,256]{3,2,1,0:T(8,128)(2,1)}, u32[]{:S(2)}) copy-start(bf16[2,32,128,256]{3,2,1,0:T(8,128)(2,1)} %refs_2_.7) | copy-start | bytes 12582916
  30.6 2.2 %copy-start.1 = (bf16[2,32,128,256]{3,2,1,0:T(8,128)(2,1)S(1)}, bf16[2,32,128,256]{3,2,1,0:T(8,128)(2,1)}, u32[]{:S(2)}) copy-start(bf16[2,32,128,256]{3,2,1,0:T(8,128)(2,1)} %refs_2_.7) | copy-start | bytes 12582916
  30.6 24.5 %copy-start.2 = (bf16[1,4,1440,256]{3,2,1,0:T(8,128)(2,1)S(1)}, bf16[1,4,1440,256]{3,2,1,0:T(8,128)(2,1)}, u32[]{:S(2)}) copy-start(bf16[1,4,1440,256]{3,2,1,0:T(8,128)(2,1)} %param.8) | copy-start | bytes 8847364
  30.6 24.5 %copy-start.3 = (bf16[256,1440]{1,0:T(8,128)(2,1)S(1)}, bf16[256,1440]{1,0:T(8,128)(2,1)}, u32[]{:S(2)}) copy-start(bf16[256,1440]{1,0:T(8,128)(2,1)} %constant.9.clone.inv_ref) | copy-start | bytes 2211844
  30.6 24.5 %copy-start.5 = (bf16[1440,256]{1,0:T(8,128)(2,1)S(1)}, bf16[1440,256]{1,0:T(8,128)(2,1)}, u32[]{:S(2)}) copy-start(bf16[1440,256]{1,0:T(8,128)(2,1)} %constant.11.clone.back_ref) | copy-start | bytes 2211844
  31.4 23.7 %collective-permute-start.14 = (bf16[16,64,256]{2,1,0:T(8,128)(2,1)S(1)}, bf16[16,64,256]{2,1,0:T(8,128)(2,1)S(1)}, u32[]{:S(2)}, u32[]{:S(2)}) collective-permute-start(bf16[16,64,256]{2,1,0:T(8,128)(2,1)S(1)} %get-tuple-element.92.refs_0_), channel_id=1, source_target_pairs={{0,1},{1,0},{2,3},{3,2},{4,5},{5,4},{6,7},{7,6},{8,9},{9,8},{10,11... | collective-permute-start | bytes 1572872 | tf_op jit(solution)/shard_map/ppermute | solution.py:386
  33.6 21.5 %collective-permute-start.13 = (bf16[16,64,256]{2,1,0:T(8,128)(2,1)S(1)}, bf16[16,64,256]{2,1,0:T(8,128)(2,1)S(1)}, u32[]{:S(2)}, u32[]{:S(2)}) collective-permute-start(bf16[16,64,256]{2,1,0:T(8,128)(2,1)S(1)} %get-tuple-element.95.refs_0_), channel_id=1, source_target_pairs={{0,1},{1,0},{2,3},{3,2},{4,5},{5,4},{6,7},{7,6},{8,9},{9,8},{10,11... | collective-permute-start | bytes 1572872 | tf_op jit(solution)/shard_map/ppermute | solution.py:386
  33.7 6.4 %collective-permute-start.9 = (bf16[16,32,128]{2,1,0:T(8,128)(2,1)S(1)}, bf16[16,32,128]{2,1,0:T(8,128)(2,1)S(1)}, u32[]{:S(2)}, u32[]{:S(2)}) collective-permute-start(bf16[16,32,128]{2,1,0:T(8,128)(2,1)S(1)} %get-tuple-element.61), channel_id=1, source_target_pairs={{0,2},{2,0},{1,3},{3,1},{4,6},{6,4},{5,7},{7,5},{8,10},{10,8},{9,1... | collective-permute-start | bytes 393224 | tf_op jit(solution)/shard_map/ppermute | solution.py:386
  35.2 7.2 %collective-permute-start.4 = (bf16[16,32,128]{2,1,0:T(8,128)(2,1)S(1)}, bf16[16,32,128]{2,1,0:T(8,128)(2,1)S(1)}, u32[]{:S(2)}, u32[]{:S(2)}) collective-permute-start(bf16[16,32,128]{2,1,0:T(8,128)(2,1)S(1)} %get-tuple-element.55), channel_id=1, source_target_pairs={{0,2},{2,0},{1,3},{3,1},{4,6},{6,4},{5,7},{7,5},{8,10},{10,8},{9,1... | collective-permute-start | bytes 393224 | tf_op jit(solution)/shard_map/ppermute | solution.py:386
  42.5 8.4 %collective-permute-start.10 = (bf16[256,256]{1,0:T(8,128)(2,1)S(1)}, bf16[256,256]{1,0:T(8,128)(2,1)S(1)}, u32[]{:S(2)}, u32[]{:S(2)}) collective-permute-start(bf16[256,256]{1,0:T(8,128)(2,1)S(1)} %get-tuple-element.62), channel_id=1, source_target_pairs={{0,12},{4,8},{8,4},{12,0},{1,13},{5,9},{9,5},{13,1},{2,14},{6,10},... | collective-permute-start | bytes 393224 | tf_op jit(solution)/shard_map/ppermute | solution.py:386
  45.5 9.6 %collective-permute-start.11 = (bf16[256,256]{1,0:T(8,128)(2,1)S(1)}, bf16[256,256]{1,0:T(8,128)(2,1)S(1)}, u32[]{:S(2)}, u32[]{:S(2)}) collective-permute-start(bf16[256,256]{1,0:T(8,128)(2,1)S(1)} %get-tuple-element.63), channel_id=1, source_target_pairs={{0,8},{4,12},{8,0},{12,4},{1,9},{5,13},{9,1},{13,5},{2,10},{6,14},... | collective-permute-start | bytes 393224 | tf_op jit(solution)/shard_map/ppermute | solution.py:386
  45.5 9.6 %collective-permute-start.12 = (bf16[256,256]{1,0:T(8,128)(2,1)S(1)}, bf16[256,256]{1,0:T(8,128)(2,1)S(1)}, u32[]{:S(2)}, u32[]{:S(2)}) collective-permute-start(bf16[256,256]{1,0:T(8,128)(2,1)S(1)} %get-tuple-element.64), channel_id=1, source_target_pairs={{0,4},{4,0},{8,12},{12,8},{1,5},{5,1},{9,13},{13,9},{2,6},{6,2},{1... | collective-permute-start | bytes 393224 | tf_op jit(solution)/shard_map/ppermute | solution.py:386
  59.0 7.1 %collective-permute-start.20 = (bf16[128,256]{1,0:T(8,128)(2,1)S(1)}, bf16[128,256]{1,0:T(8,128)(2,1)S(1)}, u32[]{:S(2)}, u32[]{:S(2)}) collective-permute-start(bf16[128,256]{1,0:T(8,128)(2,1)S(1)} %get-tuple-element.80), channel_id=1, source_target_pairs={{0,12},{4,8},{8,4},{12,0},{1,13},{5,9},{9,5},{13,1},{2,14},{6,10},... | collective-permute-start | bytes 196616 | tf_op jit(solution)/shard_map/ppermute | solution.py:386
  61.7 9.0 %collective-permute-start.21 = (bf16[128,256]{1,0:T(8,128)(2,1)S(1)}, bf16[128,256]{1,0:T(8,128)(2,1)S(1)}, u32[]{:S(2)}, u32[]{:S(2)}) collective-permute-start(bf16[128,256]{1,0:T(8,128)(2,1)S(1)} %get-tuple-element.81), channel_id=1, source_target_pairs={{0,8},{4,12},{8,0},{12,4},{1,9},{5,13},{9,1},{13,5},{2,10},{6,14},... | collective-permute-start | bytes 196616 | tf_op jit(solution)/shard_map/ppermute | solution.py:386
  61.7 9.0 %collective-permute-start.22 = (bf16[128,256]{1,0:T(8,128)(2,1)S(1)}, bf16[128,256]{1,0:T(8,128)(2,1)S(1)}, u32[]{:S(2)}, u32[]{:S(2)}) collective-permute-start(bf16[128,256]{1,0:T(8,128)(2,1)S(1)} %get-tuple-element.82), channel_id=1, source_target_pairs={{0,4},{4,0},{8,12},{12,8},{1,5},{5,1},{9,13},{13,9},{2,6},{6,2},{1... | collective-permute-start | bytes 196616 | tf_op jit(solution)/shard_map/ppermute | solution.py:386
  63.4 9.6 %collective-permute-start.15 = (bf16[128,256]{1,0:T(8,128)(2,1)S(1)}, bf16[128,256]{1,0:T(8,128)(2,1)S(1)}, u32[]{:S(2)}, u32[]{:S(2)}) collective-permute-start(bf16[128,256]{1,0:T(8,128)(2,1)S(1)} %get-tuple-element.72), channel_id=1, source_target_pairs={{0,12},{4,8},{8,4},{12,0},{1,13},{5,9},{9,5},{13,1},{2,14},{6,10},... | collective-permute-start | bytes 196616 | tf_op jit(solution)/shard_map/ppermute | solution.py:386
  66.1 7.6 %collective-permute-start.16 = (bf16[128,256]{1,0:T(8,128)(2,1)S(1)}, bf16[128,256]{1,0:T(8,128)(2,1)S(1)}, u32[]{:S(2)}, u32[]{:S(2)}) collective-permute-start(bf16[128,256]{1,0:T(8,128)(2,1)S(1)} %get-tuple-element.73), channel_id=1, source_target_pairs={{0,8},{4,12},{8,0},{12,4},{1,9},{5,13},{9,1},{13,5},{2,10},{6,14},... | collective-permute-start | bytes 196616 | tf_op jit(solution)/shard_map/ppermute | solution.py:386
  66.1 7.6 %collective-permute-start.17 = (bf16[128,256]{1,0:T(8,128)(2,1)S(1)}, bf16[128,256]{1,0:T(8,128)(2,1)S(1)}, u32[]{:S(2)}, u32[]{:S(2)}) collective-permute-start(bf16[128,256]{1,0:T(8,128)(2,1)S(1)} %get-tuple-element.74), channel_id=1, source_target_pairs={{0,4},{4,0},{8,12},{12,8},{1,5},{5,1},{9,13},{13,9},{2,6},{6,2},{1... | collective-permute-start | bytes 196616 | tf_op jit(solution)/shard_map/ppermute | solution.py:386
  70.8 5.2 %collective-permute-start.23 = (bf16[16,32,128]{2,1,0:T(8,128)(2,1)S(1)}, bf16[16,32,128]{2,1,0:T(8,128)(2,1)S(1)}, u32[]{:S(2)}, u32[]{:S(2)}) collective-permute-start(bf16[16,32,128]{2,1,0:T(8,128)(2,1)S(1)} %get-tuple-element.85), channel_id=1, source_target_pairs={{0,2},{2,0},{1,3},{3,1},{4,6},{6,4},{5,7},{7,5},{8,10},{10,8},{9,1... | collective-permute-start | bytes 393224 | tf_op jit(solution)/shard_map/ppermute | solution.py:386
  73.8 6.4 %collective-permute-start.18 = (bf16[16,32,128]{2,1,0:T(8,128)(2,1)S(1)}, bf16[16,32,128]{2,1,0:T(8,128)(2,1)S(1)}, u32[]{:S(2)}, u32[]{:S(2)}) collective-permute-start(bf16[16,32,128]{2,1,0:T(8,128)(2,1)S(1)} %get-tuple-element.77), channel_id=1, source_target_pairs={{0,2},{2,0},{1,3},{3,1},{4,6},{6,4},{5,7},{7,5},{8,10},{10,8},{9,1... | collective-permute-start | bytes 393224 | tf_op jit(solution)/shard_map/ppermute | solution.py:386
  76.4 9.6 %collective-permute-start.24 = (bf16[16,32,256]{2,1,0:T(8,128)(2,1)S(1)}, bf16[16,32,256]{2,1,0:T(8,128)(2,1)S(1)}, u32[]{:S(2)}, u32[]{:S(2)}) collective-permute-start(bf16[16,32,256]{2,1,0:T(8,128)(2,1)S(1)} %get-tuple-element.87), channel_id=1, source_target_pairs={{0,2},{2,0},{1,3},{3,1},{4,6},{6,4},{5,7},{7,5},{8,10},{10,8},{9,1... | collective-permute-start | bytes 786440 | tf_op jit(solution)/shard_map/ppermute | solution.py:386
  80.7 9.7 %collective-permute-start.19 = (bf16[16,32,256]{2,1,0:T(8,128)(2,1)S(1)}, bf16[16,32,256]{2,1,0:T(8,128)(2,1)S(1)}, u32[]{:S(2)}, u32[]{:S(2)}) collective-permute-start(bf16[16,32,256]{2,1,0:T(8,128)(2,1)S(1)} %get-tuple-element.79), channel_id=1, source_target_pairs={{0,2},{2,0},{1,3},{3,1},{4,6},{6,4},{5,7},{7,5},{8,10},{10,8},{9,1... | collective-permute-start | bytes 786440 | tf_op jit(solution)/shard_map/ppermute | solution.py:386
  82.3 12.6 %collective-permute-start.29 = (bf16[16,64,128]{2,1,0:T(8,128)(2,1)S(1)}, bf16[16,64,128]{2,1,0:T(8,128)(2,1)S(1)}, u32[]{:S(2)}, u32[]{:S(2)}) collective-permute-start(bf16[16,64,128]{2,1,0:T(8,128)(2,1)S(1)} %get-tuple-element.97.refs_2_), channel_id=1, source_target_pairs={{0,1},{1,0},{2,3},{3,2},{4,5},{5,4},{6,7},{7,6},{8,9},{9,8},{10,11... | collective-permute-start | bytes 786440 | tf_op jit(solution)/shard_map/ppermute | solution.py:386
  82.3 15.5 %collective-permute-start.28 = (bf16[16,64,128]{2,1,0:T(8,128)(2,1)S(1)}, bf16[16,64,128]{2,1,0:T(8,128)(2,1)S(1)}, u32[]{:S(2)}, u32[]{:S(2)}) collective-permute-start(bf16[16,64,128]{2,1,0:T(8,128)(2,1)S(1)} %get-tuple-element.94.refs_2_), channel_id=1, source_target_pairs={{0,1},{1,0},{2,3},{3,2},{4,5},{5,4},{6,7},{7,6},{8,9},{9,8},{10,11... | collective-permute-start | bytes 786440 | tf_op jit(solution)/shard_map/ppermute | solution.py:386
  90.5 10.4 %collective-permute-start.25 = (bf16[256,256]{1,0:T(8,128)(2,1)S(1)}, bf16[256,256]{1,0:T(8,128)(2,1)S(1)}, u32[]{:S(2)}, u32[]{:S(2)}) collective-permute-start(bf16[256,256]{1,0:T(8,128)(2,1)S(1)} %get-tuple-element.88), channel_id=1, source_target_pairs={{0,12},{4,8},{8,4},{12,0},{1,13},{5,9},{9,5},{13,1},{2,14},{6,10},... | collective-permute-start | bytes 393224 | tf_op jit(solution)/shard_map/ppermute | solution.py:386
  92.7 10.0 %collective-permute-start.26 = (bf16[256,256]{1,0:T(8,128)(2,1)S(1)}, bf16[256,256]{1,0:T(8,128)(2,1)S(1)}, u32[]{:S(2)}, u32[]{:S(2)}) collective-permute-start(bf16[256,256]{1,0:T(8,128)(2,1)S(1)} %get-tuple-element.89), channel_id=1, source_target_pairs={{0,8},{4,12},{8,0},{12,4},{1,9},{5,13},{9,1},{13,5},{2,10},{6,14},... | collective-permute-start | bytes 393224 | tf_op jit(solution)/shard_map/ppermute | solution.py:386
  92.7 10.0 %collective-permute-start.27 = (bf16[256,256]{1,0:T(8,128)(2,1)S(1)}, bf16[256,256]{1,0:T(8,128)(2,1)S(1)}, u32[]{:S(2)}, u32[]{:S(2)}) collective-permute-start(bf16[256,256]{1,0:T(8,128)(2,1)S(1)} %get-tuple-element.90), channel_id=1, source_target_pairs={{0,4},{4,0},{8,12},{12,8},{1,5},{5,1},{9,13},{13,9},{2,6},{6,2},{1... | collective-permute-start | bytes 393224 | tf_op jit(solution)/shard_map/ppermute | solution.py:386
  97.9 4.9 %copy-start.4 = (bf16[1440,256]{1,0:T(8,128)(2,1)S(1)}, bf16[1440,256]{1,0:T(8,128)(2,1)}, u32[]{:S(2)}) copy-start(bf16[1440,256]{1,0:T(8,128)(2,1)} %constant.10.clone.table_ref) | copy-start | bytes 2211844

commit v4 on v3

--- a/solution.py
+++ b/solution.py
@@ -47,11 +47,18 @@
         self.n_parts, self.n_rep = mesh.shape["parts"], mesh.shape["rep"]
         self.rows, self.lon, self.width = field[1], field[2], field[3]
         self.m_loc, self.o_w = weights[1], weights[2]
-        self.halves = 2 if self.m_loc % 16 == 0 else 1
+        self.halves = 2
         self.mu = self.m_loc // self.halves
         self.rk = 2 * self.rows
         self.wide = self.n_lat * self.rk
         self.groups = self.width // LANES
+        self.unit = self.mu // (self.n_rep * self.n_parts)
+
+    def unit_at(self, h, i):
+        return h * self.mu + i * self.unit
+
+    def unit_of(self, i):
+        return lax.axis_index("rep") * self.n_parts + i
 
 
 def params(limit=VMEM_BYTES):
@@ -95,12 +102,13 @@
 
 
 def emit_blocks(plan, held, outs):
-    at = plan.mu * plan.rk
-    for s in range(plan.n_lat):
-        for h in range(plan.halves):
-            for g in range(plan.groups):
-                block = held[s * plan.groups + g, h * at : (h + 1) * at, :].astype(BF16)
-                outs[s * plan.halves + h][:, g * LANES : (g + 1) * LANES] = block
+    pieces = len(outs) // plan.n_lat
+    at = plan.m_loc * plan.rk // pieces
+    for i, out in enumerate(outs):
+        s, h = divmod(i, pieces)
+        for g in range(plan.groups):
+            block = held[s * plan.groups + g, h * at : (h + 1) * at].astype(BF16)
+            out[:, g * LANES : (g + 1) * LANES] = block
 
 
 def collect_rows(plan, me, blocks, flat, held):
@@ -117,37 +125,41 @@
                     ]
 
 
-def block_shape(plan):
-    return (plan.mu * plan.rk, plan.width)
-
-
 def row_copies(source, target, sems):
     rows = target.shape[0]
     return [pltpu.make_async_copy(source.at[r], target.at[r], sems.at[r]) for r in range(rows)]
 
 
-def forward_dft(plan, table, field):
+def unit_like(plan):
+    return like((2, plan.unit, plan.o_w, plan.width))
+
+
+def forward_dft(plan, table, field, weights):
     n = plan.n_lat * plan.halves
-    shape = block_shape(plan)
-
-    def body(field_ref, table_ref, *refs):
-        outs, (rows, table_buf, line, held, sems, table_sem) = refs[:n], refs[n:]
+    shape = (plan.mu * plan.rk, plan.width)
+
+    def body(field_ref, table_ref, w_ref, *refs):
+        outs, (share_ref, rows, table_buf, line, held, sems, table_sem, w_sem) = refs[:n], refs[n:]
         table_copy = pltpu.make_async_copy(table_ref, table_buf, table_sem)
         table_copy.start()
         copies = row_copies(field_ref, rows, sems)
         for copy in copies:
             copy.start()
+        first = plan.unit_at(plan.halves - 1, plan.unit_of(lax.axis_index("parts")))
+        share = pltpu.make_async_copy(w_ref.at[:, pl.ds(first, plan.unit)], share_ref, w_sem)
+        share.start()
         table_copy.wait()
         for row in range(plan.rows):
             copies[row].wait()
             line[...] = jnp.dot(table_buf[...], rows[row], preferred_element_type=F32)
             spread_rows(plan, lax.axis_index("lat"), row, line, held)
         emit_blocks(plan, held, outs)
+        share.wait()
 
     return whole(
         body,
         "forward_dft",
-        [like(shape)] * n,
+        [like(shape)] * n + [unit_like(plan)],
         [
             pltpu.VMEM(field.shape, BF16),
             pltpu.VMEM(table.shape, BF16),
@@ -155,22 +167,35 @@
             pltpu.VMEM((plan.n_lat * plan.groups, plan.m_loc * plan.rk, LANES), F32),
             pltpu.SemaphoreType.DMA((plan.rows,)),
             pltpu.SemaphoreType.DMA,
+            pltpu.SemaphoreType.DMA,
         ],
-        ins=[ANY, ANY],
+        ins=[ANY, ANY, ANY],
         mebi=6,
         limit=60 * MEBI,
-    )(field, table)
-
-
-def middle(plan, inverse_t, inverse, cotangent, blocks):
-    n_in, n = len(blocks), plan.n_lat * plan.halves
+    )(field, table, weights)
+
+
+def middle(plan, inverse_t, inverse, cotangent, blocks, loose):
+    n_in, n = len(blocks), plan.n_lat
     modes2 = inverse.shape[0]
-    shape = block_shape(plan)
+    shape = (plan.m_loc * plan.rk, plan.width)
     cut = next(c for c in (288, 480, 360, 240, 160, plan.lon) if plan.lon % c == 0)
 
+    loose = [array.reshape(-1, plan.width) for array in loose]
+    ends = np.cumsum([array.shape[0] for array in loose]).tolist()
+
     def body(cot_ref, back_ref, inv_ref, *refs):
-        ins, outs = refs[:n_in][::-1], refs[n_in : n_in + n]
-        flat, held, scaled, line, out_held = refs[n_in + n :]
+        ins, refs = refs[:n_in][::-1], refs[n_in:]
+        sources, refs = refs[: len(loose)], refs[len(loose) :]
+        outs, (tied, flat, held, scaled, line, out_held, sems) = refs[:n], refs[n:]
+        copies = [
+            pltpu.make_async_copy(
+                source, tied.at[end - source.shape[0] : end], sems.at[i]
+            )
+            for i, (source, end) in enumerate(zip(sources, ends))
+        ]
+        for copy in copies:
+            copy.start()
         lat = lax.axis_index("lat")
         collect_rows(plan, lat, ins, flat, held)
         for row in range(plan.rows):
@@ -182,20 +207,24 @@
             line[row % 2] = jnp.dot(inv_ref[...], scaled[row % 2], preferred_element_type=F32)
             spread_rows(plan, lat, row, line.at[row % 2], out_held)
         emit_blocks(plan, out_held, outs)
-
-    return whole(
+        for copy in copies:
+            copy.wait()
+
+    out = whole(
         body,
         "middle",
-        [like(shape)] * n,
+        [like(shape)] * n + [like((ends[-1], plan.width))],
         [
             pltpu.VMEM((plan.groups, plan.m_loc * plan.rk, LANES), F32),
             pltpu.VMEM((plan.rows, modes2, plan.width), F32),
             pltpu.VMEM((2, plan.lon, plan.width), BF16),
             pltpu.VMEM((2, modes2, plan.width), F32),
             pltpu.VMEM((plan.n_lat * plan.groups, plan.m_loc * plan.rk, LANES), F32),
+            pltpu.SemaphoreType.DMA((len(loose),)),
         ],
         mebi=12,
-    )(cotangent, inverse_t, inverse, *blocks[::-1])
+    )(cotangent, inverse_t, inverse, *blocks[::-1], *loose)
+    return out[:n], out[n]
 
 
 def final_dft(plan, table_t, cotangent, blocks):
@@ -223,7 +252,7 @@
             pltpu.SemaphoreType.DMA((plan.rows,)),
         ],
         out_specs=[ANY],
-        mebi=8,
+        mebi=80,
     )(cotangent, table_t, *blocks[::-1])[0]
 
 
@@ -239,23 +268,24 @@
         parts = [ref[...].astype(F32).reshape(plan.mu, plan.rk, plan.width) for ref in ins]
         out[...] = jnp.concatenate(parts, axis=1).astype(BF16)
 
-    return whole(body, f"pack_{h}", [like((plan.mu, plan.wide, plan.width))])(*blocks[::-1])[0]
-
-
-def pack_gradients(plan, h, blocks):
-    part = (plan.mu, plan.wide, plan.o_w)
+    out = like((plan.mu, plan.wide, plan.width))
+    return whole(body, f"pack_{h}", [out])(*blocks[::-1])[0]
+
+
+def pack_gradients(plan, blocks):
+    part = (plan.m_loc, plan.wide, plan.o_w)
 
     def body(*refs):
         ins, outs, held = refs[: plan.n_lat][::-1], refs[plan.n_lat : -1], refs[-1]
-        blocks = [ref[...].astype(F32).reshape(plan.mu, plan.rk, plan.width) for ref in ins]
+        blocks = [ref[...].astype(F32).reshape(plan.m_loc, plan.rk, plan.width) for ref in ins]
         every = jnp.concatenate(blocks, axis=1)
         for c in range(plan.n_chan):
             held[c] = every[:, :, c * plan.o_w : (c + 1) * plan.o_w]
-        for x in range(plan.n_chan):
-            outs[x][...] = held[lax.axis_index("chan") ^ x].astype(BF16)
+        for x, out in enumerate(outs):
+            out[...] = held[lax.axis_index("chan") ^ x].astype(BF16)
 
     scratch = [pltpu.VMEM((plan.n_chan, *part), F32)]
-    return whole(body, f"pack_gradients_{h}", [like(part)] * plan.n_chan, scratch)(*blocks[::-1])
+    return whole(body, "pack_gradients", [like(part)] * plan.n_chan, scratch)(*blocks[::-1])
 
 
 def merge(plan, pieces):
@@ -283,7 +313,10 @@
 
     def body(*refs):
         ins, own_ref = refs[: plan.n_chan], refs[plan.n_chan]
-        outs, every = refs[plan.n_chan + 1 : -1], refs[-1]
+        outs, every = refs[plan.n_chan + 1 : 2 * plan.n_chan + 1], refs[2 * plan.n_chan + 1]
+        source = own_ref.at[:, pl.ds(plan.unit_at(0, plan.unit_of(h)), plan.unit)]
+        copy = pltpu.make_async_copy(source, refs[-2], refs[-1])
+        copy.start()
         dims = (((1,), (1,)), ((), ()))
         for u in range(plan.mu):
             at = h * plan.mu + u
@@ -298,96 +331,111 @@
             )
             for x in range(plan.n_chan):
                 outs[x][u] = mixed[x * plan.wide : (x + 1) * plan.wide].astype(BF16)
-
-    outs = [like(part)] * plan.n_chan + [like(tall)]
-    return whole(body, f"mix_forward_{h}", outs, mebi=3)(*spectra, own)
-
-
-def mix_backward(plan, h, grads, own):
-    wide = (plan.mu, plan.wide, plan.width)
-    tall = (plan.mu, plan.n_chan * plan.wide, plan.o_w)
+        copy.wait()
+
+    outs = [like(part)] * plan.n_chan + [like(tall), unit_like(plan)]
+    scratch = [pltpu.SemaphoreType.DMA]
+    return whole(body, f"mix_forward_{h}", outs, scratch, mebi=3)(*spectra, own)
+
+
+def mix_backward(plan, grads, own, early, late):
+    shape = (plan.m_loc * plan.rk, plan.width)
+    flat = [*early, *(array for group in late for array in group)]
+    n = plan.n_rep
 
     def body(*refs):
         ins, own_ref = refs[: plan.n_chan], refs[plan.n_chan]
-        outs, every = refs[plan.n_chan + 1 : -1], refs[-1]
-        for u in range(plan.mu):
-            at = h * plan.mu + u
-            rows = jnp.concatenate([ref[u].astype(F32) for ref in ins], axis=0)
-            every[u] = rows.astype(BF16)
-            groups = rows.reshape(-1, plan.rk, plan.o_w)
-            turn = turned(plan, groups, 1.0).reshape(rows.shape)
-            back = jnp.dot(
-                rows.astype(BF16), own_ref[0, at], preferred_element_type=F32
-            ) + jnp.dot(turn.astype(BF16), own_ref[1, at], preferred_element_type=F32)
-            for x in range(plan.n_chan):
-                outs[x][u] = back[x * plan.wide : (x + 1) * plan.wide].astype(outs[x].dtype)
-
-    outs = [like(wide, F32)] + [like(wide)] * (plan.n_chan - 1) + [like(tall)]
-    return whole(body, f"mix_backward_{h}", outs, mebi=3)(*grads, own)
-
-
-def merge_gradients(plan, parts):
-    shape = (plan.m_loc * plan.rk, plan.width)
+        there = refs[plan.n_chan + 1 : plan.n_chan + 1 + len(flat)]
+        outs, held = refs[plan.n_chan + 1 + len(flat) : -1], refs[-1]
+        me, here = lax.axis_index("rep"), lax.axis_index("parts")
+        for e in range(n):
+            base = (me ^ e) * plan.n_parts
+            units = [(plan.unit_at(1, base + (here ^ p)), True, p) for p in range(plan.n_parts)]
+            units += [(plan.unit_at(0, base), True, plan.n_parts)]
+            units += [(plan.unit_at(0, base + i), False, i - 1) for i in range(1, plan.n_parts)]
+            for first, is_early, i in units:
+                for t in range(plan.unit):
+                    u = first + t
+                    total = 0.0
+                    for x in range(plan.n_chan):
+                        rows = ins[x][u].astype(F32)
+                        turn = turned(plan, rows.reshape(-1, plan.rk, plan.o_w), 1.0)
+                        turn = turn.reshape(rows.shape)
+                        for j, values in enumerate((rows, turn)):
+                            if x == 0:
+                                weights = own_ref[j, u]
+                            else:
+                                ref, at = there[n + (x - 1) * n + e], i
+                                if is_early:
+                                    ref, at = there[e], (x - 1) * (plan.n_parts + 1) + i
+                                at = ((at * 2 + j) * plan.unit + t) * plan.o_w
+                                weights = ref[at : at + plan.o_w]
+                            total += jnp.dot(
+                                values.astype(BF16), weights, preferred_element_type=F32
+                            )
+                    held[u] = total
+        for s in range(plan.n_lat):
+            block = held[:, s * plan.rk : (s + 1) * plan.rk, :]
+            outs[s][...] = block.reshape(shape).astype(BF16)
+
+    scratch = [pltpu.VMEM((plan.m_loc, plan.wide, plan.width), F32)]
+    outs = [like(shape)] * plan.n_lat
+    return whole(body, "mix_backward", outs, scratch, mebi=9)(*grads, own, *flat)
+
+
+def weight_gradient(plan, spectra, grads):
+    n, step, slots = len(spectra), 4, 4
+    scale = 1.0 / (plan.rows * plan.n_lat * plan.n_chan)
+    tall = plan.n_chan * plan.wide
+    skipped = spectra[0].shape[0] - plan.m_loc * tall
 
     def body(*refs):
-        ins, outs = refs[: -plan.n_lat], refs[-plan.n_lat :]
-        for h in range(plan.halves):
-            total = sum(ref[...].astype(F32) for ref in ins[h * plan.n_chan : (h + 1) * plan.n_chan])
-            at = plan.mu * plan.rk
-            for s in range(plan.n_lat):
-                block = total[:, s * plan.rk : (s + 1) * plan.rk, :]
-                outs[s][h * at : (h + 1) * at, :] = block.reshape(at, plan.width).astype(BF16)
-
-    flat = [part for half in parts for part in half]
-    return whole(body, "merge_gradients", [like(shape)] * plan.n_lat)(*flat)
-
-
-def weight_gradient(plan, h, spectra, grads, before):
-    step = 4
-    n, n_g = len(spectra), len(grads)
-    scale = 1.0 / (plan.rows * plan.n_lat * plan.n_chan)
-
-    def body(*refs):
-        s_refs, g_refs, out = refs[:n], refs[n : n + n_g], refs[-1]
-        for t in range(step):
-            s_all = jnp.concatenate([ref[t].astype(F32) for ref in s_refs], axis=0).astype(BF16)
-            g_all = jnp.concatenate([ref[t].astype(F32) for ref in g_refs], axis=0)
-            groups = g_all.reshape(-1, plan.rk, plan.o_w)
-            g_turn = turned(plan, groups, 1.0).reshape(g_all.shape)
-            for j, g in enumerate((g_all, g_turn)):
+        s_refs, g_refs, (out, held, sems) = refs[:n], refs[n:-3], refs[-3:]
+        copies = []
+        for at in range(0, plan.m_loc, step):
+            slot = at // step % slots
+            if len(copies) >= slots:
+                copies[-slots].wait()
+            for t in range(at, at + step):
+                rows = slice(skipped + t * tall, skipped + (t + 1) * tall)
+                s_all = jnp.concatenate([ref[rows].astype(F32) for ref in s_refs], axis=0)
+                s_turn = turned(plan, s_all.reshape(-1, plan.rk, plan.width), -1.0)
+                pair = jnp.concatenate([s_all, s_turn.reshape(s_all.shape)], axis=1)
+                g_all = jnp.concatenate([ref[t].astype(F32) for ref in g_refs], axis=0)
                 total = lax.dot_general(
-                    g.astype(BF16), s_all, (((0,), (0,)), ((), ())), preferred_element_type=F32
+                    g_all.astype(BF16),
+                    pair.astype(BF16),
+                    (((0,), (0,)), ((), ())),
+                    preferred_element_type=F32,
                 )
-                out[j, t] = total * scale
-
-    out_shape = (2, plan.m_loc, plan.o_w, plan.width)
-    steps = plan.mu // step
-    earlier = [] if before is None else [before]
-    return pl.pallas_call(
+                held[slot, 0, t - at] = total[:, : plan.width] * scale
+                held[slot, 1, t - at] = total[:, plan.width :] * scale
+            target = out.at[:, at : at + step]
+            copies.append(pltpu.make_async_copy(held.at[slot], target, sems.at[slot]))
+            copies[-1].start()
+        for copy in copies[-slots:]:
+            copy.wait()
+
+    return whole(
         body,
-        grid=(steps,),
-        in_specs=[
-            pl.BlockSpec((step, *array.shape[1:]), lambda q: (q, 0, 0))
-            for array in (*spectra, *grads)
-        ]
-        + [pl.BlockSpec(memory_space=pl.ANY)] * len(earlier),
-        out_specs=pl.BlockSpec(
-            (2, step, plan.o_w, plan.width), lambda q: (0, h * steps + q, 0, 0)
-        ),
-        out_shape=jax.ShapeDtypeStruct(out_shape, F32),
-        input_output_aliases={n + n_g: 0} if earlier else {},
-        compiler_params=params(),
-        cost_estimate=pl.CostEstimate(flops=0, bytes_accessed=10 * MEBI, transcendentals=0),
-        name=f"weight_gradient_{h}",
-    )(*spectra, *grads, *earlier)
+        "weight_gradient",
+        [like((2, plan.m_loc, plan.o_w, plan.width), F32)],
+        [
+            pltpu.VMEM((slots, 2, step, plan.o_w, plan.width), F32),
+            pltpu.SemaphoreType.DMA((slots,)),
+        ],
+        out_specs=[ANY],
+        mebi=2,
+    )(*spectra, *grads)[0]
 
 
 def hop(value, axis, size, s):
     return lax.ppermute(value, axis, [(i, i ^ s) for i in range(size)])
 
 
-def spread(values, axis, size):
-    return [value if s == 0 else hop(value, axis, size, s) for s in range(size) for value in values]
+def spread(values, axis, size, when=()):
+    sent = [after(value, *when) for value in values] if when else values
+    return list(values) + [hop(value, axis, size, s) for s in range(1, size) for value in sent]
 
 
 def after(value, *others):
@@ -413,30 +461,57 @@
         return spread(values, "rep", plan.n_rep)
 
     field, cotangent = field[0], cotangent[0]
-    blocks = forward_dft(plan, forward, field)
-    pieces, every_s = [], []
+    def fetch(unit):
+        return [hop(unit, "chan", plan.n_chan, x) for x in range(1, plan.n_chan)]
+
+    def along(axis, values, *when):
+        return [spread([value], axis, lax.axis_size(axis), when) for value in values]
+
+    def together(values, others):
+        values, others = lax.optimization_barrier((values[::-1], others))
+        return values[::-1], others
+
+    *blocks, unit = forward_dft(plan, forward, field, weights)
+    blocks = [to_lat(blocks[h :: plan.halves]) for h in halves]
+    blocks[-1], last = together(blocks[-1], fetch(unit))
+    pieces, tall, units = [], [], []
     for h in halves:
-        packed = pack(plan, h, to_lat(blocks[h :: plan.halves]))
-        *parts, tall = mix_forward(plan, h, over_chan([packed] * plan.n_chan), weights)
+        packed = pack(plan, h, blocks[h])
+        *parts, rows, unit = mix_forward(plan, h, over_chan([packed] * plan.n_chan), weights)
         pieces.append(over_chan(parts))
-        every_s.append(rep_too([tall]))
-    mixed = to_lat(merge(plan, pieces))
-
-    mixed, every_s = lax.optimization_barrier((mixed[::-1], every_s))
-    mixed = mixed[::-1]
-    blocks = middle(plan, inverse_t, inverse, cotangent, mixed)
-    pieces, every_g = [], []
-    for h in halves:
-        grads = pack_gradients(plan, h, to_lat(blocks[h :: plan.halves]))
-        *parts, tall = mix_backward(plan, h, over_chan(grads), weights)
-        pieces.append(over_chan(parts))
-        every_g.append(rep_too([tall]))
-    spectral = to_lat(merge_gradients(plan, pieces))
+        tall.append(rows)
+        units.append(unit)
+
+    last = along("parts", last, *pieces[0])
+    first = fetch(after(units[0], *pieces[0], *pieces[1]))
+    blocks, (last, first) = together(to_lat(merge(plan, pieces)), (last, first))
+    loose = [unit for pair, unit in zip(last, first) for unit in (*pair, unit)]
+    blocks, tied = middle(plan, inverse_t, inverse, cotangent, blocks, loose + tall)
+
+    tied = along("rep", [tied], *blocks)[0]
+    late = fetch(after(units[1], *blocks))
+    blocks, (tied, late) = together(to_lat(blocks), (tied, late))
+    late = along("rep", [unit.reshape(-1, plan.width) for unit in late])
+    grads = pack_gradients(plan, blocks)
+    blocks = mix_backward(plan, grads, weights, tied, late)
+    spectral = to_lat(blocks)
+    far = [
+        lax.ppermute(
+            grads[x],
+            ("chan", "rep"),
+            [
+                (c * plan.n_rep + r, (c ^ x) * plan.n_rep + (r ^ e))
+                for c in range(plan.n_chan)
+                for r in range(plan.n_rep)
+            ],
+        )
+        for e in range(1, plan.n_rep)
+        for x in range(plan.n_chan)
+    ]
+    every_g = over_chan(grads) + far
+
+    weight_grad = weight_gradient(plan, tied, every_g)
     grad_field = final_dft(plan, forward_t, cotangent, spectral)
-
-    weight_grad = None
-    for h in halves:
-        weight_grad = weight_gradient(plan, h, every_s[h], every_g[h], weight_grad)
     return (grad_field[None], weight_grad)
 
 

time: 105 us -> 95.1 us (0.906)
  starting transfers between devices: 41.6 us -> 35.7 us
  waiting for transfers between devices: 38.4 us -> 35.5 us
  Pallas kernels: 20.2 us -> 19 us
    ppermute x30 -> x26, starting transfers between devices: 41.6 us -> 34.8 us  [hop(): return lax.ppermute(value, axis, [(i, i ^ s) for i in range(size)])]
    pallas_call x2 -> x0, Pallas kernels: 5.91 us -> none  [weight_gradient(): pl.pallas_call(body, grid=(steps,), in_specs=[pl.BlockSpec((step, *array....]
    pallas_call x13 -> x11, Pallas kernels: 14.3 us -> 19 us  [call(): pl.pallas_call(body, in_specs=ins or [VMEM] * len(operands), out_specs=ou...]
    ppermute x30 -> x26, waiting for transfers between devices: 38.4 us -> 34.6 us  [hop(): return lax.ppermute(value, axis, [(i, i ^ s) for i in range(size)])]
  transfers between devices with their start and end apart: 30 -> 28, of which waited for: 15 -> 13; matrix products, arithmetic and copies ran while one was open for 0% -> 0% of each run, Pallas kernels for 8% -> 7%
where the time goes in v4:
time: 95.1 us; the launch traced here: 94.8 us
  starting transfers between devices  35.7 us (38%)
  waiting for transfers between devices  35.5 us (37%)
  Pallas kernels  19 us (20%)
  local copies, waits for them, and re-layouts  3.9 us (4%)
    ppermute x26, starting transfers between devices, hop(): return lax.ppermute(value, axis, [(i, i ^ s) for i in range(size)])  34.8 us
    ppermute x26, waiting for transfers between devices, hop(): return lax.ppermute(value, axis, [(i, i ^ s) for i in range(size)])  34.6 us
    pallas_call x11, Pallas kernels, call(): pl.pallas_call(body, in_specs=ins or [VMEM] * len(operands), out_specs=ou...  19 us
    unnamed x16, local copies, waits for them, and re-layouts  3.9 us
  transfers between devices with their start and end apart: 28, of which 13 were waited for; matrix products, arithmetic and copies ran while one was open for 0% of the time, Pallas kernels for 7%

profile of v4, /device:TPU:0, one launch (start us, length us, event | category | flops | bytes accessed | tf_op | source)
XLA Modules:
  0.0 94.8 jit_solution(10348856680140937451)
XLA Ops:
  0.6 5.4 %forward_dft.1 = (bf16[128,256]{1,0:T(8,128)(2,1)}, bf16[128,256]{1,0:T(8,128)(2,1)}, bf16[128,256]{1,0:T(8,128)(2,1)}, bf16[128,256]{1,0:T(8,128)(2,1)}, bf16[1...) custom-call(bf16[4,1440,256]{2,1,0:T(8,128)(2,1)} %bitcast.19, ...), custom_call_target="tpu_custom_call" | custom-call | bytes 6291456 | tf_op jit(solution)/shard_map/forward_dft/pallas_call | solution.py:74
  6.0 3.0 %collective-permute-start.8 = (bf16[2,4,128,256]{3,2,1,0:T(8,128)(2,1)}, bf16[2,4,128,256]{3,2,1,0:T(8,128)(2,1)S(1)}, u32[]{:S(2)}, u32[]{:S(2)}) collective-permute-start(bf16[2,4,128,256]{3,2,1,0:T(8,128)(2,1)} %get-tuple-element.67), channel_id=1, source_target_pairs={{0,2},{2,0},{1,3},{3,1},{4,6},{6,4},{5,7},{7,5},{8,10},{10,8},{9,1... | collective-permute-start | bytes 1572872 | tf_op jit(solution)/shard_map/ppermute | solution.py:433
  9.0 3.6 %collective-permute-start = (bf16[128,256]{1,0:T(8,128)(2,1)}, bf16[128,256]{1,0:T(8,128)(2,1)S(1)}, u32[]{:S(2)}, u32[]{:S(2)}) collective-permute-start(bf16[128,256]{1,0:T(8,128)(2,1)} %get-tuple-element.57), channel_id=1, source_target_pairs={{0,12},{4,8},{8,4},{12,0},{1,13},{5,9},{9,5},{13,1},{2,14},{6,10},... | collective-permute-start | bytes 196616 | tf_op jit(solution)/shard_map/ppermute | solution.py:433
  12.6 0.8 collective-permute-start.2
  13.4 3.6 %collective-permute-start.5 = (bf16[128,256]{1,0:T(8,128)(2,1)}, bf16[128,256]{1,0:T(8,128)(2,1)S(1)}, u32[]{:S(2)}, u32[]{:S(2)}) collective-permute-start(bf16[128,256]{1,0:T(8,128)(2,1)} %get-tuple-element.63), channel_id=1, source_target_pairs={{0,12},{4,8},{8,4},{12,0},{1,13},{5,9},{9,5},{13,1},{2,14},{6,10},... | collective-permute-start | bytes 196616 | tf_op jit(solution)/shard_map/ppermute | solution.py:433
  17.0 2.1 %collective-permute-start.6 = (bf16[128,256]{1,0:T(8,128)(2,1)}, bf16[128,256]{1,0:T(8,128)(2,1)S(1)}, u32[]{:S(2)}, u32[]{:S(2)}) collective-permute-start(bf16[128,256]{1,0:T(8,128)(2,1)} %get-tuple-element.64), channel_id=1, source_target_pairs={{0,8},{4,12},{8,0},{12,4},{1,9},{5,13},{9,1},{13,5},{2,10},{6,14},... | collective-permute-start | bytes 196616 | tf_op jit(solution)/shard_map/ppermute | solution.py:433
  19.2 1.7 %collective-permute-done.1.refs_1_ = bf16[128,256]{1,0:T(8,128)(2,1)S(1)} collective-permute-done((bf16[128,256]{1,0:T(8,128)(2,1)}, bf16[128,256]{1,0:T(8,128)(2,1)S(1)}, u32[]{:S(2)}, u32[]{:S(2)}) %collective-permute-start.1) | collective-permute-done | bytes 65568 | tf_op jit(solution)/shard_map/ppermute | solution.py:433
  20.9 0.8 copy-done.7
  21.7 0.6 collective-permute-start.3
  22.3 1.4 %collective-permute-done.6.refs_1_ = bf16[128,256]{1,0:T(8,128)(2,1)S(1)} collective-permute-done((bf16[128,256]{1,0:T(8,128)(2,1)}, bf16[128,256]{1,0:T(8,128)(2,1)S(1)}, u32[]{:S(2)}, u32[]{:S(2)}) %collective-permute-start.6) | collective-permute-done | bytes 65568 | tf_op jit(solution)/shard_map/ppermute | solution.py:433
  23.8 1.6 %collective-permute-done.7.refs_2_ = bf16[128,256]{1,0:T(8,128)(2,1)S(1)} collective-permute-done((bf16[128,256]{1,0:T(8,128)(2,1)}, bf16[128,256]{1,0:T(8,128)(2,1)S(1)}, u32[]{:S(2)}, u32[]{:S(2)}) %collective-permute-start.7) | collective-permute-done | bytes 65568 | tf_op jit(solution)/shard_map/ppermute | solution.py:433
  25.4 0.8 copy-done.6
  26.2 0.6 collective-permute-start.9
  26.8 2.7 %collective-permute-done.3.refs_1_ = bf16[16,32,256]{2,1,0:T(8,128)(2,1)S(1)} collective-permute-done((bf16[16,32,256]{2,1,0:T(8,128)(2,1)S(1)}, bf16[16,32,256]{2,1,0:T(8,128)(2,1)S(1)}, u32[]{:S(2)}, u32[]{:S(2)}) %collective-permute-start.3) | collective-permute-done | bytes 262176 | tf_op jit(solution)/shard_map/ppermute | solution.py:433
  29.5 2.2 %copy-done = bf16[2,32,128,256]{3,2,1,0:T(8,128)(2,1)S(1)} copy-done((bf16[2,32,128,256]{3,2,1,0:T(8,128)(2,1)S(1)}, bf16[2,32,128,256]{3,2,1,0:T(8,128)(2,1)}, u32[]{:S(2)}) %copy-start) | copy-done | bytes 4194328
  31.7 0.9 mix_forward_0.1
  32.6 0.6 collective-permute-start.4
  33.2 2.0 %collective-permute-done.9.refs_1_ = bf16[16,32,256]{2,1,0:T(8,128)(2,1)S(1)} collective-permute-done((bf16[16,32,256]{2,1,0:T(8,128)(2,1)S(1)}, bf16[16,32,256]{2,1,0:T(8,128)(2,1)S(1)}, u32[]{:S(2)}, u32[]{:S(2)}) %collective-permute-start.9) | collective-permute-done | bytes 262176 | tf_op jit(solution)/shard_map/ppermute | solution.py:433
  35.2 0.9 mix_forward_1.1
  36.1 0.6 collective-permute-start.10
  36.7 1.8 %collective-permute-done.4.refs_1_ = bf16[16,32,128]{2,1,0:T(8,128)(2,1)S(1)} collective-permute-done((bf16[16,32,128]{2,1,0:T(8,128)(2,1)S(1)}, bf16[16,32,128]{2,1,0:T(8,128)(2,1)S(1)}, u32[]{:S(2)}, u32[]{:S(2)}) %collective-permute-start.4) | collective-permute-done | bytes 131104 | tf_op jit(solution)/shard_map/ppermute | solution.py:433
  38.5 1.5 %collective-permute-start.14 = (bf16[2,4,128,256]{3,2,1,0:T(8,128)(2,1)S(1)}, bf16[2,4,128,256]{3,2,1,0:T(8,128)(2,1)S(1)}, u32[]{:S(2)}, u32[]{:S(2)}) collective-permute-start(bf16[2,4,128,256]{3,2,1,0:T(8,128)(2,1)S(1)} %collective-permute-done.8), channel_id=1, source_target_pairs={{0,16},{16,0},{1,17},{17,1},{2,18},{18,2},{3,19},{19,3},{4,20},{20... | collective-permute-start | bytes 1572872 | tf_op jit(solution)/shard_map/ppermute | solution.py:433
  40.0 1.4 %collective-permute-done.10.refs_3_ = bf16[16,32,128]{2,1,0:T(8,128)(2,1)S(1)} collective-permute-done((bf16[16,32,128]{2,1,0:T(8,128)(2,1)S(1)}, bf16[16,32,128]{2,1,0:T(8,128)(2,1)S(1)}, u32[]{:S(2)}, u32[]{:S(2)}) %collective-permute-start.10) | collective-permute-done | bytes 131104 | tf_op jit(solution)/shard_map/ppermute | solution.py:433
  41.4 0.5 collective-permute-start.15
  42.0 0.1 merge.1
  42.1 4.6 %collective-permute-start.11 = (bf16[256,256]{1,0:T(8,128)(2,1)S(1)}, bf16[256,256]{1,0:T(8,128)(2,1)S(1)}, u32[]{:S(2)}, u32[]{:S(2)}) collective-permute-start(bf16[256,256]{1,0:T(8,128)(2,1)S(1)} %get-tuple-element.74), channel_id=1, source_target_pairs={{0,12},{4,8},{8,4},{12,0},{1,13},{5,9},{9,5},{13,1},{2,14},{6,10},... | collective-permute-start | bytes 393224 | tf_op jit(solution)/shard_map/ppermute | solution.py:433
  46.7 0.7 collective-permute-start.12
  47.4 0.3 collective-permute-start.13
  47.6 2.1 %collective-permute-done.11.refs_0_ = bf16[256,256]{1,0:T(8,128)(2,1)S(1)} collective-permute-done((bf16[256,256]{1,0:T(8,128)(2,1)S(1)}, bf16[256,256]{1,0:T(8,128)(2,1)S(1)}, u32[]{:S(2)}, u32[]{:S(2)}) %collective-permute-start.11) | collective-permute-done | bytes 131104 | tf_op jit(solution)/shard_map/ppermute | solution.py:433
  49.7 4.2 %collective-permute-done.12.refs_1_ = bf16[256,256]{1,0:T(8,128)(2,1)S(1)} collective-permute-done((bf16[256,256]{1,0:T(8,128)(2,1)S(1)}, bf16[256,256]{1,0:T(8,128)(2,1)S(1)}, u32[]{:S(2)}, u32[]{:S(2)}) %collective-permute-start.12) | collective-permute-done | bytes 131104 | tf_op jit(solution)/shard_map/ppermute | solution.py:433
  54.0 4.1 %middle.1 = (bf16[256,256]{1,0:T(8,128)(2,1)S(1)}, bf16[256,256]{1,0:T(8,128)(2,1)S(1)}, bf16[256,256]{1,0:T(8,128)(2,1)S(1)}, bf16[256,256]{1,0:T(8,128)(2,1)S(1)}, bf16[5120,256]{1,0:T(8,128)(2,1)S(1)}) custom-call(bf16[4,1440,256]{2,1,0:T(8,128)(2,1)S(1)} %bitcast.9, bf16[1440,256]{1,0:T(8,128)(2,1)S(1)} %copy-done.5, bf16[256,1440]{1,0:T(8,128)(2,1)S(1)} %copy-done.3, ...), custom_call_target="tpu_custom_call" | custom-call | bytes 12582912 | tf_op jit(solution)/shard_map/middle/pallas_call | solution.py:74
  58.1 0.1 collective-permute-start.19
  58.2 1.3 %collective-permute-start.20 = (bf16[2,4,128,256]{3,2,1,0:T(8,128)(2,1)S(1)}, bf16[2,4,128,256]{3,2,1,0:T(8,128)(2,1)S(1)}, u32[]{:S(2)}, u32[]{:S(2)}) collective-permute-start(bf16[2,4,128,256]{3,2,1,0:T(8,128)(2,1)S(1)} %get-tuple-element.98), channel_id=1, source_target_pairs={{0,2},{2,0},{1,3},{3,1},{4,6},{6,4},{5,7},{7,5},{8,10},{10,8},{9,1... | collective-permute-start | bytes 1572872 | tf_op jit(solution)/shard_map/ppermute | solution.py:433
  59.5 2.2 %collective-permute-start.16 = (bf16[256,256]{1,0:T(8,128)(2,1)S(1)}, bf16[256,256]{1,0:T(8,128)(2,1)S(1)}, u32[]{:S(2)}, u32[]{:S(2)}) collective-permute-start(bf16[256,256]{1,0:T(8,128)(2,1)S(1)} %get-tuple-element.91), channel_id=1, source_target_pairs={{0,12},{4,8},{8,4},{12,0},{1,13},{5,9},{9,5},{13,1},{2,14},{6,10},... | collective-permute-start | bytes 393224 | tf_op jit(solution)/shard_map/ppermute | solution.py:433
  61.7 2.2 %collective-permute-start.18 = (bf16[256,256]{1,0:T(8,128)(2,1)S(1)}, bf16[256,256]{1,0:T(8,128)(2,1)S(1)}, u32[]{:S(2)}, u32[]{:S(2)}) collective-permute-start(bf16[256,256]{1,0:T(8,128)(2,1)S(1)} %get-tuple-element.93), channel_id=1, source_target_pairs={{0,4},{4,0},{8,12},{12,8},{1,5},{5,1},{9,13},{13,9},{2,6},{6,2},{1... | collective-permute-start | bytes 393224 | tf_op jit(solution)/shard_map/ppermute | solution.py:433
  63.9 3.9 %collective-permute-done.16.refs_0_ = bf16[256,256]{1,0:T(8,128)(2,1)S(1)} collective-permute-done((bf16[256,256]{1,0:T(8,128)(2,1)S(1)}, bf16[256,256]{1,0:T(8,128)(2,1)S(1)}, u32[]{:S(2)}, u32[]{:S(2)}) %collective-permute-start.16) | collective-permute-done | bytes 131104 | tf_op jit(solution)/shard_map/ppermute | solution.py:433
  67.8 5.8 %collective-permute-done.17.refs_1_ = bf16[256,256]{1,0:T(8,128)(2,1)S(1)} collective-permute-done((bf16[256,256]{1,0:T(8,128)(2,1)S(1)}, bf16[256,256]{1,0:T(8,128)(2,1)S(1)}, u32[]{:S(2)}, u32[]{:S(2)}) %collective-permute-start.17) | collective-permute-done | bytes 131104 | tf_op jit(solution)/shard_map/ppermute | solution.py:433
  73.7 0.2 pack_gradients.1
  73.9 0.6 collective-permute-start.26
  74.5 0.3 collective-permute-start.27
  74.8 1.4 %collective-permute-start.25 = (bf16[32,32,128]{2,1,0:T(8,128)(2,1)S(1)}, bf16[32,32,128]{2,1,0:T(8,128)(2,1)S(1)}, u32[]{:S(2)}, u32[]{:S(2)}) collective-permute-start(bf16[32,32,128]{2,1,0:T(8,128)(2,1)S(1)} %get-tuple-element.104.refs_1_), channel_id=1, source_target_pairs={{0,2},{2,0},{1,3},{3,1},{4,6},{6,4},{5,7},{7,5},{8,10},{10,8},{9,1... | collective-permute-start | bytes 786440 | tf_op jit(solution)/shard_map/ppermute | solution.py:433
  76.2 1.3 %mix_backward.1 = (bf16[256,256]{1,0:T(8,128)(2,1)S(1)}, bf16[256,256]{1,0:T(8,128)(2,1)S(1)}, bf16[256,256]{1,0:T(8,128)(2,1)S(1)}, bf16[256,256]{1,0:T(8,128)(2,1)S(1)}) custom-call(bf16[32,32,128]{2,1,0:T(8,128)(2,1)S(1)} %get-tuple-element.103.refs_0_.refs_2_, bf16[32,32,128]{2,1,0:T(8,128)(2,1)S(1)} %get-tuple-element.104.refs_1_, ...), custom_call_target="tpu_custom_call" | custom-call | bytes 9437184 | tf_op jit(solution)/shard_map/mix_backward/pallas_call | solution.py:74
  77.5 2.1 %collective-permute-start.22 = (bf16[256,256]{1,0:T(8,128)(2,1)S(1)}, bf16[256,256]{1,0:T(8,128)(2,1)S(1)}, u32[]{:S(2)}, u32[]{:S(2)}) collective-permute-start(bf16[256,256]{1,0:T(8,128)(2,1)S(1)} %get-tuple-element.108), channel_id=1, source_target_pairs={{0,12},{4,8},{8,4},{12,0},{1,13},{5,9},{9,5},{13,1},{2,14},{6,10},... | collective-permute-start | bytes 393224 | tf_op jit(solution)/shard_map/ppermute | solution.py:433
  79.6 2.3 %collective-permute-start.24 = (bf16[256,256]{1,0:T(8,128)(2,1)S(1)}, bf16[256,256]{1,0:T(8,128)(2,1)S(1)}, u32[]{:S(2)}, u32[]{:S(2)}) collective-permute-start(bf16[256,256]{1,0:T(8,128)(2,1)S(1)} %get-tuple-element.110), channel_id=1, source_target_pairs={{0,4},{4,0},{8,12},{12,8},{1,5},{5,1},{9,13},{13,9},{2,6},{6,2},{1... | collective-permute-start | bytes 393224 | tf_op jit(solution)/shard_map/ppermute | solution.py:433
  81.9 0.9 collective-permute-done.27.refs_5_
  82.8 5.9 %collective-permute-done.25.refs_3_ = bf16[32,32,128]{2,1,0:T(8,128)(2,1)S(1)} collective-permute-done((bf16[32,32,128]{2,1,0:T(8,128)(2,1)S(1)}, bf16[32,32,128]{2,1,0:T(8,128)(2,1)S(1)}, u32[]{:S(2)}, u32[]{:S(2)}) %collective-permute-start.25) | collective-permute-done | bytes 262176 | tf_op jit(solution)/shard_map/ppermute | solution.py:433
  88.7 3.7 %weight_gradient.1 = f32[2,32,128,256]{3,2,1,0:T(8,128)} custom-call(bf16[5120,256]{1,0:T(8,128)(2,1)S(1)} %get-tuple-element.105.refs_3_.refs_0_, bf16[5120,256]{1,0:T(8,128)(2,1)S(1)} %collective-permute-done.19.refs_4_.refs_1_, bf16[32,32,128]{2,1,0:T(8,128)(2,1)S(1)} %get-tuple-element.103.refs_0_.refs_2_, ...), custom_call_target="tpu_custom_call" | custom-call | bytes 2097152 | tf_op jit(solution)/shard_map/weight_gradient/pallas_call | solution.py:74
  92.4 2.4 %final_dft.1 = bf16[4,1440,256]{2,1,0:T(8,128)(2,1)} custom-call(bf16[4,1440,256]{2,1,0:T(8,128)(2,1)S(1)} %bitcast.10, bf16[1440,256]{1,0:T(8,128)(2,1)S(1)} %copy-done.4, bf16[256,256]{1,0:T(8,128)(2,1)S(1)} %collective-permute-done.22.refs_0_, bf16[256,256]{1,0:T(8,128)(2,1)S(1)} %collective-permute-done.23.refs_1_, ...), custom_call_target="tpu_custom_call" | custom-call | bytes 83886080 | tf_op jit(solution)/shard_map/final_dft/pallas_call | solution.py:74
  (35 shorter events, 0.2 us)
Async XLA Ops:
  6.0 19.4 %collective-permute-start.8 = (bf16[2,4,128,256]{3,2,1,0:T(8,128)(2,1)}, bf16[2,4,128,256]{3,2,1,0:T(8,128)(2,1)S(1)}, u32[]{:S(2)}, u32[]{:S(2)}) collective-permute-start(bf16[2,4,128,256]{3,2,1,0:T(8,128)(2,1)} %get-tuple-element.67), channel_id=1, source_target_pairs={{0,2},{2,0},{1,3},{3,1},{4,6},{6,4},{5,7},{7,5},{8,10},{10,8},{9,1... | collective-permute-start | bytes 1572872 | tf_op jit(solution)/shard_map/ppermute | solution.py:433
  9.0 8.0 %collective-permute-start = (bf16[128,256]{1,0:T(8,128)(2,1)}, bf16[128,256]{1,0:T(8,128)(2,1)S(1)}, u32[]{:S(2)}, u32[]{:S(2)}) collective-permute-start(bf16[128,256]{1,0:T(8,128)(2,1)} %get-tuple-element.57), channel_id=1, source_target_pairs={{0,12},{4,8},{8,4},{12,0},{1,13},{5,9},{9,5},{13,1},{2,14},{6,10},... | collective-permute-start | bytes 196616 | tf_op jit(solution)/shard_map/ppermute | solution.py:433
  12.6 8.2 %collective-permute-start.1 = (bf16[128,256]{1,0:T(8,128)(2,1)}, bf16[128,256]{1,0:T(8,128)(2,1)S(1)}, u32[]{:S(2)}, u32[]{:S(2)}) collective-permute-start(bf16[128,256]{1,0:T(8,128)(2,1)} %get-tuple-element.58), channel_id=1, source_target_pairs={{0,8},{4,12},{8,0},{12,4},{1,9},{5,13},{9,1},{13,5},{2,10},{6,14},... | collective-permute-start | bytes 196616 | tf_op jit(solution)/shard_map/ppermute | solution.py:433
  12.6 8.2 %collective-permute-start.2 = (bf16[128,256]{1,0:T(8,128)(2,1)}, bf16[128,256]{1,0:T(8,128)(2,1)S(1)}, u32[]{:S(2)}, u32[]{:S(2)}) collective-permute-start(bf16[128,256]{1,0:T(8,128)(2,1)} %get-tuple-element.59), channel_id=1, source_target_pairs={{0,4},{4,0},{8,12},{12,8},{1,5},{5,1},{9,13},{13,9},{2,6},{6,2},{1... | collective-permute-start | bytes 196616 | tf_op jit(solution)/shard_map/ppermute | solution.py:433
  13.4 9.0 %collective-permute-start.5 = (bf16[128,256]{1,0:T(8,128)(2,1)}, bf16[128,256]{1,0:T(8,128)(2,1)S(1)}, u32[]{:S(2)}, u32[]{:S(2)}) collective-permute-start(bf16[128,256]{1,0:T(8,128)(2,1)} %get-tuple-element.63), channel_id=1, source_target_pairs={{0,12},{4,8},{8,4},{12,0},{1,13},{5,9},{9,5},{13,1},{2,14},{6,10},... | collective-permute-start | bytes 196616 | tf_op jit(solution)/shard_map/ppermute | solution.py:433
  17.0 6.8 %collective-permute-start.6 = (bf16[128,256]{1,0:T(8,128)(2,1)}, bf16[128,256]{1,0:T(8,128)(2,1)S(1)}, u32[]{:S(2)}, u32[]{:S(2)}) collective-permute-start(bf16[128,256]{1,0:T(8,128)(2,1)} %get-tuple-element.64), channel_id=1, source_target_pairs={{0,8},{4,12},{8,0},{12,4},{1,9},{5,13},{9,1},{13,5},{2,10},{6,14},... | collective-permute-start | bytes 196616 | tf_op jit(solution)/shard_map/ppermute | solution.py:433
  20.9 4.5 %collective-permute-start.7 = (bf16[128,256]{1,0:T(8,128)(2,1)}, bf16[128,256]{1,0:T(8,128)(2,1)S(1)}, u32[]{:S(2)}, u32[]{:S(2)}) collective-permute-start(bf16[128,256]{1,0:T(8,128)(2,1)} %get-tuple-element.65), channel_id=1, source_target_pairs={{0,4},{4,0},{8,12},{12,8},{1,5},{5,1},{9,13},{13,9},{2,6},{6,2},{1... | collective-permute-start | bytes 196616 | tf_op jit(solution)/shard_map/ppermute | solution.py:433
  20.9 0.8 copy-start.7
  21.7 7.7 %collective-permute-start.3 = (bf16[16,32,256]{2,1,0:T(8,128)(2,1)S(1)}, bf16[16,32,256]{2,1,0:T(8,128)(2,1)S(1)}, u32[]{:S(2)}, u32[]{:S(2)}) collective-permute-start(bf16[16,32,256]{2,1,0:T(8,128)(2,1)S(1)} %pack_0.1.refs_0_), channel_id=1, source_target_pairs={{0,2},{2,0},{1,3},{3,1},{4,6},{6,4},{5,7},{7,5},{8,10},{10,8},{9,1... | collective-permute-start | bytes 786440 | tf_op jit(solution)/shard_map/ppermute | solution.py:433
  25.4 0.8 copy-start.6
  26.2 9.0 %collective-permute-start.9 = (bf16[16,32,256]{2,1,0:T(8,128)(2,1)S(1)}, bf16[16,32,256]{2,1,0:T(8,128)(2,1)S(1)}, u32[]{:S(2)}, u32[]{:S(2)}) collective-permute-start(bf16[16,32,256]{2,1,0:T(8,128)(2,1)S(1)} %pack_1.1.refs_0_), channel_id=1, source_target_pairs={{0,2},{2,0},{1,3},{3,1},{4,6},{6,4},{5,7},{7,5},{8,10},{10,8},{9,1... | collective-permute-start | bytes 786440 | tf_op jit(solution)/shard_map/ppermute | solution.py:433
  29.5 2.2 %copy-start = (bf16[2,32,128,256]{3,2,1,0:T(8,128)(2,1)S(1)}, bf16[2,32,128,256]{3,2,1,0:T(8,128)(2,1)}, u32[]{:S(2)}) copy-start(bf16[2,32,128,256]{3,2,1,0:T(8,128)(2,1)} %refs_2_.5) | copy-start | bytes 12582916
  32.6 21.4 %copy-start.2 = (bf16[1,4,1440,256]{3,2,1,0:T(8,128)(2,1)S(1)}, bf16[1,4,1440,256]{3,2,1,0:T(8,128)(2,1)}, u32[]{:S(2)}) copy-start(bf16[1,4,1440,256]{3,2,1,0:T(8,128)(2,1)} %param.8) | copy-start | bytes 8847364
  32.6 21.4 %copy-start.3 = (bf16[256,1440]{1,0:T(8,128)(2,1)S(1)}, bf16[256,1440]{1,0:T(8,128)(2,1)}, u32[]{:S(2)}) copy-start(bf16[256,1440]{1,0:T(8,128)(2,1)} %constant.9.clone.inv_ref) | copy-start | bytes 2211844
  32.6 21.4 %copy-start.5 = (bf16[1440,256]{1,0:T(8,128)(2,1)S(1)}, bf16[1440,256]{1,0:T(8,128)(2,1)}, u32[]{:S(2)}) copy-start(bf16[1440,256]{1,0:T(8,128)(2,1)} %constant.11.clone.back_ref) | copy-start | bytes 2211844
  32.6 5.9 %collective-permute-start.4 = (bf16[16,32,128]{2,1,0:T(8,128)(2,1)S(1)}, bf16[16,32,128]{2,1,0:T(8,128)(2,1)S(1)}, u32[]{:S(2)}, u32[]{:S(2)}) collective-permute-start(bf16[16,32,128]{2,1,0:T(8,128)(2,1)S(1)} %get-tuple-element.62), channel_id=1, source_target_pairs={{0,2},{2,0},{1,3},{3,1},{4,6},{6,4},{5,7},{7,5},{8,10},{10,8},{9,1... | collective-permute-start | bytes 393224 | tf_op jit(solution)/shard_map/ppermute | solution.py:433
  36.1 5.3 %collective-permute-start.10 = (bf16[16,32,128]{2,1,0:T(8,128)(2,1)S(1)}, bf16[16,32,128]{2,1,0:T(8,128)(2,1)S(1)}, u32[]{:S(2)}, u32[]{:S(2)}) collective-permute-start(bf16[16,32,128]{2,1,0:T(8,128)(2,1)S(1)} %get-tuple-element.73), channel_id=1, source_target_pairs={{0,2},{2,0},{1,3},{3,1},{4,6},{6,4},{5,7},{7,5},{8,10},{10,8},{9,1... | collective-permute-start | bytes 393224 | tf_op jit(solution)/shard_map/ppermute | solution.py:433
  38.5 15.4 %collective-permute-start.14 = (bf16[2,4,128,256]{3,2,1,0:T(8,128)(2,1)S(1)}, bf16[2,4,128,256]{3,2,1,0:T(8,128)(2,1)S(1)}, u32[]{:S(2)}, u32[]{:S(2)}) collective-permute-start(bf16[2,4,128,256]{3,2,1,0:T(8,128)(2,1)S(1)} %collective-permute-done.8), channel_id=1, source_target_pairs={{0,16},{16,0},{1,17},{17,1},{2,18},{18,2},{3,19},{19,3},{4,20},{20... | collective-permute-start | bytes 1572872 | tf_op jit(solution)/shard_map/ppermute | solution.py:433
  41.4 12.6 %collective-permute-start.15 = (bf16[2,4,128,256]{3,2,1,0:T(8,128)(2,1)S(1)}, bf16[2,4,128,256]{3,2,1,0:T(8,128)(2,1)S(1)}, u32[]{:S(2)}, u32[]{:S(2)}) collective-permute-start(bf16[2,4,128,256]{3,2,1,0:T(8,128)(2,1)S(1)} %get-tuple-element.81), channel_id=1, source_target_pairs={{0,2},{2,0},{1,3},{3,1},{4,6},{6,4},{5,7},{7,5},{8,10},{10,8},{9,1... | collective-permute-start | bytes 1572872 | tf_op jit(solution)/shard_map/ppermute | solution.py:433
  42.1 7.6 %collective-permute-start.11 = (bf16[256,256]{1,0:T(8,128)(2,1)S(1)}, bf16[256,256]{1,0:T(8,128)(2,1)S(1)}, u32[]{:S(2)}, u32[]{:S(2)}) collective-permute-start(bf16[256,256]{1,0:T(8,128)(2,1)S(1)} %get-tuple-element.74), channel_id=1, source_target_pairs={{0,12},{4,8},{8,4},{12,0},{1,13},{5,9},{9,5},{13,1},{2,14},{6,10},... | collective-permute-start | bytes 393224 | tf_op jit(solution)/shard_map/ppermute | solution.py:433
  46.7 7.3 %collective-permute-start.12 = (bf16[256,256]{1,0:T(8,128)(2,1)S(1)}, bf16[256,256]{1,0:T(8,128)(2,1)S(1)}, u32[]{:S(2)}, u32[]{:S(2)}) collective-permute-start(bf16[256,256]{1,0:T(8,128)(2,1)S(1)} %get-tuple-element.75), channel_id=1, source_target_pairs={{0,8},{4,12},{8,0},{12,4},{1,9},{5,13},{9,1},{13,5},{2,10},{6,14},... | collective-permute-start | bytes 393224 | tf_op jit(solution)/shard_map/ppermute | solution.py:433
  47.4 6.6 %collective-permute-start.13 = (bf16[256,256]{1,0:T(8,128)(2,1)S(1)}, bf16[256,256]{1,0:T(8,128)(2,1)S(1)}, u32[]{:S(2)}, u32[]{:S(2)}) collective-permute-start(bf16[256,256]{1,0:T(8,128)(2,1)S(1)} %get-tuple-element.76), channel_id=1, source_target_pairs={{0,4},{4,0},{8,12},{12,8},{1,5},{5,1},{9,13},{13,9},{2,6},{6,2},{1... | collective-permute-start | bytes 393224 | tf_op jit(solution)/shard_map/ppermute | solution.py:433
  54.0 22.2 %copy-start.1 = (bf16[2,32,128,256]{3,2,1,0:T(8,128)(2,1)S(1)}, bf16[2,32,128,256]{3,2,1,0:T(8,128)(2,1)}, u32[]{:S(2)}) copy-start(bf16[2,32,128,256]{3,2,1,0:T(8,128)(2,1)} %refs_2_.5) | copy-start | bytes 12582916
  58.1 15.5 %collective-permute-start.19 = (bf16[5120,256]{1,0:T(8,128)(2,1)S(1)}, bf16[5120,256]{1,0:T(8,128)(2,1)S(1)}, u32[]{:S(2)}, u32[]{:S(2)}) collective-permute-start(bf16[5120,256]{1,0:T(8,128)(2,1)S(1)} %get-tuple-element.105.refs_3_.refs_0_), channel_id=1, source_target_pairs={{0,1},{1,0},{2,3},{3,2},{4,5},{5,4},{6,7},{7,6},{8,9},{9,8},{10,11... | collective-permute-start | bytes 7864328 | tf_op jit(solution)/shard_map/ppermute | solution.py:433
  58.2 15.4 %collective-permute-start.20 = (bf16[2,4,128,256]{3,2,1,0:T(8,128)(2,1)S(1)}, bf16[2,4,128,256]{3,2,1,0:T(8,128)(2,1)S(1)}, u32[]{:S(2)}, u32[]{:S(2)}) collective-permute-start(bf16[2,4,128,256]{3,2,1,0:T(8,128)(2,1)S(1)} %get-tuple-element.98), channel_id=1, source_target_pairs={{0,2},{2,0},{1,3},{3,1},{4,6},{6,4},{5,7},{7,5},{8,10},{10,8},{9,1... | collective-permute-start | bytes 1572872 | tf_op jit(solution)/shard_map/ppermute | solution.py:433
  59.5 8.3 %collective-permute-start.16 = (bf16[256,256]{1,0:T(8,128)(2,1)S(1)}, bf16[256,256]{1,0:T(8,128)(2,1)S(1)}, u32[]{:S(2)}, u32[]{:S(2)}) collective-permute-start(bf16[256,256]{1,0:T(8,128)(2,1)S(1)} %get-tuple-element.91), channel_id=1, source_target_pairs={{0,12},{4,8},{8,4},{12,0},{1,13},{5,9},{9,5},{13,1},{2,14},{6,10},... | collective-permute-start | bytes 393224 | tf_op jit(solution)/shard_map/ppermute | solution.py:433
  61.7 11.9 %collective-permute-start.17 = (bf16[256,256]{1,0:T(8,128)(2,1)S(1)}, bf16[256,256]{1,0:T(8,128)(2,1)S(1)}, u32[]{:S(2)}, u32[]{:S(2)}) collective-permute-start(bf16[256,256]{1,0:T(8,128)(2,1)S(1)} %get-tuple-element.92), channel_id=1, source_target_pairs={{0,8},{4,12},{8,0},{12,4},{1,9},{5,13},{9,1},{13,5},{2,10},{6,14},... | collective-permute-start | bytes 393224 | tf_op jit(solution)/shard_map/ppermute | solution.py:433
  61.7 11.9 %collective-permute-start.18 = (bf16[256,256]{1,0:T(8,128)(2,1)S(1)}, bf16[256,256]{1,0:T(8,128)(2,1)S(1)}, u32[]{:S(2)}, u32[]{:S(2)}) collective-permute-start(bf16[256,256]{1,0:T(8,128)(2,1)S(1)} %get-tuple-element.93), channel_id=1, source_target_pairs={{0,4},{4,0},{8,12},{12,8},{1,5},{5,1},{9,13},{13,9},{2,6},{6,2},{1... | collective-permute-start | bytes 393224 | tf_op jit(solution)/shard_map/ppermute | solution.py:433
  73.6 2.5 %collective-permute-start.21 = (bf16[1024,256]{1,0:T(8,128)(2,1)S(1)}, bf16[1024,256]{1,0:T(8,128)(2,1)S(1)}, u32[]{:S(2)}, u32[]{:S(2)}) collective-permute-start(bf16[1024,256]{1,0:T(8,128)(2,1)S(1)} %bitcast.14), channel_id=1, source_target_pairs={{0,1},{1,0},{2,3},{3,2},{4,5},{5,4},{6,7},{7,6},{8,9},{9,8},{10,11... | collective-permute-start | bytes 1572872 | tf_op jit(solution)/shard_map/ppermute | solution.py:433
  73.9 5.7 %collective-permute-start.26 = (bf16[32,32,128]{2,1,0:T(8,128)(2,1)S(1)}, bf16[32,32,128]{2,1,0:T(8,128)(2,1)S(1)}, u32[]{:S(2)}, u32[]{:S(2)}) collective-permute-start(bf16[32,32,128]{2,1,0:T(8,128)(2,1)S(1)} %get-tuple-element.103.refs_0_.refs_2_), channel_id=1, source_target_pairs={{0,1},{1,0},{2,3},{3,2},{4,5},{5,4},{6,7},{7,6},{8,9},{9,8},{10,11... | collective-permute-start | bytes 786440 | tf_op jit(solution)/shard_map/ppermute | solution.py:499
  74.5 8.3 %collective-permute-start.27 = (bf16[32,32,128]{2,1,0:T(8,128)(2,1)S(1)}, bf16[32,32,128]{2,1,0:T(8,128)(2,1)S(1)}, u32[]{:S(2)}, u32[]{:S(2)}) collective-permute-start(bf16[32,32,128]{2,1,0:T(8,128)(2,1)S(1)} %get-tuple-element.104.refs_1_), channel_id=1, source_target_pairs={{0,3},{1,2},{2,1},{3,0},{4,7},{5,6},{6,5},{7,4},{8,11},{9,10},{10,... | collective-permute-start | bytes 786440 | tf_op jit(solution)/shard_map/ppermute | solution.py:499
  74.8 13.9 %collective-permute-start.25 = (bf16[32,32,128]{2,1,0:T(8,128)(2,1)S(1)}, bf16[32,32,128]{2,1,0:T(8,128)(2,1)S(1)}, u32[]{:S(2)}, u32[]{:S(2)}) collective-permute-start(bf16[32,32,128]{2,1,0:T(8,128)(2,1)S(1)} %get-tuple-element.104.refs_1_), channel_id=1, source_target_pairs={{0,2},{2,0},{1,3},{3,1},{4,6},{6,4},{5,7},{7,5},{8,10},{10,8},{9,1... | collective-permute-start | bytes 786440 | tf_op jit(solution)/shard_map/ppermute | solution.py:433
  77.5 14.9 %collective-permute-start.22 = (bf16[256,256]{1,0:T(8,128)(2,1)S(1)}, bf16[256,256]{1,0:T(8,128)(2,1)S(1)}, u32[]{:S(2)}, u32[]{:S(2)}) collective-permute-start(bf16[256,256]{1,0:T(8,128)(2,1)S(1)} %get-tuple-element.108), channel_id=1, source_target_pairs={{0,12},{4,8},{8,4},{12,0},{1,13},{5,9},{9,5},{13,1},{2,14},{6,10},... | collective-permute-start | bytes 393224 | tf_op jit(solution)/shard_map/ppermute | solution.py:433
  79.6 12.8 %collective-permute-start.23 = (bf16[256,256]{1,0:T(8,128)(2,1)S(1)}, bf16[256,256]{1,0:T(8,128)(2,1)S(1)}, u32[]{:S(2)}, u32[]{:S(2)}) collective-permute-start(bf16[256,256]{1,0:T(8,128)(2,1)S(1)} %get-tuple-element.109), channel_id=1, source_target_pairs={{0,8},{4,12},{8,0},{12,4},{1,9},{5,13},{9,1},{13,5},{2,10},{6,14},... | collective-permute-start | bytes 393224 | tf_op jit(solution)/shard_map/ppermute | solution.py:433
  79.6 12.8 %copy-start.4 = (bf16[1440,256]{1,0:T(8,128)(2,1)S(1)}, bf16[1440,256]{1,0:T(8,128)(2,1)}, u32[]{:S(2)}) copy-start(bf16[1440,256]{1,0:T(8,128)(2,1)} %constant.10.clone.table_ref) | copy-start | bytes 2211844
  79.6 12.8 %collective-permute-start.24 = (bf16[256,256]{1,0:T(8,128)(2,1)S(1)}, bf16[256,256]{1,0:T(8,128)(2,1)S(1)}, u32[]{:S(2)}, u32[]{:S(2)}) collective-permute-start(bf16[256,256]{1,0:T(8,128)(2,1)S(1)} %get-tuple-element.110), channel_id=1, source_target_pairs={{0,4},{4,0},{8,12},{12,8},{1,5},{5,1},{9,13},{13,9},{2,6},{6,2},{1... | collective-permute-start | bytes 393224 | tf_op jit(solution)/shard_map/ppermute | solution.py:433

commit v5 on v4

--- a/solution.py
+++ b/solution.py
@@ -134,7 +134,7 @@
     return like((2, plan.unit, plan.o_w, plan.width))
 
 
-def forward_dft(plan, table, field, weights):
+def forward_dft(plan, table, field, weights, ahead=2):
     n = plan.n_lat * plan.halves
     shape = (plan.mu * plan.rk, plan.width)
 
@@ -143,7 +143,7 @@
         table_copy = pltpu.make_async_copy(table_ref, table_buf, table_sem)
         table_copy.start()
         copies = row_copies(field_ref, rows, sems)
-        for copy in copies:
+        for copy in copies[:ahead]:
             copy.start()
         first = plan.unit_at(plan.halves - 1, plan.unit_of(lax.axis_index("parts")))
         share = pltpu.make_async_copy(w_ref.at[:, pl.ds(first, plan.unit)], share_ref, w_sem)
@@ -151,6 +151,8 @@
         table_copy.wait()
         for row in range(plan.rows):
             copies[row].wait()
+            if row + ahead < plan.rows:
+                copies[row + ahead].start()
             line[...] = jnp.dot(table_buf[...], rows[row], preferred_element_type=F32)
             spread_rows(plan, lax.axis_index("lat"), row, line, held)
         emit_blocks(plan, held, outs)
@@ -488,9 +490,9 @@
     loose = [unit for pair, unit in zip(last, first) for unit in (*pair, unit)]
     blocks, tied = middle(plan, inverse_t, inverse, cotangent, blocks, loose + tall)
 
+    late = fetch(after(units[1], *blocks))
+    blocks, late = together(to_lat(blocks), late)
     tied = along("rep", [tied], *blocks)[0]
-    late = fetch(after(units[1], *blocks))
-    blocks, (tied, late) = together(to_lat(blocks), (tied, late))
     late = along("rep", [unit.reshape(-1, plan.width) for unit in late])
     grads = pack_gradients(plan, blocks)
     blocks = mix_backward(plan, grads, weights, tied, late)

time: 95.1 us -> 92.2 us (0.970)
  waiting for transfers between devices: 35.5 us -> 32.7 us
    ppermute x26, waiting for transfers between devices: 34.6 us -> 32.7 us  [hop(): return lax.ppermute(value, axis, [(i, i ^ s) for i in range(size)])]
  transfers between devices with their start and end apart: 28 -> 28, of which waited for: 13 -> 14; matrix products, arithmetic and copies ran while one was open for 0% -> 0% of each run, Pallas kernels for 7% -> 8%
where the time goes in v5:
time: 92.2 us; the launch traced here: 91.9 us
  starting transfers between devices  35.9 us (39%)
  waiting for transfers between devices  32.7 us (35%)
  Pallas kernels  18.5 us (20%)
  local copies, waits for them, and re-layouts  3.9 us (4%)
    ppermute x26, starting transfers between devices, hop(): return lax.ppermute(value, axis, [(i, i ^ s) for i in range(size)])  34.8 us
    ppermute x26, waiting for transfers between devices, hop(): return lax.ppermute(value, axis, [(i, i ^ s) for i in range(size)])  32.7 us
    pallas_call x11, Pallas kernels, call(): pl.pallas_call(body, in_specs=ins or [VMEM] * len(operands), out_specs=ou...  18.5 us
    unnamed x16, local copies, waits for them, and re-layouts  3.9 us
  transfers between devices with their start and end apart: 28, of which 14 were waited for; matrix products, arithmetic and copies ran while one was open for 0% of the time, Pallas kernels for 8%

profile of v5, /device:TPU:0, one launch (start us, length us, event | category | flops | bytes accessed | tf_op | source)
XLA Modules:
  0.0 91.9 jit_solution(17179549356488998033)
XLA Ops:
  0.6 4.9 %forward_dft.1 = (bf16[128,256]{1,0:T(8,128)(2,1)}, bf16[128,256]{1,0:T(8,128)(2,1)}, bf16[128,256]{1,0:T(8,128)(2,1)}, bf16[128,256]{1,0:T(8,128)(2,1)}, bf16[1...) custom-call(bf16[4,1440,256]{2,1,0:T(8,128)(2,1)} %bitcast.19, ...), custom_call_target="tpu_custom_call" | custom-call | bytes 6291456 | tf_op jit(solution)/shard_map/forward_dft/pallas_call | solution.py:74
  5.6 3.0 %collective-permute-start.8 = (bf16[2,4,128,256]{3,2,1,0:T(8,128)(2,1)}, bf16[2,4,128,256]{3,2,1,0:T(8,128)(2,1)S(1)}, u32[]{:S(2)}, u32[]{:S(2)}) collective-permute-start(bf16[2,4,128,256]{3,2,1,0:T(8,128)(2,1)} %get-tuple-element.65), channel_id=1, source_target_pairs={{0,2},{2,0},{1,3},{3,1},{4,6},{6,4},{5,7},{7,5},{8,10},{10,8},{9,1... | collective-permute-start | bytes 1572872 | tf_op jit(solution)/shard_map/ppermute | solution.py:435
  8.6 3.6 %collective-permute-start = (bf16[128,256]{1,0:T(8,128)(2,1)}, bf16[128,256]{1,0:T(8,128)(2,1)S(1)}, u32[]{:S(2)}, u32[]{:S(2)}) collective-permute-start(bf16[128,256]{1,0:T(8,128)(2,1)} %get-tuple-element.55), channel_id=1, source_target_pairs={{0,12},{4,8},{8,4},{12,0},{1,13},{5,9},{9,5},{13,1},{2,14},{6,10},... | collective-permute-start | bytes 196616 | tf_op jit(solution)/shard_map/ppermute | solution.py:435
  12.2 0.8 collective-permute-start.2
  12.9 3.6 %collective-permute-start.5 = (bf16[128,256]{1,0:T(8,128)(2,1)}, bf16[128,256]{1,0:T(8,128)(2,1)S(1)}, u32[]{:S(2)}, u32[]{:S(2)}) collective-permute-start(bf16[128,256]{1,0:T(8,128)(2,1)} %get-tuple-element.61), channel_id=1, source_target_pairs={{0,12},{4,8},{8,4},{12,0},{1,13},{5,9},{9,5},{13,1},{2,14},{6,10},... | collective-permute-start | bytes 196616 | tf_op jit(solution)/shard_map/ppermute | solution.py:435
  16.6 2.1 %collective-permute-start.6 = (bf16[128,256]{1,0:T(8,128)(2,1)}, bf16[128,256]{1,0:T(8,128)(2,1)S(1)}, u32[]{:S(2)}, u32[]{:S(2)}) collective-permute-start(bf16[128,256]{1,0:T(8,128)(2,1)} %get-tuple-element.62), channel_id=1, source_target_pairs={{0,8},{4,12},{8,0},{12,4},{1,9},{5,13},{9,1},{13,5},{2,10},{6,14},... | collective-permute-start | bytes 196616 | tf_op jit(solution)/shard_map/ppermute | solution.py:435
  18.7 1.8 %collective-permute-done.1.refs_1_ = bf16[128,256]{1,0:T(8,128)(2,1)S(1)} collective-permute-done((bf16[128,256]{1,0:T(8,128)(2,1)}, bf16[128,256]{1,0:T(8,128)(2,1)S(1)}, u32[]{:S(2)}, u32[]{:S(2)}) %collective-permute-start.1) | collective-permute-done | bytes 65568 | tf_op jit(solution)/shard_map/ppermute | solution.py:435
  20.4 0.8 copy-done.7
  21.3 0.6 collective-permute-start.3
  21.9 1.4 %collective-permute-done.6.refs_1_ = bf16[128,256]{1,0:T(8,128)(2,1)S(1)} collective-permute-done((bf16[128,256]{1,0:T(8,128)(2,1)}, bf16[128,256]{1,0:T(8,128)(2,1)S(1)}, u32[]{:S(2)}, u32[]{:S(2)}) %collective-permute-start.6) | collective-permute-done | bytes 65568 | tf_op jit(solution)/shard_map/ppermute | solution.py:435
  23.3 1.6 %collective-permute-done.7.refs_2_ = bf16[128,256]{1,0:T(8,128)(2,1)S(1)} collective-permute-done((bf16[128,256]{1,0:T(8,128)(2,1)}, bf16[128,256]{1,0:T(8,128)(2,1)S(1)}, u32[]{:S(2)}, u32[]{:S(2)}) %collective-permute-start.7) | collective-permute-done | bytes 65568 | tf_op jit(solution)/shard_map/ppermute | solution.py:435
  24.9 0.8 copy-done.6
  25.8 0.6 collective-permute-start.9
  26.4 2.7 %collective-permute-done.3.refs_1_ = bf16[16,32,256]{2,1,0:T(8,128)(2,1)S(1)} collective-permute-done((bf16[16,32,256]{2,1,0:T(8,128)(2,1)S(1)}, bf16[16,32,256]{2,1,0:T(8,128)(2,1)S(1)}, u32[]{:S(2)}, u32[]{:S(2)}) %collective-permute-start.3) | collective-permute-done | bytes 262176 | tf_op jit(solution)/shard_map/ppermute | solution.py:435
  29.1 2.2 %copy-done = bf16[2,32,128,256]{3,2,1,0:T(8,128)(2,1)S(1)} copy-done((bf16[2,32,128,256]{3,2,1,0:T(8,128)(2,1)S(1)}, bf16[2,32,128,256]{3,2,1,0:T(8,128)(2,1)}, u32[]{:S(2)}) %copy-start) | copy-done | bytes 4194328
  31.2 0.9 mix_forward_0.1
  32.2 0.6 collective-permute-start.4
  32.8 2.0 %collective-permute-done.9.refs_1_ = bf16[16,32,256]{2,1,0:T(8,128)(2,1)S(1)} collective-permute-done((bf16[16,32,256]{2,1,0:T(8,128)(2,1)S(1)}, bf16[16,32,256]{2,1,0:T(8,128)(2,1)S(1)}, u32[]{:S(2)}, u32[]{:S(2)}) %collective-permute-start.9) | collective-permute-done | bytes 262176 | tf_op jit(solution)/shard_map/ppermute | solution.py:435
  34.8 0.9 mix_forward_1.1
  35.6 0.6 collective-permute-start.10
  36.2 1.8 %collective-permute-done.4.refs_1_ = bf16[16,32,128]{2,1,0:T(8,128)(2,1)S(1)} collective-permute-done((bf16[16,32,128]{2,1,0:T(8,128)(2,1)S(1)}, bf16[16,32,128]{2,1,0:T(8,128)(2,1)S(1)}, u32[]{:S(2)}, u32[]{:S(2)}) %collective-permute-start.4) | collective-permute-done | bytes 131104 | tf_op jit(solution)/shard_map/ppermute | solution.py:435
  38.1 1.5 %collective-permute-start.14 = (bf16[2,4,128,256]{3,2,1,0:T(8,128)(2,1)S(1)}, bf16[2,4,128,256]{3,2,1,0:T(8,128)(2,1)S(1)}, u32[]{:S(2)}, u32[]{:S(2)}) collective-permute-start(bf16[2,4,128,256]{3,2,1,0:T(8,128)(2,1)S(1)} %collective-permute-done.8), channel_id=1, source_target_pairs={{0,16},{16,0},{1,17},{17,1},{2,18},{18,2},{3,19},{19,3},{4,20},{20... | collective-permute-start | bytes 1572872 | tf_op jit(solution)/shard_map/ppermute | solution.py:435
  39.6 1.4 %collective-permute-done.10.refs_3_ = bf16[16,32,128]{2,1,0:T(8,128)(2,1)S(1)} collective-permute-done((bf16[16,32,128]{2,1,0:T(8,128)(2,1)S(1)}, bf16[16,32,128]{2,1,0:T(8,128)(2,1)S(1)}, u32[]{:S(2)}, u32[]{:S(2)}) %collective-permute-start.10) | collective-permute-done | bytes 131104 | tf_op jit(solution)/shard_map/ppermute | solution.py:435
  41.0 0.5 collective-permute-start.15
  41.6 4.6 %collective-permute-start.11 = (bf16[256,256]{1,0:T(8,128)(2,1)S(1)}, bf16[256,256]{1,0:T(8,128)(2,1)S(1)}, u32[]{:S(2)}, u32[]{:S(2)}) collective-permute-start(bf16[256,256]{1,0:T(8,128)(2,1)S(1)} %get-tuple-element.72), channel_id=1, source_target_pairs={{0,12},{4,8},{8,4},{12,0},{1,13},{5,9},{9,5},{13,1},{2,14},{6,10},... | collective-permute-start | bytes 393224 | tf_op jit(solution)/shard_map/ppermute | solution.py:435
  46.3 0.7 collective-permute-start.12
  46.9 0.3 collective-permute-start.13
  47.2 2.1 %collective-permute-done.11.refs_0_ = bf16[256,256]{1,0:T(8,128)(2,1)S(1)} collective-permute-done((bf16[256,256]{1,0:T(8,128)(2,1)S(1)}, bf16[256,256]{1,0:T(8,128)(2,1)S(1)}, u32[]{:S(2)}, u32[]{:S(2)}) %collective-permute-start.11) | collective-permute-done | bytes 131104 | tf_op jit(solution)/shard_map/ppermute | solution.py:435
  49.3 4.2 %collective-permute-done.12.refs_1_ = bf16[256,256]{1,0:T(8,128)(2,1)S(1)} collective-permute-done((bf16[256,256]{1,0:T(8,128)(2,1)S(1)}, bf16[256,256]{1,0:T(8,128)(2,1)S(1)}, u32[]{:S(2)}, u32[]{:S(2)}) %collective-permute-start.12) | collective-permute-done | bytes 131104 | tf_op jit(solution)/shard_map/ppermute | solution.py:435
  53.6 4.1 %middle.1 = (bf16[256,256]{1,0:T(8,128)(2,1)S(1)}, bf16[256,256]{1,0:T(8,128)(2,1)S(1)}, bf16[256,256]{1,0:T(8,128)(2,1)S(1)}, bf16[256,256]{1,0:T(8,128)(2,1)S(1)}, bf16[5120,256]{1,0:T(8,128)(2,1)S(1)}) custom-call(bf16[4,1440,256]{2,1,0:T(8,128)(2,1)S(1)} %bitcast.9, bf16[1440,256]{1,0:T(8,128)(2,1)S(1)} %copy-done.5, bf16[256,1440]{1,0:T(8,128)(2,1)S(1)} %copy-done.3, ...), custom_call_target="tpu_custom_call" | custom-call | bytes 12582912 | tf_op jit(solution)/shard_map/middle/pallas_call | solution.py:74
  57.7 1.3 %collective-permute-start.19 = (bf16[2,4,128,256]{3,2,1,0:T(8,128)(2,1)S(1)}, bf16[2,4,128,256]{3,2,1,0:T(8,128)(2,1)S(1)}, u32[]{:S(2)}, u32[]{:S(2)}) collective-permute-start(bf16[2,4,128,256]{3,2,1,0:T(8,128)(2,1)S(1)} %get-tuple-element.94), channel_id=1, source_target_pairs={{0,2},{2,0},{1,3},{3,1},{4,6},{6,4},{5,7},{7,5},{8,10},{10,8},{9,1... | collective-permute-start | bytes 1572872 | tf_op jit(solution)/shard_map/ppermute | solution.py:435
  59.0 2.2 %collective-permute-start.16 = (bf16[256,256]{1,0:T(8,128)(2,1)S(1)}, bf16[256,256]{1,0:T(8,128)(2,1)S(1)}, u32[]{:S(2)}, u32[]{:S(2)}) collective-permute-start(bf16[256,256]{1,0:T(8,128)(2,1)S(1)} %get-tuple-element.89), channel_id=1, source_target_pairs={{0,12},{4,8},{8,4},{12,0},{1,13},{5,9},{9,5},{13,1},{2,14},{6,10},... | collective-permute-start | bytes 393224 | tf_op jit(solution)/shard_map/ppermute | solution.py:435
  61.2 2.2 %collective-permute-start.18 = (bf16[256,256]{1,0:T(8,128)(2,1)S(1)}, bf16[256,256]{1,0:T(8,128)(2,1)S(1)}, u32[]{:S(2)}, u32[]{:S(2)}) collective-permute-start(bf16[256,256]{1,0:T(8,128)(2,1)S(1)} %get-tuple-element.91), channel_id=1, source_target_pairs={{0,4},{4,0},{8,12},{12,8},{1,5},{5,1},{9,13},{13,9},{2,6},{6,2},{1... | collective-permute-start | bytes 393224 | tf_op jit(solution)/shard_map/ppermute | solution.py:435
  63.4 2.5 %collective-permute-done.16.refs_0_ = bf16[256,256]{1,0:T(8,128)(2,1)S(1)} collective-permute-done((bf16[256,256]{1,0:T(8,128)(2,1)S(1)}, bf16[256,256]{1,0:T(8,128)(2,1)S(1)}, u32[]{:S(2)}, u32[]{:S(2)}) %collective-permute-start.16) | collective-permute-done | bytes 131104 | tf_op jit(solution)/shard_map/ppermute | solution.py:435
  65.9 2.7 %collective-permute-done.17.refs_1_ = bf16[256,256]{1,0:T(8,128)(2,1)S(1)} collective-permute-done((bf16[256,256]{1,0:T(8,128)(2,1)S(1)}, bf16[256,256]{1,0:T(8,128)(2,1)S(1)}, u32[]{:S(2)}, u32[]{:S(2)}) %collective-permute-start.17) | collective-permute-done | bytes 131104 | tf_op jit(solution)/shard_map/ppermute | solution.py:435
  68.6 0.5 collective-permute-start.21
  69.1 0.2 pack_gradients.1
  69.3 0.1 collective-permute-start.26
  69.4 1.0 %collective-permute-start.27 = (bf16[32,32,128]{2,1,0:T(8,128)(2,1)S(1)}, bf16[32,32,128]{2,1,0:T(8,128)(2,1)S(1)}, u32[]{:S(2)}, u32[]{:S(2)}) collective-permute-start(bf16[32,32,128]{2,1,0:T(8,128)(2,1)S(1)} %get-tuple-element.100.refs_1_), channel_id=1, source_target_pairs={{0,3},{1,2},{2,1},{3,0},{4,7},{5,6},{6,5},{7,4},{8,11},{9,10},{10,... | collective-permute-start | bytes 786440 | tf_op jit(solution)/shard_map/ppermute | solution.py:501
  70.4 1.1 %collective-permute-start.25 = (bf16[32,32,128]{2,1,0:T(8,128)(2,1)S(1)}, bf16[32,32,128]{2,1,0:T(8,128)(2,1)S(1)}, u32[]{:S(2)}, u32[]{:S(2)}) collective-permute-start(bf16[32,32,128]{2,1,0:T(8,128)(2,1)S(1)} %get-tuple-element.100.refs_1_), channel_id=1, source_target_pairs={{0,2},{2,0},{1,3},{3,1},{4,6},{6,4},{5,7},{7,5},{8,10},{10,8},{9,1... | collective-permute-start | bytes 786440 | tf_op jit(solution)/shard_map/ppermute | solution.py:435
  71.5 2.7 %collective-permute-done.21.refs_6_ = bf16[1024,256]{1,0:T(8,128)(2,1)S(1)} collective-permute-done((bf16[1024,256]{1,0:T(8,128)(2,1)S(1)}, bf16[1024,256]{1,0:T(8,128)(2,1)S(1)}, u32[]{:S(2)}, u32[]{:S(2)}) %collective-permute-start.21) | collective-permute-done | bytes 524320 | tf_op jit(solution)/shard_map/ppermute | solution.py:435
  74.2 1.3 %mix_backward.1 = (bf16[256,256]{1,0:T(8,128)(2,1)S(1)}, bf16[256,256]{1,0:T(8,128)(2,1)S(1)}, bf16[256,256]{1,0:T(8,128)(2,1)S(1)}, bf16[256,256]{1,0:T(8,128)(2,1)S(1)}) custom-call(bf16[32,32,128]{2,1,0:T(8,128)(2,1)S(1)} %get-tuple-element.99.refs_0_.refs_2_, bf16[32,32,128]{2,1,0:T(8,128)(2,1)S(1)} %get-tuple-element.100.refs_1_, ...), custom_call_target="tpu_custom_call" | custom-call | bytes 9437184 | tf_op jit(solution)/shard_map/mix_backward/pallas_call | solution.py:74
  75.5 2.3 %collective-permute-start.22 = (bf16[256,256]{1,0:T(8,128)(2,1)S(1)}, bf16[256,256]{1,0:T(8,128)(2,1)S(1)}, u32[]{:S(2)}, u32[]{:S(2)}) collective-permute-start(bf16[256,256]{1,0:T(8,128)(2,1)S(1)} %get-tuple-element.104), channel_id=1, source_target_pairs={{0,12},{4,8},{8,4},{12,0},{1,13},{5,9},{9,5},{13,1},{2,14},{6,10},... | collective-permute-start | bytes 393224 | tf_op jit(solution)/shard_map/ppermute | solution.py:435
  77.8 2.2 %collective-permute-start.24 = (bf16[256,256]{1,0:T(8,128)(2,1)S(1)}, bf16[256,256]{1,0:T(8,128)(2,1)S(1)}, u32[]{:S(2)}, u32[]{:S(2)}) collective-permute-start(bf16[256,256]{1,0:T(8,128)(2,1)S(1)} %get-tuple-element.106), channel_id=1, source_target_pairs={{0,4},{4,0},{8,12},{12,8},{1,5},{5,1},{9,13},{13,9},{2,6},{6,2},{1... | collective-permute-start | bytes 393224 | tf_op jit(solution)/shard_map/ppermute | solution.py:435
  80.0 3.7 %collective-permute-done.25.refs_3_ = bf16[32,32,128]{2,1,0:T(8,128)(2,1)S(1)} collective-permute-done((bf16[32,32,128]{2,1,0:T(8,128)(2,1)S(1)}, bf16[32,32,128]{2,1,0:T(8,128)(2,1)S(1)}, u32[]{:S(2)}, u32[]{:S(2)}) %collective-permute-start.25) | collective-permute-done | bytes 262176 | tf_op jit(solution)/shard_map/ppermute | solution.py:435
  83.6 3.7 %weight_gradient.1 = f32[2,32,128,256]{3,2,1,0:T(8,128)} custom-call(bf16[5120,256]{1,0:T(8,128)(2,1)S(1)} %get-tuple-element.102.refs_3_.refs_0_, bf16[5120,256]{1,0:T(8,128)(2,1)S(1)} %collective-permute-done.20.refs_4_.refs_1_, bf16[32,32,128]{2,1,0:T(8,128)(2,1)S(1)} %get-tuple-element.99.refs_0_.refs_2_, ...), custom_call_target="tpu_custom_call" | custom-call | bytes 2097152 | tf_op jit(solution)/shard_map/weight_gradient/pallas_call | solution.py:74
  87.3 2.1 %collective-permute-done.23.refs_1_ = bf16[256,256]{1,0:T(8,128)(2,1)S(1)} collective-permute-done((bf16[256,256]{1,0:T(8,128)(2,1)S(1)}, bf16[256,256]{1,0:T(8,128)(2,1)S(1)}, u32[]{:S(2)}, u32[]{:S(2)}) %collective-permute-start.23) | collective-permute-done | bytes 131104 | tf_op jit(solution)/shard_map/ppermute | solution.py:435
  89.5 2.4 %final_dft.1 = bf16[4,1440,256]{2,1,0:T(8,128)(2,1)} custom-call(bf16[4,1440,256]{2,1,0:T(8,128)(2,1)S(1)} %bitcast.10, bf16[1440,256]{1,0:T(8,128)(2,1)S(1)} %copy-done.4, bf16[256,256]{1,0:T(8,128)(2,1)S(1)} %collective-permute-done.22.refs_0_, bf16[256,256]{1,0:T(8,128)(2,1)S(1)} %collective-permute-done.23.refs_1_, ...), custom_call_target="tpu_custom_call" | custom-call | bytes 83886080 | tf_op jit(solution)/shard_map/final_dft/pallas_call | solution.py:74
  (35 shorter events, 0.3 us)
Async XLA Ops:
  5.6 19.4 %collective-permute-start.8 = (bf16[2,4,128,256]{3,2,1,0:T(8,128)(2,1)}, bf16[2,4,128,256]{3,2,1,0:T(8,128)(2,1)S(1)}, u32[]{:S(2)}, u32[]{:S(2)}) collective-permute-start(bf16[2,4,128,256]{3,2,1,0:T(8,128)(2,1)} %get-tuple-element.65), channel_id=1, source_target_pairs={{0,2},{2,0},{1,3},{3,1},{4,6},{6,4},{5,7},{7,5},{8,10},{10,8},{9,1... | collective-permute-start | bytes 1572872 | tf_op jit(solution)/shard_map/ppermute | solution.py:435
  8.6 8.0 %collective-permute-start = (bf16[128,256]{1,0:T(8,128)(2,1)}, bf16[128,256]{1,0:T(8,128)(2,1)S(1)}, u32[]{:S(2)}, u32[]{:S(2)}) collective-permute-start(bf16[128,256]{1,0:T(8,128)(2,1)} %get-tuple-element.55), channel_id=1, source_target_pairs={{0,12},{4,8},{8,4},{12,0},{1,13},{5,9},{9,5},{13,1},{2,14},{6,10},... | collective-permute-start | bytes 196616 | tf_op jit(solution)/shard_map/ppermute | solution.py:435
  12.2 8.2 %collective-permute-start.1 = (bf16[128,256]{1,0:T(8,128)(2,1)}, bf16[128,256]{1,0:T(8,128)(2,1)S(1)}, u32[]{:S(2)}, u32[]{:S(2)}) collective-permute-start(bf16[128,256]{1,0:T(8,128)(2,1)} %get-tuple-element.56), channel_id=1, source_target_pairs={{0,8},{4,12},{8,0},{12,4},{1,9},{5,13},{9,1},{13,5},{2,10},{6,14},... | collective-permute-start | bytes 196616 | tf_op jit(solution)/shard_map/ppermute | solution.py:435
  12.2 8.2 %collective-permute-start.2 = (bf16[128,256]{1,0:T(8,128)(2,1)}, bf16[128,256]{1,0:T(8,128)(2,1)S(1)}, u32[]{:S(2)}, u32[]{:S(2)}) collective-permute-start(bf16[128,256]{1,0:T(8,128)(2,1)} %get-tuple-element.57), channel_id=1, source_target_pairs={{0,4},{4,0},{8,12},{12,8},{1,5},{5,1},{9,13},{13,9},{2,6},{6,2},{1... | collective-permute-start | bytes 196616 | tf_op jit(solution)/shard_map/ppermute | solution.py:435
  12.9 9.0 %collective-permute-start.5 = (bf16[128,256]{1,0:T(8,128)(2,1)}, bf16[128,256]{1,0:T(8,128)(2,1)S(1)}, u32[]{:S(2)}, u32[]{:S(2)}) collective-permute-start(bf16[128,256]{1,0:T(8,128)(2,1)} %get-tuple-element.61), channel_id=1, source_target_pairs={{0,12},{4,8},{8,4},{12,0},{1,13},{5,9},{9,5},{13,1},{2,14},{6,10},... | collective-permute-start | bytes 196616 | tf_op jit(solution)/shard_map/ppermute | solution.py:435
  16.6 6.8 %collective-permute-start.6 = (bf16[128,256]{1,0:T(8,128)(2,1)}, bf16[128,256]{1,0:T(8,128)(2,1)S(1)}, u32[]{:S(2)}, u32[]{:S(2)}) collective-permute-start(bf16[128,256]{1,0:T(8,128)(2,1)} %get-tuple-element.62), channel_id=1, source_target_pairs={{0,8},{4,12},{8,0},{12,4},{1,9},{5,13},{9,1},{13,5},{2,10},{6,14},... | collective-permute-start | bytes 196616 | tf_op jit(solution)/shard_map/ppermute | solution.py:435
  20.4 4.5 %collective-permute-start.7 = (bf16[128,256]{1,0:T(8,128)(2,1)}, bf16[128,256]{1,0:T(8,128)(2,1)S(1)}, u32[]{:S(2)}, u32[]{:S(2)}) collective-permute-start(bf16[128,256]{1,0:T(8,128)(2,1)} %get-tuple-element.63), channel_id=1, source_target_pairs={{0,4},{4,0},{8,12},{12,8},{1,5},{5,1},{9,13},{13,9},{2,6},{6,2},{1... | collective-permute-start | bytes 196616 | tf_op jit(solution)/shard_map/ppermute | solution.py:435
  20.4 0.8 copy-start.7
  21.3 7.7 %collective-permute-start.3 = (bf16[16,32,256]{2,1,0:T(8,128)(2,1)S(1)}, bf16[16,32,256]{2,1,0:T(8,128)(2,1)S(1)}, u32[]{:S(2)}, u32[]{:S(2)}) collective-permute-start(bf16[16,32,256]{2,1,0:T(8,128)(2,1)S(1)} %pack_0.1.refs_0_), channel_id=1, source_target_pairs={{0,2},{2,0},{1,3},{3,1},{4,6},{6,4},{5,7},{7,5},{8,10},{10,8},{9,1... | collective-permute-start | bytes 786440 | tf_op jit(solution)/shard_map/ppermute | solution.py:435
  24.9 0.8 copy-start.6
  25.8 9.0 %collective-permute-start.9 = (bf16[16,32,256]{2,1,0:T(8,128)(2,1)S(1)}, bf16[16,32,256]{2,1,0:T(8,128)(2,1)S(1)}, u32[]{:S(2)}, u32[]{:S(2)}) collective-permute-start(bf16[16,32,256]{2,1,0:T(8,128)(2,1)S(1)} %pack_1.1.refs_0_), channel_id=1, source_target_pairs={{0,2},{2,0},{1,3},{3,1},{4,6},{6,4},{5,7},{7,5},{8,10},{10,8},{9,1... | collective-permute-start | bytes 786440 | tf_op jit(solution)/shard_map/ppermute | solution.py:435
  29.1 2.2 %copy-start = (bf16[2,32,128,256]{3,2,1,0:T(8,128)(2,1)S(1)}, bf16[2,32,128,256]{3,2,1,0:T(8,128)(2,1)}, u32[]{:S(2)}) copy-start(bf16[2,32,128,256]{3,2,1,0:T(8,128)(2,1)} %refs_2_.5) | copy-start | bytes 12582916
  32.1 21.4 %copy-start.2 = (bf16[1,4,1440,256]{3,2,1,0:T(8,128)(2,1)S(1)}, bf16[1,4,1440,256]{3,2,1,0:T(8,128)(2,1)}, u32[]{:S(2)}) copy-start(bf16[1,4,1440,256]{3,2,1,0:T(8,128)(2,1)} %param.8) | copy-start | bytes 8847364
  32.1 21.4 %copy-start.3 = (bf16[256,1440]{1,0:T(8,128)(2,1)S(1)}, bf16[256,1440]{1,0:T(8,128)(2,1)}, u32[]{:S(2)}) copy-start(bf16[256,1440]{1,0:T(8,128)(2,1)} %constant.9.clone.inv_ref) | copy-start | bytes 2211844
  32.1 21.4 %copy-start.5 = (bf16[1440,256]{1,0:T(8,128)(2,1)S(1)}, bf16[1440,256]{1,0:T(8,128)(2,1)}, u32[]{:S(2)}) copy-start(bf16[1440,256]{1,0:T(8,128)(2,1)} %constant.11.clone.back_ref) | copy-start | bytes 2211844
  32.2 5.9 %collective-permute-start.4 = (bf16[16,32,128]{2,1,0:T(8,128)(2,1)S(1)}, bf16[16,32,128]{2,1,0:T(8,128)(2,1)S(1)}, u32[]{:S(2)}, u32[]{:S(2)}) collective-permute-start(bf16[16,32,128]{2,1,0:T(8,128)(2,1)S(1)} %get-tuple-element.60), channel_id=1, source_target_pairs={{0,2},{2,0},{1,3},{3,1},{4,6},{6,4},{5,7},{7,5},{8,10},{10,8},{9,1... | collective-permute-start | bytes 393224 | tf_op jit(solution)/shard_map/ppermute | solution.py:435
  35.6 5.3 %collective-permute-start.10 = (bf16[16,32,128]{2,1,0:T(8,128)(2,1)S(1)}, bf16[16,32,128]{2,1,0:T(8,128)(2,1)S(1)}, u32[]{:S(2)}, u32[]{:S(2)}) collective-permute-start(bf16[16,32,128]{2,1,0:T(8,128)(2,1)S(1)} %get-tuple-element.71), channel_id=1, source_target_pairs={{0,2},{2,0},{1,3},{3,1},{4,6},{6,4},{5,7},{7,5},{8,10},{10,8},{9,1... | collective-permute-start | bytes 393224 | tf_op jit(solution)/shard_map/ppermute | solution.py:435
  38.1 15.4 %collective-permute-start.14 = (bf16[2,4,128,256]{3,2,1,0:T(8,128)(2,1)S(1)}, bf16[2,4,128,256]{3,2,1,0:T(8,128)(2,1)S(1)}, u32[]{:S(2)}, u32[]{:S(2)}) collective-permute-start(bf16[2,4,128,256]{3,2,1,0:T(8,128)(2,1)S(1)} %collective-permute-done.8), channel_id=1, source_target_pairs={{0,16},{16,0},{1,17},{17,1},{2,18},{18,2},{3,19},{19,3},{4,20},{20... | collective-permute-start | bytes 1572872 | tf_op jit(solution)/shard_map/ppermute | solution.py:435
  41.0 12.5 %collective-permute-start.15 = (bf16[2,4,128,256]{3,2,1,0:T(8,128)(2,1)S(1)}, bf16[2,4,128,256]{3,2,1,0:T(8,128)(2,1)S(1)}, u32[]{:S(2)}, u32[]{:S(2)}) collective-permute-start(bf16[2,4,128,256]{3,2,1,0:T(8,128)(2,1)S(1)} %get-tuple-element.79), channel_id=1, source_target_pairs={{0,2},{2,0},{1,3},{3,1},{4,6},{6,4},{5,7},{7,5},{8,10},{10,8},{9,1... | collective-permute-start | bytes 1572872 | tf_op jit(solution)/shard_map/ppermute | solution.py:435
  41.6 7.6 %collective-permute-start.11 = (bf16[256,256]{1,0:T(8,128)(2,1)S(1)}, bf16[256,256]{1,0:T(8,128)(2,1)S(1)}, u32[]{:S(2)}, u32[]{:S(2)}) collective-permute-start(bf16[256,256]{1,0:T(8,128)(2,1)S(1)} %get-tuple-element.72), channel_id=1, source_target_pairs={{0,12},{4,8},{8,4},{12,0},{1,13},{5,9},{9,5},{13,1},{2,14},{6,10},... | collective-permute-start | bytes 393224 | tf_op jit(solution)/shard_map/ppermute | solution.py:435
  46.3 7.3 %collective-permute-start.12 = (bf16[256,256]{1,0:T(8,128)(2,1)S(1)}, bf16[256,256]{1,0:T(8,128)(2,1)S(1)}, u32[]{:S(2)}, u32[]{:S(2)}) collective-permute-start(bf16[256,256]{1,0:T(8,128)(2,1)S(1)} %get-tuple-element.73), channel_id=1, source_target_pairs={{0,8},{4,12},{8,0},{12,4},{1,9},{5,13},{9,1},{13,5},{2,10},{6,14},... | collective-permute-start | bytes 393224 | tf_op jit(solution)/shard_map/ppermute | solution.py:435
  46.9 6.6 %collective-permute-start.13 = (bf16[256,256]{1,0:T(8,128)(2,1)S(1)}, bf16[256,256]{1,0:T(8,128)(2,1)S(1)}, u32[]{:S(2)}, u32[]{:S(2)}) collective-permute-start(bf16[256,256]{1,0:T(8,128)(2,1)S(1)} %get-tuple-element.74), channel_id=1, source_target_pairs={{0,4},{4,0},{8,12},{12,8},{1,5},{5,1},{9,13},{13,9},{2,6},{6,2},{1... | collective-permute-start | bytes 393224 | tf_op jit(solution)/shard_map/ppermute | solution.py:435
  53.6 20.7 %copy-start.1 = (bf16[2,32,128,256]{3,2,1,0:T(8,128)(2,1)S(1)}, bf16[2,32,128,256]{3,2,1,0:T(8,128)(2,1)}, u32[]{:S(2)}) copy-start(bf16[2,32,128,256]{3,2,1,0:T(8,128)(2,1)} %refs_2_.5) | copy-start | bytes 12582916
  57.7 10.9 %collective-permute-start.19 = (bf16[2,4,128,256]{3,2,1,0:T(8,128)(2,1)S(1)}, bf16[2,4,128,256]{3,2,1,0:T(8,128)(2,1)S(1)}, u32[]{:S(2)}, u32[]{:S(2)}) collective-permute-start(bf16[2,4,128,256]{3,2,1,0:T(8,128)(2,1)S(1)} %get-tuple-element.94), channel_id=1, source_target_pairs={{0,2},{2,0},{1,3},{3,1},{4,6},{6,4},{5,7},{7,5},{8,10},{10,8},{9,1... | collective-permute-start | bytes 1572872 | tf_op jit(solution)/shard_map/ppermute | solution.py:435
  59.0 6.9 %collective-permute-start.16 = (bf16[256,256]{1,0:T(8,128)(2,1)S(1)}, bf16[256,256]{1,0:T(8,128)(2,1)S(1)}, u32[]{:S(2)}, u32[]{:S(2)}) collective-permute-start(bf16[256,256]{1,0:T(8,128)(2,1)S(1)} %get-tuple-element.89), channel_id=1, source_target_pairs={{0,12},{4,8},{8,4},{12,0},{1,13},{5,9},{9,5},{13,1},{2,14},{6,10},... | collective-permute-start | bytes 393224 | tf_op jit(solution)/shard_map/ppermute | solution.py:435
  61.2 7.4 %collective-permute-start.17 = (bf16[256,256]{1,0:T(8,128)(2,1)S(1)}, bf16[256,256]{1,0:T(8,128)(2,1)S(1)}, u32[]{:S(2)}, u32[]{:S(2)}) collective-permute-start(bf16[256,256]{1,0:T(8,128)(2,1)S(1)} %get-tuple-element.90), channel_id=1, source_target_pairs={{0,8},{4,12},{8,0},{12,4},{1,9},{5,13},{9,1},{13,5},{2,10},{6,14},... | collective-permute-start | bytes 393224 | tf_op jit(solution)/shard_map/ppermute | solution.py:435
  61.2 7.4 %collective-permute-start.18 = (bf16[256,256]{1,0:T(8,128)(2,1)S(1)}, bf16[256,256]{1,0:T(8,128)(2,1)S(1)}, u32[]{:S(2)}, u32[]{:S(2)}) collective-permute-start(bf16[256,256]{1,0:T(8,128)(2,1)S(1)} %get-tuple-element.91), channel_id=1, source_target_pairs={{0,4},{4,0},{8,12},{12,8},{1,5},{5,1},{9,13},{13,9},{2,6},{6,2},{1... | collective-permute-start | bytes 393224 | tf_op jit(solution)/shard_map/ppermute | solution.py:435
  68.6 5.7 %collective-permute-start.20 = (bf16[5120,256]{1,0:T(8,128)(2,1)S(1)}, bf16[5120,256]{1,0:T(8,128)(2,1)S(1)}, u32[]{:S(2)}, u32[]{:S(2)}) collective-permute-start(bf16[5120,256]{1,0:T(8,128)(2,1)S(1)} %get-tuple-element.102.refs_3_.refs_0_), channel_id=1, source_target_pairs={{0,1},{1,0},{2,3},{3,2},{4,5},{5,4},{6,7},{7,6},{8,9},{9,8},{10,11... | collective-permute-start | bytes 7864328 | tf_op jit(solution)/shard_map/ppermute | solution.py:435
  68.6 5.7 %collective-permute-start.21 = (bf16[1024,256]{1,0:T(8,128)(2,1)S(1)}, bf16[1024,256]{1,0:T(8,128)(2,1)S(1)}, u32[]{:S(2)}, u32[]{:S(2)}) collective-permute-start(bf16[1024,256]{1,0:T(8,128)(2,1)S(1)} %bitcast.14), channel_id=1, source_target_pairs={{0,1},{1,0},{2,3},{3,2},{4,5},{5,4},{6,7},{7,6},{8,9},{9,8},{10,11... | collective-permute-start | bytes 1572872 | tf_op jit(solution)/shard_map/ppermute | solution.py:435
  69.3 8.5 %collective-permute-start.26 = (bf16[32,32,128]{2,1,0:T(8,128)(2,1)S(1)}, bf16[32,32,128]{2,1,0:T(8,128)(2,1)S(1)}, u32[]{:S(2)}, u32[]{:S(2)}) collective-permute-start(bf16[32,32,128]{2,1,0:T(8,128)(2,1)S(1)} %get-tuple-element.99.refs_0_.refs_2_), channel_id=1, source_target_pairs={{0,1},{1,0},{2,3},{3,2},{4,5},{5,4},{6,7},{7,6},{8,9},{9,8},{10,11... | collective-permute-start | bytes 786440 | tf_op jit(solution)/shard_map/ppermute | solution.py:501
  69.4 10.6 %collective-permute-start.27 = (bf16[32,32,128]{2,1,0:T(8,128)(2,1)S(1)}, bf16[32,32,128]{2,1,0:T(8,128)(2,1)S(1)}, u32[]{:S(2)}, u32[]{:S(2)}) collective-permute-start(bf16[32,32,128]{2,1,0:T(8,128)(2,1)S(1)} %get-tuple-element.100.refs_1_), channel_id=1, source_target_pairs={{0,3},{1,2},{2,1},{3,0},{4,7},{5,6},{6,5},{7,4},{8,11},{9,10},{10,... | collective-permute-start | bytes 786440 | tf_op jit(solution)/shard_map/ppermute | solution.py:501
  70.4 13.2 %collective-permute-start.25 = (bf16[32,32,128]{2,1,0:T(8,128)(2,1)S(1)}, bf16[32,32,128]{2,1,0:T(8,128)(2,1)S(1)}, u32[]{:S(2)}, u32[]{:S(2)}) collective-permute-start(bf16[32,32,128]{2,1,0:T(8,128)(2,1)S(1)} %get-tuple-element.100.refs_1_), channel_id=1, source_target_pairs={{0,2},{2,0},{1,3},{3,1},{4,6},{6,4},{5,7},{7,5},{8,10},{10,8},{9,1... | collective-permute-start | bytes 786440 | tf_op jit(solution)/shard_map/ppermute | solution.py:435
  75.5 11.8 %collective-permute-start.22 = (bf16[256,256]{1,0:T(8,128)(2,1)S(1)}, bf16[256,256]{1,0:T(8,128)(2,1)S(1)}, u32[]{:S(2)}, u32[]{:S(2)}) collective-permute-start(bf16[256,256]{1,0:T(8,128)(2,1)S(1)} %get-tuple-element.104), channel_id=1, source_target_pairs={{0,12},{4,8},{8,4},{12,0},{1,13},{5,9},{9,5},{13,1},{2,14},{6,10},... | collective-permute-start | bytes 393224 | tf_op jit(solution)/shard_map/ppermute | solution.py:435
  77.8 11.6 %collective-permute-start.23 = (bf16[256,256]{1,0:T(8,128)(2,1)S(1)}, bf16[256,256]{1,0:T(8,128)(2,1)S(1)}, u32[]{:S(2)}, u32[]{:S(2)}) collective-permute-start(bf16[256,256]{1,0:T(8,128)(2,1)S(1)} %get-tuple-element.105), channel_id=1, source_target_pairs={{0,8},{4,12},{8,0},{12,4},{1,9},{5,13},{9,1},{13,5},{2,10},{6,14},... | collective-permute-start | bytes 393224 | tf_op jit(solution)/shard_map/ppermute | solution.py:435
  77.8 11.6 %copy-start.4 = (bf16[1440,256]{1,0:T(8,128)(2,1)S(1)}, bf16[1440,256]{1,0:T(8,128)(2,1)}, u32[]{:S(2)}) copy-start(bf16[1440,256]{1,0:T(8,128)(2,1)} %constant.10.clone.table_ref) | copy-start | bytes 2211844
  77.8 11.6 %collective-permute-start.24 = (bf16[256,256]{1,0:T(8,128)(2,1)S(1)}, bf16[256,256]{1,0:T(8,128)(2,1)S(1)}, u32[]{:S(2)}, u32[]{:S(2)}) collective-permute-start(bf16[256,256]{1,0:T(8,128)(2,1)S(1)} %get-tuple-element.106), channel_id=1, source_target_pairs={{0,4},{4,0},{8,12},{12,8},{1,5},{5,1},{9,13},{13,9},{2,6},{6,2},{1... | collective-permute-start | bytes 393224 | tf_op jit(solution)/shard_map/ppermute | solution.py:435

commit v6 on v5

--- a/solution.py
+++ b/solution.py
@@ -340,18 +340,19 @@
     return whole(body, f"mix_forward_{h}", outs, scratch, mebi=3)(*spectra, own)
 
 
-def mix_backward(plan, grads, own, early, late):
+def mix_backward(plan, grads, own, early, late, e, before=None):
     shape = (plan.m_loc * plan.rk, plan.width)
-    flat = [*early, *(array for group in late for array in group)]
-    n = plan.n_rep
+    flat = [early[e], *(group[e] for group in late)]
 
     def body(*refs):
         ins, own_ref = refs[: plan.n_chan], refs[plan.n_chan]
         there = refs[plan.n_chan + 1 : plan.n_chan + 1 + len(flat)]
         outs, held = refs[plan.n_chan + 1 + len(flat) : -1], refs[-1]
         me, here = lax.axis_index("rep"), lax.axis_index("parts")
-        for e in range(n):
-            base = (me ^ e) * plan.n_parts
+        if before is not None:
+            held[...] = outs[0][...]
+            outs = outs[1:]
+        for base in [(me ^ e) * plan.n_parts]:
             units = [(plan.unit_at(1, base + (here ^ p)), True, p) for p in range(plan.n_parts)]
             units += [(plan.unit_at(0, base), True, plan.n_parts)]
             units += [(plan.unit_at(0, base + i), False, i - 1) for i in range(1, plan.n_parts)]
@@ -367,22 +368,25 @@
                             if x == 0:
                                 weights = own_ref[j, u]
                             else:
-                                ref, at = there[n + (x - 1) * n + e], i
+                                ref, at = there[x], i
                                 if is_early:
-                                    ref, at = there[e], (x - 1) * (plan.n_parts + 1) + i
+                                    ref, at = there[0], (x - 1) * (plan.n_parts + 1) + i
                                 at = ((at * 2 + j) * plan.unit + t) * plan.o_w
                                 weights = ref[at : at + plan.o_w]
                             total += jnp.dot(
                                 values.astype(BF16), weights, preferred_element_type=F32
                             )
                     held[u] = total
-        for s in range(plan.n_lat):
+        for s, out in enumerate(outs):
             block = held[:, s * plan.rk : (s + 1) * plan.rk, :]
-            outs[s][...] = block.reshape(shape).astype(BF16)
-
-    scratch = [pltpu.VMEM((plan.m_loc, plan.wide, plan.width), F32)]
+            out[...] = block.reshape(shape).astype(BF16)
+
+    wide = (plan.m_loc, plan.wide, plan.width)
+    if before is None:
+        return whole(body, "mix_backward_own", [like(wide, F32)], mebi=5)(*grads, own, *flat)[0]
+    scratch = [pltpu.VMEM(wide, F32)]
     outs = [like(shape)] * plan.n_lat
-    return whole(body, "mix_backward", outs, scratch, mebi=9)(*grads, own, *flat)
+    return whole(body, "mix_backward", outs, scratch, mebi=5)(*grads, own, *flat, before)
 
 
 def weight_gradient(plan, spectra, grads):
@@ -495,7 +499,9 @@
     tied = along("rep", [tied], *blocks)[0]
     late = along("rep", [unit.reshape(-1, plan.width) for unit in late])
     grads = pack_gradients(plan, blocks)
-    blocks = mix_backward(plan, grads, weights, tied, late)
+    blocks = None
+    for e in range(plan.n_rep):
+        blocks = mix_backward(plan, grads, weights, tied, late, e, blocks)
     spectral = to_lat(blocks)
     far = [
         lax.ppermute(

time: 92.2 us -> 91.7 us (level)
    pallas_call x11 -> x12, Pallas kernels: 18.5 us -> 18.7 us  [call(): pl.pallas_call(body, in_specs=ins or [VMEM] * len(operands), out_specs=ou...]
where the time goes in v6:
time: 91.7 us; the launch traced here: 91.4 us
  starting transfers between devices  35.9 us (39%)
  waiting for transfers between devices  32.1 us (35%)
  Pallas kernels  18.7 us (20%)
  local copies, waits for them, and re-layouts  3.9 us (4%)
    ppermute x26, starting transfers between devices, hop(): return lax.ppermute(value, axis, [(i, i ^ s) for i in range(size)])  34.8 us
    ppermute x26, waiting for transfers between devices, hop(): return lax.ppermute(value, axis, [(i, i ^ s) for i in range(size)])  32.1 us
    pallas_call x12, Pallas kernels, call(): pl.pallas_call(body, in_specs=ins or [VMEM] * len(operands), out_specs=ou...  18.7 us
    unnamed x16, local copies, waits for them, and re-layouts  3.9 us
  transfers between devices with their start and end apart: 28, of which 14 were waited for; matrix products, arithmetic and copies ran while one was open for 0% of the time, Pallas kernels for 8%

profile of v6, /device:TPU:0, one launch (start us, length us, event | category | flops | bytes accessed | tf_op | source)
XLA Modules:
  0.0 91.4 jit_solution(6958494147918799026)
XLA Ops:
  0.6 4.9 %forward_dft.1 = (bf16[128,256]{1,0:T(8,128)(2,1)}, bf16[128,256]{1,0:T(8,128)(2,1)}, bf16[128,256]{1,0:T(8,128)(2,1)}, bf16[128,256]{1,0:T(8,128)(2,1)}, bf16[1...) custom-call(bf16[4,1440,256]{2,1,0:T(8,128)(2,1)} %bitcast.19, ...), custom_call_target="tpu_custom_call" | custom-call | bytes 6291456 | tf_op jit(solution)/shard_map/forward_dft/pallas_call | solution.py:74
  5.6 3.0 %collective-permute-start.8 = (bf16[2,4,128,256]{3,2,1,0:T(8,128)(2,1)}, bf16[2,4,128,256]{3,2,1,0:T(8,128)(2,1)S(1)}, u32[]{:S(2)}, u32[]{:S(2)}) collective-permute-start(bf16[2,4,128,256]{3,2,1,0:T(8,128)(2,1)} %get-tuple-element.65), channel_id=1, source_target_pairs={{0,2},{2,0},{1,3},{3,1},{4,6},{6,4},{5,7},{7,5},{8,10},{10,8},{9,1... | collective-permute-start | bytes 1572872 | tf_op jit(solution)/shard_map/ppermute | solution.py:439
  8.6 3.6 %collective-permute-start = (bf16[128,256]{1,0:T(8,128)(2,1)}, bf16[128,256]{1,0:T(8,128)(2,1)S(1)}, u32[]{:S(2)}, u32[]{:S(2)}) collective-permute-start(bf16[128,256]{1,0:T(8,128)(2,1)} %get-tuple-element.55), channel_id=1, source_target_pairs={{0,12},{4,8},{8,4},{12,0},{1,13},{5,9},{9,5},{13,1},{2,14},{6,10},... | collective-permute-start | bytes 196616 | tf_op jit(solution)/shard_map/ppermute | solution.py:439
  12.2 0.8 collective-permute-start.2
  12.9 3.6 %collective-permute-start.5 = (bf16[128,256]{1,0:T(8,128)(2,1)}, bf16[128,256]{1,0:T(8,128)(2,1)S(1)}, u32[]{:S(2)}, u32[]{:S(2)}) collective-permute-start(bf16[128,256]{1,0:T(8,128)(2,1)} %get-tuple-element.61), channel_id=1, source_target_pairs={{0,12},{4,8},{8,4},{12,0},{1,13},{5,9},{9,5},{13,1},{2,14},{6,10},... | collective-permute-start | bytes 196616 | tf_op jit(solution)/shard_map/ppermute | solution.py:439
  16.6 2.1 %collective-permute-start.6 = (bf16[128,256]{1,0:T(8,128)(2,1)}, bf16[128,256]{1,0:T(8,128)(2,1)S(1)}, u32[]{:S(2)}, u32[]{:S(2)}) collective-permute-start(bf16[128,256]{1,0:T(8,128)(2,1)} %get-tuple-element.62), channel_id=1, source_target_pairs={{0,8},{4,12},{8,0},{12,4},{1,9},{5,13},{9,1},{13,5},{2,10},{6,14},... | collective-permute-start | bytes 196616 | tf_op jit(solution)/shard_map/ppermute | solution.py:439
  18.7 1.8 %collective-permute-done.1.refs_1_ = bf16[128,256]{1,0:T(8,128)(2,1)S(1)} collective-permute-done((bf16[128,256]{1,0:T(8,128)(2,1)}, bf16[128,256]{1,0:T(8,128)(2,1)S(1)}, u32[]{:S(2)}, u32[]{:S(2)}) %collective-permute-start.1) | collective-permute-done | bytes 65568 | tf_op jit(solution)/shard_map/ppermute | solution.py:439
  20.4 0.8 copy-done.7
  21.3 0.6 collective-permute-start.3
  21.9 1.4 %collective-permute-done.6.refs_1_ = bf16[128,256]{1,0:T(8,128)(2,1)S(1)} collective-permute-done((bf16[128,256]{1,0:T(8,128)(2,1)}, bf16[128,256]{1,0:T(8,128)(2,1)S(1)}, u32[]{:S(2)}, u32[]{:S(2)}) %collective-permute-start.6) | collective-permute-done | bytes 65568 | tf_op jit(solution)/shard_map/ppermute | solution.py:439
  23.3 1.6 %collective-permute-done.7.refs_2_ = bf16[128,256]{1,0:T(8,128)(2,1)S(1)} collective-permute-done((bf16[128,256]{1,0:T(8,128)(2,1)}, bf16[128,256]{1,0:T(8,128)(2,1)S(1)}, u32[]{:S(2)}, u32[]{:S(2)}) %collective-permute-start.7) | collective-permute-done | bytes 65568 | tf_op jit(solution)/shard_map/ppermute | solution.py:439
  24.9 0.8 copy-done.6
  25.8 0.6 collective-permute-start.9
  26.4 2.7 %collective-permute-done.3.refs_1_ = bf16[16,32,256]{2,1,0:T(8,128)(2,1)S(1)} collective-permute-done((bf16[16,32,256]{2,1,0:T(8,128)(2,1)S(1)}, bf16[16,32,256]{2,1,0:T(8,128)(2,1)S(1)}, u32[]{:S(2)}, u32[]{:S(2)}) %collective-permute-start.3) | collective-permute-done | bytes 262176 | tf_op jit(solution)/shard_map/ppermute | solution.py:439
  29.1 2.2 %copy-done = bf16[2,32,128,256]{3,2,1,0:T(8,128)(2,1)S(1)} copy-done((bf16[2,32,128,256]{3,2,1,0:T(8,128)(2,1)S(1)}, bf16[2,32,128,256]{3,2,1,0:T(8,128)(2,1)}, u32[]{:S(2)}) %copy-start) | copy-done | bytes 4194328
  31.2 0.9 mix_forward_0.1
  32.2 0.6 collective-permute-start.4
  32.8 2.0 %collective-permute-done.9.refs_1_ = bf16[16,32,256]{2,1,0:T(8,128)(2,1)S(1)} collective-permute-done((bf16[16,32,256]{2,1,0:T(8,128)(2,1)S(1)}, bf16[16,32,256]{2,1,0:T(8,128)(2,1)S(1)}, u32[]{:S(2)}, u32[]{:S(2)}) %collective-permute-start.9) | collective-permute-done | bytes 262176 | tf_op jit(solution)/shard_map/ppermute | solution.py:439
  34.8 0.9 mix_forward_1.1
  35.6 0.6 collective-permute-start.10
  36.2 1.8 %collective-permute-done.4.refs_1_ = bf16[16,32,128]{2,1,0:T(8,128)(2,1)S(1)} collective-permute-done((bf16[16,32,128]{2,1,0:T(8,128)(2,1)S(1)}, bf16[16,32,128]{2,1,0:T(8,128)(2,1)S(1)}, u32[]{:S(2)}, u32[]{:S(2)}) %collective-permute-start.4) | collective-permute-done | bytes 131104 | tf_op jit(solution)/shard_map/ppermute | solution.py:439
  38.1 1.5 %collective-permute-start.14 = (bf16[2,4,128,256]{3,2,1,0:T(8,128)(2,1)S(1)}, bf16[2,4,128,256]{3,2,1,0:T(8,128)(2,1)S(1)}, u32[]{:S(2)}, u32[]{:S(2)}) collective-permute-start(bf16[2,4,128,256]{3,2,1,0:T(8,128)(2,1)S(1)} %collective-permute-done.8), channel_id=1, source_target_pairs={{0,16},{16,0},{1,17},{17,1},{2,18},{18,2},{3,19},{19,3},{4,20},{20... | collective-permute-start | bytes 1572872 | tf_op jit(solution)/shard_map/ppermute | solution.py:439
  39.6 1.4 %collective-permute-done.10.refs_3_ = bf16[16,32,128]{2,1,0:T(8,128)(2,1)S(1)} collective-permute-done((bf16[16,32,128]{2,1,0:T(8,128)(2,1)S(1)}, bf16[16,32,128]{2,1,0:T(8,128)(2,1)S(1)}, u32[]{:S(2)}, u32[]{:S(2)}) %collective-permute-start.10) | collective-permute-done | bytes 131104 | tf_op jit(solution)/shard_map/ppermute | solution.py:439
  41.0 0.5 collective-permute-start.15
  41.6 4.6 %collective-permute-start.11 = (bf16[256,256]{1,0:T(8,128)(2,1)S(1)}, bf16[256,256]{1,0:T(8,128)(2,1)S(1)}, u32[]{:S(2)}, u32[]{:S(2)}) collective-permute-start(bf16[256,256]{1,0:T(8,128)(2,1)S(1)} %get-tuple-element.72), channel_id=1, source_target_pairs={{0,12},{4,8},{8,4},{12,0},{1,13},{5,9},{9,5},{13,1},{2,14},{6,10},... | collective-permute-start | bytes 393224 | tf_op jit(solution)/shard_map/ppermute | solution.py:439
  46.3 0.7 collective-permute-start.12
  46.9 0.3 collective-permute-start.13
  47.2 2.1 %collective-permute-done.11.refs_0_ = bf16[256,256]{1,0:T(8,128)(2,1)S(1)} collective-permute-done((bf16[256,256]{1,0:T(8,128)(2,1)S(1)}, bf16[256,256]{1,0:T(8,128)(2,1)S(1)}, u32[]{:S(2)}, u32[]{:S(2)}) %collective-permute-start.11) | collective-permute-done | bytes 131104 | tf_op jit(solution)/shard_map/ppermute | solution.py:439
  49.3 4.2 %collective-permute-done.12.refs_1_ = bf16[256,256]{1,0:T(8,128)(2,1)S(1)} collective-permute-done((bf16[256,256]{1,0:T(8,128)(2,1)S(1)}, bf16[256,256]{1,0:T(8,128)(2,1)S(1)}, u32[]{:S(2)}, u32[]{:S(2)}) %collective-permute-start.12) | collective-permute-done | bytes 131104 | tf_op jit(solution)/shard_map/ppermute | solution.py:439
  53.6 4.1 %middle.1 = (bf16[256,256]{1,0:T(8,128)(2,1)S(1)}, bf16[256,256]{1,0:T(8,128)(2,1)S(1)}, bf16[256,256]{1,0:T(8,128)(2,1)S(1)}, bf16[256,256]{1,0:T(8,128)(2,1)S(1)}, bf16[5120,256]{1,0:T(8,128)(2,1)S(1)}) custom-call(bf16[4,1440,256]{2,1,0:T(8,128)(2,1)S(1)} %bitcast.9, bf16[1440,256]{1,0:T(8,128)(2,1)S(1)} %copy-done.5, bf16[256,1440]{1,0:T(8,128)(2,1)S(1)} %copy-done.3, ...), custom_call_target="tpu_custom_call" | custom-call | bytes 12582912 | tf_op jit(solution)/shard_map/middle/pallas_call | solution.py:74
  57.7 1.3 %collective-permute-start.19 = (bf16[2,4,128,256]{3,2,1,0:T(8,128)(2,1)S(1)}, bf16[2,4,128,256]{3,2,1,0:T(8,128)(2,1)S(1)}, u32[]{:S(2)}, u32[]{:S(2)}) collective-permute-start(bf16[2,4,128,256]{3,2,1,0:T(8,128)(2,1)S(1)} %get-tuple-element.94), channel_id=1, source_target_pairs={{0,2},{2,0},{1,3},{3,1},{4,6},{6,4},{5,7},{7,5},{8,10},{10,8},{9,1... | collective-permute-start | bytes 1572872 | tf_op jit(solution)/shard_map/ppermute | solution.py:439
  59.0 2.2 %collective-permute-start.16 = (bf16[256,256]{1,0:T(8,128)(2,1)S(1)}, bf16[256,256]{1,0:T(8,128)(2,1)S(1)}, u32[]{:S(2)}, u32[]{:S(2)}) collective-permute-start(bf16[256,256]{1,0:T(8,128)(2,1)S(1)} %get-tuple-element.89), channel_id=1, source_target_pairs={{0,12},{4,8},{8,4},{12,0},{1,13},{5,9},{9,5},{13,1},{2,14},{6,10},... | collective-permute-start | bytes 393224 | tf_op jit(solution)/shard_map/ppermute | solution.py:439
  61.2 2.2 %collective-permute-start.18 = (bf16[256,256]{1,0:T(8,128)(2,1)S(1)}, bf16[256,256]{1,0:T(8,128)(2,1)S(1)}, u32[]{:S(2)}, u32[]{:S(2)}) collective-permute-start(bf16[256,256]{1,0:T(8,128)(2,1)S(1)} %get-tuple-element.91), channel_id=1, source_target_pairs={{0,4},{4,0},{8,12},{12,8},{1,5},{5,1},{9,13},{13,9},{2,6},{6,2},{1... | collective-permute-start | bytes 393224 | tf_op jit(solution)/shard_map/ppermute | solution.py:439
  63.4 2.5 %collective-permute-done.16.refs_0_ = bf16[256,256]{1,0:T(8,128)(2,1)S(1)} collective-permute-done((bf16[256,256]{1,0:T(8,128)(2,1)S(1)}, bf16[256,256]{1,0:T(8,128)(2,1)S(1)}, u32[]{:S(2)}, u32[]{:S(2)}) %collective-permute-start.16) | collective-permute-done | bytes 131104 | tf_op jit(solution)/shard_map/ppermute | solution.py:439
  65.9 2.7 %collective-permute-done.17.refs_1_ = bf16[256,256]{1,0:T(8,128)(2,1)S(1)} collective-permute-done((bf16[256,256]{1,0:T(8,128)(2,1)S(1)}, bf16[256,256]{1,0:T(8,128)(2,1)S(1)}, u32[]{:S(2)}, u32[]{:S(2)}) %collective-permute-start.17) | collective-permute-done | bytes 131104 | tf_op jit(solution)/shard_map/ppermute | solution.py:439
  68.6 0.5 collective-permute-start.21
  69.1 0.2 pack_gradients.1
  69.4 1.0 %collective-permute-start.27 = (bf16[32,32,128]{2,1,0:T(8,128)(2,1)S(1)}, bf16[32,32,128]{2,1,0:T(8,128)(2,1)S(1)}, u32[]{:S(2)}, u32[]{:S(2)}) collective-permute-start(bf16[32,32,128]{2,1,0:T(8,128)(2,1)S(1)} %get-tuple-element.100.refs_1_), channel_id=1, source_target_pairs={{0,3},{1,2},{2,1},{3,0},{4,7},{5,6},{6,5},{7,4},{8,11},{9,10},{10,... | collective-permute-start | bytes 786440 | tf_op jit(solution)/shard_map/ppermute | solution.py:507
  70.4 1.1 %collective-permute-start.25 = (bf16[32,32,128]{2,1,0:T(8,128)(2,1)S(1)}, bf16[32,32,128]{2,1,0:T(8,128)(2,1)S(1)}, u32[]{:S(2)}, u32[]{:S(2)}) collective-permute-start(bf16[32,32,128]{2,1,0:T(8,128)(2,1)S(1)} %get-tuple-element.100.refs_1_), channel_id=1, source_target_pairs={{0,2},{2,0},{1,3},{3,1},{4,6},{6,4},{5,7},{7,5},{8,10},{10,8},{9,1... | collective-permute-start | bytes 786440 | tf_op jit(solution)/shard_map/ppermute | solution.py:439
  71.5 0.7 mix_backward_own.1.refs_5_
  72.2 2.1 %collective-permute-done.21.refs_4_ = bf16[1024,256]{1,0:T(8,128)(2,1)S(1)} collective-permute-done((bf16[1024,256]{1,0:T(8,128)(2,1)S(1)}, bf16[1024,256]{1,0:T(8,128)(2,1)S(1)}, u32[]{:S(2)}, u32[]{:S(2)}) %collective-permute-start.21) | collective-permute-done | bytes 524320 | tf_op jit(solution)/shard_map/ppermute | solution.py:439
  74.2 0.7 mix_backward.1
  75.0 2.3 %collective-permute-start.22 = (bf16[256,256]{1,0:T(8,128)(2,1)S(1)}, bf16[256,256]{1,0:T(8,128)(2,1)S(1)}, u32[]{:S(2)}, u32[]{:S(2)}) collective-permute-start(bf16[256,256]{1,0:T(8,128)(2,1)S(1)} %get-tuple-element.104), channel_id=1, source_target_pairs={{0,12},{4,8},{8,4},{12,0},{1,13},{5,9},{9,5},{13,1},{2,14},{6,10},... | collective-permute-start | bytes 393224 | tf_op jit(solution)/shard_map/ppermute | solution.py:439
  77.3 2.2 %collective-permute-start.24 = (bf16[256,256]{1,0:T(8,128)(2,1)S(1)}, bf16[256,256]{1,0:T(8,128)(2,1)S(1)}, u32[]{:S(2)}, u32[]{:S(2)}) collective-permute-start(bf16[256,256]{1,0:T(8,128)(2,1)S(1)} %get-tuple-element.106), channel_id=1, source_target_pairs={{0,4},{4,0},{8,12},{12,8},{1,5},{5,1},{9,13},{13,9},{2,6},{6,2},{1... | collective-permute-start | bytes 393224 | tf_op jit(solution)/shard_map/ppermute | solution.py:439
  79.5 4.2 %collective-permute-done.25.refs_3_ = bf16[32,32,128]{2,1,0:T(8,128)(2,1)S(1)} collective-permute-done((bf16[32,32,128]{2,1,0:T(8,128)(2,1)S(1)}, bf16[32,32,128]{2,1,0:T(8,128)(2,1)S(1)}, u32[]{:S(2)}, u32[]{:S(2)}) %collective-permute-start.25) | collective-permute-done | bytes 262176 | tf_op jit(solution)/shard_map/ppermute | solution.py:439
  83.6 3.7 %weight_gradient.1 = f32[2,32,128,256]{3,2,1,0:T(8,128)} custom-call(bf16[5120,256]{1,0:T(8,128)(2,1)S(1)} %get-tuple-element.102.refs_3_.refs_0_, bf16[5120,256]{1,0:T(8,128)(2,1)S(1)} %collective-permute-done.20.refs_3_.refs_1_, bf16[32,32,128]{2,1,0:T(8,128)(2,1)S(1)} %get-tuple-element.99.refs_0_.refs_2_, ...), custom_call_target="tpu_custom_call" | custom-call | bytes 2097152 | tf_op jit(solution)/shard_map/weight_gradient/pallas_call | solution.py:74
  87.3 1.6 %collective-permute-done.23.refs_1_ = bf16[256,256]{1,0:T(8,128)(2,1)S(1)} collective-permute-done((bf16[256,256]{1,0:T(8,128)(2,1)S(1)}, bf16[256,256]{1,0:T(8,128)(2,1)S(1)}, u32[]{:S(2)}, u32[]{:S(2)}) %collective-permute-start.23) | collective-permute-done | bytes 131104 | tf_op jit(solution)/shard_map/ppermute | solution.py:439
  88.9 2.4 %final_dft.1 = bf16[4,1440,256]{2,1,0:T(8,128)(2,1)} custom-call(bf16[4,1440,256]{2,1,0:T(8,128)(2,1)S(1)} %bitcast.10, bf16[1440,256]{1,0:T(8,128)(2,1)S(1)} %copy-done.4, bf16[256,256]{1,0:T(8,128)(2,1)S(1)} %collective-permute-done.22.refs_0_, bf16[256,256]{1,0:T(8,128)(2,1)S(1)} %collective-permute-done.23.refs_1_, ...), custom_call_target="tpu_custom_call" | custom-call | bytes 83886080 | tf_op jit(solution)/shard_map/final_dft/pallas_call | solution.py:74
  (36 shorter events, 0.4 us)
Async XLA Ops:
  5.6 19.4 %collective-permute-start.8 = (bf16[2,4,128,256]{3,2,1,0:T(8,128)(2,1)}, bf16[2,4,128,256]{3,2,1,0:T(8,128)(2,1)S(1)}, u32[]{:S(2)}, u32[]{:S(2)}) collective-permute-start(bf16[2,4,128,256]{3,2,1,0:T(8,128)(2,1)} %get-tuple-element.65), channel_id=1, source_target_pairs={{0,2},{2,0},{1,3},{3,1},{4,6},{6,4},{5,7},{7,5},{8,10},{10,8},{9,1... | collective-permute-start | bytes 1572872 | tf_op jit(solution)/shard_map/ppermute | solution.py:439
  8.6 8.0 %collective-permute-start = (bf16[128,256]{1,0:T(8,128)(2,1)}, bf16[128,256]{1,0:T(8,128)(2,1)S(1)}, u32[]{:S(2)}, u32[]{:S(2)}) collective-permute-start(bf16[128,256]{1,0:T(8,128)(2,1)} %get-tuple-element.55), channel_id=1, source_target_pairs={{0,12},{4,8},{8,4},{12,0},{1,13},{5,9},{9,5},{13,1},{2,14},{6,10},... | collective-permute-start | bytes 196616 | tf_op jit(solution)/shard_map/ppermute | solution.py:439
  12.2 8.2 %collective-permute-start.1 = (bf16[128,256]{1,0:T(8,128)(2,1)}, bf16[128,256]{1,0:T(8,128)(2,1)S(1)}, u32[]{:S(2)}, u32[]{:S(2)}) collective-permute-start(bf16[128,256]{1,0:T(8,128)(2,1)} %get-tuple-element.56), channel_id=1, source_target_pairs={{0,8},{4,12},{8,0},{12,4},{1,9},{5,13},{9,1},{13,5},{2,10},{6,14},... | collective-permute-start | bytes 196616 | tf_op jit(solution)/shard_map/ppermute | solution.py:439
  12.2 8.2 %collective-permute-start.2 = (bf16[128,256]{1,0:T(8,128)(2,1)}, bf16[128,256]{1,0:T(8,128)(2,1)S(1)}, u32[]{:S(2)}, u32[]{:S(2)}) collective-permute-start(bf16[128,256]{1,0:T(8,128)(2,1)} %get-tuple-element.57), channel_id=1, source_target_pairs={{0,4},{4,0},{8,12},{12,8},{1,5},{5,1},{9,13},{13,9},{2,6},{6,2},{1... | collective-permute-start | bytes 196616 | tf_op jit(solution)/shard_map/ppermute | solution.py:439
  12.9 9.0 %collective-permute-start.5 = (bf16[128,256]{1,0:T(8,128)(2,1)}, bf16[128,256]{1,0:T(8,128)(2,1)S(1)}, u32[]{:S(2)}, u32[]{:S(2)}) collective-permute-start(bf16[128,256]{1,0:T(8,128)(2,1)} %get-tuple-element.61), channel_id=1, source_target_pairs={{0,12},{4,8},{8,4},{12,0},{1,13},{5,9},{9,5},{13,1},{2,14},{6,10},... | collective-permute-start | bytes 196616 | tf_op jit(solution)/shard_map/ppermute | solution.py:439
  16.6 6.8 %collective-permute-start.6 = (bf16[128,256]{1,0:T(8,128)(2,1)}, bf16[128,256]{1,0:T(8,128)(2,1)S(1)}, u32[]{:S(2)}, u32[]{:S(2)}) collective-permute-start(bf16[128,256]{1,0:T(8,128)(2,1)} %get-tuple-element.62), channel_id=1, source_target_pairs={{0,8},{4,12},{8,0},{12,4},{1,9},{5,13},{9,1},{13,5},{2,10},{6,14},... | collective-permute-start | bytes 196616 | tf_op jit(solution)/shard_map/ppermute | solution.py:439
  20.4 4.5 %collective-permute-start.7 = (bf16[128,256]{1,0:T(8,128)(2,1)}, bf16[128,256]{1,0:T(8,128)(2,1)S(1)}, u32[]{:S(2)}, u32[]{:S(2)}) collective-permute-start(bf16[128,256]{1,0:T(8,128)(2,1)} %get-tuple-element.63), channel_id=1, source_target_pairs={{0,4},{4,0},{8,12},{12,8},{1,5},{5,1},{9,13},{13,9},{2,6},{6,2},{1... | collective-permute-start | bytes 196616 | tf_op jit(solution)/shard_map/ppermute | solution.py:439
  20.4 0.8 copy-start.7
  21.3 7.7 %collective-permute-start.3 = (bf16[16,32,256]{2,1,0:T(8,128)(2,1)S(1)}, bf16[16,32,256]{2,1,0:T(8,128)(2,1)S(1)}, u32[]{:S(2)}, u32[]{:S(2)}) collective-permute-start(bf16[16,32,256]{2,1,0:T(8,128)(2,1)S(1)} %pack_0.1.refs_0_), channel_id=1, source_target_pairs={{0,2},{2,0},{1,3},{3,1},{4,6},{6,4},{5,7},{7,5},{8,10},{10,8},{9,1... | collective-permute-start | bytes 786440 | tf_op jit(solution)/shard_map/ppermute | solution.py:439
  24.9 0.8 copy-start.6
  25.8 9.0 %collective-permute-start.9 = (bf16[16,32,256]{2,1,0:T(8,128)(2,1)S(1)}, bf16[16,32,256]{2,1,0:T(8,128)(2,1)S(1)}, u32[]{:S(2)}, u32[]{:S(2)}) collective-permute-start(bf16[16,32,256]{2,1,0:T(8,128)(2,1)S(1)} %pack_1.1.refs_0_), channel_id=1, source_target_pairs={{0,2},{2,0},{1,3},{3,1},{4,6},{6,4},{5,7},{7,5},{8,10},{10,8},{9,1... | collective-permute-start | bytes 786440 | tf_op jit(solution)/shard_map/ppermute | solution.py:439
  29.1 2.2 %copy-start = (bf16[2,32,128,256]{3,2,1,0:T(8,128)(2,1)S(1)}, bf16[2,32,128,256]{3,2,1,0:T(8,128)(2,1)}, u32[]{:S(2)}) copy-start(bf16[2,32,128,256]{3,2,1,0:T(8,128)(2,1)} %refs_2_.7) | copy-start | bytes 12582916
  32.1 21.4 %copy-start.2 = (bf16[1,4,1440,256]{3,2,1,0:T(8,128)(2,1)S(1)}, bf16[1,4,1440,256]{3,2,1,0:T(8,128)(2,1)}, u32[]{:S(2)}) copy-start(bf16[1,4,1440,256]{3,2,1,0:T(8,128)(2,1)} %param.8) | copy-start | bytes 8847364
  32.1 21.4 %copy-start.3 = (bf16[256,1440]{1,0:T(8,128)(2,1)S(1)}, bf16[256,1440]{1,0:T(8,128)(2,1)}, u32[]{:S(2)}) copy-start(bf16[256,1440]{1,0:T(8,128)(2,1)} %constant.9.clone.inv_ref) | copy-start | bytes 2211844
  32.1 21.4 %copy-start.5 = (bf16[1440,256]{1,0:T(8,128)(2,1)S(1)}, bf16[1440,256]{1,0:T(8,128)(2,1)}, u32[]{:S(2)}) copy-start(bf16[1440,256]{1,0:T(8,128)(2,1)} %constant.11.clone.back_ref) | copy-start | bytes 2211844
  32.2 5.9 %collective-permute-start.4 = (bf16[16,32,128]{2,1,0:T(8,128)(2,1)S(1)}, bf16[16,32,128]{2,1,0:T(8,128)(2,1)S(1)}, u32[]{:S(2)}, u32[]{:S(2)}) collective-permute-start(bf16[16,32,128]{2,1,0:T(8,128)(2,1)S(1)} %get-tuple-element.60), channel_id=1, source_target_pairs={{0,2},{2,0},{1,3},{3,1},{4,6},{6,4},{5,7},{7,5},{8,10},{10,8},{9,1... | collective-permute-start | bytes 393224 | tf_op jit(solution)/shard_map/ppermute | solution.py:439
  35.6 5.3 %collective-permute-start.10 = (bf16[16,32,128]{2,1,0:T(8,128)(2,1)S(1)}, bf16[16,32,128]{2,1,0:T(8,128)(2,1)S(1)}, u32[]{:S(2)}, u32[]{:S(2)}) collective-permute-start(bf16[16,32,128]{2,1,0:T(8,128)(2,1)S(1)} %get-tuple-element.71), channel_id=1, source_target_pairs={{0,2},{2,0},{1,3},{3,1},{4,6},{6,4},{5,7},{7,5},{8,10},{10,8},{9,1... | collective-permute-start | bytes 393224 | tf_op jit(solution)/shard_map/ppermute | solution.py:439
  38.1 15.4 %collective-permute-start.14 = (bf16[2,4,128,256]{3,2,1,0:T(8,128)(2,1)S(1)}, bf16[2,4,128,256]{3,2,1,0:T(8,128)(2,1)S(1)}, u32[]{:S(2)}, u32[]{:S(2)}) collective-permute-start(bf16[2,4,128,256]{3,2,1,0:T(8,128)(2,1)S(1)} %collective-permute-done.8), channel_id=1, source_target_pairs={{0,16},{16,0},{1,17},{17,1},{2,18},{18,2},{3,19},{19,3},{4,20},{20... | collective-permute-start | bytes 1572872 | tf_op jit(solution)/shard_map/ppermute | solution.py:439
  41.0 12.5 %collective-permute-start.15 = (bf16[2,4,128,256]{3,2,1,0:T(8,128)(2,1)S(1)}, bf16[2,4,128,256]{3,2,1,0:T(8,128)(2,1)S(1)}, u32[]{:S(2)}, u32[]{:S(2)}) collective-permute-start(bf16[2,4,128,256]{3,2,1,0:T(8,128)(2,1)S(1)} %get-tuple-element.79), channel_id=1, source_target_pairs={{0,2},{2,0},{1,3},{3,1},{4,6},{6,4},{5,7},{7,5},{8,10},{10,8},{9,1... | collective-permute-start | bytes 1572872 | tf_op jit(solution)/shard_map/ppermute | solution.py:439
  41.6 7.6 %collective-permute-start.11 = (bf16[256,256]{1,0:T(8,128)(2,1)S(1)}, bf16[256,256]{1,0:T(8,128)(2,1)S(1)}, u32[]{:S(2)}, u32[]{:S(2)}) collective-permute-start(bf16[256,256]{1,0:T(8,128)(2,1)S(1)} %get-tuple-element.72), channel_id=1, source_target_pairs={{0,12},{4,8},{8,4},{12,0},{1,13},{5,9},{9,5},{13,1},{2,14},{6,10},... | collective-permute-start | bytes 393224 | tf_op jit(solution)/shard_map/ppermute | solution.py:439
  46.3 7.3 %collective-permute-start.12 = (bf16[256,256]{1,0:T(8,128)(2,1)S(1)}, bf16[256,256]{1,0:T(8,128)(2,1)S(1)}, u32[]{:S(2)}, u32[]{:S(2)}) collective-permute-start(bf16[256,256]{1,0:T(8,128)(2,1)S(1)} %get-tuple-element.73), channel_id=1, source_target_pairs={{0,8},{4,12},{8,0},{12,4},{1,9},{5,13},{9,1},{13,5},{2,10},{6,14},... | collective-permute-start | bytes 393224 | tf_op jit(solution)/shard_map/ppermute | solution.py:439
  46.9 6.6 %collective-permute-start.13 = (bf16[256,256]{1,0:T(8,128)(2,1)S(1)}, bf16[256,256]{1,0:T(8,128)(2,1)S(1)}, u32[]{:S(2)}, u32[]{:S(2)}) collective-permute-start(bf16[256,256]{1,0:T(8,128)(2,1)S(1)} %get-tuple-element.74), channel_id=1, source_target_pairs={{0,4},{4,0},{8,12},{12,8},{1,5},{5,1},{9,13},{13,9},{2,6},{6,2},{1... | collective-permute-start | bytes 393224 | tf_op jit(solution)/shard_map/ppermute | solution.py:439
  53.6 17.9 %copy-start.1 = (bf16[2,32,128,256]{3,2,1,0:T(8,128)(2,1)S(1)}, bf16[2,32,128,256]{3,2,1,0:T(8,128)(2,1)}, u32[]{:S(2)}) copy-start(bf16[2,32,128,256]{3,2,1,0:T(8,128)(2,1)} %refs_2_.7) | copy-start | bytes 12582916
  57.7 10.9 %collective-permute-start.19 = (bf16[2,4,128,256]{3,2,1,0:T(8,128)(2,1)S(1)}, bf16[2,4,128,256]{3,2,1,0:T(8,128)(2,1)S(1)}, u32[]{:S(2)}, u32[]{:S(2)}) collective-permute-start(bf16[2,4,128,256]{3,2,1,0:T(8,128)(2,1)S(1)} %get-tuple-element.94), channel_id=1, source_target_pairs={{0,2},{2,0},{1,3},{3,1},{4,6},{6,4},{5,7},{7,5},{8,10},{10,8},{9,1... | collective-permute-start | bytes 1572872 | tf_op jit(solution)/shard_map/ppermute | solution.py:439
  59.0 6.9 %collective-permute-start.16 = (bf16[256,256]{1,0:T(8,128)(2,1)S(1)}, bf16[256,256]{1,0:T(8,128)(2,1)S(1)}, u32[]{:S(2)}, u32[]{:S(2)}) collective-permute-start(bf16[256,256]{1,0:T(8,128)(2,1)S(1)} %get-tuple-element.89), channel_id=1, source_target_pairs={{0,12},{4,8},{8,4},{12,0},{1,13},{5,9},{9,5},{13,1},{2,14},{6,10},... | collective-permute-start | bytes 393224 | tf_op jit(solution)/shard_map/ppermute | solution.py:439
  61.2 7.4 %collective-permute-start.17 = (bf16[256,256]{1,0:T(8,128)(2,1)S(1)}, bf16[256,256]{1,0:T(8,128)(2,1)S(1)}, u32[]{:S(2)}, u32[]{:S(2)}) collective-permute-start(bf16[256,256]{1,0:T(8,128)(2,1)S(1)} %get-tuple-element.90), channel_id=1, source_target_pairs={{0,8},{4,12},{8,0},{12,4},{1,9},{5,13},{9,1},{13,5},{2,10},{6,14},... | collective-permute-start | bytes 393224 | tf_op jit(solution)/shard_map/ppermute | solution.py:439
  61.2 7.4 %collective-permute-start.18 = (bf16[256,256]{1,0:T(8,128)(2,1)S(1)}, bf16[256,256]{1,0:T(8,128)(2,1)S(1)}, u32[]{:S(2)}, u32[]{:S(2)}) collective-permute-start(bf16[256,256]{1,0:T(8,128)(2,1)S(1)} %get-tuple-element.91), channel_id=1, source_target_pairs={{0,4},{4,0},{8,12},{12,8},{1,5},{5,1},{9,13},{13,9},{2,6},{6,2},{1... | collective-permute-start | bytes 393224 | tf_op jit(solution)/shard_map/ppermute | solution.py:439
  68.6 5.7 %collective-permute-start.20 = (bf16[5120,256]{1,0:T(8,128)(2,1)S(1)}, bf16[5120,256]{1,0:T(8,128)(2,1)S(1)}, u32[]{:S(2)}, u32[]{:S(2)}) collective-permute-start(bf16[5120,256]{1,0:T(8,128)(2,1)S(1)} %get-tuple-element.102.refs_3_.refs_0_), channel_id=1, source_target_pairs={{0,1},{1,0},{2,3},{3,2},{4,5},{5,4},{6,7},{7,6},{8,9},{9,8},{10,11... | collective-permute-start | bytes 7864328 | tf_op jit(solution)/shard_map/ppermute | solution.py:439
  68.6 5.7 %collective-permute-start.21 = (bf16[1024,256]{1,0:T(8,128)(2,1)S(1)}, bf16[1024,256]{1,0:T(8,128)(2,1)S(1)}, u32[]{:S(2)}, u32[]{:S(2)}) collective-permute-start(bf16[1024,256]{1,0:T(8,128)(2,1)S(1)} %bitcast.11), channel_id=1, source_target_pairs={{0,1},{1,0},{2,3},{3,2},{4,5},{5,4},{6,7},{7,6},{8,9},{9,8},{10,11... | collective-permute-start | bytes 1572872 | tf_op jit(solution)/shard_map/ppermute | solution.py:439
  69.3 8.0 %collective-permute-start.26 = (bf16[32,32,128]{2,1,0:T(8,128)(2,1)S(1)}, bf16[32,32,128]{2,1,0:T(8,128)(2,1)S(1)}, u32[]{:S(2)}, u32[]{:S(2)}) collective-permute-start(bf16[32,32,128]{2,1,0:T(8,128)(2,1)S(1)} %get-tuple-element.99.refs_0_.refs_2_), channel_id=1, source_target_pairs={{0,1},{1,0},{2,3},{3,2},{4,5},{5,4},{6,7},{7,6},{8,9},{9,8},{10,11... | collective-permute-start | bytes 786440 | tf_op jit(solution)/shard_map/ppermute | solution.py:507
  69.4 10.0 %collective-permute-start.27 = (bf16[32,32,128]{2,1,0:T(8,128)(2,1)S(1)}, bf16[32,32,128]{2,1,0:T(8,128)(2,1)S(1)}, u32[]{:S(2)}, u32[]{:S(2)}) collective-permute-start(bf16[32,32,128]{2,1,0:T(8,128)(2,1)S(1)} %get-tuple-element.100.refs_1_), channel_id=1, source_target_pairs={{0,3},{1,2},{2,1},{3,0},{4,7},{5,6},{6,5},{7,4},{8,11},{9,10},{10,... | collective-permute-start | bytes 786440 | tf_op jit(solution)/shard_map/ppermute | solution.py:507
  70.4 13.2 %collective-permute-start.25 = (bf16[32,32,128]{2,1,0:T(8,128)(2,1)S(1)}, bf16[32,32,128]{2,1,0:T(8,128)(2,1)S(1)}, u32[]{:S(2)}, u32[]{:S(2)}) collective-permute-start(bf16[32,32,128]{2,1,0:T(8,128)(2,1)S(1)} %get-tuple-element.100.refs_1_), channel_id=1, source_target_pairs={{0,2},{2,0},{1,3},{3,1},{4,6},{6,4},{5,7},{7,5},{8,10},{10,8},{9,1... | collective-permute-start | bytes 786440 | tf_op jit(solution)/shard_map/ppermute | solution.py:439
  75.0 12.3 %collective-permute-start.22 = (bf16[256,256]{1,0:T(8,128)(2,1)S(1)}, bf16[256,256]{1,0:T(8,128)(2,1)S(1)}, u32[]{:S(2)}, u32[]{:S(2)}) collective-permute-start(bf16[256,256]{1,0:T(8,128)(2,1)S(1)} %get-tuple-element.104), channel_id=1, source_target_pairs={{0,12},{4,8},{8,4},{12,0},{1,13},{5,9},{9,5},{13,1},{2,14},{6,10},... | collective-permute-start | bytes 393224 | tf_op jit(solution)/shard_map/ppermute | solution.py:439
  77.3 11.6 %collective-permute-start.23 = (bf16[256,256]{1,0:T(8,128)(2,1)S(1)}, bf16[256,256]{1,0:T(8,128)(2,1)S(1)}, u32[]{:S(2)}, u32[]{:S(2)}) collective-permute-start(bf16[256,256]{1,0:T(8,128)(2,1)S(1)} %get-tuple-element.105), channel_id=1, source_target_pairs={{0,8},{4,12},{8,0},{12,4},{1,9},{5,13},{9,1},{13,5},{2,10},{6,14},... | collective-permute-start | bytes 393224 | tf_op jit(solution)/shard_map/ppermute | solution.py:439
  77.3 11.6 %copy-start.4 = (bf16[1440,256]{1,0:T(8,128)(2,1)S(1)}, bf16[1440,256]{1,0:T(8,128)(2,1)}, u32[]{:S(2)}) copy-start(bf16[1440,256]{1,0:T(8,128)(2,1)} %constant.10.clone.table_ref) | copy-start | bytes 2211844
  77.3 11.6 %collective-permute-start.24 = (bf16[256,256]{1,0:T(8,128)(2,1)S(1)}, bf16[256,256]{1,0:T(8,128)(2,1)S(1)}, u32[]{:S(2)}, u32[]{:S(2)}) collective-permute-start(bf16[256,256]{1,0:T(8,128)(2,1)S(1)} %get-tuple-element.106), channel_id=1, source_target_pairs={{0,4},{4,0},{8,12},{12,8},{1,5},{5,1},{9,13},{13,9},{2,6},{6,2},{1... | collective-permute-start | bytes 393224 | tf_op jit(solution)/shard_map/ppermute | solution.py:439

commit v7 on v6

--- a/solution.py
+++ b/solution.py
@@ -488,7 +488,7 @@
         tall.append(rows)
         units.append(unit)
 
-    last = along("parts", last, *pieces[0])
+    last = along("parts", last, *(group[0] for group in pieces))
     first = fetch(after(units[0], *pieces[0], *pieces[1]))
     blocks, (last, first) = together(to_lat(merge(plan, pieces)), (last, first))
     loose = [unit for pair, unit in zip(last, first) for unit in (*pair, unit)]

time: 91.7 us -> 91.7 us (level)
  no operation moved by 1% of the time
where the time goes in v7:
time: 91.7 us; the launch traced here: 91.4 us
  starting transfers between devices  35.9 us (39%)
  waiting for transfers between devices  32.1 us (35%)
  Pallas kernels  18.7 us (20%)
  local copies, waits for them, and re-layouts  3.9 us (4%)
    ppermute x26, starting transfers between devices, hop(): return lax.ppermute(value, axis, [(i, i ^ s) for i in range(size)])  34.8 us
    ppermute x26, waiting for transfers between devices, hop(): return lax.ppermute(value, axis, [(i, i ^ s) for i in range(size)])  32.1 us
    pallas_call x12, Pallas kernels, call(): pl.pallas_call(body, in_specs=ins or [VMEM] * len(operands), out_specs=ou...  18.7 us
    unnamed x16, local copies, waits for them, and re-layouts  3.9 us
  transfers between devices with their start and end apart: 28, of which 14 were waited for; matrix products, arithmetic and copies ran while one was open for 0% of the time, Pallas kernels for 8%

profile of v7, /device:TPU:0, one launch (start us, length us, event | category | flops | bytes accessed | tf_op | source)
XLA Modules:
  0.0 91.4 jit_solution(4774777734988194713)
XLA Ops:
  0.6 4.9 %forward_dft.1 = (bf16[128,256]{1,0:T(8,128)(2,1)}, bf16[128,256]{1,0:T(8,128)(2,1)}, bf16[128,256]{1,0:T(8,128)(2,1)}, bf16[128,256]{1,0:T(8,128)(2,1)}, bf16[1...) custom-call(bf16[4,1440,256]{2,1,0:T(8,128)(2,1)} %bitcast.19, ...), custom_call_target="tpu_custom_call" | custom-call | bytes 6291456 | tf_op jit(solution)/shard_map/forward_dft/pallas_call | solution.py:74
  5.6 3.0 %collective-permute-start.8 = (bf16[2,4,128,256]{3,2,1,0:T(8,128)(2,1)}, bf16[2,4,128,256]{3,2,1,0:T(8,128)(2,1)S(1)}, u32[]{:S(2)}, u32[]{:S(2)}) collective-permute-start(bf16[2,4,128,256]{3,2,1,0:T(8,128)(2,1)} %get-tuple-element.65), channel_id=1, source_target_pairs={{0,2},{2,0},{1,3},{3,1},{4,6},{6,4},{5,7},{7,5},{8,10},{10,8},{9,1... | collective-permute-start | bytes 1572872 | tf_op jit(solution)/shard_map/ppermute | solution.py:439
  8.6 3.6 %collective-permute-start = (bf16[128,256]{1,0:T(8,128)(2,1)}, bf16[128,256]{1,0:T(8,128)(2,1)S(1)}, u32[]{:S(2)}, u32[]{:S(2)}) collective-permute-start(bf16[128,256]{1,0:T(8,128)(2,1)} %get-tuple-element.55), channel_id=1, source_target_pairs={{0,12},{4,8},{8,4},{12,0},{1,13},{5,9},{9,5},{13,1},{2,14},{6,10},... | collective-permute-start | bytes 196616 | tf_op jit(solution)/shard_map/ppermute | solution.py:439
  12.2 0.8 collective-permute-start.2
  12.9 3.6 %collective-permute-start.5 = (bf16[128,256]{1,0:T(8,128)(2,1)}, bf16[128,256]{1,0:T(8,128)(2,1)S(1)}, u32[]{:S(2)}, u32[]{:S(2)}) collective-permute-start(bf16[128,256]{1,0:T(8,128)(2,1)} %get-tuple-element.61), channel_id=1, source_target_pairs={{0,12},{4,8},{8,4},{12,0},{1,13},{5,9},{9,5},{13,1},{2,14},{6,10},... | collective-permute-start | bytes 196616 | tf_op jit(solution)/shard_map/ppermute | solution.py:439
  16.6 2.1 %collective-permute-start.6 = (bf16[128,256]{1,0:T(8,128)(2,1)}, bf16[128,256]{1,0:T(8,128)(2,1)S(1)}, u32[]{:S(2)}, u32[]{:S(2)}) collective-permute-start(bf16[128,256]{1,0:T(8,128)(2,1)} %get-tuple-element.62), channel_id=1, source_target_pairs={{0,8},{4,12},{8,0},{12,4},{1,9},{5,13},{9,1},{13,5},{2,10},{6,14},... | collective-permute-start | bytes 196616 | tf_op jit(solution)/shard_map/ppermute | solution.py:439
  18.7 1.8 %collective-permute-done.1.refs_1_ = bf16[128,256]{1,0:T(8,128)(2,1)S(1)} collective-permute-done((bf16[128,256]{1,0:T(8,128)(2,1)}, bf16[128,256]{1,0:T(8,128)(2,1)S(1)}, u32[]{:S(2)}, u32[]{:S(2)}) %collective-permute-start.1) | collective-permute-done | bytes 65568 | tf_op jit(solution)/shard_map/ppermute | solution.py:439
  20.4 0.8 copy-done.7
  21.3 0.6 collective-permute-start.3
  21.9 1.4 %collective-permute-done.6.refs_1_ = bf16[128,256]{1,0:T(8,128)(2,1)S(1)} collective-permute-done((bf16[128,256]{1,0:T(8,128)(2,1)}, bf16[128,256]{1,0:T(8,128)(2,1)S(1)}, u32[]{:S(2)}, u32[]{:S(2)}) %collective-permute-start.6) | collective-permute-done | bytes 65568 | tf_op jit(solution)/shard_map/ppermute | solution.py:439
  23.3 1.6 %collective-permute-done.7.refs_2_ = bf16[128,256]{1,0:T(8,128)(2,1)S(1)} collective-permute-done((bf16[128,256]{1,0:T(8,128)(2,1)}, bf16[128,256]{1,0:T(8,128)(2,1)S(1)}, u32[]{:S(2)}, u32[]{:S(2)}) %collective-permute-start.7) | collective-permute-done | bytes 65568 | tf_op jit(solution)/shard_map/ppermute | solution.py:439
  24.9 0.8 copy-done.6
  25.8 0.6 collective-permute-start.9
  26.4 2.7 %collective-permute-done.3.refs_1_ = bf16[16,32,256]{2,1,0:T(8,128)(2,1)S(1)} collective-permute-done((bf16[16,32,256]{2,1,0:T(8,128)(2,1)S(1)}, bf16[16,32,256]{2,1,0:T(8,128)(2,1)S(1)}, u32[]{:S(2)}, u32[]{:S(2)}) %collective-permute-start.3) | collective-permute-done | bytes 262176 | tf_op jit(solution)/shard_map/ppermute | solution.py:439
  29.1 2.2 %copy-done = bf16[2,32,128,256]{3,2,1,0:T(8,128)(2,1)S(1)} copy-done((bf16[2,32,128,256]{3,2,1,0:T(8,128)(2,1)S(1)}, bf16[2,32,128,256]{3,2,1,0:T(8,128)(2,1)}, u32[]{:S(2)}) %copy-start) | copy-done | bytes 4194328
  31.2 0.9 mix_forward_0.1
  32.2 0.6 collective-permute-start.4
  32.8 2.0 %collective-permute-done.9.refs_1_ = bf16[16,32,256]{2,1,0:T(8,128)(2,1)S(1)} collective-permute-done((bf16[16,32,256]{2,1,0:T(8,128)(2,1)S(1)}, bf16[16,32,256]{2,1,0:T(8,128)(2,1)S(1)}, u32[]{:S(2)}, u32[]{:S(2)}) %collective-permute-start.9) | collective-permute-done | bytes 262176 | tf_op jit(solution)/shard_map/ppermute | solution.py:439
  34.8 0.9 mix_forward_1.1
  35.6 0.6 collective-permute-start.10
  36.2 1.5 %collective-permute-start.14 = (bf16[2,4,128,256]{3,2,1,0:T(8,128)(2,1)S(1)}, bf16[2,4,128,256]{3,2,1,0:T(8,128)(2,1)S(1)}, u32[]{:S(2)}, u32[]{:S(2)}) collective-permute-start(bf16[2,4,128,256]{3,2,1,0:T(8,128)(2,1)S(1)} %collective-permute-done.8), channel_id=1, source_target_pairs={{0,16},{16,0},{1,17},{17,1},{2,18},{18,2},{3,19},{19,3},{4,20},{20... | collective-permute-start | bytes 1572872 | tf_op jit(solution)/shard_map/ppermute | solution.py:439
  37.8 0.3 collective-permute-done.4.refs_1_
  38.1 2.9 %collective-permute-done.10.refs_3_ = bf16[16,32,128]{2,1,0:T(8,128)(2,1)S(1)} collective-permute-done((bf16[16,32,128]{2,1,0:T(8,128)(2,1)S(1)}, bf16[16,32,128]{2,1,0:T(8,128)(2,1)S(1)}, u32[]{:S(2)}, u32[]{:S(2)}) %collective-permute-start.10) | collective-permute-done | bytes 131104 | tf_op jit(solution)/shard_map/ppermute | solution.py:439
  41.0 0.5 collective-permute-start.15
  41.6 4.6 %collective-permute-start.11 = (bf16[256,256]{1,0:T(8,128)(2,1)S(1)}, bf16[256,256]{1,0:T(8,128)(2,1)S(1)}, u32[]{:S(2)}, u32[]{:S(2)}) collective-permute-start(bf16[256,256]{1,0:T(8,128)(2,1)S(1)} %get-tuple-element.72), channel_id=1, source_target_pairs={{0,12},{4,8},{8,4},{12,0},{1,13},{5,9},{9,5},{13,1},{2,14},{6,10},... | collective-permute-start | bytes 393224 | tf_op jit(solution)/shard_map/ppermute | solution.py:439
  46.3 0.7 collective-permute-start.12
  46.9 0.3 collective-permute-start.13
  47.2 2.1 %collective-permute-done.11.refs_0_ = bf16[256,256]{1,0:T(8,128)(2,1)S(1)} collective-permute-done((bf16[256,256]{1,0:T(8,128)(2,1)S(1)}, bf16[256,256]{1,0:T(8,128)(2,1)S(1)}, u32[]{:S(2)}, u32[]{:S(2)}) %collective-permute-start.11) | collective-permute-done | bytes 131104 | tf_op jit(solution)/shard_map/ppermute | solution.py:439
  49.3 4.2 %collective-permute-done.12.refs_1_ = bf16[256,256]{1,0:T(8,128)(2,1)S(1)} collective-permute-done((bf16[256,256]{1,0:T(8,128)(2,1)S(1)}, bf16[256,256]{1,0:T(8,128)(2,1)S(1)}, u32[]{:S(2)}, u32[]{:S(2)}) %collective-permute-start.12) | collective-permute-done | bytes 131104 | tf_op jit(solution)/shard_map/ppermute | solution.py:439
  53.6 4.1 %middle.1 = (bf16[256,256]{1,0:T(8,128)(2,1)S(1)}, bf16[256,256]{1,0:T(8,128)(2,1)S(1)}, bf16[256,256]{1,0:T(8,128)(2,1)S(1)}, bf16[256,256]{1,0:T(8,128)(2,1)S(1)}, bf16[5120,256]{1,0:T(8,128)(2,1)S(1)}) custom-call(bf16[4,1440,256]{2,1,0:T(8,128)(2,1)S(1)} %bitcast.9, bf16[1440,256]{1,0:T(8,128)(2,1)S(1)} %copy-done.5, bf16[256,1440]{1,0:T(8,128)(2,1)S(1)} %copy-done.3, ...), custom_call_target="tpu_custom_call" | custom-call | bytes 12582912 | tf_op jit(solution)/shard_map/middle/pallas_call | solution.py:74
  57.7 1.3 %collective-permute-start.19 = (bf16[2,4,128,256]{3,2,1,0:T(8,128)(2,1)S(1)}, bf16[2,4,128,256]{3,2,1,0:T(8,128)(2,1)S(1)}, u32[]{:S(2)}, u32[]{:S(2)}) collective-permute-start(bf16[2,4,128,256]{3,2,1,0:T(8,128)(2,1)S(1)} %get-tuple-element.94), channel_id=1, source_target_pairs={{0,2},{2,0},{1,3},{3,1},{4,6},{6,4},{5,7},{7,5},{8,10},{10,8},{9,1... | collective-permute-start | bytes 1572872 | tf_op jit(solution)/shard_map/ppermute | solution.py:439
  59.0 2.2 %collective-permute-start.16 = (bf16[256,256]{1,0:T(8,128)(2,1)S(1)}, bf16[256,256]{1,0:T(8,128)(2,1)S(1)}, u32[]{:S(2)}, u32[]{:S(2)}) collective-permute-start(bf16[256,256]{1,0:T(8,128)(2,1)S(1)} %get-tuple-element.89), channel_id=1, source_target_pairs={{0,12},{4,8},{8,4},{12,0},{1,13},{5,9},{9,5},{13,1},{2,14},{6,10},... | collective-permute-start | bytes 393224 | tf_op jit(solution)/shard_map/ppermute | solution.py:439
  61.2 2.2 %collective-permute-start.18 = (bf16[256,256]{1,0:T(8,128)(2,1)S(1)}, bf16[256,256]{1,0:T(8,128)(2,1)S(1)}, u32[]{:S(2)}, u32[]{:S(2)}) collective-permute-start(bf16[256,256]{1,0:T(8,128)(2,1)S(1)} %get-tuple-element.91), channel_id=1, source_target_pairs={{0,4},{4,0},{8,12},{12,8},{1,5},{5,1},{9,13},{13,9},{2,6},{6,2},{1... | collective-permute-start | bytes 393224 | tf_op jit(solution)/shard_map/ppermute | solution.py:439
  63.4 2.5 %collective-permute-done.16.refs_0_ = bf16[256,256]{1,0:T(8,128)(2,1)S(1)} collective-permute-done((bf16[256,256]{1,0:T(8,128)(2,1)S(1)}, bf16[256,256]{1,0:T(8,128)(2,1)S(1)}, u32[]{:S(2)}, u32[]{:S(2)}) %collective-permute-start.16) | collective-permute-done | bytes 131104 | tf_op jit(solution)/shard_map/ppermute | solution.py:439
  65.9 2.7 %collective-permute-done.17.refs_1_ = bf16[256,256]{1,0:T(8,128)(2,1)S(1)} collective-permute-done((bf16[256,256]{1,0:T(8,128)(2,1)S(1)}, bf16[256,256]{1,0:T(8,128)(2,1)S(1)}, u32[]{:S(2)}, u32[]{:S(2)}) %collective-permute-start.17) | collective-permute-done | bytes 131104 | tf_op jit(solution)/shard_map/ppermute | solution.py:439
  68.6 0.5 collective-permute-start.21
  69.1 0.2 pack_gradients.1
  69.4 1.0 %collective-permute-start.27 = (bf16[32,32,128]{2,1,0:T(8,128)(2,1)S(1)}, bf16[32,32,128]{2,1,0:T(8,128)(2,1)S(1)}, u32[]{:S(2)}, u32[]{:S(2)}) collective-permute-start(bf16[32,32,128]{2,1,0:T(8,128)(2,1)S(1)} %get-tuple-element.100.refs_1_), channel_id=1, source_target_pairs={{0,3},{1,2},{2,1},{3,0},{4,7},{5,6},{6,5},{7,4},{8,11},{9,10},{10,... | collective-permute-start | bytes 786440 | tf_op jit(solution)/shard_map/ppermute | solution.py:507
  70.4 1.1 %collective-permute-start.25 = (bf16[32,32,128]{2,1,0:T(8,128)(2,1)S(1)}, bf16[32,32,128]{2,1,0:T(8,128)(2,1)S(1)}, u32[]{:S(2)}, u32[]{:S(2)}) collective-permute-start(bf16[32,32,128]{2,1,0:T(8,128)(2,1)S(1)} %get-tuple-element.100.refs_1_), channel_id=1, source_target_pairs={{0,2},{2,0},{1,3},{3,1},{4,6},{6,4},{5,7},{7,5},{8,10},{10,8},{9,1... | collective-permute-start | bytes 786440 | tf_op jit(solution)/shard_map/ppermute | solution.py:439
  71.5 0.7 mix_backward_own.1.refs_5_
  72.2 2.1 %collective-permute-done.21.refs_4_ = bf16[1024,256]{1,0:T(8,128)(2,1)S(1)} collective-permute-done((bf16[1024,256]{1,0:T(8,128)(2,1)S(1)}, bf16[1024,256]{1,0:T(8,128)(2,1)S(1)}, u32[]{:S(2)}, u32[]{:S(2)}) %collective-permute-start.21) | collective-permute-done | bytes 524320 | tf_op jit(solution)/shard_map/ppermute | solution.py:439
  74.2 0.7 mix_backward.1
  75.0 2.3 %collective-permute-start.22 = (bf16[256,256]{1,0:T(8,128)(2,1)S(1)}, bf16[256,256]{1,0:T(8,128)(2,1)S(1)}, u32[]{:S(2)}, u32[]{:S(2)}) collective-permute-start(bf16[256,256]{1,0:T(8,128)(2,1)S(1)} %get-tuple-element.104), channel_id=1, source_target_pairs={{0,12},{4,8},{8,4},{12,0},{1,13},{5,9},{9,5},{13,1},{2,14},{6,10},... | collective-permute-start | bytes 393224 | tf_op jit(solution)/shard_map/ppermute | solution.py:439
  77.3 2.2 %collective-permute-start.24 = (bf16[256,256]{1,0:T(8,128)(2,1)S(1)}, bf16[256,256]{1,0:T(8,128)(2,1)S(1)}, u32[]{:S(2)}, u32[]{:S(2)}) collective-permute-start(bf16[256,256]{1,0:T(8,128)(2,1)S(1)} %get-tuple-element.106), channel_id=1, source_target_pairs={{0,4},{4,0},{8,12},{12,8},{1,5},{5,1},{9,13},{13,9},{2,6},{6,2},{1... | collective-permute-start | bytes 393224 | tf_op jit(solution)/shard_map/ppermute | solution.py:439
  79.5 4.2 %collective-permute-done.25.refs_3_ = bf16[32,32,128]{2,1,0:T(8,128)(2,1)S(1)} collective-permute-done((bf16[32,32,128]{2,1,0:T(8,128)(2,1)S(1)}, bf16[32,32,128]{2,1,0:T(8,128)(2,1)S(1)}, u32[]{:S(2)}, u32[]{:S(2)}) %collective-permute-start.25) | collective-permute-done | bytes 262176 | tf_op jit(solution)/shard_map/ppermute | solution.py:439
  83.6 3.7 %weight_gradient.1 = f32[2,32,128,256]{3,2,1,0:T(8,128)} custom-call(bf16[5120,256]{1,0:T(8,128)(2,1)S(1)} %get-tuple-element.102.refs_3_.refs_0_, bf16[5120,256]{1,0:T(8,128)(2,1)S(1)} %collective-permute-done.20.refs_3_.refs_1_, bf16[32,32,128]{2,1,0:T(8,128)(2,1)S(1)} %get-tuple-element.99.refs_0_.refs_2_, ...), custom_call_target="tpu_custom_call" | custom-call | bytes 2097152 | tf_op jit(solution)/shard_map/weight_gradient/pallas_call | solution.py:74
  87.3 1.6 %collective-permute-done.23.refs_1_ = bf16[256,256]{1,0:T(8,128)(2,1)S(1)} collective-permute-done((bf16[256,256]{1,0:T(8,128)(2,1)S(1)}, bf16[256,256]{1,0:T(8,128)(2,1)S(1)}, u32[]{:S(2)}, u32[]{:S(2)}) %collective-permute-start.23) | collective-permute-done | bytes 131104 | tf_op jit(solution)/shard_map/ppermute | solution.py:439
  88.9 2.4 %final_dft.1 = bf16[4,1440,256]{2,1,0:T(8,128)(2,1)} custom-call(bf16[4,1440,256]{2,1,0:T(8,128)(2,1)S(1)} %bitcast.10, bf16[1440,256]{1,0:T(8,128)(2,1)S(1)} %copy-done.4, bf16[256,256]{1,0:T(8,128)(2,1)S(1)} %collective-permute-done.22.refs_0_, bf16[256,256]{1,0:T(8,128)(2,1)S(1)} %collective-permute-done.23.refs_1_, ...), custom_call_target="tpu_custom_call" | custom-call | bytes 83886080 | tf_op jit(solution)/shard_map/final_dft/pallas_call | solution.py:74
  (36 shorter events, 0.4 us)
Async XLA Ops:
  5.6 19.4 %collective-permute-start.8 = (bf16[2,4,128,256]{3,2,1,0:T(8,128)(2,1)}, bf16[2,4,128,256]{3,2,1,0:T(8,128)(2,1)S(1)}, u32[]{:S(2)}, u32[]{:S(2)}) collective-permute-start(bf16[2,4,128,256]{3,2,1,0:T(8,128)(2,1)} %get-tuple-element.65), channel_id=1, source_target_pairs={{0,2},{2,0},{1,3},{3,1},{4,6},{6,4},{5,7},{7,5},{8,10},{10,8},{9,1... | collective-permute-start | bytes 1572872 | tf_op jit(solution)/shard_map/ppermute | solution.py:439
  8.6 8.0 %collective-permute-start = (bf16[128,256]{1,0:T(8,128)(2,1)}, bf16[128,256]{1,0:T(8,128)(2,1)S(1)}, u32[]{:S(2)}, u32[]{:S(2)}) collective-permute-start(bf16[128,256]{1,0:T(8,128)(2,1)} %get-tuple-element.55), channel_id=1, source_target_pairs={{0,12},{4,8},{8,4},{12,0},{1,13},{5,9},{9,5},{13,1},{2,14},{6,10},... | collective-permute-start | bytes 196616 | tf_op jit(solution)/shard_map/ppermute | solution.py:439
  12.2 8.2 %collective-permute-start.1 = (bf16[128,256]{1,0:T(8,128)(2,1)}, bf16[128,256]{1,0:T(8,128)(2,1)S(1)}, u32[]{:S(2)}, u32[]{:S(2)}) collective-permute-start(bf16[128,256]{1,0:T(8,128)(2,1)} %get-tuple-element.56), channel_id=1, source_target_pairs={{0,8},{4,12},{8,0},{12,4},{1,9},{5,13},{9,1},{13,5},{2,10},{6,14},... | collective-permute-start | bytes 196616 | tf_op jit(solution)/shard_map/ppermute | solution.py:439
  12.2 8.2 %collective-permute-start.2 = (bf16[128,256]{1,0:T(8,128)(2,1)}, bf16[128,256]{1,0:T(8,128)(2,1)S(1)}, u32[]{:S(2)}, u32[]{:S(2)}) collective-permute-start(bf16[128,256]{1,0:T(8,128)(2,1)} %get-tuple-element.57), channel_id=1, source_target_pairs={{0,4},{4,0},{8,12},{12,8},{1,5},{5,1},{9,13},{13,9},{2,6},{6,2},{1... | collective-permute-start | bytes 196616 | tf_op jit(solution)/shard_map/ppermute | solution.py:439
  12.9 9.0 %collective-permute-start.5 = (bf16[128,256]{1,0:T(8,128)(2,1)}, bf16[128,256]{1,0:T(8,128)(2,1)S(1)}, u32[]{:S(2)}, u32[]{:S(2)}) collective-permute-start(bf16[128,256]{1,0:T(8,128)(2,1)} %get-tuple-element.61), channel_id=1, source_target_pairs={{0,12},{4,8},{8,4},{12,0},{1,13},{5,9},{9,5},{13,1},{2,14},{6,10},... | collective-permute-start | bytes 196616 | tf_op jit(solution)/shard_map/ppermute | solution.py:439
  16.6 6.8 %collective-permute-start.6 = (bf16[128,256]{1,0:T(8,128)(2,1)}, bf16[128,256]{1,0:T(8,128)(2,1)S(1)}, u32[]{:S(2)}, u32[]{:S(2)}) collective-permute-start(bf16[128,256]{1,0:T(8,128)(2,1)} %get-tuple-element.62), channel_id=1, source_target_pairs={{0,8},{4,12},{8,0},{12,4},{1,9},{5,13},{9,1},{13,5},{2,10},{6,14},... | collective-permute-start | bytes 196616 | tf_op jit(solution)/shard_map/ppermute | solution.py:439
  20.4 4.5 %collective-permute-start.7 = (bf16[128,256]{1,0:T(8,128)(2,1)}, bf16[128,256]{1,0:T(8,128)(2,1)S(1)}, u32[]{:S(2)}, u32[]{:S(2)}) collective-permute-start(bf16[128,256]{1,0:T(8,128)(2,1)} %get-tuple-element.63), channel_id=1, source_target_pairs={{0,4},{4,0},{8,12},{12,8},{1,5},{5,1},{9,13},{13,9},{2,6},{6,2},{1... | collective-permute-start | bytes 196616 | tf_op jit(solution)/shard_map/ppermute | solution.py:439
  20.4 0.8 copy-start.7
  21.3 7.7 %collective-permute-start.3 = (bf16[16,32,256]{2,1,0:T(8,128)(2,1)S(1)}, bf16[16,32,256]{2,1,0:T(8,128)(2,1)S(1)}, u32[]{:S(2)}, u32[]{:S(2)}) collective-permute-start(bf16[16,32,256]{2,1,0:T(8,128)(2,1)S(1)} %pack_0.1.refs_0_), channel_id=1, source_target_pairs={{0,2},{2,0},{1,3},{3,1},{4,6},{6,4},{5,7},{7,5},{8,10},{10,8},{9,1... | collective-permute-start | bytes 786440 | tf_op jit(solution)/shard_map/ppermute | solution.py:439
  24.9 0.8 copy-start.6
  25.8 9.0 %collective-permute-start.9 = (bf16[16,32,256]{2,1,0:T(8,128)(2,1)S(1)}, bf16[16,32,256]{2,1,0:T(8,128)(2,1)S(1)}, u32[]{:S(2)}, u32[]{:S(2)}) collective-permute-start(bf16[16,32,256]{2,1,0:T(8,128)(2,1)S(1)} %pack_1.1.refs_0_), channel_id=1, source_target_pairs={{0,2},{2,0},{1,3},{3,1},{4,6},{6,4},{5,7},{7,5},{8,10},{10,8},{9,1... | collective-permute-start | bytes 786440 | tf_op jit(solution)/shard_map/ppermute | solution.py:439
  29.1 2.2 %copy-start = (bf16[2,32,128,256]{3,2,1,0:T(8,128)(2,1)S(1)}, bf16[2,32,128,256]{3,2,1,0:T(8,128)(2,1)}, u32[]{:S(2)}) copy-start(bf16[2,32,128,256]{3,2,1,0:T(8,128)(2,1)} %refs_2_.7) | copy-start | bytes 12582916
  32.1 21.4 %copy-start.2 = (bf16[1,4,1440,256]{3,2,1,0:T(8,128)(2,1)S(1)}, bf16[1,4,1440,256]{3,2,1,0:T(8,128)(2,1)}, u32[]{:S(2)}) copy-start(bf16[1,4,1440,256]{3,2,1,0:T(8,128)(2,1)} %param.8) | copy-start | bytes 8847364
  32.1 21.4 %copy-start.3 = (bf16[256,1440]{1,0:T(8,128)(2,1)S(1)}, bf16[256,1440]{1,0:T(8,128)(2,1)}, u32[]{:S(2)}) copy-start(bf16[256,1440]{1,0:T(8,128)(2,1)} %constant.9.clone.inv_ref) | copy-start | bytes 2211844
  32.1 21.4 %copy-start.5 = (bf16[1440,256]{1,0:T(8,128)(2,1)S(1)}, bf16[1440,256]{1,0:T(8,128)(2,1)}, u32[]{:S(2)}) copy-start(bf16[1440,256]{1,0:T(8,128)(2,1)} %constant.11.clone.back_ref) | copy-start | bytes 2211844
  32.2 5.9 %collective-permute-start.4 = (bf16[16,32,128]{2,1,0:T(8,128)(2,1)S(1)}, bf16[16,32,128]{2,1,0:T(8,128)(2,1)S(1)}, u32[]{:S(2)}, u32[]{:S(2)}) collective-permute-start(bf16[16,32,128]{2,1,0:T(8,128)(2,1)S(1)} %get-tuple-element.60), channel_id=1, source_target_pairs={{0,2},{2,0},{1,3},{3,1},{4,6},{6,4},{5,7},{7,5},{8,10},{10,8},{9,1... | collective-permute-start | bytes 393224 | tf_op jit(solution)/shard_map/ppermute | solution.py:439
  35.6 5.3 %collective-permute-start.10 = (bf16[16,32,128]{2,1,0:T(8,128)(2,1)S(1)}, bf16[16,32,128]{2,1,0:T(8,128)(2,1)S(1)}, u32[]{:S(2)}, u32[]{:S(2)}) collective-permute-start(bf16[16,32,128]{2,1,0:T(8,128)(2,1)S(1)} %get-tuple-element.71), channel_id=1, source_target_pairs={{0,2},{2,0},{1,3},{3,1},{4,6},{6,4},{5,7},{7,5},{8,10},{10,8},{9,1... | collective-permute-start | bytes 393224 | tf_op jit(solution)/shard_map/ppermute | solution.py:439
  36.2 17.3 %collective-permute-start.14 = (bf16[2,4,128,256]{3,2,1,0:T(8,128)(2,1)S(1)}, bf16[2,4,128,256]{3,2,1,0:T(8,128)(2,1)S(1)}, u32[]{:S(2)}, u32[]{:S(2)}) collective-permute-start(bf16[2,4,128,256]{3,2,1,0:T(8,128)(2,1)S(1)} %collective-permute-done.8), channel_id=1, source_target_pairs={{0,16},{16,0},{1,17},{17,1},{2,18},{18,2},{3,19},{19,3},{4,20},{20... | collective-permute-start | bytes 1572872 | tf_op jit(solution)/shard_map/ppermute | solution.py:439
  41.0 12.5 %collective-permute-start.15 = (bf16[2,4,128,256]{3,2,1,0:T(8,128)(2,1)S(1)}, bf16[2,4,128,256]{3,2,1,0:T(8,128)(2,1)S(1)}, u32[]{:S(2)}, u32[]{:S(2)}) collective-permute-start(bf16[2,4,128,256]{3,2,1,0:T(8,128)(2,1)S(1)} %get-tuple-element.79), channel_id=1, source_target_pairs={{0,2},{2,0},{1,3},{3,1},{4,6},{6,4},{5,7},{7,5},{8,10},{10,8},{9,1... | collective-permute-start | bytes 1572872 | tf_op jit(solution)/shard_map/ppermute | solution.py:439
  41.6 7.6 %collective-permute-start.11 = (bf16[256,256]{1,0:T(8,128)(2,1)S(1)}, bf16[256,256]{1,0:T(8,128)(2,1)S(1)}, u32[]{:S(2)}, u32[]{:S(2)}) collective-permute-start(bf16[256,256]{1,0:T(8,128)(2,1)S(1)} %get-tuple-element.72), channel_id=1, source_target_pairs={{0,12},{4,8},{8,4},{12,0},{1,13},{5,9},{9,5},{13,1},{2,14},{6,10},... | collective-permute-start | bytes 393224 | tf_op jit(solution)/shard_map/ppermute | solution.py:439
  46.3 7.3 %collective-permute-start.12 = (bf16[256,256]{1,0:T(8,128)(2,1)S(1)}, bf16[256,256]{1,0:T(8,128)(2,1)S(1)}, u32[]{:S(2)}, u32[]{:S(2)}) collective-permute-start(bf16[256,256]{1,0:T(8,128)(2,1)S(1)} %get-tuple-element.73), channel_id=1, source_target_pairs={{0,8},{4,12},{8,0},{12,4},{1,9},{5,13},{9,1},{13,5},{2,10},{6,14},... | collective-permute-start | bytes 393224 | tf_op jit(solution)/shard_map/ppermute | solution.py:439
  46.9 6.6 %collective-permute-start.13 = (bf16[256,256]{1,0:T(8,128)(2,1)S(1)}, bf16[256,256]{1,0:T(8,128)(2,1)S(1)}, u32[]{:S(2)}, u32[]{:S(2)}) collective-permute-start(bf16[256,256]{1,0:T(8,128)(2,1)S(1)} %get-tuple-element.74), channel_id=1, source_target_pairs={{0,4},{4,0},{8,12},{12,8},{1,5},{5,1},{9,13},{13,9},{2,6},{6,2},{1... | collective-permute-start | bytes 393224 | tf_op jit(solution)/shard_map/ppermute | solution.py:439
  53.6 17.9 %copy-start.1 = (bf16[2,32,128,256]{3,2,1,0:T(8,128)(2,1)S(1)}, bf16[2,32,128,256]{3,2,1,0:T(8,128)(2,1)}, u32[]{:S(2)}) copy-start(bf16[2,32,128,256]{3,2,1,0:T(8,128)(2,1)} %refs_2_.7) | copy-start | bytes 12582916
  57.7 10.9 %collective-permute-start.19 = (bf16[2,4,128,256]{3,2,1,0:T(8,128)(2,1)S(1)}, bf16[2,4,128,256]{3,2,1,0:T(8,128)(2,1)S(1)}, u32[]{:S(2)}, u32[]{:S(2)}) collective-permute-start(bf16[2,4,128,256]{3,2,1,0:T(8,128)(2,1)S(1)} %get-tuple-element.94), channel_id=1, source_target_pairs={{0,2},{2,0},{1,3},{3,1},{4,6},{6,4},{5,7},{7,5},{8,10},{10,8},{9,1... | collective-permute-start | bytes 1572872 | tf_op jit(solution)/shard_map/ppermute | solution.py:439
  59.0 6.9 %collective-permute-start.16 = (bf16[256,256]{1,0:T(8,128)(2,1)S(1)}, bf16[256,256]{1,0:T(8,128)(2,1)S(1)}, u32[]{:S(2)}, u32[]{:S(2)}) collective-permute-start(bf16[256,256]{1,0:T(8,128)(2,1)S(1)} %get-tuple-element.89), channel_id=1, source_target_pairs={{0,12},{4,8},{8,4},{12,0},{1,13},{5,9},{9,5},{13,1},{2,14},{6,10},... | collective-permute-start | bytes 393224 | tf_op jit(solution)/shard_map/ppermute | solution.py:439
  61.2 7.4 %collective-permute-start.17 = (bf16[256,256]{1,0:T(8,128)(2,1)S(1)}, bf16[256,256]{1,0:T(8,128)(2,1)S(1)}, u32[]{:S(2)}, u32[]{:S(2)}) collective-permute-start(bf16[256,256]{1,0:T(8,128)(2,1)S(1)} %get-tuple-element.90), channel_id=1, source_target_pairs={{0,8},{4,12},{8,0},{12,4},{1,9},{5,13},{9,1},{13,5},{2,10},{6,14},... | collective-permute-start | bytes 393224 | tf_op jit(solution)/shard_map/ppermute | solution.py:439
  61.2 7.4 %collective-permute-start.18 = (bf16[256,256]{1,0:T(8,128)(2,1)S(1)}, bf16[256,256]{1,0:T(8,128)(2,1)S(1)}, u32[]{:S(2)}, u32[]{:S(2)}) collective-permute-start(bf16[256,256]{1,0:T(8,128)(2,1)S(1)} %get-tuple-element.91), channel_id=1, source_target_pairs={{0,4},{4,0},{8,12},{12,8},{1,5},{5,1},{9,13},{13,9},{2,6},{6,2},{1... | collective-permute-start | bytes 393224 | tf_op jit(solution)/shard_map/ppermute | solution.py:439
  68.6 5.7 %collective-permute-start.20 = (bf16[5120,256]{1,0:T(8,128)(2,1)S(1)}, bf16[5120,256]{1,0:T(8,128)(2,1)S(1)}, u32[]{:S(2)}, u32[]{:S(2)}) collective-permute-start(bf16[5120,256]{1,0:T(8,128)(2,1)S(1)} %get-tuple-element.102.refs_3_.refs_0_), channel_id=1, source_target_pairs={{0,1},{1,0},{2,3},{3,2},{4,5},{5,4},{6,7},{7,6},{8,9},{9,8},{10,11... | collective-permute-start | bytes 7864328 | tf_op jit(solution)/shard_map/ppermute | solution.py:439
  68.6 5.7 %collective-permute-start.21 = (bf16[1024,256]{1,0:T(8,128)(2,1)S(1)}, bf16[1024,256]{1,0:T(8,128)(2,1)S(1)}, u32[]{:S(2)}, u32[]{:S(2)}) collective-permute-start(bf16[1024,256]{1,0:T(8,128)(2,1)S(1)} %bitcast.11), channel_id=1, source_target_pairs={{0,1},{1,0},{2,3},{3,2},{4,5},{5,4},{6,7},{7,6},{8,9},{9,8},{10,11... | collective-permute-start | bytes 1572872 | tf_op jit(solution)/shard_map/ppermute | solution.py:439
  69.3 8.0 %collective-permute-start.26 = (bf16[32,32,128]{2,1,0:T(8,128)(2,1)S(1)}, bf16[32,32,128]{2,1,0:T(8,128)(2,1)S(1)}, u32[]{:S(2)}, u32[]{:S(2)}) collective-permute-start(bf16[32,32,128]{2,1,0:T(8,128)(2,1)S(1)} %get-tuple-element.99.refs_0_.refs_2_), channel_id=1, source_target_pairs={{0,1},{1,0},{2,3},{3,2},{4,5},{5,4},{6,7},{7,6},{8,9},{9,8},{10,11... | collective-permute-start | bytes 786440 | tf_op jit(solution)/shard_map/ppermute | solution.py:507
  69.4 10.0 %collective-permute-start.27 = (bf16[32,32,128]{2,1,0:T(8,128)(2,1)S(1)}, bf16[32,32,128]{2,1,0:T(8,128)(2,1)S(1)}, u32[]{:S(2)}, u32[]{:S(2)}) collective-permute-start(bf16[32,32,128]{2,1,0:T(8,128)(2,1)S(1)} %get-tuple-element.100.refs_1_), channel_id=1, source_target_pairs={{0,3},{1,2},{2,1},{3,0},{4,7},{5,6},{6,5},{7,4},{8,11},{9,10},{10,... | collective-permute-start | bytes 786440 | tf_op jit(solution)/shard_map/ppermute | solution.py:507
  70.4 13.2 %collective-permute-start.25 = (bf16[32,32,128]{2,1,0:T(8,128)(2,1)S(1)}, bf16[32,32,128]{2,1,0:T(8,128)(2,1)S(1)}, u32[]{:S(2)}, u32[]{:S(2)}) collective-permute-start(bf16[32,32,128]{2,1,0:T(8,128)(2,1)S(1)} %get-tuple-element.100.refs_1_), channel_id=1, source_target_pairs={{0,2},{2,0},{1,3},{3,1},{4,6},{6,4},{5,7},{7,5},{8,10},{10,8},{9,1... | collective-permute-start | bytes 786440 | tf_op jit(solution)/shard_map/ppermute | solution.py:439
  75.0 12.3 %collective-permute-start.22 = (bf16[256,256]{1,0:T(8,128)(2,1)S(1)}, bf16[256,256]{1,0:T(8,128)(2,1)S(1)}, u32[]{:S(2)}, u32[]{:S(2)}) collective-permute-start(bf16[256,256]{1,0:T(8,128)(2,1)S(1)} %get-tuple-element.104), channel_id=1, source_target_pairs={{0,12},{4,8},{8,4},{12,0},{1,13},{5,9},{9,5},{13,1},{2,14},{6,10},... | collective-permute-start | bytes 393224 | tf_op jit(solution)/shard_map/ppermute | solution.py:439
  77.3 11.6 %collective-permute-start.23 = (bf16[256,256]{1,0:T(8,128)(2,1)S(1)}, bf16[256,256]{1,0:T(8,128)(2,1)S(1)}, u32[]{:S(2)}, u32[]{:S(2)}) collective-permute-start(bf16[256,256]{1,0:T(8,128)(2,1)S(1)} %get-tuple-element.105), channel_id=1, source_target_pairs={{0,8},{4,12},{8,0},{12,4},{1,9},{5,13},{9,1},{13,5},{2,10},{6,14},... | collective-permute-start | bytes 393224 | tf_op jit(solution)/shard_map/ppermute | solution.py:439
  77.3 11.6 %copy-start.4 = (bf16[1440,256]{1,0:T(8,128)(2,1)S(1)}, bf16[1440,256]{1,0:T(8,128)(2,1)}, u32[]{:S(2)}) copy-start(bf16[1440,256]{1,0:T(8,128)(2,1)} %constant.10.clone.table_ref) | copy-start | bytes 2211844
  77.3 11.6 %collective-permute-start.24 = (bf16[256,256]{1,0:T(8,128)(2,1)S(1)}, bf16[256,256]{1,0:T(8,128)(2,1)S(1)}, u32[]{:S(2)}, u32[]{:S(2)}) collective-permute-start(bf16[256,256]{1,0:T(8,128)(2,1)S(1)} %get-tuple-element.106), channel_id=1, source_target_pairs={{0,4},{4,0},{8,12},{12,8},{1,5},{5,1},{9,13},{13,9},{2,6},{6,2},{1... | collective-permute-start | bytes 393224 | tf_op jit(solution)/shard_map/ppermute | solution.py:439
